TPU v7x, 32 devices: a whole 2x2x4 slice. The times are simulated.
32 devices in a mesh: group: 2 (over y), lat: 8 (over z, x), lon: 2 (over core).
Axes of the slice: x: 2, y: 2, z: 4, core: 2. Of those that a mesh axis runs over, the one named last changes fastest.
Arguments:
- tracers: float32 [8, 32, 32, 1152], P('group', None, 'lat', 'lon'), parts along dimension 0, may hold values from -6 to 6
- courant_lat: float32 [64, 32, 1152], P('group', 'lat', 'lon'), parts along dimension 0, may hold values from -0.45 to 0.45
- courant_lon: float32 [64, 32, 1152], P('group', 'lat', 'lon'), parts along dimension 0, may hold values from -0.45 to 0.45
- surface_flux: float32 [8, 32, 1152], P('group', 'lat', 'lon'), parts along dimension 0, may hold values from -6 to 6
- mixing: float32 [32, 32], replicated, may hold values from -1 to 1
- decay_rate: float32 [4, 32], replicated, may hold values from 0.05 to 1
- owners: int32 [16, 2, 18, 1], P(('group', 'lat'), 'lon'), parts along dimension 0, may hold values from 0 to 7; in each aligned block of 18 rows (0 to 17, 18 to 35, ..., all dimensions but the last counted through in order) at most 5 rows name the same one
- polar_mask: int32 [64], P(('group', 'lat')), parts along dimension 0, may hold values 0 or 1
Outputs:
- tracers_out: float32 [8, 32, 32, 1152], P('group', None, 'lat', 'lon'), parts along dimension 0
- owner_energy: float32 [16, 2], P(('group', 'lat'), 'lon'), parts along dimension 0
There are 2 independent parts, one for each index of `group`. A program takes and returns all parts, laid end to end along the dimension named above; an argument that names none is the same for every part. Nothing has to cross between parts.
Inputs may be any that keep to these rules, and one draw needn't show every extreme that they name: `owners`: the 18 blocks of one lat index and one lon index name one owner at most 5 times; in every draw some lat and lon index names one owner exactly 5 times.
All inputs are finite; a program needn't handle non-finite values. No bound on the sum of `polar_mask` on one device may be relied on, other than what follows from the above.
Results may differ from a plain program's by a relative error of at most 0.000073.
Values sent between devices are 32-bit elements; how exact they have to be, the bound alone decides.
No kernel may reach another device: no remote copies, remote signals or barrier semaphores. Data moves between devices by JAX's collectives and lax.ppermute only.
A program may use at most 128 MiB of HBM per device.

v0:
```python
import functools
import math

import jax
import jax.numpy as jnp
import numpy as np
from jax import lax
from jax.experimental import pallas as pl
from jax.experimental.pallas import tpu as pltpu
from jax.sharding import PartitionSpec as P

LANES = 128
BLOCK = 128
VMEM_BYTES = 6 * 1024 * 1024
RESULT_PIECES = 4
NEAR = 7.0 / 12.0
FAR = 1.0 / 12.0


def params():
    return pltpu.CompilerParams(vmem_limit_bytes=VMEM_BYTES)


def cost(flops, bytes_accessed):
    return pl.CostEstimate(flops=flops, bytes_accessed=bytes_accessed, transcendentals=0)


def split_high_low(value):
    high = value.astype(jnp.bfloat16)
    low = (value - high.astype(jnp.float32)).astype(jnp.bfloat16)
    return high, low


def split_table(table):
    high = table.astype(jnp.bfloat16.dtype)
    return high, (table - high.astype(np.float64)).astype(jnp.bfloat16.dtype)


def spectral_tables(length):
    radix = length // LANES
    pairs = (radix - 1) // 2
    spot = np.arange(LANES)[:, None]
    number = np.arange(LANES)[None, :]
    is_cosine = number <= LANES // 2
    wave = np.where(is_cosine, number, number - LANES // 2)
    angle = 2.0 * np.pi * ((spot * wave) % LANES) / LANES
    first = np.where(is_cosine, np.cos(angle), np.sin(angle))
    others, numbers = [], [radix * wave[0]]
    weights = [np.where((wave[0] == 0) | (wave[0] == LANES // 2), 1.0, 2.0) / length]
    for residue in range(1, pairs + 1):
        whole = residue + radix * number
        angle = 2.0 * np.pi * ((spot * whole) % length) / length
        cosine, sine = np.cos(angle), np.sin(angle)
        others.append(np.block([[cosine, -sine], [sine, cosine]]))
        folded = np.minimum(whole[0], length - whole[0])
        numbers += [folded, folded]
        weights.append(np.full(2 * LANES, 2.0 / length))
    others += [table.T for table in others]
    return np.concatenate([first, first.T]), np.concatenate(others), np.concatenate(numbers), np.concatenate(weights)


def pack_rows(first, second):
    return jnp.concatenate([first, second], axis=1)


def second_half(packed, sector):
    skip, shift = sector // LANES, sector % LANES
    segments = [packed[:, LANES * i : LANES * (i + 1)] for i in range(packed.shape[1] // LANES)]
    if shift == 0:
        return jnp.concatenate(segments[skip:], axis=1)
    turned = [pltpu.roll(segment, LANES - shift, 1) for segment in segments[skip:]]
    lane = lax.broadcasted_iota(jnp.int32, turned[0].shape, 1)
    parts = [jnp.where(lane < LANES - shift, turned[i], turned[min(i + 1, len(turned) - 1)]) for i in range(len(turned))]
    return jnp.concatenate(parts, axis=1)


def pack_kernel(split, rows, levels, tracer_hbm, courant_hbm, *refs):
    up_refs, down_refs = refs[: len(split)], refs[len(split) : 2 * len(split)]
    tracer_ref, courant_ref, sems = refs[2 * len(split) :]
    tracer_count = tracer_ref.shape[0]
    copies = [pltpu.make_async_copy(courant_hbm, courant_ref, sems.at[tracer_count])]
    copies += [pltpu.make_async_copy(tracer_hbm.at[t], tracer_ref.at[t], sems.at[t]) for t in range(tracer_count)]
    for copy in copies:
        copy.start()
    copies[0].wait()
    courant = courant_ref[:, 0, :]
    place = levels * (split[0][1] - split[0][0])
    down_refs[0][place : place + levels // 2, :] = pack_rows(courant[: levels // 2], courant[levels // 2 :])
    for (begin, end), up_ref, down_ref in zip(split, up_refs, down_refs):
        for t in range(begin, end):
            copies[t + 1].wait()
            place = slice(levels * (t - begin), levels * (t - begin + 1))
            up_ref[place, :] = pack_rows(tracer_ref[t, :, rows - 2, :], tracer_ref[t, :, rows - 1, :])
            down_ref[place, :] = pack_rows(tracer_ref[t, :, 0, :], tracer_ref[t, :, 1, :])


def base_kernel(rows, width, padded_ref, east_courant_ref, lat_courant_ref, base_ref, north_ref):
    q = [padded_ref[0, r] for r in range(rows)]
    north_ref[0] = NEAR * q[3] - FAR * q[2]
    own_flux = [None] * (rows + 1)
    own_flux[0] = lat_courant_ref[0] * (NEAR * q[0] - FAR * q[1])
    own_flux[1] = lat_courant_ref[1] * (NEAR * (q[1] + q[0]) - FAR * q[2])
    own_flux[2] = lat_courant_ref[2] * (NEAR * (q[2] + q[1]) - FAR * (q[3] + q[0]))
    own_flux[3] = lat_courant_ref[3] * (NEAR * (q[3] + q[2]) - FAR * q[1])
    for r in range(rows):
        west, west2, east = pltpu.roll(q[r], 1, 1), pltpu.roll(q[r], 2, 1), pltpu.roll(q[r], width - 1, 1)
        flux = east_courant_ref[r] * (NEAR * (q[r] + west) - FAR * (east + west2))
        value = q[r] - (pltpu.roll(flux, width - 1, 1) - flux) + own_flux[r]
        if r + 1 < rows:
            value = value - own_flux[r + 1]
        base_ref[0, r] = value


def physics_kernel(begin, levels, sector, owner_count, *refs):
    base_ref, north_ref, low_ref, high_ref, top_ref, courant_ref, surface_ref, mixing_ref, decay_ref, owner_ref, energy_in_ref = refs[:11]
    physics_ref, energy_ref = refs[11:]
    rows, width = base_ref.shape[1], base_ref.shape[-1]
    count = physics_ref.shape[0]
    courant = [courant_ref[r] for r in range(rows)]
    top = top_ref[top_ref.shape[0] - levels // 2 :, :]
    top = jnp.concatenate([top[:, :width], second_half(top, sector)], axis=0)
    mix_high, mix_low = split_high_low(mixing_ref[...])
    mix = jnp.concatenate([mix_high, mix_high, mix_low, mix_low], axis=1)
    level = lax.broadcasted_iota(jnp.int32, (8, width), 0)
    lane = lax.broadcasted_iota(jnp.int32, (8, width), 1)
    energies = [energy_in_ref[r] for r in range(rows)]
    for i in range(count):
        t = begin + i
        low = low_ref[levels * i : levels * (i + 1), :]
        high = high_ref[levels * i : levels * (i + 1), :]
        low_a, low_b = low[:, :width], second_half(low, sector)
        high_a, high_b = high[:, :width], second_half(high, sector)
        south = courant[0] * (NEAR * low_b - FAR * low_a)
        south_in = courant[1] * (FAR * low_b)
        north_in = courant[3] * (FAR * high_a)
        north = top * (NEAR * high_a - FAR * high_b + north_ref[t])
        extra = [south + south_in, -south_in, north_in, -north_in - north]
        for r in range(rows):
            advected = base_ref[t, r] + extra[r]
            part_high, part_low = split_high_low(advected)
            stacked = jnp.concatenate([part_high, part_low, part_high, part_low], axis=0)
            mixed = jnp.dot(mix, stacked, preferred_element_type=jnp.float32)
            surface = jnp.where(level == 7, surface_ref[t, r : r + 1, :], 0.0)
            mixed = jnp.concatenate([mixed[: levels - 8], mixed[levels - 8 :] + surface], axis=0)
            physics = mixed / (1.0 + decay_ref[t] * mixed * mixed)
            physics_ref[i, r] = physics
            gap = physics - advected
            squared = gap * gap
            for k in range(levels // 8):
                energies[r] = energies[r] + squared[8 * k : 8 * k + 8]
    if not owner_count:
        for r in range(rows):
            energy_ref[r] = energies[r]
        return
    energies = [jnp.where(lane < sector, energy, 0.0) for energy in energies]
    spot = lax.broadcasted_iota(jnp.int32, (1, LANES), 1)
    result = jnp.zeros((1, LANES), jnp.float32)
    for owner in range(owner_count):
        chosen = jnp.zeros((8, LANES), jnp.float32)
        for r in range(rows):
            picked = jnp.where(owner_ref[r : r + 1, :] == owner, energies[r], 0.0)
            for k in range(width // LANES):
                chosen = chosen + picked[:, LANES * k : LANES * (k + 1)]
        total = jnp.sum(jnp.sum(chosen, axis=0, keepdims=True), axis=1, keepdims=True)
        result = jnp.where(spot == owner, total, result)
    energy_ref[...] = result


def filter_kernel(first_tracer, chosen, radix, has_alias, *refs):
    out_hbm, stack_ref, wave_ref, result_ref, sems = refs[8 + has_alias :]
    levels = out_hbm.shape[1]
    piece = levels // RESULT_PIECES
    copies = []
    for place, i in enumerate(chosen):
        filter_tracer(radix, refs[0], refs[1].at[i], refs[2].at[i], *refs[3:8], result_ref.at[place], stack_ref, wave_ref)
        for part in range(RESULT_PIECES):
            span = pl.ds(piece * part, piece)
            copies.append(
                pltpu.make_async_copy(result_ref.at[place, span], out_hbm.at[first_tracer + i, span], sems.at[place, part])
            )
            copies[-1].start()
    for copy in copies:
        copy.wait()


def filter_tracer(
    radix, mask_ref, own_ref, other_ref, table_high_ref, table_low_ref, first_high_ref, first_low_ref, scale_ref, out_ref,
    stack_ref, wave_ref,
):
    levels, rows, sector = out_ref.shape
    pairs = (radix - 1) // 2
    shift = sector % LANES
    own_segments = -(-sector // LANES)
    lane = lax.broadcasted_iota(jnp.int32, (levels, LANES), 1)
    cosine = lambda k, i: math.cos(2.0 * math.pi * ((k * i) % radix) / radix)
    sine = lambda k, i: math.sin(2.0 * math.pi * ((k * i) % radix) / radix)

    def store_stack(r, begin, size, wave):
        part_high, part_low = split_high_low(wave)
        place = slice(levels * r, levels * (r + 1))
        for i, part in enumerate((part_high, part_low, part_high)):
            stack_ref[place, begin + size * i : begin + size * i + LANES] = part

    for r in range(rows):
        own = [own_ref[r, :, LANES * i : LANES * (i + 1)] for i in range(own_segments)]
        turned = [pltpu.roll(other_ref[r, :, LANES * i : LANES * (i + 1)], shift, 1) for i in range(own_segments)]
        joined = own[:-1] + [jnp.where(lane < shift, own[-1], turned[0])]
        joined += [jnp.where(lane < shift, turned[i], turned[i + 1]) for i in range(own_segments - 1)]
        plus = [joined[i] + joined[radix - i] for i in range(1, pairs + 1)]
        minus = [joined[radix - i] - joined[i] for i in range(1, pairs + 1)]
        store_stack(r, 0, LANES, sum(plus, joined[0]))
        for k in range(1, pairs + 1):
            begin = 3 * LANES * (2 * k - 1)
            real = sum((cosine(k, i) * plus[i - 1] for i in range(1, pairs + 1)), joined[0])
            imaginary = sine(k, 1) * minus[0]
            for i in range(2, pairs + 1):
                imaginary = imaginary + sine(k, i) * minus[i - 1]
            store_stack(r, begin, 2 * LANES, real)
            store_stack(r, begin + LANES, 2 * LANES, imaginary)

    def both_ways(begin, size, forward, inverse):
        spectrum = jnp.dot(stack_ref[:, 3 * begin : 3 * (begin + size)], forward, preferred_element_type=jnp.float32)
        scaled = jnp.concatenate(
            [spectrum[levels * r : levels * (r + 1)] * scale_ref[r : r + 1, begin : begin + size] for r in range(rows)], axis=0
        )
        part_high, part_low = split_high_low(scaled)
        stacked = jnp.concatenate([part_high, part_low, part_high], axis=1)
        wave_ref[:, begin : begin + size] = jnp.dot(stacked, inverse, preferred_element_type=jnp.float32)

    def table_of(high, low, begin, size):
        part_high = high[begin : begin + size, :]
        return jnp.concatenate([part_high, part_high, low[begin : begin + size, :]], axis=0)

    both_ways(0, LANES, *(table_of(first_high_ref, first_low_ref, LANES * i, LANES) for i in range(2)))
    for k in range(pairs):
        tables = (table_of(table_high_ref, table_low_ref, 2 * LANES * (k + pairs * i), 2 * LANES) for i in range(2))
        both_ways(LANES * (2 * k + 1), 2 * LANES, *tables)

    for r in range(rows):
        waves = [wave_ref[levels * r : levels * (r + 1), LANES * i : LANES * (i + 1)] for i in range(radix)]
        filtered_row = mask_ref[r] == 1
        for n in range(own_segments):
            value = waves[0]
            for k in range(1, pairs + 1):
                value = value + (cosine(k, n) * waves[2 * k - 1] if n else waves[2 * k - 1])
                if n:
                    value = value - sine(k, n) * waves[2 * k]
            begin = LANES * n
            size = min(LANES, sector - begin)
            value = jnp.where(filtered_row, value, own_ref[r, :, begin : begin + LANES])
            out_ref[:, r, begin : begin + size] = value[:, :size]


def vmem(shape, index=None):
    index = index or (0,) * len(shape)
    return pl.BlockSpec(shape, lambda i: index)


def on_device(tracers, courant_lat, courant_lon, surface_flux, mixing, decay_rate, owners, polar_mask):
    tracer_count, levels, rows, sector = tracers.shape
    assert rows == 4 and sector % 64 == 0 and lax.axis_size("lon") == 2
    f32 = jnp.float32
    lat_count, lat = lax.axis_size("lat"), lax.axis_index("lat")
    length = 2 * sector
    width = -(-sector // LANES) * LANES
    radix = length // LANES
    upward = [(i, i + 1) for i in range(lat_count - 1)]
    downward = [(i + 1, i) for i in range(lat_count - 1)]
    swap = [(0, 1), (1, 0)]

    whole = pl.BlockSpec(memory_space=pltpu.VMEM)
    in_hbm = pl.BlockSpec(memory_space=pltpu.HBM)
    split = [(0, tracer_count // 2), (tracer_count // 2, tracer_count)]
    up_rows = [levels * (end - begin) for begin, end in split]
    packed_shapes = [(count, length) for count in up_rows + [up_rows[0] + levels // 2] + up_rows[1:]]
    packed = pl.pallas_call(
        functools.partial(pack_kernel, split, rows, levels),
        in_specs=[in_hbm, in_hbm],
        out_specs=[whole] * len(packed_shapes),
        out_shape=[jax.ShapeDtypeStruct(shape, f32) for shape in packed_shapes],
        scratch_shapes=[
            pltpu.VMEM(tracers.shape, f32),
            pltpu.VMEM(courant_lat.shape, f32),
            pltpu.SemaphoreType.DMA((tracer_count + 1,)),
        ],
        compiler_params=params(),
        cost_estimate=cost(0, 600_000),
        name="pack",
    )(*(pltpu.with_memory_space_constraint(array, pltpu.HBM) for array in (tracers, courant_lat)))
    up, down = packed[: len(split)], packed[len(split) :]
    from_north = [lax.ppermute(down[0], "lat", downward)]
    from_south = [lax.ppermute(up[0], "lat", upward)]
    tracers, courant_lat, courant_lon, up, down = lax.optimization_barrier((tracers, courant_lat, courant_lon, up, down))

    by_row = jnp.transpose(tracers, (0, 2, 1, 3))
    lon_by_row = jnp.transpose(courant_lon, (1, 0, 2))
    lat_by_row = jnp.transpose(courant_lat, (1, 0, 2))
    ends = jnp.concatenate([by_row[..., -2:], by_row[..., :2]], axis=-1)
    lon_end = jnp.pad(lon_by_row[..., :1], ((0, 0), (0, 0), (0, 3)))
    sides = lax.ppermute(jnp.concatenate([ends, lon_end[None]], axis=0), "lon", swap)
    gap = jnp.zeros((tracer_count, rows, levels, width - sector - 4), f32)
    padded = jnp.concatenate([by_row, sides[:tracer_count, ..., 2:], gap, sides[:tracer_count, ..., :2]], axis=-1)
    east_courant = jnp.concatenate(
        [lon_by_row, sides[tracer_count, ..., :1], jnp.zeros((rows, levels, width - sector - 1), f32)], axis=-1
    )
    not_pole = jnp.where((lat > 0) | (jnp.arange(rows) > 0), 1.0, 0.0)
    lat_courant = jnp.pad(lat_by_row * not_pole[:, None, None], ((0, 0), (0, 0), (0, width - sector)))
    base, north = pl.pallas_call(
        functools.partial(base_kernel, rows, width),
        grid=(tracer_count,),
        in_specs=[
            pl.BlockSpec((1, rows, levels, width), lambda t: (t, 0, 0, 0)),
            vmem((rows, levels, width)),
            vmem((rows, levels, width)),
        ],
        out_specs=[
            pl.BlockSpec((1, rows, levels, width), lambda t: (t, 0, 0, 0)),
            pl.BlockSpec((1, levels, width), lambda t: (t, 0, 0)),
        ],
        out_shape=[
            jax.ShapeDtypeStruct((tracer_count, rows, levels, width), f32),
            jax.ShapeDtypeStruct((tracer_count, levels, width), f32),
        ],
        compiler_params=params(),
        cost_estimate=cost(0, 3_000_000),
        name="base",
    )(padded, east_courant, lat_courant)

    surface = jnp.pad(surface_flux, ((0, 0), (0, 0), (0, width - sector)))
    decay = decay_rate[:, :, None]
    block_count = rows * sector // BLOCK
    block_of = (np.arange(rows)[:, None] * sector + np.minimum(np.arange(width), sector - 1)[None]) // BLOCK
    owner_of = jnp.repeat(owners.reshape(block_count), BLOCK).reshape(rows, sector)
    owner_of = jnp.pad(owner_of, ((0, 0), (0, width - sector)))
    first, others, numbers, weights = spectral_tables(length)
    row_ids = (lat * rows + jnp.arange(rows)).astype(f32)
    latitude = (-0.5 + (row_ids + 0.5) / (lat_count * rows)) * math.pi
    inverse_sine = np.where(numbers == 0, 1.0, 1.0 / np.where(numbers == 0, 1.0, np.sin(np.pi * numbers / length)))
    ratio = 2.0 * jnp.cos(latitude)[:, None] * jnp.asarray(inverse_sine, f32)[None]
    damping = jnp.where(jnp.asarray(numbers == 0)[None], 1.0, jnp.minimum(1.0, ratio * ratio))
    scale = damping * jnp.asarray(weights, f32)[None]

    base, scale, owner_of, surface, decay, up, down = lax.optimization_barrier((base, scale, owner_of, surface, decay, up, down))
    from_north.append(lax.ppermute(down[1], "lat", downward))
    from_south.append(lax.ppermute(up[1], "lat", upward))

    tables = [jnp.asarray(part) for table in (others, first) for part in split_table(table)]
    physics, other = [], []

    def run_physics(chunk, energy):
        begin, end = split[chunk]
        last = chunk == len(split) - 1
        shapes = [(end - begin, rows, levels, width), (1, LANES) if last else energy.shape]
        result, energy = pl.pallas_call(
            functools.partial(physics_kernel, begin, levels, sector, lat_count if last else 0),
            in_specs=[whole] * 11,
            out_specs=[whole] * 2,
            out_shape=[jax.ShapeDtypeStruct(shape, f32) for shape in shapes],
            compiler_params=params(),
            cost_estimate=cost(0, 0),
            name="physics",
        )(base, north, from_south[chunk], from_north[chunk], from_north[0], lat_courant, surface, mixing, decay, owner_of, energy)
        physics.append(result)
        other.append(lax.ppermute(result, "lon", swap))
        return energy

    def run_filter(chunk, chosen, out):
        has_alias = int(out is not None)
        return pl.pallas_call(
            functools.partial(filter_kernel, split[chunk][0], chosen, radix, has_alias),
            in_specs=[pl.BlockSpec(memory_space=pltpu.SMEM)]
            + [whole] * (3 + len(tables))
            + [pl.BlockSpec(memory_space=pl.ANY)] * has_alias,
            out_specs=in_hbm,
            out_shape=jax.ShapeDtypeStruct((tracer_count, levels, rows, sector), f32),
            scratch_shapes=[
                pltpu.VMEM((rows * levels, 3 * length), jnp.bfloat16),
                pltpu.VMEM((rows * levels, length), f32),
                pltpu.VMEM((len(chosen), levels, rows, sector), f32),
                pltpu.SemaphoreType.DMA((len(chosen), RESULT_PIECES)),
            ],
            input_output_aliases={8: 0} if has_alias else {},
            compiler_params=params(),
            cost_estimate=cost(0, 0),
            name="filter",
        )(polar_mask, physics[chunk], other[chunk], *tables, scale, *([out] if has_alias else []))

    energy = run_physics(0, jnp.zeros((rows, 8, width), f32))
    out = run_filter(0, range(split[0][1] - split[0][0]), None)
    energy, out = lax.optimization_barrier((energy, out))
    energy = run_physics(1, energy)

    left = list(range(split[1][1] - split[1][0]))
    distance = 1
    while distance < lat_count:
        received = lax.ppermute(energy, "lat", [(i, i ^ distance) for i in range(lat_count)])
        distance *= 2
        if left:
            out = run_filter(1, left[:1], out)
            left = left[1:]
            received, out = lax.optimization_barrier((received, out))
        energy = energy + received
        energy, out = lax.optimization_barrier((energy, out))
    if left:
        out = run_filter(1, left, out)

    owner_energy = lax.dynamic_slice(energy, (0, lat), (1, 1)) / (block_count * BLOCK)
    return out, owner_energy


def solution(mesh):
    placed = (
        P("group", None, "lat", "lon"),
        P("group", "lat", "lon"),
        P("group", "lat", "lon"),
        P("group", "lat", "lon"),
        P(),
        P(),
        P(("group", "lat"), "lon", None, None),
        P(("group", "lat")),
    )
    return jax.shard_map(
        on_device,
        mesh=mesh,
        in_specs=placed,
        out_specs=(P("group", None, "lat", "lon"), P(("group", "lat"), "lon")),
        check_vma=False,
    )
```

profile of v0, /device:TPU:0, one launch (start us, length us, event | category | flops | bytes accessed | tf_op | source)
XLA Modules:
  0.0 58.9 jit_solution(13021727034970932763)
XLA Ops:
  0.6 2.4 %pack.1 = (f32[64,1152]{1,0:T(8,128)}, f32[64,1152]{1,0:T(8,128)S(1)}, f32[80,1152]{1,0:T(8,128)S(1)}, f32[64,1152]{1,0:T(8,128)S(1)}) custom-call(f32[4,32,4,576]{3,2,1,0:T(4,128)} %tracer_hbm.1, f32[32,4,576]{2,1,0:T(4,128)} %courant_hbm.1), custom_call_target="tpu_custom_call" | custom-call | bytes 600000 | tf_op jit(solution)/shard_map/pack/pallas_call | solution.py:276
  3.0 0.7 %copy-done.6 = f32[64,1152]{1,0:T(8,128)} copy-done((f32[64,1152]{1,0:T(8,128)}, f32[64,1152]{1,0:T(8,128)S(1)}, u32[]{:S(2)}) %copy-start.6) | copy-done | bytes 294936
  3.7 4.8 %collective-permute-start.4 = (f32[64,1152]{1,0:T(8,128)}, f32[64,1152]{1,0:T(8,128)S(1)}, u32[]{:S(2)}, u32[]{:S(2)}) collective-permute-start(f32[64,1152]{1,0:T(8,128)} %get-tuple-element.36), channel_id=1, source_target_pairs={{0,2},{2,4},{4,6},{6,8},{8,10},{10,12},{12,14},{1,3},{3,5},{5,7},{... | collective-permute-start | bytes 884744 | tf_op jit(solution)/shard_map/ppermute | solution.py:292
  8.6 1.3 %collective-permute-start.3 = (f32[80,1152]{1,0:T(8,128)S(1)}, f32[80,1152]{1,0:T(8,128)S(1)}, u32[]{:S(2)}, u32[]{:S(2)}) collective-permute-start(f32[80,1152]{1,0:T(8,128)S(1)} %get-tuple-element.38), channel_id=1, source_target_pairs={{2,0},{4,2},{6,4},{8,6},{10,8},{12,10},{14,12},{3,1},{5,3},{7,5},{... | collective-permute-start | bytes 1105928 | tf_op jit(solution)/shard_map/ppermute | solution.py:291
  9.9 0.0 copy-start.16
  10.0 0.1 copy.61
  10.1 0.0 copy-start.12
  10.1 0.0 copy-start.13
  10.1 0.0 copy-start.15
  10.1 0.0 copy-start.9
  10.2 0.0 copy-start.17
  10.2 0.0 copy-start.11
  10.2 0.1 fusion.2
  10.3 0.3 copy-done.16
  10.6 0.9 %pad_maximum_fusion.1 = f32[5,4,32,4]{3,2,1,0:T(8,128)} fusion(f32[1,4,32,4]{3,2,1,0:T(8,128)S(1)} %fusion.1, f32[4,4,32,2]{3,2,1,0:T(8,128)S(1)} %get-tuple-element.71, f32[4,4,32,2]{3,2,1,0:T(8,128)S(1)} %get-tuple-element.70), kind=kLoop, calls=%fused_computation.2 | loop fusion | flops 5120 | bytes 20480 | tf_op jit(solution)/shard_map/concatenate | solution.py:300
  11.5 0.0 collective-permute-start
  11.5 0.1 cosine_multiply_fusion
  11.6 0.1 select_multiply_fusion.refs_7_
  11.7 0.8 %fusion = f32[4,32,576]{2,1,0:T(8,128)} fusion(f32[32,4,576]{2,1,0:T(4,128)S(1)} %copy-done.9, f32[4]{0:T(128)S(1)} %or_select_fusion), kind=kLoop, calls=%fused_computation.5 | loop fusion | flops 73728 | bytes 589840 | tf_op jit(solution)/shard_map/mul | solution.py:307
  12.5 0.1 pad.25.clone
  12.5 0.1 pad.22.clone
  12.6 0.0 copy-done.17
  12.6 0.1 broadcast_in_dim.50
  12.7 0.1 reshape_reshape.3
  12.8 1.0 %pad.17.lat_courant_ref.refs_5_ = f32[4,32,640]{2,1,0:T(8,128)S(1)} pad(f32[4,32,576]{2,1,0:T(8,128)} %fusion, f32[]{:T(128)} %constant.22.clone.1), padding=0_0x0_0x0_64 | pad | bytes 622596 | tf_op jit(solution)/shard_map/jit(_pad)/pad | solution.py:307
  13.8 0.0 collective-permute-done
  13.8 0.8 %slice_bitcast_fusion = f32[4,32,1]{2,1,0:T(8,128)S(1)} fusion(f32[5,4,32,4]{3,2,1,0:T(8,128)} %collective-permute-done), kind=kLoop, calls=%fused_computation.7 | loop fusion | bytes 1024 | tf_op jit(solution)/shard_map/squeeze | solution.py:304
  14.7 1.2 %fusion.3 = (f32[4,4,32,2]{3,2,1,0:T(8,128)S(1)}, f32[4,4,32,2]{3,2,1,0:T(8,128)S(1)}) fusion(f32[5,4,32,4]{3,2,1,0:T(8,128)} %collective-permute-done), kind=kLoop, calls=%fused_computation.15 | loop fusion | bytes 16384 | tf_op jit(solution)/shard_map/slice | solution.py:302
  15.8 0.1 maximum_maximum_fusion.east_courant_ref
  15.9 0.3 pad_maximum_fusion.padded_ref
  16.2 0.0 copy-start.14
  16.2 0.0 copy-start.4
  16.2 2.6 %base.1 = (f32[4,4,32,640]{3,2,1,0:T(8,128)S(1)}, f32[4,32,640]{2,1,0:T(8,128)S(1)}) custom-call(f32[4,4,32,640]{3,2,1,0:T(8,128)S(1)} %pad_maximum_fusion.padded_ref, f32[4,32,640]{2,1,0:T(8,128)S(1)} %maximum_maximum_fusion.east_courant_ref, f32[4,32,640]{2,1,0:T(8,128)S(1)} %pad.17.lat_courant_ref.refs_5_), custom_call_target="tpu_custom_call" | custom-call | bytes 3000000 | tf_op jit(solution)/shard_map/base/pallas_call | solution.py:308
  18.8 0.1 copy.55.refs_8_
  18.9 4.1 %collective-permute-done.4.refs_2_ = f32[64,1152]{1,0:T(8,128)S(1)} collective-permute-done((f32[64,1152]{1,0:T(8,128)}, f32[64,1152]{1,0:T(8,128)S(1)}, u32[]{:S(2)}, u32[]{:S(2)}) %collective-permute-start.4) | collective-permute-done | bytes 294944 | tf_op jit(solution)/shard_map/ppermute | solution.py:292
  23.0 0.0 collective-permute-done.3.refs_3_.refs_4_
  23.1 0.0 copy-done.4
  23.1 0.0 copy-start.7
  23.1 0.0 copy-start
  23.1 0.0 copy-start.1
  23.1 0.0 copy-start.2
  23.1 0.0 copy-start.3
  23.1 0.0 copy-start.5
  23.1 0.5 physics.2
  23.6 0.1 collective-permute-start.5
  23.7 0.3 copy-done.7
  24.0 4.3 %collective-permute-start.1 = (f32[64,1152]{1,0:T(8,128)S(1)}, f32[64,1152]{1,0:T(8,128)S(1)}, u32[]{:S(2)}, u32[]{:S(2)}) collective-permute-start(f32[64,1152]{1,0:T(8,128)S(1)} %copy-done.7), channel_id=1, source_target_pairs={{0,2},{2,4},{4,6},{6,8},{8,10},{10,12},{12,14},{1,3},{3,5},{5,7},{... | collective-permute-start | bytes 884744 | tf_op jit(solution)/shard_map/ppermute | solution.py:345
  28.3 1.3 %collective-permute-start.2 = (f32[64,1152]{1,0:T(8,128)S(1)}, f32[64,1152]{1,0:T(8,128)S(1)}, u32[]{:S(2)}, u32[]{:S(2)}) collective-permute-start(f32[64,1152]{1,0:T(8,128)S(1)} %get-tuple-element.49), channel_id=1, source_target_pairs={{2,0},{4,2},{6,4},{8,6},{10,8},{12,10},{14,12},{3,1},{5,3},{7,5},{... | collective-permute-start | bytes 884744 | tf_op jit(solution)/shard_map/ppermute | solution.py:344
  29.6 0.0 collective-permute-done.5.refs_2_
  29.7 3.9 %filter.3.refs_8_ = f32[4,32,4,576]{3,2,1,0:T(4,128)} custom-call(s32[4]{0:T(128)S(1)} %copy-done.5, f32[2,4,32,640]{3,2,1,0:T(8,128)S(1)} %get-tuple-element.54.refs_1_, f32[2,4,32,640]{3,2,1,0:T(8,128)S(1)} %collective-permute-done.5.refs_2_, bf16[2048,256]{1,0:T(8,128)(2,1)S(1)} %copy-done.1, bf16[2048,256]{1,0:T(8,128)(2,1)S(1)} %copy-done, ...), custom_call_target="tpu_custom_call" | custom-call | tf_op jit(solution)/shard_map/filter/pallas_call | solution.py:369
  33.6 7.6 %collective-permute-done.1.refs_2_ = f32[64,1152]{1,0:T(8,128)S(1)} collective-permute-done((f32[64,1152]{1,0:T(8,128)S(1)}, f32[64,1152]{1,0:T(8,128)S(1)}, u32[]{:S(2)}, u32[]{:S(2)}) %collective-permute-start.1) | collective-permute-done | bytes 294944 | tf_op jit(solution)/shard_map/ppermute | solution.py:345
  41.2 0.0 collective-permute-done.2.refs_3_
  41.2 0.7 %physics.3 = (f32[2,4,32,640]{3,2,1,0:T(8,128)S(1)}, f32[1,128]{1,0:T(1,128)S(1)}) custom-call(f32[4,4,32,640]{3,2,1,0:T(8,128)S(1)} %get-tuple-element.46.refs_0_, f32[4,32,640]{2,1,0:T(8,128)S(1)} %get-tuple-element.47.refs_1_, f32[64,1152]{1,0:T(8,128)S(1)} %collective-permute-done.1.refs_2_, f32[64,1152]{1,0:T(8,128)S(1)} %collective-permute-done.2.refs_3_, ...), custom_call_target="tpu_custom_call" | custom-call | tf_op jit(solution)/shard_map/physics/pallas_call | solution.py:354
  41.9 0.0 collective-permute-start.7
  41.9 2.5 %collective-permute-start.6 = (f32[1,128]{1,0:T(1,128)S(1)}, f32[1,128]{1,0:T(1,128)S(1)}, u32[]{:S(2)}, u32[]{:S(2)}) collective-permute-start(f32[1,128]{1,0:T(1,128)S(1)} %get-tuple-element.57), channel_id=1, source_target_pairs={{0,2},{2,0},{4,6},{6,4},{8,10},{10,8},{12,14},{14,12},{1,3},{3,1},... | collective-permute-start | bytes 1544 | tf_op jit(solution)/shard_map/ppermute | solution.py:396
  44.5 0.0 collective-permute-done.7.refs_2_
  44.5 2.7 %filter.4.refs_8_ = f32[4,32,4,576]{3,2,1,0:T(4,128)} custom-call(s32[4]{0:T(128)S(1)} %copy-done.5, f32[2,4,32,640]{3,2,1,0:T(8,128)S(1)} %get-tuple-element.58.refs_1_, f32[2,4,32,640]{3,2,1,0:T(8,128)S(1)} %collective-permute-done.7.refs_2_, bf16[2048,256]{1,0:T(8,128)(2,1)S(1)} %copy-done.1, ...), custom_call_target="tpu_custom_call", output_to_operand_aliasing={{}: (8, {})} | custom-call | tf_op jit(solution)/shard_map/filter/pallas_call | solution.py:369
  47.2 0.0 collective-permute-done.6
  47.2 4.0 %collective-permute-start.8 = (f32[1,128]{1,0:T(1,128)S(1)}, f32[1,128]{1,0:T(1,128)S(1)}, u32[]{:S(2)}, u32[]{:S(2)}) collective-permute-start(f32[1,128]{1,0:T(1,128)S(1)} %add.46), channel_id=1, source_target_pairs={{0,4},{2,6},{4,0},{6,2},{8,12},{10,14},{12,8},{14,10},{1,5},{3,7},... | collective-permute-start | bytes 1544 | tf_op jit(solution)/shard_map/ppermute | solution.py:396
  51.1 2.7 %filter.5 = f32[4,32,4,576]{3,2,1,0:T(4,128)} custom-call(s32[4]{0:T(128)S(1)} %copy-done.5, f32[2,4,32,640]{3,2,1,0:T(8,128)S(1)} %get-tuple-element.58.refs_1_, f32[2,4,32,640]{3,2,1,0:T(8,128)S(1)} %collective-permute-done.7.refs_2_, bf16[2048,256]{1,0:T(8,128)(2,1)S(1)} %copy-done.1, ...), custom_call_target="tpu_custom_call", output_to_operand_aliasing={{}: (8, {})} | custom-call | tf_op jit(solution)/shard_map/filter/pallas_call | solution.py:369
  53.8 0.0 collective-permute-done.8
  53.8 2.7 %collective-permute-start.9 = (f32[1,128]{1,0:T(1,128)S(1)}, f32[1,128]{1,0:T(1,128)S(1)}, u32[]{:S(2)}, u32[]{:S(2)}) collective-permute-start(f32[1,128]{1,0:T(1,128)S(1)} %add.47), channel_id=1, source_target_pairs={{0,8},{2,10},{4,12},{6,14},{8,0},{10,2},{12,4},{14,6},{1,9},{3,11}... | collective-permute-start | bytes 1544 | tf_op jit(solution)/shard_map/ppermute | solution.py:396
  56.5 1.9 %collective-permute-done.9 = f32[1,128]{1,0:T(1,128)S(1)} collective-permute-done((f32[1,128]{1,0:T(1,128)S(1)}, f32[1,128]{1,0:T(1,128)S(1)}, u32[]{:S(2)}, u32[]{:S(2)}) %collective-permute-start.9) | collective-permute-done | bytes 544 | tf_op jit(solution)/shard_map/ppermute | solution.py:396
  58.4 0.6 fusion.4
  (27 shorter events, 0.1 us)
Async XLA Ops:
  0.6 9.3 %copy-start.8 = (f32[4,32,4,576]{3,2,1,0:T(4,128)S(1)}, f32[4,32,4,576]{3,2,1,0:T(4,128)}, u32[]{:S(2)}) copy-start(f32[4,32,4,576]{3,2,1,0:T(4,128)} %tracer_hbm.1) | copy-start | bytes 3538948
  0.6 9.3 %copy-start.10 = (f32[32,4,576]{2,1,0:T(4,128)S(1)}, f32[32,4,576]{2,1,0:T(4,128)}, u32[]{:S(2)}) copy-start(f32[32,4,576]{2,1,0:T(4,128)} %param.17) | copy-start | bytes 884740
  3.0 0.7 %copy-start.6 = (f32[64,1152]{1,0:T(8,128)}, f32[64,1152]{1,0:T(8,128)S(1)}, u32[]{:S(2)}) copy-start(f32[64,1152]{1,0:T(8,128)S(1)} %get-tuple-element.48) | copy-start | bytes 884740
  3.7 19.3 %collective-permute-start.4 = (f32[64,1152]{1,0:T(8,128)}, f32[64,1152]{1,0:T(8,128)S(1)}, u32[]{:S(2)}, u32[]{:S(2)}) collective-permute-start(f32[64,1152]{1,0:T(8,128)} %get-tuple-element.36), channel_id=1, source_target_pairs={{0,2},{2,4},{4,6},{6,8},{8,10},{10,12},{12,14},{1,3},{3,5},{5,7},{... | collective-permute-start | bytes 884744 | tf_op jit(solution)/shard_map/ppermute | solution.py:292
  8.6 14.4 %collective-permute-start.3 = (f32[80,1152]{1,0:T(8,128)S(1)}, f32[80,1152]{1,0:T(8,128)S(1)}, u32[]{:S(2)}, u32[]{:S(2)}) collective-permute-start(f32[80,1152]{1,0:T(8,128)S(1)} %get-tuple-element.38), channel_id=1, source_target_pairs={{2,0},{4,2},{6,4},{8,6},{10,8},{12,10},{14,12},{3,1},{5,3},{7,5},{... | collective-permute-start | bytes 1105928 | tf_op jit(solution)/shard_map/ppermute | solution.py:291
  9.9 0.7 %copy-start.16 = (pred[4]{0:T(512)(128)(4,1)S(1)}, pred[4]{0:T(512)(128)(4,1)}, u32[]{:S(2)}) copy-start(pred[4]{0:T(512)(128)(4,1)} %constant.21.clone.1) | copy-start | bytes 16
  10.1 1.4 %copy-start.12 = (f32[1152]{0:T(1024)S(1)}, f32[1152]{0:T(1024)}, u32[]{:S(2)}) copy-start(f32[1152]{0:T(1024)} %constant.54.clone) | copy-start | bytes 13828
  10.1 1.4 %copy-start.13 = (f32[1152]{0:T(1024)S(1)}, f32[1152]{0:T(1024)}, u32[]{:S(2)}) copy-start(f32[1152]{0:T(1024)} %constant.52.clone) | copy-start | bytes 13828
  10.1 1.4 %copy-start.15 = (pred[1152]{0:T(1024)(128)(4,1)S(1)}, pred[1152]{0:T(1024)(128)(4,1)}, u32[]{:S(2)}) copy-start(pred[1152]{0:T(1024)(128)(4,1)} %constant.53.clone) | copy-start | bytes 3460
  10.1 1.5 %copy-start.9 = (f32[32,4,576]{2,1,0:T(4,128)S(1)}, f32[32,4,576]{2,1,0:T(4,128)}, u32[]{:S(2)}) copy-start(f32[32,4,576]{2,1,0:T(4,128)} %courant_hbm.1) | copy-start | bytes 884740
  10.2 2.5 %copy-start.17 = (s32[1,1,18,1]{2,3,1,0:T(1,128)S(1)}, s32[1,1,18,1]{2,3,1,0:T(1,128)}, u32[]{:S(2)}) copy-start(s32[1,1,18,1]{2,3,1,0:T(1,128)} %param.21) | copy-start | bytes 220
  10.2 2.6 %copy-start.11 = (f32[4,4,576]{2,1,0:T(4,128)S(1)}, f32[4,4,576]{2,1,0:T(4,128)}, u32[]{:S(2)}) copy-start(f32[4,4,576]{2,1,0:T(4,128)} %param.18) | copy-start | bytes 110596
  11.5 2.3 %collective-permute-start = (f32[5,4,32,4]{3,2,1,0:T(8,128)}, f32[5,4,32,4]{3,2,1,0:T(8,128)}, u32[]{:S(2)}, u32[]{:S(2)}) collective-permute-start(f32[5,4,32,4]{3,2,1,0:T(8,128)} %pad_maximum_fusion.1), channel_id=1, source_target_pairs={{0,1},{1,0},{2,3},{3,2},{4,5},{5,4},{6,7},{7,6},{8,9},{9,8},{10,11... | collective-permute-start | bytes 30728 | tf_op jit(solution)/shard_map/ppermute | solution.py:300
  16.2 2.6 %copy-start.14 = (f32[4,32]{1,0:T(4,128)S(1)}, f32[4,32]{1,0:T(4,128)}, u32[]{:S(2)}) copy-start(f32[4,32]{1,0:T(4,128)} %param.20) | copy-start | bytes 1540
  16.2 6.9 %copy-start.4 = (f32[32,32]{1,0:T(8,128)S(1)}, f32[32,32]{1,0:T(8,128)}, u32[]{:S(2)}) copy-start(f32[32,32]{1,0:T(8,128)} %refs_7_.3) | copy-start | bytes 12292
  23.1 1.0 %copy-start.7 = (f32[64,1152]{1,0:T(8,128)S(1)}, f32[64,1152]{1,0:T(8,128)}, u32[]{:S(2)}) copy-start(f32[64,1152]{1,0:T(8,128)} %copy-done.6) | copy-start | bytes 884740
  23.1 6.6 %copy-start = (bf16[2048,256]{1,0:T(8,128)(2,1)S(1)}, bf16[2048,256]{1,0:T(8,128)(2,1)}, u32[]{:S(2)}) copy-start(bf16[2048,256]{1,0:T(8,128)(2,1)} %constant.56.clone.refs_4_) | copy-start | bytes 3145732
  23.1 6.6 %copy-start.1 = (bf16[2048,256]{1,0:T(8,128)(2,1)S(1)}, bf16[2048,256]{1,0:T(8,128)(2,1)}, u32[]{:S(2)}) copy-start(bf16[2048,256]{1,0:T(8,128)(2,1)} %constant.55.clone.refs_3_) | copy-start | bytes 3145732
  23.1 6.6 %copy-start.2 = (bf16[256,128]{1,0:T(8,128)(2,1)S(1)}, bf16[256,128]{1,0:T(8,128)(2,1)}, u32[]{:S(2)}) copy-start(bf16[256,128]{1,0:T(8,128)(2,1)} %constant.58.clone.refs_6_) | copy-start | bytes 196612
  23.1 6.6 %copy-start.3 = (bf16[256,128]{1,0:T(8,128)(2,1)S(1)}, bf16[256,128]{1,0:T(8,128)(2,1)}, u32[]{:S(2)}) copy-start(bf16[256,128]{1,0:T(8,128)(2,1)} %constant.57.clone.refs_5_) | copy-start | bytes 196612
  23.1 6.5 %copy-start.5 = (s32[4]{0:T(128)S(1)}, s32[4]{0:T(128)}, u32[]{:S(2)}) copy-start(s32[4]{0:T(128)} %refs_0_.5) | copy-start | bytes 52
  23.6 6.0 %collective-permute-start.5 = (f32[2,4,32,640]{3,2,1,0:T(8,128)S(1)}, f32[2,4,32,640]{3,2,1,0:T(8,128)S(1)}, u32[]{:S(2)}, u32[]{:S(2)}) collective-permute-start(f32[2,4,32,640]{3,2,1,0:T(8,128)S(1)} %get-tuple-element.54.refs_1_), channel_id=1, source_target_pairs={{0,1},{1,0},{2,3},{3,2},{4,5},{5,4},{6,7},{7,6},{8,9},{9,8},{10,11... | collective-permute-start | bytes 1966088 | tf_op jit(solution)/shard_map/ppermute | solution.py:364
  24.0 17.2 %collective-permute-start.1 = (f32[64,1152]{1,0:T(8,128)S(1)}, f32[64,1152]{1,0:T(8,128)S(1)}, u32[]{:S(2)}, u32[]{:S(2)}) collective-permute-start(f32[64,1152]{1,0:T(8,128)S(1)} %copy-done.7), channel_id=1, source_target_pairs={{0,2},{2,4},{4,6},{6,8},{8,10},{10,12},{12,14},{1,3},{3,5},{5,7},{... | collective-permute-start | bytes 884744 | tf_op jit(solution)/shard_map/ppermute | solution.py:345
  28.3 12.9 %collective-permute-start.2 = (f32[64,1152]{1,0:T(8,128)S(1)}, f32[64,1152]{1,0:T(8,128)S(1)}, u32[]{:S(2)}, u32[]{:S(2)}) collective-permute-start(f32[64,1152]{1,0:T(8,128)S(1)} %get-tuple-element.49), channel_id=1, source_target_pairs={{2,0},{4,2},{6,4},{8,6},{10,8},{12,10},{14,12},{3,1},{5,3},{7,5},{... | collective-permute-start | bytes 884744 | tf_op jit(solution)/shard_map/ppermute | solution.py:344
  41.9 2.6 %collective-permute-start.7 = (f32[2,4,32,640]{3,2,1,0:T(8,128)S(1)}, f32[2,4,32,640]{3,2,1,0:T(8,128)S(1)}, u32[]{:S(2)}, u32[]{:S(2)}) collective-permute-start(f32[2,4,32,640]{3,2,1,0:T(8,128)S(1)} %get-tuple-element.58.refs_1_), channel_id=1, source_target_pairs={{0,1},{1,0},{2,3},{3,2},{4,5},{5,4},{6,7},{7,6},{8,9},{9,8},{10,11... | collective-permute-start | bytes 1966088 | tf_op jit(solution)/shard_map/ppermute | solution.py:364
  41.9 5.2 %collective-permute-start.6 = (f32[1,128]{1,0:T(1,128)S(1)}, f32[1,128]{1,0:T(1,128)S(1)}, u32[]{:S(2)}, u32[]{:S(2)}) collective-permute-start(f32[1,128]{1,0:T(1,128)S(1)} %get-tuple-element.57), channel_id=1, source_target_pairs={{0,2},{2,0},{4,6},{6,4},{8,10},{10,8},{12,14},{14,12},{1,3},{3,1},... | collective-permute-start | bytes 1544 | tf_op jit(solution)/shard_map/ppermute | solution.py:396
  47.2 6.6 %collective-permute-start.8 = (f32[1,128]{1,0:T(1,128)S(1)}, f32[1,128]{1,0:T(1,128)S(1)}, u32[]{:S(2)}, u32[]{:S(2)}) collective-permute-start(f32[1,128]{1,0:T(1,128)S(1)} %add.46), channel_id=1, source_target_pairs={{0,4},{2,6},{4,0},{6,2},{8,12},{10,14},{12,8},{14,10},{1,5},{3,7},... | collective-permute-start | bytes 1544 | tf_op jit(solution)/shard_map/ppermute | solution.py:396
  53.8 4.5 %collective-permute-start.9 = (f32[1,128]{1,0:T(1,128)S(1)}, f32[1,128]{1,0:T(1,128)S(1)}, u32[]{:S(2)}, u32[]{:S(2)}) collective-permute-start(f32[1,128]{1,0:T(1,128)S(1)} %add.47), channel_id=1, source_target_pairs={{0,8},{2,10},{4,12},{6,14},{8,0},{10,2},{12,4},{14,6},{1,9},{3,11}... | collective-permute-start | bytes 1544 | tf_op jit(solution)/shard_map/ppermute | solution.py:396
where the time goes:
time: 59.3 us; the launch traced here: 58.9 us
  starting transfers between devices  21 us (35%)
  Pallas kernels  15.4 us (26%)
  waiting for transfers between devices  13.6 us (23%)
  local copies, waits for them, and re-layouts  5.14 us (9%)
  other arithmetic  2.76 us (5%)
  between operations  1.08 us (2%)
    pallas_call x3, Pallas kernels, run_filter(): pl.pallas_call(functools.partial(filter_kernel, split[chunk][0], chosen,...  9.26 us
    ppermute x3, starting transfers between devices, on_device(): lax.ppermute(energy, 'lat', [(i, i ^ distance) for i in range(lat_count)])  9.15 us
    ppermute x1, waiting for transfers between devices, on_device(): from_south.append(lax.ppermute(up[1], 'lat', upward))  7.64 us
    ppermute x1, starting transfers between devices, on_device(): from_south = [lax.ppermute(up[0], 'lat', upward)]  4.85 us
    ppermute x1, starting transfers between devices, on_device(): from_south.append(lax.ppermute(up[1], 'lat', upward))  4.29 us
    ppermute x1, waiting for transfers between devices, on_device(): from_south = [lax.ppermute(up[0], 'lat', upward)]  4.11 us
    pallas_call x1, Pallas kernels, on_device(): pl.pallas_call(functools.partial(base_kernel, rows, width), grid=(tracer_...  2.6 us
    pallas_call x1, Pallas kernels, on_device(): pl.pallas_call(functools.partial(pack_kernel, split, rows, levels), in_sp...  2.37 us
  transfers between devices with their start and end apart: 10, of which 3 were waited for; matrix products, arithmetic and copies ran while one was open for 10% of the time, Pallas kernels for 20%

commit v1 on v0

--- a/solution.py
+++ b/solution.py
@@ -74,24 +74,20 @@
     return jnp.concatenate(parts, axis=1)
 
 
-def pack_kernel(split, rows, levels, tracer_hbm, courant_hbm, *refs):
-    up_refs, down_refs = refs[: len(split)], refs[len(split) : 2 * len(split)]
-    tracer_ref, courant_ref, sems = refs[2 * len(split) :]
+def pack_kernel(rows, levels, tracer_hbm, courant_hbm, up_ref, down_ref, tracer_ref, courant_ref, sems):
     tracer_count = tracer_ref.shape[0]
-    copies = [pltpu.make_async_copy(courant_hbm, courant_ref, sems.at[tracer_count])]
-    copies += [pltpu.make_async_copy(tracer_hbm.at[t], tracer_ref.at[t], sems.at[t]) for t in range(tracer_count)]
+    copies = [pltpu.make_async_copy(tracer_hbm.at[t], tracer_ref.at[t], sems.at[t]) for t in range(tracer_count)]
+    copies.append(pltpu.make_async_copy(courant_hbm, courant_ref, sems.at[tracer_count]))
     for copy in copies:
         copy.start()
-    copies[0].wait()
+    for t in range(tracer_count):
+        copies[t].wait()
+        place = slice(levels * t, levels * (t + 1))
+        up_ref[place, :] = pack_rows(tracer_ref[t, :, rows - 2, :], tracer_ref[t, :, rows - 1, :])
+        down_ref[place, :] = pack_rows(tracer_ref[t, :, 0, :], tracer_ref[t, :, 1, :])
+    copies[tracer_count].wait()
     courant = courant_ref[:, 0, :]
-    place = levels * (split[0][1] - split[0][0])
-    down_refs[0][place : place + levels // 2, :] = pack_rows(courant[: levels // 2], courant[levels // 2 :])
-    for (begin, end), up_ref, down_ref in zip(split, up_refs, down_refs):
-        for t in range(begin, end):
-            copies[t + 1].wait()
-            place = slice(levels * (t - begin), levels * (t - begin + 1))
-            up_ref[place, :] = pack_rows(tracer_ref[t, :, rows - 2, :], tracer_ref[t, :, rows - 1, :])
-            down_ref[place, :] = pack_rows(tracer_ref[t, :, 0, :], tracer_ref[t, :, 1, :])
+    down_ref[levels * tracer_count :, :] = pack_rows(courant[: levels // 2], courant[levels // 2 :])
 
 
 def base_kernel(rows, width, padded_ref, east_courant_ref, lat_courant_ref, base_ref, north_ref):
@@ -111,23 +107,22 @@
         base_ref[0, r] = value
 
 
-def physics_kernel(begin, levels, sector, owner_count, *refs):
-    base_ref, north_ref, low_ref, high_ref, top_ref, courant_ref, surface_ref, mixing_ref, decay_ref, owner_ref, energy_in_ref = refs[:11]
-    physics_ref, energy_ref = refs[11:]
+def physics_kernel(levels, sector, owner_count, first_ref, *refs):
+    base_ref, north_ref, low_ref, high_ref, courant_ref, surface_ref, mixing_ref, decay_ref, owner_ref, energy_in_ref = refs[:10]
+    physics_refs, energy_ref = refs[10:-1], refs[-1]
     rows, width = base_ref.shape[1], base_ref.shape[-1]
-    count = physics_ref.shape[0]
     courant = [courant_ref[r] for r in range(rows)]
-    top = top_ref[top_ref.shape[0] - levels // 2 :, :]
+    top = high_ref[high_ref.shape[0] - levels // 2 :, :]
     top = jnp.concatenate([top[:, :width], second_half(top, sector)], axis=0)
     mix_high, mix_low = split_high_low(mixing_ref[...])
     mix = jnp.concatenate([mix_high, mix_high, mix_low, mix_low], axis=1)
     level = lax.broadcasted_iota(jnp.int32, (8, width), 0)
     lane = lax.broadcasted_iota(jnp.int32, (8, width), 1)
     energies = [energy_in_ref[r] for r in range(rows)]
-    for i in range(count):
-        t = begin + i
-        low = low_ref[levels * i : levels * (i + 1), :]
-        high = high_ref[levels * i : levels * (i + 1), :]
+    for i, physics_ref in enumerate(physics_refs):
+        t = first_ref[0] + i
+        place = pl.ds(pl.multiple_of(levels * t, levels), levels)
+        low, high = low_ref[place, :], high_ref[place, :]
         low_a, low_b = low[:, :width], second_half(low, sector)
         high_a, high_b = high[:, :width], second_half(high, sector)
         south = courant[0] * (NEAR * low_b - FAR * low_a)
@@ -143,7 +138,7 @@
             surface = jnp.where(level == 7, surface_ref[t, r : r + 1, :], 0.0)
             mixed = jnp.concatenate([mixed[: levels - 8], mixed[levels - 8 :] + surface], axis=0)
             physics = mixed / (1.0 + decay_ref[t] * mixed * mixed)
-            physics_ref[i, r] = physics
+            physics_ref[r] = physics
             gap = physics - advected
             squared = gap * gap
             for k in range(levels // 8):
@@ -166,25 +161,44 @@
     energy_ref[...] = result
 
 
-def filter_kernel(first_tracer, chosen, radix, has_alias, *refs):
-    out_hbm, stack_ref, wave_ref, result_ref, sems = refs[8 + has_alias :]
-    levels = out_hbm.shape[1]
-    piece = levels // RESULT_PIECES
+def send_result(result_ref, out_hbm, tracer, sems):
+    piece = result_ref.shape[0] // RESULT_PIECES
     copies = []
-    for place, i in enumerate(chosen):
-        filter_tracer(radix, refs[0], refs[1].at[i], refs[2].at[i], *refs[3:8], result_ref.at[place], stack_ref, wave_ref)
-        for part in range(RESULT_PIECES):
-            span = pl.ds(piece * part, piece)
-            copies.append(
-                pltpu.make_async_copy(result_ref.at[place, span], out_hbm.at[first_tracer + i, span], sems.at[place, part])
-            )
-            copies[-1].start()
+    for part in range(RESULT_PIECES):
+        span = pl.ds(piece * part, piece)
+        copies.append(pltpu.make_async_copy(result_ref.at[span], out_hbm.at[tracer, span], sems.at[part]))
+        copies[-1].start()
+    return copies
+
+
+def filter_kernel(radix, place, first_ref, *refs):
+    inputs, refs = refs[:8], refs[8:]
+    copies = []
+    if place:
+        before_ref, result_ref, back_ref, out_hbm, stack_ref, wave_ref, sems = refs
+        copies = send_result(before_ref, out_hbm, first_ref[0] + place - 1, sems)
+    else:
+        result_ref, back_ref, stack_ref, wave_ref = refs
+    filter_tracer(radix, *inputs, result_ref, back_ref, stack_ref, wave_ref)
     for copy in copies:
         copy.wait()
 
 
+def finish_kernel(place, keep_ref, first_ref, *refs):
+    before_ref, received_refs = refs[0], refs[1 : 2 + place]
+    out_hbm, result_ref, sems = refs[3 + place :]
+    levels, rows, sector = before_ref.shape
+    copies = send_result(before_ref, out_hbm, keep_ref[0] + place, sems.at[place + 1])
+    for i, received_ref in enumerate(received_refs):
+        for r in range(rows):
+            result_ref[i, :, r, :] = received_ref[r, :, :sector]
+        copies += send_result(result_ref.at[i], out_hbm, first_ref[0] + i, sems.at[i])
+    for copy in copies:
+        copy.wait()
+
+
 def filter_tracer(
-    radix, mask_ref, own_ref, other_ref, table_high_ref, table_low_ref, first_high_ref, first_low_ref, scale_ref, out_ref,
+    radix, mask_ref, own_ref, other_ref, table_high_ref, table_low_ref, first_high_ref, first_low_ref, scale_ref, out_ref, back_ref,
     stack_ref, wave_ref,
 ):
     levels, rows, sector = out_ref.shape
@@ -238,17 +252,23 @@
 
     for r in range(rows):
         waves = [wave_ref[levels * r : levels * (r + 1), LANES * i : LANES * (i + 1)] for i in range(radix)]
+        results = [None] * radix
+        results[0] = sum((waves[2 * k - 1] for k in range(1, pairs + 1)), waves[0])
+        for n in range(1, pairs + 1):
+            even = sum((cosine(k, n) * waves[2 * k - 1] for k in range(1, pairs + 1)), waves[0])
+            odd = sine(1, n) * waves[2]
+            for k in range(2, pairs + 1):
+                odd = odd + sine(k, n) * waves[2 * k]
+            results[n], results[radix - n] = even - odd, even + odd
         filtered_row = mask_ref[r] == 1
+        turned = [pltpu.roll(result, LANES - shift, 1) for result in results[own_segments - 1 :]]
         for n in range(own_segments):
-            value = waves[0]
-            for k in range(1, pairs + 1):
-                value = value + (cosine(k, n) * waves[2 * k - 1] if n else waves[2 * k - 1])
-                if n:
-                    value = value - sine(k, n) * waves[2 * k]
             begin = LANES * n
             size = min(LANES, sector - begin)
-            value = jnp.where(filtered_row, value, own_ref[r, :, begin : begin + LANES])
+            value = jnp.where(filtered_row, results[n], own_ref[r, :, begin : begin + LANES])
             out_ref[:, r, begin : begin + size] = value[:, :size]
+            value = jnp.where(lane < LANES - shift, turned[n], turned[min(n + 1, own_segments - 1)])
+            back_ref[r, :, begin : begin + LANES] = jnp.where(filtered_row, value, other_ref[r, :, begin : begin + LANES])
 
 
 def vmem(shape, index=None):
@@ -270,14 +290,15 @@
 
     whole = pl.BlockSpec(memory_space=pltpu.VMEM)
     in_hbm = pl.BlockSpec(memory_space=pltpu.HBM)
-    split = [(0, tracer_count // 2), (tracer_count // 2, tracer_count)]
-    up_rows = [levels * (end - begin) for begin, end in split]
-    packed_shapes = [(count, length) for count in up_rows + [up_rows[0] + levels // 2] + up_rows[1:]]
-    packed = pl.pallas_call(
-        functools.partial(pack_kernel, split, rows, levels),
+    scalars = pl.BlockSpec(memory_space=pltpu.SMEM)
+    up, down = pl.pallas_call(
+        functools.partial(pack_kernel, rows, levels),
         in_specs=[in_hbm, in_hbm],
-        out_specs=[whole] * len(packed_shapes),
-        out_shape=[jax.ShapeDtypeStruct(shape, f32) for shape in packed_shapes],
+        out_specs=[whole, whole],
+        out_shape=[
+            jax.ShapeDtypeStruct((levels * tracer_count, length), f32),
+            jax.ShapeDtypeStruct((levels * tracer_count + levels // 2, length), f32),
+        ],
         scratch_shapes=[
             pltpu.VMEM(tracers.shape, f32),
             pltpu.VMEM(courant_lat.shape, f32),
@@ -287,9 +308,8 @@
         cost_estimate=cost(0, 600_000),
         name="pack",
     )(*(pltpu.with_memory_space_constraint(array, pltpu.HBM) for array in (tracers, courant_lat)))
-    up, down = packed[: len(split)], packed[len(split) :]
-    from_north = [lax.ppermute(down[0], "lat", downward)]
-    from_south = [lax.ppermute(up[0], "lat", upward)]
+    from_north = lax.ppermute(down, "lat", downward)
+    from_south = lax.ppermute(up, "lat", upward)
     tracers, courant_lat, courant_lon, up, down = lax.optimization_barrier((tracers, courant_lat, courant_lon, up, down))
 
     by_row = jnp.transpose(tracers, (0, 2, 1, 3))
@@ -340,69 +360,84 @@
     damping = jnp.where(jnp.asarray(numbers == 0)[None], 1.0, jnp.minimum(1.0, ratio * ratio))
     scale = damping * jnp.asarray(weights, f32)[None]
 
-    base, scale, owner_of, surface, decay, up, down = lax.optimization_barrier((base, scale, owner_of, surface, decay, up, down))
-    from_north.append(lax.ppermute(down[1], "lat", downward))
-    from_south.append(lax.ppermute(up[1], "lat", upward))
+    base, scale, owner_of, surface, decay = lax.optimization_barrier((base, scale, owner_of, surface, decay))
+
+    half = tracer_count // 2
+    keep = (half * lax.axis_index("lon")).reshape(1)
+    give = half - keep
+    sector_shape = jax.ShapeDtypeStruct((rows, levels, width), f32)
+    result_shape = jax.ShapeDtypeStruct((levels, rows, sector), f32)
+    out_shape = jax.ShapeDtypeStruct((tracer_count, levels, rows, sector), f32)
+
+    def run_physics(first, energy, last):
+        energy_shape = (1, LANES) if last else energy.shape
+        *results, energy = pl.pallas_call(
+            functools.partial(physics_kernel, levels, sector, lat_count if last else 0),
+            in_specs=[scalars] + [whole] * 10,
+            out_specs=[whole] * (half + 1),
+            out_shape=[sector_shape] * half + [jax.ShapeDtypeStruct(energy_shape, f32)],
+            compiler_params=params(),
+            cost_estimate=cost(50_000_000, 2_000_000),
+            name="physics",
+        )(first, base, north, from_south, from_north, lat_courant, surface, mixing, decay, owner_of, energy)
+        return results, energy
+
+    given, energy = run_physics(give, jnp.zeros((rows, 8, width), f32), False)
+    other = [lax.ppermute(part, "lon", swap) for part in given]
+    kept, energy = run_physics(keep, energy, True)
 
     tables = [jnp.asarray(part) for table in (others, first) for part in split_table(table)]
-    physics, other = [], []
-
-    def run_physics(chunk, energy):
-        begin, end = split[chunk]
-        last = chunk == len(split) - 1
-        shapes = [(end - begin, rows, levels, width), (1, LANES) if last else energy.shape]
-        result, energy = pl.pallas_call(
-            functools.partial(physics_kernel, begin, levels, sector, lat_count if last else 0),
-            in_specs=[whole] * 11,
-            out_specs=[whole] * 2,
-            out_shape=[jax.ShapeDtypeStruct(shape, f32) for shape in shapes],
-            compiler_params=params(),
-            cost_estimate=cost(0, 0),
-            name="physics",
-        )(base, north, from_south[chunk], from_north[chunk], from_north[0], lat_courant, surface, mixing, decay, owner_of, energy)
-        physics.append(result)
-        other.append(lax.ppermute(result, "lon", swap))
-        return energy
-
-    def run_filter(chunk, chosen, out):
-        has_alias = int(out is not None)
-        return pl.pallas_call(
-            functools.partial(filter_kernel, split[chunk][0], chosen, radix, has_alias),
-            in_specs=[pl.BlockSpec(memory_space=pltpu.SMEM)]
-            + [whole] * (3 + len(tables))
-            + [pl.BlockSpec(memory_space=pl.ANY)] * has_alias,
-            out_specs=in_hbm,
-            out_shape=jax.ShapeDtypeStruct((tracer_count, levels, rows, sector), f32),
+    distances = [1 << i for i in range(lat_count.bit_length() - 1)]
+
+    def send_energy(energy):
+        distance = distances.pop(0)
+        return lax.ppermute(energy, "lat", [(i, i ^ distance) for i in range(lat_count)])
+
+    result, received = None, []
+    for i in range(half):
+        coming = send_energy(energy)
+        outputs = [result_shape, sector_shape] + ([out_shape] if i else [])
+        outputs = pl.pallas_call(
+            functools.partial(filter_kernel, radix, i),
+            in_specs=[scalars, scalars] + [whole] * (7 + min(i, 1)),
+            out_specs=[whole, whole] + ([in_hbm] if i else []),
+            out_shape=outputs,
             scratch_shapes=[
                 pltpu.VMEM((rows * levels, 3 * length), jnp.bfloat16),
                 pltpu.VMEM((rows * levels, length), f32),
-                pltpu.VMEM((len(chosen), levels, rows, sector), f32),
-                pltpu.SemaphoreType.DMA((len(chosen), RESULT_PIECES)),
-            ],
-            input_output_aliases={8: 0} if has_alias else {},
+            ]
+            + ([pltpu.SemaphoreType.DMA((RESULT_PIECES,))] if i else []),
             compiler_params=params(),
-            cost_estimate=cost(0, 0),
+            cost_estimate=cost(2_000_000_000, 6_000_000),
             name="filter",
-        )(polar_mask, physics[chunk], other[chunk], *tables, scale, *([out] if has_alias else []))
-
-    energy = run_physics(0, jnp.zeros((rows, 8, width), f32))
-    out = run_filter(0, range(split[0][1] - split[0][0]), None)
-    energy, out = lax.optimization_barrier((energy, out))
-    energy = run_physics(1, energy)
-
-    left = list(range(split[1][1] - split[1][0]))
-    distance = 1
-    while distance < lat_count:
-        received = lax.ppermute(energy, "lat", [(i, i ^ distance) for i in range(lat_count)])
-        distance *= 2
-        if left:
-            out = run_filter(1, left[:1], out)
-            left = left[1:]
-            received, out = lax.optimization_barrier((received, out))
-        energy = energy + received
-        energy, out = lax.optimization_barrier((energy, out))
-    if left:
-        out = run_filter(1, left, out)
+        )(keep, polar_mask, kept[i], other[i], *tables, scale, *([result] if i else []))
+        result, back = outputs[:2]
+        coming, result = lax.optimization_barrier((coming, result))
+        energy = energy + coming
+        energy, back = lax.optimization_barrier((energy, back))
+        received.append(lax.ppermute(back, "lon", swap))
+        if i + 1 < half:
+            energy, kept[i + 1] = lax.optimization_barrier((energy, kept[i + 1]))
+        out = outputs[-1]
+    coming = send_energy(energy)
+    out = pl.pallas_call(
+        functools.partial(finish_kernel, half - 1),
+        in_specs=[scalars, scalars] + [whole] * (1 + half) + [in_hbm],
+        out_specs=in_hbm,
+        out_shape=out_shape,
+        scratch_shapes=[
+            pltpu.VMEM((half,) + result_shape.shape, f32),
+            pltpu.SemaphoreType.DMA((half + 1, RESULT_PIECES)),
+        ],
+        input_output_aliases={3 + half: 0},
+        compiler_params=params(),
+        cost_estimate=cost(0, 3_000_000),
+        name="finish",
+    )(keep, give, result, *received, out)
+    coming, out = lax.optimization_barrier((coming, out))
+    energy = energy + coming
+    while distances:
+        energy = energy + send_energy(energy)
 
     owner_energy = lax.dynamic_slice(energy, (0, lat), (1, 1)) / (block_count * BLOCK)
     return out, owner_energy

time: 59.3 us -> 52.6 us (0.89)
  starting transfers between devices: 21 us -> 13.7 us
  waiting for transfers between devices: 13.6 us -> 18.6 us
  Pallas kernels: 15.4 us -> 12.1 us
  local copies, waits for them, and re-layouts: 5.14 us -> 4.22 us
    ppermute x9, starting transfers between devices: 21 us -> 13.7 us  [the longest x1 5.64 us: on_device(): from_south = lax.ppermute(up, 'lat', upward)]
    ppermute x9, waiting for transfers between devices: 13.6 us -> 18.6 us  [the longest x1 16.7 us: on_device(): from_south = lax.ppermute(up, 'lat', upward)]
    pallas_call x6, Pallas kernels: 12.8 us -> 9.5 us  [the longest x2 4.68 us: on_device(): pl.pallas_call(functools.partial(filter_kernel, radix, i), in_specs=[scal...]
    unnamed x36 -> x32, local copies, waits for them, and re-layouts: 1.41 us -> 0.49 us
  transfers between devices with their start and end apart: 10 -> 10, of which waited for: 3 -> 2; matrix products, arithmetic and copies ran while one was open for 10% -> 11% of each run, Pallas kernels for 20% -> 17%
where the time goes in v1:
time: 52.6 us; the launch traced here: 52.3 us
  waiting for transfers between devices  18.6 us (35%)
  starting transfers between devices  13.7 us (26%)
  Pallas kernels  12.1 us (23%)
  local copies, waits for them, and re-layouts  4.22 us (8%)
  other arithmetic  2.77 us (5%)
  between operations  0.99 us (2%)
    ppermute x1, waiting for transfers between devices, on_device(): from_south = lax.ppermute(up, 'lat', upward)  16.7 us
    ppermute x1, starting transfers between devices, on_device(): from_south = lax.ppermute(up, 'lat', upward)  5.64 us
    ppermute x3, starting transfers between devices, send_energy(): lax.ppermute(energy, 'lat', [(i, i ^ distance) for i in range(lat_count)])  5.6 us
    pallas_call x2, Pallas kernels, on_device(): pl.pallas_call(functools.partial(filter_kernel, radix, i), in_specs=[scal...  4.68 us
    pallas_call x1, Pallas kernels, on_device(): pl.pallas_call(functools.partial(pack_kernel, rows, levels), in_specs=[in...  2.63 us
    pallas_call x1, Pallas kernels, on_device(): pl.pallas_call(functools.partial(base_kernel, rows, width), grid=(tracer_...  2.6 us
    ppermute x3, waiting for transfers between devices, send_energy(): lax.ppermute(energy, 'lat', [(i, i ^ distance) for i in range(lat_count)])  1.83 us
    ppermute x1, starting transfers between devices, on_device(): from_north = lax.ppermute(down, 'lat', downward)  1.29 us
  transfers between devices with their start and end apart: 10, of which 2 were waited for; matrix products, arithmetic and copies ran while one was open for 11% of the time, Pallas kernels for 17%

profile of v1, /device:TPU:0, one launch (start us, length us, event | category | flops | bytes accessed | tf_op | source)
XLA Modules:
  0.0 52.3 jit_solution(14422212220104728390)
XLA Ops:
  0.6 0.0 copy-start.6
  0.6 2.6 %pack.1 = (f32[128,1152]{1,0:T(8,128)}, f32[144,1152]{1,0:T(8,128)}) custom-call(f32[4,32,4,576]{3,2,1,0:T(4,128)} %tracer_hbm.1, f32[32,4,576]{2,1,0:T(4,128)} %courant_hbm.1), custom_call_target="tpu_custom_call" | custom-call | bytes 600000 | tf_op jit(solution)/shard_map/pack/pallas_call | solution.py:294
  3.3 1.3 %collective-permute-start.2 = (f32[144,1152]{1,0:T(8,128)}, f32[144,1152]{1,0:T(8,128)S(1)}, u32[]{:S(2)}, u32[]{:S(2)}) collective-permute-start(f32[144,1152]{1,0:T(8,128)} %get-tuple-element.38), channel_id=1, source_target_pairs={{2,0},{4,2},{6,4},{8,6},{10,8},{12,10},{14,12},{3,1},{5,3},{7,5},{... | collective-permute-start | bytes 1990664 | tf_op jit(solution)/shard_map/ppermute | solution.py:311
  4.6 0.0 copy-start.8
  4.6 5.6 %collective-permute-start.1 = (f32[128,1152]{1,0:T(8,128)}, f32[128,1152]{1,0:T(8,128)S(1)}, u32[]{:S(2)}, u32[]{:S(2)}) collective-permute-start(f32[128,1152]{1,0:T(8,128)} %get-tuple-element.37), channel_id=1, source_target_pairs={{0,2},{2,4},{4,6},{6,8},{8,10},{10,12},{12,14},{1,3},{3,5},{5,7},{... | collective-permute-start | bytes 1769480 | tf_op jit(solution)/shard_map/ppermute | solution.py:312
  10.2 0.0 copy-done.6
  10.2 0.1 copy.60
  10.4 0.0 copy-start.14
  10.4 0.0 copy-start.10
  10.4 0.0 copy-start.11
  10.4 0.0 copy-start.13
  10.4 0.0 copy-start.7
  10.5 0.1 fusion.2
  10.6 0.0 copy-done.8
  10.6 0.0 copy-start.9
  10.6 0.0 copy-start.15
  10.7 0.4 copy-done.14
  11.1 0.9 %pad_maximum_fusion.1 = f32[5,4,32,4]{3,2,1,0:T(8,128)} fusion(f32[1,4,32,4]{3,2,1,0:T(8,128)S(1)} %fusion.1, f32[4,4,32,2]{3,2,1,0:T(8,128)S(1)} %get-tuple-element.73, f32[4,4,32,2]{3,2,1,0:T(8,128)S(1)} %get-tuple-element.72), kind=kLoop, calls=%fused_computation.2 | loop fusion | flops 5120 | bytes 20480 | tf_op jit(solution)/shard_map/concatenate | solution.py:320
  11.9 0.0 collective-permute-start
  12.0 0.0 copy-done.10
  12.0 0.0 copy-done.11
  12.0 0.1 select_multiply_fusion.refs_7_
  12.1 0.8 %fusion = f32[4,32,576]{2,1,0:T(8,128)} fusion(f32[32,4,576]{2,1,0:T(4,128)S(1)} %copy-done.7, f32[4]{0:T(128)S(1)} %or_select_fusion), kind=kLoop, calls=%fused_computation.5 | loop fusion | flops 73728 | bytes 589840 | tf_op jit(solution)/shard_map/mul | solution.py:327
  12.9 0.1 pad.25.clone
  13.0 0.1 pad.22.clone
  13.1 1.0 %pad.17.lat_courant_ref.refs_4_ = f32[4,32,640]{2,1,0:T(8,128)S(1)} pad(f32[4,32,576]{2,1,0:T(8,128)} %fusion, f32[]{:T(128)} %constant.26.clone.1), padding=0_0x0_0x0_64 | pad | bytes 622596 | tf_op jit(solution)/shard_map/jit(_pad)/pad | solution.py:327
  14.1 0.1 broadcast_in_dim.50
  14.2 0.1 reshape_reshape.3
  14.3 0.0 collective-permute-done
  14.3 0.8 %slice_bitcast_fusion = f32[4,32,1]{2,1,0:T(8,128)S(1)} fusion(f32[5,4,32,4]{3,2,1,0:T(8,128)} %collective-permute-done), kind=kLoop, calls=%fused_computation.7 | loop fusion | bytes 1024 | tf_op jit(solution)/shard_map/squeeze | solution.py:324
  15.1 0.1 maximum_maximum_fusion.east_courant_ref
  15.2 1.2 %fusion.3 = (f32[4,4,32,2]{3,2,1,0:T(8,128)S(1)}, f32[4,4,32,2]{3,2,1,0:T(8,128)S(1)}) fusion(f32[5,4,32,4]{3,2,1,0:T(8,128)} %collective-permute-done), kind=kLoop, calls=%fused_computation.15 | loop fusion | bytes 16384 | tf_op jit(solution)/shard_map/slice | solution.py:322
  16.4 0.3 pad_maximum_fusion.padded_ref
  16.7 0.0 copy-start.12
  16.7 0.0 copy-start
  16.7 2.6 %base.1 = (f32[4,4,32,640]{3,2,1,0:T(8,128)S(1)}, f32[4,32,640]{2,1,0:T(8,128)S(1)}) custom-call(f32[4,4,32,640]{3,2,1,0:T(8,128)S(1)} %pad_maximum_fusion.padded_ref, f32[4,32,640]{2,1,0:T(8,128)S(1)} %maximum_maximum_fusion.east_courant_ref, f32[4,32,640]{2,1,0:T(8,128)S(1)} %pad.17.lat_courant_ref.refs_4_), custom_call_target="tpu_custom_call" | custom-call | bytes 3000000 | tf_op jit(solution)/shard_map/base/pallas_call | solution.py:328
  19.3 0.1 copy.54.refs_7_
  19.4 16.7 %collective-permute-done.1.refs_2_ = f32[128,1152]{1,0:T(8,128)S(1)} collective-permute-done((f32[128,1152]{1,0:T(8,128)}, f32[128,1152]{1,0:T(8,128)S(1)}, u32[]{:S(2)}, u32[]{:S(2)}) %collective-permute-start.1) | collective-permute-done | bytes 589856 | tf_op jit(solution)/shard_map/ppermute | solution.py:312
  36.1 0.0 collective-permute-done.2.refs_3_
  36.2 0.5 physics.2
  36.7 0.1 collective-permute-start.4
  36.7 0.5 collective-permute-start.6
  37.2 0.0 copy-start.5
  37.3 0.7 %physics.3 = (f32[4,32,640]{2,1,0:T(8,128)S(1)}, f32[4,32,640]{2,1,0:T(8,128)S(1)}, f32[1,128]{1,0:T(1,128)S(1)}) custom-call(s32[1]{0:T(128)} %bitcast.first_ref.keep_ref, f32[4,4,32,640]{3,2,1,0:T(8,128)S(1)} %get-tuple-element.43.refs_0_, f32[4,32,640]{2,1,0:T(8,128)S(1)} %get-tuple-element.44.refs_1_, f32[128,1152]{1,0:T(8,128)S(1)} %collective-permute-done.1.refs_2_, ...), custom_call_target="tpu_custom_call" | custom-call | flops 50000000 | bytes 2000000 | tf_op jit(solution)/shard_map/physics/pallas_call | solution.py:374
  37.9 2.4 %collective-permute-start.3 = (f32[1,128]{1,0:T(1,128)S(1)}, f32[1,128]{1,0:T(1,128)S(1)}, u32[]{:S(2)}, u32[]{:S(2)}) collective-permute-start(f32[1,128]{1,0:T(1,128)S(1)} %get-tuple-element.49), channel_id=1, source_target_pairs={{0,2},{2,0},{4,6},{6,4},{8,10},{10,8},{12,14},{14,12},{1,3},{3,1},... | collective-permute-start | bytes 1544 | tf_op jit(solution)/shard_map/ppermute | solution.py:394
  40.3 0.0 collective-permute-done.4.refs_2_
  40.3 0.0 copy-done.2
  40.3 0.0 copy-done.3
  40.3 0.0 copy-done.4
  40.3 0.0 copy-done.5
  40.3 2.0 %filter.2 = (f32[32,4,576]{2,1,0:T(4,128)S(1)}, f32[4,32,640]{2,1,0:T(8,128)S(1)}) custom-call(s32[1]{0:T(128)} %bitcast.first_ref.keep_ref, s32[4]{0:T(128)S(1)} %copy-done.1, f32[4,32,640]{2,1,0:T(8,128)S(1)} %get-tuple-element.50.refs_1_, f32[4,32,640]{2,1,0:T(8,128)S(1)} %collective-permute-done.4.refs_2_, bf16[2048,256]{1,0:T(8,128)(2,1)S(1)} %copy-done.2, ...), custom_call_target="tpu_custom_call" | custom-call | flops 2000000000 | bytes 6000000 | tf_op jit(solution)/shard_map/filter/pallas_call | solution.py:400
  42.4 0.0 collective-permute-done.3
  42.4 1.6 %collective-permute-start.5 = (f32[1,128]{1,0:T(1,128)S(1)}, f32[1,128]{1,0:T(1,128)S(1)}, u32[]{:S(2)}, u32[]{:S(2)}) collective-permute-start(f32[1,128]{1,0:T(1,128)S(1)} %add.46), channel_id=1, source_target_pairs={{0,4},{2,6},{4,0},{6,2},{8,12},{10,14},{12,8},{14,10},{1,5},{3,7},... | collective-permute-start | bytes 1544 | tf_op jit(solution)/shard_map/ppermute | solution.py:394
  44.1 0.0 collective-permute-start.8
  44.1 0.0 collective-permute-done.6.refs_2_
  44.1 2.6 %filter.3 = (f32[32,4,576]{2,1,0:T(4,128)S(1)}, f32[4,32,640]{2,1,0:T(8,128)S(1)}, f32[4,32,4,576]{3,2,1,0:T(4,128)}) custom-call(s32[1]{0:T(128)} %bitcast.first_ref.keep_ref, s32[4]{0:T(128)S(1)} %copy-done.1, f32[4,32,640]{2,1,0:T(8,128)S(1)} %get-tuple-element.59.refs_1_, f32[4,32,640]{2,1,0:T(8,128)S(1)} %collective-permute-done.6.refs_2_, ...), custom_call_target="tpu_custom_call" | custom-call | flops 2000000000 | bytes 6000000 | tf_op jit(solution)/shard_map/filter/pallas_call | solution.py:400
  46.7 0.0 collective-permute-done.5
  46.7 0.6 %collective-permute-start.9 = (f32[4,32,640]{2,1,0:T(8,128)S(1)}, f32[4,32,640]{2,1,0:T(8,128)S(1)}, u32[]{:S(2)}, u32[]{:S(2)}) collective-permute-start(f32[4,32,640]{2,1,0:T(8,128)S(1)} %get-tuple-element.68), channel_id=1, source_target_pairs={{0,1},{1,0},{2,3},{3,2},{4,5},{5,4},{6,7},{7,6},{8,9},{9,8},{10,11... | collective-permute-start | bytes 983048 | tf_op jit(solution)/shard_map/ppermute | solution.py:418
  47.3 1.6 %collective-permute-start.7 = (f32[1,128]{1,0:T(1,128)S(1)}, f32[1,128]{1,0:T(1,128)S(1)}, u32[]{:S(2)}, u32[]{:S(2)}) collective-permute-start(f32[1,128]{1,0:T(1,128)S(1)} %add.47), channel_id=1, source_target_pairs={{0,8},{2,10},{4,12},{6,14},{8,0},{10,2},{12,4},{14,6},{1,9},{3,11}... | collective-permute-start | bytes 1544 | tf_op jit(solution)/shard_map/ppermute | solution.py:394
  48.9 0.0 collective-permute-done.8.refs_1_
  48.9 0.0 collective-permute-done.9.refs_2_
  48.9 1.0 %finish.1 = f32[4,32,4,576]{3,2,1,0:T(4,128)} custom-call(s32[1]{0:T(128)} %bitcast.first_ref.keep_ref, s32[1]{0:T(128)S(6)} %sub.3.first_ref, f32[32,4,576]{2,1,0:T(4,128)S(1)} %get-tuple-element.66.refs_0_, f32[4,32,640]{2,1,0:T(8,128)S(1)} %collective-permute-done.8.refs_1_, ...), custom_call_target="tpu_custom_call", output_to_operand_aliasing={{}: (5, {})} | custom-call | bytes 3000000 | tf_op jit(solution)/shard_map/finish/pallas_call | solution.py:423
  49.9 1.8 %collective-permute-done.7 = f32[1,128]{1,0:T(1,128)S(1)} collective-permute-done((f32[1,128]{1,0:T(1,128)S(1)}, f32[1,128]{1,0:T(1,128)S(1)}, u32[]{:S(2)}, u32[]{:S(2)}) %collective-permute-start.7) | collective-permute-done | bytes 544 | tf_op jit(solution)/shard_map/ppermute | solution.py:394
  51.8 0.6 %fusion.4 = f32[1,1]{1,0:T(1,128)} fusion(f32[1,128]{1,0:T(1,128)S(1)} %add.48, s32[]{:T(128)S(6)} %select_n.17), kind=kLoop, calls=%fused_computation.16 | loop fusion | flops 1 | bytes 12 | tf_op jit(solution)/shard_map/div | solution.py:442
  (23 shorter events, 0.1 us)
Async XLA Ops:
  0.6 9.6 %copy-start.6 = (f32[4,32,4,576]{3,2,1,0:T(4,128)S(1)}, f32[4,32,4,576]{3,2,1,0:T(4,128)}, u32[]{:S(2)}) copy-start(f32[4,32,4,576]{3,2,1,0:T(4,128)} %tracer_hbm.1) | copy-start | bytes 3538948
  3.3 32.9 %collective-permute-start.2 = (f32[144,1152]{1,0:T(8,128)}, f32[144,1152]{1,0:T(8,128)S(1)}, u32[]{:S(2)}, u32[]{:S(2)}) collective-permute-start(f32[144,1152]{1,0:T(8,128)} %get-tuple-element.38), channel_id=1, source_target_pairs={{2,0},{4,2},{6,4},{8,6},{10,8},{12,10},{14,12},{3,1},{5,3},{7,5},{... | collective-permute-start | bytes 1990664 | tf_op jit(solution)/shard_map/ppermute | solution.py:311
  4.6 6.0 %copy-start.8 = (f32[32,4,576]{2,1,0:T(4,128)S(1)}, f32[32,4,576]{2,1,0:T(4,128)}, u32[]{:S(2)}) copy-start(f32[32,4,576]{2,1,0:T(4,128)} %param.17) | copy-start | bytes 884740
  4.6 31.5 %collective-permute-start.1 = (f32[128,1152]{1,0:T(8,128)}, f32[128,1152]{1,0:T(8,128)S(1)}, u32[]{:S(2)}, u32[]{:S(2)}) collective-permute-start(f32[128,1152]{1,0:T(8,128)} %get-tuple-element.37), channel_id=1, source_target_pairs={{0,2},{2,4},{4,6},{6,8},{8,10},{10,12},{12,14},{1,3},{3,5},{5,7},{... | collective-permute-start | bytes 1769480 | tf_op jit(solution)/shard_map/ppermute | solution.py:312
  10.4 0.7 %copy-start.14 = (pred[4]{0:T(512)(128)(4,1)S(1)}, pred[4]{0:T(512)(128)(4,1)}, u32[]{:S(2)}) copy-start(pred[4]{0:T(512)(128)(4,1)} %constant.25.clone.1) | copy-start | bytes 16
  10.4 1.6 %copy-start.10 = (f32[1152]{0:T(1024)S(1)}, f32[1152]{0:T(1024)}, u32[]{:S(2)}) copy-start(f32[1152]{0:T(1024)} %constant.58.clone) | copy-start | bytes 13828
  10.4 1.6 %copy-start.11 = (f32[1152]{0:T(1024)S(1)}, f32[1152]{0:T(1024)}, u32[]{:S(2)}) copy-start(f32[1152]{0:T(1024)} %constant.60.clone) | copy-start | bytes 13828
  10.4 1.6 %copy-start.13 = (pred[1152]{0:T(1024)(128)(4,1)S(1)}, pred[1152]{0:T(1024)(128)(4,1)}, u32[]{:S(2)}) copy-start(pred[1152]{0:T(1024)(128)(4,1)} %constant.59.clone) | copy-start | bytes 3460
  10.4 1.7 %copy-start.7 = (f32[32,4,576]{2,1,0:T(4,128)S(1)}, f32[32,4,576]{2,1,0:T(4,128)}, u32[]{:S(2)}) copy-start(f32[32,4,576]{2,1,0:T(4,128)} %courant_hbm.1) | copy-start | bytes 884740
  10.6 3.5 %copy-start.9 = (f32[4,4,576]{2,1,0:T(4,128)S(1)}, f32[4,4,576]{2,1,0:T(4,128)}, u32[]{:S(2)}) copy-start(f32[4,4,576]{2,1,0:T(4,128)} %param.18) | copy-start | bytes 110596
  10.6 3.5 %copy-start.15 = (s32[1,1,18,1]{2,3,1,0:T(1,128)S(1)}, s32[1,1,18,1]{2,3,1,0:T(1,128)}, u32[]{:S(2)}) copy-start(s32[1,1,18,1]{2,3,1,0:T(1,128)} %param.21) | copy-start | bytes 220
  11.9 2.4 %collective-permute-start = (f32[5,4,32,4]{3,2,1,0:T(8,128)}, f32[5,4,32,4]{3,2,1,0:T(8,128)}, u32[]{:S(2)}, u32[]{:S(2)}) collective-permute-start(f32[5,4,32,4]{3,2,1,0:T(8,128)} %pad_maximum_fusion.1), channel_id=1, source_target_pairs={{0,1},{1,0},{2,3},{3,2},{4,5},{5,4},{6,7},{7,6},{8,9},{9,8},{10,11... | collective-permute-start | bytes 30728 | tf_op jit(solution)/shard_map/ppermute | solution.py:320
  16.7 2.6 %copy-start.12 = (f32[4,32]{1,0:T(4,128)S(1)}, f32[4,32]{1,0:T(4,128)}, u32[]{:S(2)}) copy-start(f32[4,32]{1,0:T(4,128)} %param.20) | copy-start | bytes 1540
  16.7 19.5 %copy-start = (f32[32,32]{1,0:T(8,128)S(1)}, f32[32,32]{1,0:T(8,128)}, u32[]{:S(2)}) copy-start(f32[32,32]{1,0:T(8,128)} %refs_6_.5) | copy-start | bytes 12292
  36.7 3.7 %collective-permute-start.4 = (f32[4,32,640]{2,1,0:T(8,128)S(1)}, f32[4,32,640]{2,1,0:T(8,128)S(1)}, u32[]{:S(2)}, u32[]{:S(2)}) collective-permute-start(f32[4,32,640]{2,1,0:T(8,128)S(1)} %get-tuple-element.51), channel_id=1, source_target_pairs={{0,1},{1,0},{2,3},{3,2},{4,5},{5,4},{6,7},{7,6},{8,9},{9,8},{10,11... | collective-permute-start | bytes 983048 | tf_op jit(solution)/shard_map/ppermute | solution.py:386
  36.7 7.3 %collective-permute-start.6 = (f32[4,32,640]{2,1,0:T(8,128)S(1)}, f32[4,32,640]{2,1,0:T(8,128)S(1)}, u32[]{:S(2)}, u32[]{:S(2)}) collective-permute-start(f32[4,32,640]{2,1,0:T(8,128)S(1)} %get-tuple-element.60), channel_id=1, source_target_pairs={{0,1},{1,0},{2,3},{3,2},{4,5},{5,4},{6,7},{7,6},{8,9},{9,8},{10,11... | collective-permute-start | bytes 983048 | tf_op jit(solution)/shard_map/ppermute | solution.py:386
  37.2 3.1 %copy-start.1 = (s32[4]{0:T(128)S(1)}, s32[4]{0:T(128)}, u32[]{:S(2)}) copy-start(s32[4]{0:T(128)} %refs_0_.3) | copy-start | bytes 52
  37.2 3.1 %copy-start.2 = (bf16[2048,256]{1,0:T(8,128)(2,1)S(1)}, bf16[2048,256]{1,0:T(8,128)(2,1)}, u32[]{:S(2)}) copy-start(bf16[2048,256]{1,0:T(8,128)(2,1)} %constant.61.clone.refs_3_) | copy-start | bytes 3145732
  37.2 3.1 %copy-start.3 = (bf16[2048,256]{1,0:T(8,128)(2,1)S(1)}, bf16[2048,256]{1,0:T(8,128)(2,1)}, u32[]{:S(2)}) copy-start(bf16[2048,256]{1,0:T(8,128)(2,1)} %constant.62.clone.refs_4_) | copy-start | bytes 3145732
  37.2 3.1 %copy-start.4 = (bf16[256,128]{1,0:T(8,128)(2,1)S(1)}, bf16[256,128]{1,0:T(8,128)(2,1)}, u32[]{:S(2)}) copy-start(bf16[256,128]{1,0:T(8,128)(2,1)} %constant.63.clone.refs_5_) | copy-start | bytes 196612
  37.2 3.1 %copy-start.5 = (bf16[256,128]{1,0:T(8,128)(2,1)S(1)}, bf16[256,128]{1,0:T(8,128)(2,1)}, u32[]{:S(2)}) copy-start(bf16[256,128]{1,0:T(8,128)(2,1)} %constant.64.clone.refs_6_) | copy-start | bytes 196612
  37.9 4.5 %collective-permute-start.3 = (f32[1,128]{1,0:T(1,128)S(1)}, f32[1,128]{1,0:T(1,128)S(1)}, u32[]{:S(2)}, u32[]{:S(2)}) collective-permute-start(f32[1,128]{1,0:T(1,128)S(1)} %get-tuple-element.49), channel_id=1, source_target_pairs={{0,2},{2,0},{4,6},{6,4},{8,10},{10,8},{12,14},{14,12},{1,3},{3,1},... | collective-permute-start | bytes 1544 | tf_op jit(solution)/shard_map/ppermute | solution.py:394
  42.4 4.3 %collective-permute-start.5 = (f32[1,128]{1,0:T(1,128)S(1)}, f32[1,128]{1,0:T(1,128)S(1)}, u32[]{:S(2)}, u32[]{:S(2)}) collective-permute-start(f32[1,128]{1,0:T(1,128)S(1)} %add.46), channel_id=1, source_target_pairs={{0,4},{2,6},{4,0},{6,2},{8,12},{10,14},{12,8},{14,10},{1,5},{3,7},... | collective-permute-start | bytes 1544 | tf_op jit(solution)/shard_map/ppermute | solution.py:394
  44.1 4.8 %collective-permute-start.8 = (f32[4,32,640]{2,1,0:T(8,128)S(1)}, f32[4,32,640]{2,1,0:T(8,128)S(1)}, u32[]{:S(2)}, u32[]{:S(2)}) collective-permute-start(f32[4,32,640]{2,1,0:T(8,128)S(1)} %get-tuple-element.67), channel_id=1, source_target_pairs={{0,1},{1,0},{2,3},{3,2},{4,5},{5,4},{6,7},{7,6},{8,9},{9,8},{10,11... | collective-permute-start | bytes 983048 | tf_op jit(solution)/shard_map/ppermute | solution.py:418
  46.7 2.1 %collective-permute-start.9 = (f32[4,32,640]{2,1,0:T(8,128)S(1)}, f32[4,32,640]{2,1,0:T(8,128)S(1)}, u32[]{:S(2)}, u32[]{:S(2)}) collective-permute-start(f32[4,32,640]{2,1,0:T(8,128)S(1)} %get-tuple-element.68), channel_id=1, source_target_pairs={{0,1},{1,0},{2,3},{3,2},{4,5},{5,4},{6,7},{7,6},{8,9},{9,8},{10,11... | collective-permute-start | bytes 983048 | tf_op jit(solution)/shard_map/ppermute | solution.py:418
  47.3 4.4 %collective-permute-start.7 = (f32[1,128]{1,0:T(1,128)S(1)}, f32[1,128]{1,0:T(1,128)S(1)}, u32[]{:S(2)}, u32[]{:S(2)}) collective-permute-start(f32[1,128]{1,0:T(1,128)S(1)} %add.47), channel_id=1, source_target_pairs={{0,8},{2,10},{4,12},{6,14},{8,0},{10,2},{12,4},{14,6},{1,9},{3,11}... | collective-permute-start | bytes 1544 | tf_op jit(solution)/shard_map/ppermute | solution.py:394

commit v2 on v1

v2 whole, which is shorter than its diff:
```python
import functools
import math

import jax
import jax.numpy as jnp
import numpy as np
from jax import lax
from jax.experimental import pallas as pl
from jax.experimental.pallas import tpu as pltpu
from jax.sharding import PartitionSpec as P

LANES = 128
BLOCK = 128
VMEM_BYTES = 6 * 1024 * 1024
RESULT_PIECES = 4
NEAR = 7.0 / 12.0
FAR = 1.0 / 12.0


def params():
    return pltpu.CompilerParams(vmem_limit_bytes=VMEM_BYTES)


def cost(flops, bytes_accessed):
    return pl.CostEstimate(flops=flops, bytes_accessed=bytes_accessed, transcendentals=0)


def split_high_low(value):
    high = value.astype(jnp.bfloat16)
    low = (value - high.astype(jnp.float32)).astype(jnp.bfloat16)
    return high, low


def split_table(table):
    high = table.astype(jnp.bfloat16.dtype)
    return high, (table - high.astype(np.float64)).astype(jnp.bfloat16.dtype)


def spectral_tables(length):
    radix = length // LANES
    pairs = (radix - 1) // 2
    spot = np.arange(LANES)[:, None]
    number = np.arange(LANES)[None, :]
    is_cosine = number <= LANES // 2
    wave = np.where(is_cosine, number, number - LANES // 2)
    angle = 2.0 * np.pi * ((spot * wave) % LANES) / LANES
    first = np.where(is_cosine, np.cos(angle), np.sin(angle))
    others, numbers = [], [radix * wave[0]]
    weights = [np.where((wave[0] == 0) | (wave[0] == LANES // 2), 1.0, 2.0) / length]
    for residue in range(1, pairs + 1):
        whole = residue + radix * number
        angle = 2.0 * np.pi * ((spot * whole) % length) / length
        cosine, sine = np.cos(angle), np.sin(angle)
        others.append(np.block([[cosine, -sine], [sine, cosine]]))
        folded = np.minimum(whole[0], length - whole[0])
        numbers += [folded, folded]
        weights.append(np.full(2 * LANES, 2.0 / length))
    forward = np.concatenate(others), first
    inverse = np.concatenate([table.T for table in others]), first.T
    return forward, inverse, np.concatenate(numbers), np.concatenate(weights)


def pack_rows(first, second):
    return jnp.concatenate([first, second], axis=1)


def second_half(packed, sector):
    skip, shift = sector // LANES, sector % LANES
    segments = [packed[:, LANES * i : LANES * (i + 1)] for i in range(packed.shape[1] // LANES)]
    if shift == 0:
        return jnp.concatenate(segments[skip:], axis=1)
    turned = [pltpu.roll(segment, LANES - shift, 1) for segment in segments[skip:]]
    lane = lax.broadcasted_iota(jnp.int32, turned[0].shape, 1)
    parts = [jnp.where(lane < LANES - shift, turned[i], turned[min(i + 1, len(turned) - 1)]) for i in range(len(turned))]
    return jnp.concatenate(parts, axis=1)


def pack_kernel(rows, levels, tracer_hbm, courant_hbm, up_ref, down_ref, tracer_ref, courant_ref, sems):
    tracer_count = tracer_ref.shape[0]
    copies = [pltpu.make_async_copy(tracer_hbm.at[t], tracer_ref.at[t], sems.at[t]) for t in range(tracer_count)]
    copies.append(pltpu.make_async_copy(courant_hbm, courant_ref, sems.at[tracer_count]))
    for copy in copies:
        copy.start()
    for t in range(tracer_count):
        copies[t].wait()
        place = slice(levels * t, levels * (t + 1))
        up_ref[place, :] = pack_rows(tracer_ref[t, :, rows - 2, :], tracer_ref[t, :, rows - 1, :])
        down_ref[place, :] = pack_rows(tracer_ref[t, :, 0, :], tracer_ref[t, :, 1, :])
    copies[tracer_count].wait()
    courant = courant_ref[:, 0, :]
    down_ref[levels * tracer_count :, :] = pack_rows(courant[: levels // 2], courant[levels // 2 :])


def base_kernel(width, not_pole_ref, tracer_hbm, lat_hbm, lon_hbm, side_ref, base_ref, north_ref, courant_ref, *scratch):
    tracer_ref, lat_ref, lon_ref, sems = scratch
    tracer_count, levels, rows, sector = tracer_ref.shape
    whole = sector // LANES * LANES
    copies = [pltpu.make_async_copy(source, target, sems.at[i]) for i, (source, target) in enumerate(((lat_hbm, lat_ref), (lon_hbm, lon_ref)))]
    copies += [pltpu.make_async_copy(tracer_hbm.at[t], tracer_ref.at[t], sems.at[t + 2]) for t in range(tracer_count)]
    for copy in copies:
        copy.start()

    def beside(values, side):
        return jnp.concatenate([values[:, :whole], values[:, whole:], side[:, sector - whole :]], axis=1)

    copies[0].wait()
    copies[1].wait()
    nothing = jnp.zeros((levels, LANES), jnp.float32)
    for r in range(rows):
        courant = lat_ref[:, r, :] if r else lat_ref[:, r, :] * not_pole_ref[0]
        courant_ref[r] = beside(courant, nothing)
    for t in range(tracer_count):
        copies[t + 2].wait()
        q = [beside(tracer_ref[t, :, r, :], side_ref[t, r]) for r in range(rows)]
        north_ref[t] = NEAR * q[3] - FAR * q[2]
        own_flux = [
            courant_ref[0] * (NEAR * q[0] - FAR * q[1]),
            courant_ref[1] * (NEAR * (q[1] + q[0]) - FAR * q[2]),
            courant_ref[2] * (NEAR * (q[2] + q[1]) - FAR * (q[3] + q[0])),
            courant_ref[3] * (NEAR * (q[3] + q[2]) - FAR * q[1]),
        ]
        for r in range(rows):
            west, west2, east = pltpu.roll(q[r], 1, 1), pltpu.roll(q[r], 2, 1), pltpu.roll(q[r], width - 1, 1)
            flux = beside(lon_ref[:, r, :], side_ref[tracer_count, r]) * (NEAR * (q[r] + west) - FAR * (east + west2))
            value = q[r] - (pltpu.roll(flux, width - 1, 1) - flux) + own_flux[r]
            if r + 1 < rows:
                value = value - own_flux[r + 1]
            base_ref[t, r] = value


def physics_kernel(levels, sector, owner_count, first_ref, *refs):
    base_ref, north_ref, low_ref, high_ref, courant_ref, surface_ref, mixing_ref, decay_ref, owner_ref, energy_in_ref = refs[:10]
    physics_refs, energy_ref = refs[10:-1], refs[-1]
    if len(physics_refs) == 1:
        physics_refs = [physics_refs[0].at[i] for i in range(physics_refs[0].shape[0])]
    rows, width = base_ref.shape[1], base_ref.shape[-1]
    courant = [courant_ref[r] for r in range(rows)]
    top = high_ref[high_ref.shape[0] - levels // 2 :, :]
    top = jnp.concatenate([top[:, :width], second_half(top, sector)], axis=0)
    mix_high, mix_low = split_high_low(mixing_ref[...])
    mix = jnp.concatenate([mix_high, mix_high, mix_low, mix_low], axis=1)
    level = lax.broadcasted_iota(jnp.int32, (8, width), 0)
    lane = lax.broadcasted_iota(jnp.int32, (8, width), 1)
    energies = [energy_in_ref[r] for r in range(rows)]
    for i, physics_ref in enumerate(physics_refs):
        t = first_ref[0] + i
        place = pl.ds(pl.multiple_of(levels * t, levels), levels)
        low, high = low_ref[place, :], high_ref[place, :]
        low_a, low_b = low[:, :width], second_half(low, sector)
        high_a, high_b = high[:, :width], second_half(high, sector)
        south = courant[0] * (NEAR * low_b - FAR * low_a)
        south_in = courant[1] * (FAR * low_b)
        north_in = courant[3] * (FAR * high_a)
        north = top * (NEAR * high_a - FAR * high_b + north_ref[t])
        extra = [south + south_in, -south_in, north_in, -north_in - north]
        for r in range(rows):
            advected = base_ref[t, r] + extra[r]
            part_high, part_low = split_high_low(advected)
            stacked = jnp.concatenate([part_high, part_low, part_high, part_low], axis=0)
            mixed = jnp.dot(mix, stacked, preferred_element_type=jnp.float32)
            surface = jnp.where(level == 7, surface_ref[t, r : r + 1, :], 0.0)
            mixed = jnp.concatenate([mixed[: levels - 8], mixed[levels - 8 :] + surface], axis=0)
            physics = mixed / (1.0 + decay_ref[t] * mixed * mixed)
            physics_ref[r] = physics
            gap = physics - advected
            squared = gap * gap
            for k in range(levels // 8):
                energies[r] = energies[r] + squared[8 * k : 8 * k + 8]
    if not owner_count:
        for r in range(rows):
            energy_ref[r] = energies[r]
        return
    energies = [jnp.where(lane < sector, energy, 0.0) for energy in energies]
    spot = lax.broadcasted_iota(jnp.int32, (1, LANES), 1)
    result = jnp.zeros((1, LANES), jnp.float32)
    for owner in range(owner_count):
        chosen = jnp.zeros((8, LANES), jnp.float32)
        for r in range(rows):
            picked = jnp.where(owner_ref[r : r + 1, :] == owner, energies[r], 0.0)
            for k in range(width // LANES):
                chosen = chosen + picked[:, LANES * k : LANES * (k + 1)]
        total = jnp.sum(jnp.sum(chosen, axis=0, keepdims=True), axis=1, keepdims=True)
        result = jnp.where(spot == owner, total, result)
    energy_ref[...] = result


def send_result(result_ref, out_hbm, tracer, sems):
    piece = result_ref.shape[0] // RESULT_PIECES
    copies = []
    for part in range(RESULT_PIECES):
        span = pl.ds(piece * part, piece)
        copies.append(pltpu.make_async_copy(result_ref.at[span], out_hbm.at[tracer, span], sems.at[part]))
        copies[-1].start()
    return copies


def waves_of(radix):
    pairs = (radix - 1) // 2
    cosine = lambda k, i: math.cos(2.0 * math.pi * ((k * i) % radix) / radix)
    sine = lambda k, i: math.sin(2.0 * math.pi * ((k * i) % radix) / radix)
    return pairs, cosine, sine


def stacked_table(high_ref, low_ref, begin, size):
    high = high_ref[begin : begin + size, :]
    return jnp.concatenate([high, high, low_ref[begin : begin + size, :]], axis=0)


def product_of(high_ref, low_ref, begin, size, table):
    high = high_ref[:, begin : begin + size]
    stacked = jnp.concatenate([high, low_ref[:, begin : begin + size], high], axis=1)
    return jnp.dot(stacked, table, preferred_element_type=jnp.float32)


def forward_kernel(radix, count, *refs):
    own_refs, refs = refs[:count], refs[count:]
    other_ref, table_high_ref, table_low_ref, first_high_ref, first_low_ref, scale_ref = refs[:6]
    out_high_ref, out_low_ref, high_ref, low_ref = refs[6:]
    rows, levels, width = own_refs[0].shape
    pairs, cosine, sine = waves_of(radix)
    segments = width // LANES
    shift = radix * LANES // 2 % LANES
    lane = lax.broadcasted_iota(jnp.int32, (levels, LANES), 1)

    def store(place, column, wave):
        high_ref[place, column : column + LANES], low_ref[place, column : column + LANES] = split_high_low(wave)

    for i, own_ref in enumerate(own_refs):
        for r in range(rows):
            place = slice(levels * (rows * i + r), levels * (rows * i + r + 1))
            own = [own_ref[r, :, LANES * n : LANES * (n + 1)] for n in range(segments)]
            turned = [pltpu.roll(other_ref[i, r, :, LANES * n : LANES * (n + 1)], shift, 1) for n in range(segments)]
            joined = own[:-1] + [jnp.where(lane < shift, own[-1], turned[0])]
            joined += [jnp.where(lane < shift, turned[n], turned[n + 1]) for n in range(segments - 1)]
            plus = [joined[n] + joined[radix - n] for n in range(1, pairs + 1)]
            minus = [joined[radix - n] - joined[n] for n in range(1, pairs + 1)]
            store(place, 0, sum(plus, joined[0]))
            for k in range(1, pairs + 1):
                real = sum((cosine(k, n) * plus[n - 1] for n in range(1, pairs + 1)), joined[0])
                imaginary = sine(k, 1) * minus[0]
                for n in range(2, pairs + 1):
                    imaginary = imaginary + sine(k, n) * minus[n - 1]
                store(place, LANES * (2 * k - 1), real)
                store(place, LANES * 2 * k, imaginary)

    def transform(begin, size, table):
        spectrum = product_of(high_ref, low_ref, begin, size, table)
        for i in range(count * rows):
            place = slice(levels * i, levels * (i + 1))
            damped = spectrum[place] * scale_ref[i % rows : i % rows + 1, begin : begin + size]
            out_high_ref[place, begin : begin + size], out_low_ref[place, begin : begin + size] = split_high_low(damped)

    transform(0, LANES, stacked_table(first_high_ref, first_low_ref, 0, LANES))
    for k in range(pairs):
        transform(LANES * (2 * k + 1), 2 * LANES, stacked_table(table_high_ref, table_low_ref, 2 * LANES * k, 2 * LANES))


def inverse_kernel(radix, count, mask_ref, *refs):
    own_refs, refs = refs[:count], refs[count:]
    other_ref, high_ref, low_ref, table_high_ref, table_low_ref, first_high_ref, first_low_ref = refs[:7]
    result_refs, back_ref, wave_ref = refs[7 : 7 + count], refs[7 + count], refs[8 + count]
    rows, levels, width = own_refs[0].shape
    sector = result_refs[0].shape[-1]
    pairs, cosine, sine = waves_of(radix)
    segments = width // LANES
    shift = radix * LANES // 2 % LANES
    lane = lax.broadcasted_iota(jnp.int32, (levels, LANES), 1)

    def transform(begin, size, table):
        wave_ref[:, begin : begin + size] = product_of(high_ref, low_ref, begin, size, table)

    transform(0, LANES, stacked_table(first_high_ref, first_low_ref, 0, LANES))
    for k in range(pairs):
        transform(LANES * (2 * k + 1), 2 * LANES, stacked_table(table_high_ref, table_low_ref, 2 * LANES * k, 2 * LANES))

    for i, (own_ref, result_ref) in enumerate(zip(own_refs, result_refs)):
        for r in range(rows):
            place = slice(levels * (rows * i + r), levels * (rows * i + r + 1))
            waves = [wave_ref[place, LANES * n : LANES * (n + 1)] for n in range(radix)]
            results = [None] * radix
            results[0] = sum((waves[2 * k - 1] for k in range(1, pairs + 1)), waves[0])
            for n in range(1, pairs + 1):
                even = sum((cosine(k, n) * waves[2 * k - 1] for k in range(1, pairs + 1)), waves[0])
                odd = sine(1, n) * waves[2]
                for k in range(2, pairs + 1):
                    odd = odd + sine(k, n) * waves[2 * k]
                results[n], results[radix - n] = even - odd, even + odd
            filtered_row = mask_ref[r] == 1
            turned = [pltpu.roll(result, LANES - shift, 1) for result in results[segments - 1 :]]
            for n in range(segments):
                begin = LANES * n
                size = min(LANES, sector - begin)
                value = jnp.where(filtered_row, results[n], own_ref[r, :, begin : begin + LANES])
                result_ref[:, r, begin : begin + size] = value[:, :size]
                value = jnp.where(lane < LANES - shift, turned[n], turned[min(n + 1, segments - 1)])
                back_ref[i, r, :, begin : begin + LANES] = jnp.where(
                    filtered_row, value, other_ref[i, r, :, begin : begin + LANES]
                )


def finish_kernel(keep_ref, give_ref, *refs):
    result_refs, (received_ref, out_hbm, turned_ref, sems) = refs[:-4], refs[-4:]
    count, rows, levels, width = received_ref.shape
    sector = out_hbm.shape[-1]
    piece = levels // RESULT_PIECES
    copies = []

    def send(source_ref, tracer, slot):
        for part in range(RESULT_PIECES):
            span = pl.ds(piece * part, piece)
            copies.append(pltpu.make_async_copy(source_ref.at[span], out_hbm.at[tracer, span], sems.at[slot, part]))
            copies[-1].start()

    for i, result_ref in enumerate(result_refs):
        send(result_ref, keep_ref[0] + i, i)
    for i in range(count):
        for r in range(rows):
            turned_ref[i, :, r, :] = received_ref[i, r, :, :sector]
        send(turned_ref.at[i], give_ref[0] + i, count + i)
    for copy in copies:
        copy.wait()


def on_device(tracers, courant_lat, courant_lon, surface_flux, mixing, decay_rate, owners, polar_mask):
    tracer_count, levels, rows, sector = tracers.shape
    assert rows == 4 and sector % 64 == 0 and lax.axis_size("lon") == 2
    f32 = jnp.float32
    lat_count, lat = lax.axis_size("lat"), lax.axis_index("lat")
    length = 2 * sector
    width = -(-sector // LANES) * LANES
    radix = length // LANES
    upward = [(i, i + 1) for i in range(lat_count - 1)]
    downward = [(i + 1, i) for i in range(lat_count - 1)]
    swap = [(0, 1), (1, 0)]

    whole = pl.BlockSpec(memory_space=pltpu.VMEM)
    in_hbm = pl.BlockSpec(memory_space=pltpu.HBM)
    scalars = pl.BlockSpec(memory_space=pltpu.SMEM)
    up, down = pl.pallas_call(
        functools.partial(pack_kernel, rows, levels),
        in_specs=[in_hbm, in_hbm],
        out_specs=[whole, whole],
        out_shape=[
            jax.ShapeDtypeStruct((levels * tracer_count, length), f32),
            jax.ShapeDtypeStruct((levels * tracer_count + levels // 2, length), f32),
        ],
        scratch_shapes=[
            pltpu.VMEM(tracers.shape, f32),
            pltpu.VMEM(courant_lat.shape, f32),
            pltpu.SemaphoreType.DMA((tracer_count + 1,)),
        ],
        compiler_params=params(),
        cost_estimate=cost(0, 600_000),
        name="pack",
    )(*(pltpu.with_memory_space_constraint(array, pltpu.HBM) for array in (tracers, courant_lat)))
    from_north = lax.ppermute(down, "lat", downward)
    from_south = lax.ppermute(up, "lat", upward)
    tracers, courant_lat, courant_lon, up, down = lax.optimization_barrier((tracers, courant_lat, courant_lon, up, down))

    ends = [jnp.concatenate([tracers[..., -2:], tracers[..., :2]], axis=-1), jnp.pad(courant_lon[None, ..., :1], ((0, 0),) * 3 + ((2, 1),))]
    sides = lax.ppermute(jnp.concatenate(ends, axis=0), "lon", swap)
    sides = jnp.transpose(sides, (0, 2, 1, 3))
    gap = jnp.zeros(sides.shape[:-1] + (width - sector - 4,), f32)
    sides = jnp.concatenate([jnp.zeros(sides.shape[:-1] + (LANES + sector - width,), f32), sides[..., 2:], gap, sides[..., :2]], axis=-1)
    not_pole = (lat > 0).astype(f32).reshape(1)
    base, north, lat_courant = pl.pallas_call(
        functools.partial(base_kernel, width),
        in_specs=[scalars, in_hbm, in_hbm, in_hbm, whole],
        out_specs=[whole] * 3,
        out_shape=[
            jax.ShapeDtypeStruct((tracer_count, rows, levels, width), f32),
            jax.ShapeDtypeStruct((tracer_count, levels, width), f32),
            jax.ShapeDtypeStruct((rows, levels, width), f32),
        ],
        scratch_shapes=[
            pltpu.VMEM(tracers.shape, f32),
            pltpu.VMEM(courant_lat.shape, f32),
            pltpu.VMEM(courant_lon.shape, f32),
            pltpu.SemaphoreType.DMA((tracer_count + 2,)),
        ],
        compiler_params=params(),
        cost_estimate=cost(0, 3_000_000),
        name="base",
    )(not_pole, *(pltpu.with_memory_space_constraint(array, pltpu.HBM) for array in (tracers, courant_lat, courant_lon)), sides)

    surface = jnp.pad(surface_flux, ((0, 0), (0, 0), (0, width - sector)))
    decay = decay_rate[:, :, None]
    block_count = rows * sector // BLOCK
    block_of = (np.arange(rows)[:, None] * sector + np.minimum(np.arange(width), sector - 1)[None]) // BLOCK
    owner_of = jnp.repeat(owners.reshape(block_count), BLOCK).reshape(rows, sector)
    owner_of = jnp.pad(owner_of, ((0, 0), (0, width - sector)))
    forward, inverse, numbers, weights = spectral_tables(length)
    row_ids = (lat * rows + jnp.arange(rows)).astype(f32)
    latitude = (-0.5 + (row_ids + 0.5) / (lat_count * rows)) * math.pi
    inverse_sine = np.where(numbers == 0, 1.0, 1.0 / np.where(numbers == 0, 1.0, np.sin(np.pi * numbers / length)))
    ratio = 2.0 * jnp.cos(latitude)[:, None] * jnp.asarray(inverse_sine, f32)[None]
    damping = jnp.where(jnp.asarray(numbers == 0)[None], 1.0, jnp.minimum(1.0, ratio * ratio))
    scale = damping * jnp.asarray(weights, f32)[None]

    base, scale, owner_of, surface, decay = lax.optimization_barrier((base, scale, owner_of, surface, decay))

    half = tracer_count // 2
    keep = (half * lax.axis_index("lon")).reshape(1)
    give = half - keep
    circles = jax.ShapeDtypeStruct((half, rows, levels, width), f32)
    result_shape = jax.ShapeDtypeStruct((levels, rows, sector), f32)
    spectra = jax.ShapeDtypeStruct((half * rows * levels, length), jnp.bfloat16)
    out_shape = jax.ShapeDtypeStruct(tracers.shape, f32)

    def run_physics(first, energy, shapes, last):
        shapes = shapes + [jax.ShapeDtypeStruct((1, LANES) if last else energy.shape, f32)]
        *results, energy = pl.pallas_call(
            functools.partial(physics_kernel, levels, sector, lat_count if last else 0),
            in_specs=[scalars] + [whole] * 10,
            out_specs=[whole] * len(shapes),
            out_shape=shapes,
            compiler_params=params(),
            cost_estimate=cost(50_000_000, 2_000_000),
            name="physics",
        )(first, base, north, from_south, from_north, lat_courant, surface, mixing, decay, owner_of, energy)
        return results, energy

    (given,), energy = run_physics(give, jnp.zeros((rows, 8, width), f32), [circles], False)
    other = lax.ppermute(given, "lon", swap)
    kept, energy = run_physics(keep, energy, [jax.ShapeDtypeStruct(circles.shape[1:], f32)] * half, True)

    forward, inverse = ([jnp.asarray(part) for table in tables for part in split_table(table)] for tables in (forward, inverse))
    distances = [1 << i for i in range(lat_count.bit_length() - 1)]

    def send_energy(energy):
        distance = distances.pop(0)
        return lax.ppermute(energy, "lat", [(i, i ^ distance) for i in range(lat_count)])

    coming = send_energy(energy)
    high, low = pl.pallas_call(
        functools.partial(forward_kernel, radix, half),
        in_specs=[whole] * (half + 6),
        out_specs=[whole] * 2,
        out_shape=[spectra] * 2,
        scratch_shapes=[pltpu.VMEM(spectra.shape, jnp.bfloat16)] * 2,
        compiler_params=params(),
        cost_estimate=cost(2_000_000_000, 6_000_000),
        name="forward",
    )(*kept, other, *forward, scale)
    coming, high = lax.optimization_barrier((coming, high))
    energy = energy + coming
    energy, high = lax.optimization_barrier((energy, high))

    coming = send_energy(energy)
    *results, back = pl.pallas_call(
        functools.partial(inverse_kernel, radix, half),
        in_specs=[scalars] + [whole] * (half + 7),
        out_specs=[whole] * (half + 1),
        out_shape=[result_shape] * half + [circles],
        scratch_shapes=[pltpu.VMEM(spectra.shape, f32)],
        compiler_params=params(),
        cost_estimate=cost(2_000_000_000, 6_000_000),
        name="inverse",
    )(polar_mask, *kept, other, high, low, *inverse)
    coming, back = lax.optimization_barrier((coming, back))
    energy = energy + coming
    energy, back = lax.optimization_barrier((energy, back))
    received = lax.ppermute(back, "lon", swap)

    coming = send_energy(energy)
    out = pl.pallas_call(
        finish_kernel,
        in_specs=[scalars] * 2 + [whole] * (half + 1),
        out_specs=in_hbm,
        out_shape=out_shape,
        scratch_shapes=[
            pltpu.VMEM((half,) + result_shape.shape, f32),
            pltpu.SemaphoreType.DMA((2 * half, RESULT_PIECES)),
        ],
        compiler_params=params(),
        cost_estimate=cost(0, 3_000_000),
        name="finish",
    )(keep, give, *results, received)
    coming, out = lax.optimization_barrier((coming, out))
    energy = energy + coming
    while distances:
        energy = energy + send_energy(energy)

    owner_energy = lax.dynamic_slice(energy, (0, lat), (1, 1)) / (block_count * BLOCK)
    return out, owner_energy


def solution(mesh):
    placed = (
        P("group", None, "lat", "lon"),
        P("group", "lat", "lon"),
        P("group", "lat", "lon"),
        P("group", "lat", "lon"),
        P(),
        P(),
        P(("group", "lat"), "lon", None, None),
        P(("group", "lat")),
    )
    return jax.shard_map(
        on_device,
        mesh=mesh,
        in_specs=placed,
        out_specs=(P("group", None, "lat", "lon"), P(("group", "lat"), "lon")),
        check_vma=False,
    )
```

time: 52.6 us -> 50.3 us (0.956)
  waiting for transfers between devices: 18.6 us -> 16.9 us
  other arithmetic: 2.77 us -> 1.08 us
  local copies, waits for them, and re-layouts: 4.22 us -> 5.45 us
    optimization_barrier x2 -> x1, local copies, waits for them, and re-layouts: 0.16 us -> 3.5 us  [on_device(): lax.optimization_barrier((tracers, courant_lat, courant_lon, up, down))]
    ppermute x1, waiting for transfers between devices: 16.7 us -> 14.7 us  [on_device(): from_south = lax.ppermute(up, 'lat', upward)]
    ppermute x5 -> x3, waiting for transfers between devices: 0.01 us -> 1.16 us  [the longest x1 1.16 us: on_device(): sides = lax.ppermute(jnp.concatenate(ends, axis=0), 'lon', swap)]
    ppermute x5 -> x3, starting transfers between devices: 1.15 us -> 0.14 us  [the longest x1 0.09 us: on_device(): other = lax.ppermute(given, 'lon', swap)]
    pad x1 -> x0, local copies, waits for them, and re-layouts: 0.99 us -> none  [on_device(): jnp.pad(lat_by_row * not_pole[:, None, None], ((0, 0), (0, 0), (0, width...]
    ppermute x3, starting transfers between devices: 5.6 us -> 6.56 us  [send_energy(): lax.ppermute(energy, 'lat', [(i, i ^ distance) for i in range(lat_count)])]
    concatenate x3, other arithmetic: 1.22 us -> 0.36 us  [the longest x1 0.24 us: on_device(): jnp.concatenate([jnp.zeros(sides.shape[:-1] + (LANES + sector - width,),...]
    squeeze x1 -> x0, local copies, waits for them, and re-layouts: 0.85 us -> none  [on_device(): sides[tracer_count, ..., :1]]
  transfers between devices with their start and end apart: 10 -> 8, of which waited for: 2 -> 5; matrix products, arithmetic and copies ran while one was open for 11% -> 12% of each run, Pallas kernels for 17% -> 18%
where the time goes in v2:
time: 50.3 us; the launch traced here: 50 us
  waiting for transfers between devices  16.9 us (34%)
  starting transfers between devices  13.6 us (27%)
  Pallas kernels  12 us (24%)
  local copies, waits for them, and re-layouts  5.45 us (11%)
  other arithmetic  1.08 us (2%)
  between operations  0.96 us (2%)
    ppermute x1, waiting for transfers between devices, on_device(): from_south = lax.ppermute(up, 'lat', upward)  14.7 us
    ppermute x3, starting transfers between devices, send_energy(): lax.ppermute(energy, 'lat', [(i, i ^ distance) for i in range(lat_count)])  6.56 us
    ppermute x1, starting transfers between devices, on_device(): from_south = lax.ppermute(up, 'lat', upward)  5.64 us
    pallas_call x1, Pallas kernels, on_device(): pl.pallas_call(functools.partial(base_kernel, width), in_specs=[scalars,...  3.99 us
    optimization_barrier x1, local copies, waits for them, and re-layouts, on_device(): lax.optimization_barrier((tracers, courant_lat, courant_lon, up, down))  3.5 us
    pallas_call x1, Pallas kernels, on_device(): pl.pallas_call(functools.partial(pack_kernel, rows, levels), in_specs=[in...  2.63 us
    pallas_call x1, Pallas kernels, on_device(): pl.pallas_call(functools.partial(inverse_kernel, radix, half), in_specs=[...  1.81 us
    ppermute x1, starting transfers between devices, on_device(): from_north = lax.ppermute(down, 'lat', downward)  1.29 us
  transfers between devices with their start and end apart: 8, of which 5 were waited for; matrix products, arithmetic and copies ran while one was open for 12% of the time, Pallas kernels for 18%

profile of v2, /device:TPU:0, one launch (start us, length us, event | category | flops | bytes accessed | tf_op | source)
XLA Modules:
  0.0 50.0 jit_solution(9846393752547784631)
XLA Ops:
  0.6 0.0 copy-start.10
  0.6 2.6 %pack.1 = (f32[128,1152]{1,0:T(8,128)}, f32[144,1152]{1,0:T(8,128)}) custom-call(f32[4,32,4,576]{3,2,1,0:T(4,128)} %tracer_hbm.2, f32[32,4,576]{2,1,0:T(4,128)} %lat_hbm), custom_call_target="tpu_custom_call" | custom-call | bytes 600000 | tf_op jit(solution)/shard_map/pack/pallas_call | solution.py:339
  3.3 1.3 %collective-permute-start.2 = (f32[144,1152]{1,0:T(8,128)}, f32[144,1152]{1,0:T(8,128)S(1)}, u32[]{:S(2)}, u32[]{:S(2)}) collective-permute-start(f32[144,1152]{1,0:T(8,128)} %get-tuple-element.36), channel_id=1, source_target_pairs={{2,0},{4,2},{6,4},{8,6},{10,8},{12,10},{14,12},{3,1},{5,3},{7,5},{... | collective-permute-start | bytes 1990664 | tf_op jit(solution)/shard_map/ppermute | solution.py:356
  4.6 0.0 slice-start
  4.6 5.6 %collective-permute-start.1 = (f32[128,1152]{1,0:T(8,128)}, f32[128,1152]{1,0:T(8,128)S(1)}, u32[]{:S(2)}, u32[]{:S(2)}) collective-permute-start(f32[128,1152]{1,0:T(8,128)} %get-tuple-element.35), channel_id=1, source_target_pairs={{0,2},{2,4},{4,6},{6,8},{8,10},{10,12},{12,14},{1,3},{3,5},{5,7},{... | collective-permute-start | bytes 1769480 | tf_op jit(solution)/shard_map/ppermute | solution.py:357
  10.2 0.0 copy-done.10
  10.3 3.5 %copy.34 = f32[4,32,4,576]{1,3,2,0:T(8,128)} copy(f32[4,32,4,576]{3,2,1,0:T(4,128)S(1)} %copy-done.10) | data formatting | bytes 2359296 | tf_op jit(solution)/shard_map/optimization_barrier | solution.py:358
  13.8 0.0 copy-start.16
  13.8 0.9 %fusion = (f32[4,32,4,2]{1,3,2,0:T(2,128)S(1)}, f32[4,32,4,2]{1,3,2,0:T(2,128)S(1)}) fusion(f32[4,32,4,576]{1,3,2,0:T(8,128)} %copy.34), kind=kLoop, calls=%fused_computation.7 | loop fusion | bytes 16384 | tf_op jit(solution)/shard_map/slice | solution.py:360
  14.8 0.2 copy.38
  14.9 0.0 slice-done
  14.9 0.1 copy.36
  15.0 0.1 copy.37
  15.1 0.1 select_maximum_fusion
  15.2 0.0 collective-permute-start
  15.3 0.0 copy-done.12
  15.4 0.0 copy-done.13
  15.4 0.0 copy-done.15
  15.4 0.1 select_multiply_fusion.refs_7_
  15.5 0.1 pad.17.clone
  15.6 0.0 copy-done.11
  15.6 0.0 copy-done.16
  15.6 0.1 broadcast_in_dim.39
  15.7 0.1 reshape_reshape.3
  15.7 1.2 %collective-permute-done = f32[5,32,4,4]{3,1,2,0:T(8,128)S(1)} collective-permute-done((f32[5,32,4,4]{3,1,2,0:T(8,128)S(1)}, f32[5,32,4,4]{3,1,2,0:T(8,128)S(1)}, u32[]{:S(2)}, u32[]{:S(2)}) %collective-permute-start) | collective-permute-done | bytes 10272 | tf_op jit(solution)/shard_map/ppermute | solution.py:361
  16.9 0.2 fusion.1
  17.1 0.2 pad_maximum_fusion.side_ref
  17.3 0.0 copy-start.14
  17.3 0.0 copy-start
  17.3 4.0 %base.1 = (f32[4,4,32,640]{3,2,1,0:T(8,128)S(1)}, f32[4,32,640]{2,1,0:T(8,128)S(1)}, f32[4,32,640]{2,1,0:T(8,128)S(1)}) custom-call(f32[1]{0:T(128)} %bitcast.1.not_pole_ref, f32[4,32,4,576]{3,2,1,0:T(4,128)} %tracer_hbm.2, f32[32,4,576]{2,1,0:T(4,128)} %lat_hbm, f32[32,4,576]{2,1,0:T(4,128)} %lon_hbm, f32[5,4,32,128]{3,2,1,0:T(8,128)S(1)} %pad_maximum_fusion.side_ref), custom_call_target="tpu_custom_call" | custom-call | bytes 3000000 | tf_op jit(solution)/shard_map/base/pallas_call | solution.py:366
  21.3 0.0 copy-done.14
  21.3 0.1 copy.40.refs_7_
  21.4 14.7 %collective-permute-done.1.refs_2_ = f32[128,1152]{1,0:T(8,128)S(1)} collective-permute-done((f32[128,1152]{1,0:T(8,128)}, f32[128,1152]{1,0:T(8,128)S(1)}, u32[]{:S(2)}, u32[]{:S(2)}) %collective-permute-start.1) | collective-permute-done | bytes 589856 | tf_op jit(solution)/shard_map/ppermute | solution.py:357
  36.1 0.0 collective-permute-done.2.refs_3_
  36.1 0.0 copy-done
  36.2 0.5 physics.2
  36.6 0.1 collective-permute-start.4
  36.7 0.0 copy-start.5
  36.8 0.0 copy-start.8
  36.8 0.0 copy-start.9
  36.8 0.6 %physics.3 = (f32[4,32,640]{2,1,0:T(8,128)S(1)}, f32[4,32,640]{2,1,0:T(8,128)S(1)}, f32[1,128]{1,0:T(1,128)S(1)}) custom-call(s32[1]{0:T(128)} %bitcast.first_ref.keep_ref, f32[4,4,32,640]{3,2,1,0:T(8,128)S(1)} %get-tuple-element.41.refs_0_, f32[4,32,640]{2,1,0:T(8,128)S(1)} %get-tuple-element.42.refs_1_, f32[128,1152]{1,0:T(8,128)S(1)} %collective-permute-done.1.refs_2_, ...), custom_call_target="tpu_custom_call" | custom-call | flops 50000000 | bytes 2000000 | tf_op jit(solution)/shard_map/physics/pallas_call | solution.py:412
  37.4 2.4 %collective-permute-start.3 = (f32[1,128]{1,0:T(1,128)S(1)}, f32[1,128]{1,0:T(1,128)S(1)}, u32[]{:S(2)}, u32[]{:S(2)}) collective-permute-start(f32[1,128]{1,0:T(1,128)S(1)} %get-tuple-element.48), channel_id=1, source_target_pairs={{0,2},{2,0},{4,6},{6,4},{8,10},{10,8},{12,14},{14,12},{1,3},{3,1},... | collective-permute-start | bytes 1544 | tf_op jit(solution)/shard_map/ppermute | solution.py:432
  39.8 0.0 collective-permute-done.4.refs_2_
  39.8 0.0 copy-done.4
  39.8 0.0 copy-done.5
  39.8 0.0 copy-done.8
  39.9 0.0 copy-start.1
  39.9 0.0 copy-start.2
  39.9 0.0 copy-start.3
  39.9 0.0 copy-start.6
  39.9 0.0 copy-start.7
  39.9 1.2 %forward.1 = (bf16[256,1152]{1,0:T(8,128)(2,1)S(1)}, bf16[256,1152]{1,0:T(8,128)(2,1)S(1)}) custom-call(f32[4,32,640]{2,1,0:T(8,128)S(1)} %get-tuple-element.49.refs_0_, f32[4,32,640]{2,1,0:T(8,128)S(1)} %get-tuple-element.50.refs_1_, f32[2,4,32,640]{3,2,1,0:T(8,128)S(1)} %collective-permute-done.4.refs_2_, bf16[1024,256]{1,0:T(8,128)(2,1)S(1)} %copy-done.4, ...), custom_call_target="tpu_custom_call" | custom-call | flops 2000000000 | bytes 6000000 | tf_op jit(solution)/shard_map/forward/pallas_call | solution.py:435
  41.1 0.2 collective-permute-done.3
  41.4 1.6 %collective-permute-start.5 = (f32[1,128]{1,0:T(1,128)S(1)}, f32[1,128]{1,0:T(1,128)S(1)}, u32[]{:S(2)}, u32[]{:S(2)}) collective-permute-start(f32[1,128]{1,0:T(1,128)S(1)} %add.46), channel_id=1, source_target_pairs={{0,4},{2,6},{4,0},{6,2},{8,12},{10,14},{12,8},{14,10},{1,5},{3,7},... | collective-permute-start | bytes 1544 | tf_op jit(solution)/shard_map/ppermute | solution.py:432
  42.9 0.0 copy-done.2
  42.9 0.0 copy-done.6
  43.0 1.8 %inverse.1 = (f32[32,4,576]{2,1,0:T(4,128)S(1)}, f32[32,4,576]{2,1,0:T(4,128)S(1)}, f32[2,4,32,640]{3,2,1,0:T(8,128)S(1)}) custom-call(s32[4]{0:T(128)S(1)} %copy-done.1, f32[4,32,640]{2,1,0:T(8,128)S(1)} %get-tuple-element.49.refs_0_, f32[4,32,640]{2,1,0:T(8,128)S(1)} %get-tuple-element.50.refs_1_, f32[2,4,32,640]{3,2,1,0:T(8,128)S(1)} %collective-permute-done.4.refs_2_, ...), custom_call_target="tpu_custom_call" | custom-call | flops 2000000000 | bytes 6000000 | tf_op jit(solution)/shard_map/inverse/pallas_call | solution.py:450
  44.8 0.1 collective-permute-done.5
  44.9 0.0 collective-permute-start.7
  44.9 2.6 %collective-permute-start.6 = (f32[1,128]{1,0:T(1,128)S(1)}, f32[1,128]{1,0:T(1,128)S(1)}, u32[]{:S(2)}, u32[]{:S(2)}) collective-permute-start(f32[1,128]{1,0:T(1,128)S(1)} %add.47), channel_id=1, source_target_pairs={{0,8},{2,10},{4,12},{6,14},{8,0},{10,2},{12,4},{14,6},{1,9},{3,11}... | collective-permute-start | bytes 1544 | tf_op jit(solution)/shard_map/ppermute | solution.py:432
  47.5 0.0 collective-permute-done.7.refs_2_
  47.5 1.2 %finish.1 = f32[4,32,4,576]{3,2,1,0:T(4,128)} custom-call(s32[1]{0:T(128)} %bitcast.first_ref.keep_ref, s32[1]{0:T(128)S(6)} %sub.3.first_ref.give_ref, f32[32,4,576]{2,1,0:T(4,128)S(1)} %get-tuple-element.63.refs_0_, f32[32,4,576]{2,1,0:T(4,128)S(1)} %get-tuple-element.64.refs_1_, f32[2,4,32,640]{3,2,1,0:T(8,128)S(1)} %collective-permute-done.7.refs_2_), custom_call_target="tpu_custom_call" | custom-call | bytes 3000000 | tf_op jit(solution)/shard_map/finish/pallas_call | solution.py:466
  48.7 0.7 %collective-permute-done.6 = f32[1,128]{1,0:T(1,128)S(1)} collective-permute-done((f32[1,128]{1,0:T(1,128)S(1)}, f32[1,128]{1,0:T(1,128)S(1)}, u32[]{:S(2)}, u32[]{:S(2)}) %collective-permute-start.6) | collective-permute-done | bytes 544 | tf_op jit(solution)/shard_map/ppermute | solution.py:432
  49.4 0.6 %fusion.2 = f32[1,1]{1,0:T(1,128)} fusion(f32[1,128]{1,0:T(1,128)S(1)} %add.48, s32[]{:T(128)S(6)} %select_n.8), kind=kLoop, calls=%fused_computation.9 | loop fusion | flops 1 | bytes 12 | tf_op jit(solution)/shard_map/div | solution.py:484
  (20 shorter events, 0.1 us)
Async XLA Ops:
  0.6 9.6 %copy-start.10 = (f32[4,32,4,576]{3,2,1,0:T(4,128)S(1)}, f32[4,32,4,576]{3,2,1,0:T(4,128)}, u32[]{:S(2)}) copy-start(f32[4,32,4,576]{3,2,1,0:T(4,128)} %tracer_hbm.2) | copy-start | bytes 3538948
  3.3 32.9 %collective-permute-start.2 = (f32[144,1152]{1,0:T(8,128)}, f32[144,1152]{1,0:T(8,128)S(1)}, u32[]{:S(2)}, u32[]{:S(2)}) collective-permute-start(f32[144,1152]{1,0:T(8,128)} %get-tuple-element.36), channel_id=1, source_target_pairs={{2,0},{4,2},{6,4},{8,6},{10,8},{12,10},{14,12},{3,1},{5,3},{7,5},{... | collective-permute-start | bytes 1990664 | tf_op jit(solution)/shard_map/ppermute | solution.py:356
  4.6 10.3 %slice-start = ((f32[32,4,576]{2,1,0:T(4,128)}), f32[32,4,1]{2,1,0:T(4,128)S(1)}, s32[]{:S(2)}) async-start(f32[32,4,576]{2,1,0:T(4,128)} %lon_hbm), calls=%async_computation | async-start | bytes 131072 | tf_op jit(solution)/shard_map/slice | solution.py:360
  4.6 31.5 %collective-permute-start.1 = (f32[128,1152]{1,0:T(8,128)}, f32[128,1152]{1,0:T(8,128)S(1)}, u32[]{:S(2)}, u32[]{:S(2)}) collective-permute-start(f32[128,1152]{1,0:T(8,128)} %get-tuple-element.35), channel_id=1, source_target_pairs={{0,2},{2,4},{4,6},{6,8},{8,10},{10,12},{12,14},{1,3},{3,5},{5,7},{... | collective-permute-start | bytes 1769480 | tf_op jit(solution)/shard_map/ppermute | solution.py:357
  13.8 1.6 %copy-start.12 = (f32[1152]{0:T(1024)S(1)}, f32[1152]{0:T(1024)}, u32[]{:S(2)}) copy-start(f32[1152]{0:T(1024)} %constant.62.clone) | copy-start | bytes 13828
  13.8 1.6 %copy-start.13 = (f32[1152]{0:T(1024)S(1)}, f32[1152]{0:T(1024)}, u32[]{:S(2)}) copy-start(f32[1152]{0:T(1024)} %constant.64.clone) | copy-start | bytes 13828
  13.8 1.6 %copy-start.15 = (pred[1152]{0:T(1024)(128)(4,1)S(1)}, pred[1152]{0:T(1024)(128)(4,1)}, u32[]{:S(2)}) copy-start(pred[1152]{0:T(1024)(128)(4,1)} %constant.63.clone) | copy-start | bytes 3460
  13.8 1.8 %copy-start.11 = (f32[4,4,576]{2,1,0:T(4,128)S(1)}, f32[4,4,576]{2,1,0:T(4,128)}, u32[]{:S(2)}) copy-start(f32[4,4,576]{2,1,0:T(4,128)} %param.22) | copy-start | bytes 110596
  13.8 1.8 %copy-start.16 = (s32[1,1,18,1]{2,3,1,0:T(1,128)S(1)}, s32[1,1,18,1]{2,3,1,0:T(1,128)}, u32[]{:S(2)}) copy-start(s32[1,1,18,1]{2,3,1,0:T(1,128)} %param.25) | copy-start | bytes 220
  15.2 1.7 %collective-permute-start = (f32[5,32,4,4]{3,1,2,0:T(8,128)S(1)}, f32[5,32,4,4]{3,1,2,0:T(8,128)S(1)}, u32[]{:S(2)}, u32[]{:S(2)}) collective-permute-start(f32[5,32,4,4]{3,1,2,0:T(8,128)S(1)} %select_maximum_fusion), channel_id=1, source_target_pairs={{0,1},{1,0},{2,3},{3,2},{4,5},{5,4},{6,7},{7,6},{8,9},{9,8},{10,11... | collective-permute-start | bytes 30728 | tf_op jit(solution)/shard_map/ppermute | solution.py:361
  17.3 4.0 %copy-start.14 = (f32[4,32]{1,0:T(4,128)S(1)}, f32[4,32]{1,0:T(4,128)}, u32[]{:S(2)}) copy-start(f32[4,32]{1,0:T(4,128)} %param.24) | copy-start | bytes 1540
  17.3 18.8 %copy-start = (f32[32,32]{1,0:T(8,128)S(1)}, f32[32,32]{1,0:T(8,128)}, u32[]{:S(2)}) copy-start(f32[32,32]{1,0:T(8,128)} %refs_6_.5) | copy-start | bytes 12292
  36.6 3.2 %collective-permute-start.4 = (f32[2,4,32,640]{3,2,1,0:T(8,128)S(1)}, f32[2,4,32,640]{3,2,1,0:T(8,128)S(1)}, u32[]{:S(2)}, u32[]{:S(2)}) collective-permute-start(f32[2,4,32,640]{3,2,1,0:T(8,128)S(1)} %get-tuple-element.51), channel_id=1, source_target_pairs={{0,1},{1,0},{2,3},{3,2},{4,5},{5,4},{6,7},{7,6},{8,9},{9,8},{10,11... | collective-permute-start | bytes 1966088 | tf_op jit(solution)/shard_map/ppermute | solution.py:424
  36.7 3.1 %copy-start.4 = (bf16[1024,256]{1,0:T(8,128)(2,1)S(1)}, bf16[1024,256]{1,0:T(8,128)(2,1)}, u32[]{:S(2)}) copy-start(bf16[1024,256]{1,0:T(8,128)(2,1)} %constant.65.clone.refs_3_) | copy-start | bytes 1572868
  36.7 3.1 %copy-start.5 = (bf16[1024,256]{1,0:T(8,128)(2,1)S(1)}, bf16[1024,256]{1,0:T(8,128)(2,1)}, u32[]{:S(2)}) copy-start(bf16[1024,256]{1,0:T(8,128)(2,1)} %constant.66.clone.refs_4_) | copy-start | bytes 1572868
  36.8 3.1 %copy-start.8 = (bf16[128,128]{1,0:T(8,128)(2,1)S(1)}, bf16[128,128]{1,0:T(8,128)(2,1)}, u32[]{:S(2)}) copy-start(bf16[128,128]{1,0:T(8,128)(2,1)} %constant.67.clone.refs_5_) | copy-start | bytes 98308
  36.8 3.1 %copy-start.9 = (bf16[128,128]{1,0:T(8,128)(2,1)S(1)}, bf16[128,128]{1,0:T(8,128)(2,1)}, u32[]{:S(2)}) copy-start(bf16[128,128]{1,0:T(8,128)(2,1)} %constant.68.clone.refs_6_) | copy-start | bytes 98308
  37.4 3.9 %collective-permute-start.3 = (f32[1,128]{1,0:T(1,128)S(1)}, f32[1,128]{1,0:T(1,128)S(1)}, u32[]{:S(2)}, u32[]{:S(2)}) collective-permute-start(f32[1,128]{1,0:T(1,128)S(1)} %get-tuple-element.48), channel_id=1, source_target_pairs={{0,2},{2,0},{4,6},{6,4},{8,10},{10,8},{12,14},{14,12},{1,3},{3,1},... | collective-permute-start | bytes 1544 | tf_op jit(solution)/shard_map/ppermute | solution.py:432
  39.9 3.1 %copy-start.1 = (s32[4]{0:T(128)S(1)}, s32[4]{0:T(128)}, u32[]{:S(2)}) copy-start(s32[4]{0:T(128)} %mask_ref.1) | copy-start | bytes 52
  39.9 3.1 %copy-start.2 = (bf16[1024,256]{1,0:T(8,128)(2,1)S(1)}, bf16[1024,256]{1,0:T(8,128)(2,1)}, u32[]{:S(2)}) copy-start(bf16[1024,256]{1,0:T(8,128)(2,1)} %constant.69.clone.refs_5_) | copy-start | bytes 1572868
  39.9 3.1 %copy-start.3 = (bf16[1024,256]{1,0:T(8,128)(2,1)S(1)}, bf16[1024,256]{1,0:T(8,128)(2,1)}, u32[]{:S(2)}) copy-start(bf16[1024,256]{1,0:T(8,128)(2,1)} %constant.70.clone.refs_6_) | copy-start | bytes 1572868
  39.9 3.0 %copy-start.6 = (bf16[128,128]{1,0:T(8,128)(2,1)S(1)}, bf16[128,128]{1,0:T(8,128)(2,1)}, u32[]{:S(2)}) copy-start(bf16[128,128]{1,0:T(8,128)(2,1)} %constant.71.clone.refs_7_) | copy-start | bytes 98308
  39.9 3.0 %copy-start.7 = (bf16[128,128]{1,0:T(8,128)(2,1)S(1)}, bf16[128,128]{1,0:T(8,128)(2,1)}, u32[]{:S(2)}) copy-start(bf16[128,128]{1,0:T(8,128)(2,1)} %constant.72.clone.refs_8_) | copy-start | bytes 98308
  41.4 3.5 %collective-permute-start.5 = (f32[1,128]{1,0:T(1,128)S(1)}, f32[1,128]{1,0:T(1,128)S(1)}, u32[]{:S(2)}, u32[]{:S(2)}) collective-permute-start(f32[1,128]{1,0:T(1,128)S(1)} %add.46), channel_id=1, source_target_pairs={{0,4},{2,6},{4,0},{6,2},{8,12},{10,14},{12,8},{14,10},{1,5},{3,7},... | collective-permute-start | bytes 1544 | tf_op jit(solution)/shard_map/ppermute | solution.py:432
  44.9 2.6 %collective-permute-start.7 = (f32[2,4,32,640]{3,2,1,0:T(8,128)S(1)}, f32[2,4,32,640]{3,2,1,0:T(8,128)S(1)}, u32[]{:S(2)}, u32[]{:S(2)}) collective-permute-start(f32[2,4,32,640]{3,2,1,0:T(8,128)S(1)} %get-tuple-element.65), channel_id=1, source_target_pairs={{0,1},{1,0},{2,3},{3,2},{4,5},{5,4},{6,7},{7,6},{8,9},{9,8},{10,11... | collective-permute-start | bytes 1966088 | tf_op jit(solution)/shard_map/ppermute | solution.py:463
  44.9 4.5 %collective-permute-start.6 = (f32[1,128]{1,0:T(1,128)S(1)}, f32[1,128]{1,0:T(1,128)S(1)}, u32[]{:S(2)}, u32[]{:S(2)}) collective-permute-start(f32[1,128]{1,0:T(1,128)S(1)} %add.47), channel_id=1, source_target_pairs={{0,8},{2,10},{4,12},{6,14},{8,0},{10,2},{12,4},{14,6},{1,9},{3,11}... | collective-permute-start | bytes 1544 | tf_op jit(solution)/shard_map/ppermute | solution.py:432

commit v3 on v2

--- a/solution.py
+++ b/solution.py
@@ -75,30 +75,60 @@
     return jnp.concatenate(parts, axis=1)
 
 
-def pack_kernel(rows, levels, tracer_hbm, courant_hbm, up_ref, down_ref, tracer_ref, courant_ref, sems):
-    tracer_count = tracer_ref.shape[0]
-    copies = [pltpu.make_async_copy(tracer_hbm.at[t], tracer_ref.at[t], sems.at[t]) for t in range(tracer_count)]
-    copies.append(pltpu.make_async_copy(courant_hbm, courant_ref, sems.at[tracer_count]))
+def start_copies(pairs, sems):
+    copies = [pltpu.make_async_copy(source, target, sems.at[i]) for i, (source, target) in enumerate(pairs)]
     for copy in copies:
         copy.start()
-    for t in range(tracer_count):
+    return copies
+
+
+def pack_halo(tracer_ref, t, out_ref, upward):
+    levels, rows = tracer_ref.shape[1:3]
+    place = slice(levels * t, levels * (t + 1))
+
+    @pl.when(upward)
+    def _():
+        out_ref[place, :] = pack_rows(tracer_ref[t, :, rows - 2, :], tracer_ref[t, :, rows - 1, :])
+
+    @pl.when(jnp.logical_not(upward))
+    def _():
+        out_ref[place, :] = pack_rows(tracer_ref[t, :, 0, :], tracer_ref[t, :, 1, :])
+
+
+def pack_kernel(even_ref, tracer_hbm, lat_hbm, inner_ref, outer_ref, courant_ref, tracer_ref, lat_ref, sems):
+    count = tracer_ref.shape[0]
+    levels = tracer_ref.shape[1]
+    copies = start_copies([(tracer_hbm.at[t], tracer_ref.at[t]) for t in range(count)] + [(lat_hbm, lat_ref)], sems)
+    even = even_ref[0] == 1
+    for t in range(count):
         copies[t].wait()
-        place = slice(levels * t, levels * (t + 1))
-        up_ref[place, :] = pack_rows(tracer_ref[t, :, rows - 2, :], tracer_ref[t, :, rows - 1, :])
-        down_ref[place, :] = pack_rows(tracer_ref[t, :, 0, :], tracer_ref[t, :, 1, :])
-    copies[tracer_count].wait()
-    courant = courant_ref[:, 0, :]
-    down_ref[levels * tracer_count :, :] = pack_rows(courant[: levels // 2], courant[levels // 2 :])
+        pack_halo(tracer_ref, t, inner_ref, even)
+        pack_halo(tracer_ref, t, outer_ref, jnp.logical_not(even))
+    copies[count].wait()
+    courant = lat_ref[:, 0, :]
+    courant_ref[...] = pack_rows(courant[: levels // 2], courant[levels // 2 :])
+
+
+def side_kernel(tracer_hbm, lon_hbm, side_ref, tracer_ref, lon_ref, sems):
+    count, levels, rows, sector = tracer_ref.shape
+    copies = start_copies([(tracer_hbm.at[t], tracer_ref.at[t]) for t in range(count)] + [(lon_hbm, lon_ref)], sems)
+    shift, whole = sector % LANES, sector // LANES * LANES
+    lane = lax.broadcasted_iota(jnp.int32, (levels, LANES), 1)
+    for i in range(count + 1):
+        copies[i].wait()
+        for r in range(rows):
+            values = tracer_ref[i, :, r, :] if i < count else lon_ref[:, r, :]
+            first = pltpu.roll(values[:, :LANES], shift, 1)
+            last = jnp.concatenate([values[:, whole:], values[:, whole:]], axis=1)
+            side_ref[i, r] = jnp.where(lane < LANES - 2, first, last)
 
 
 def base_kernel(width, not_pole_ref, tracer_hbm, lat_hbm, lon_hbm, side_ref, base_ref, north_ref, courant_ref, *scratch):
     tracer_ref, lat_ref, lon_ref, sems = scratch
     tracer_count, levels, rows, sector = tracer_ref.shape
     whole = sector // LANES * LANES
-    copies = [pltpu.make_async_copy(source, target, sems.at[i]) for i, (source, target) in enumerate(((lat_hbm, lat_ref), (lon_hbm, lon_ref)))]
-    copies += [pltpu.make_async_copy(tracer_hbm.at[t], tracer_ref.at[t], sems.at[t + 2]) for t in range(tracer_count)]
-    for copy in copies:
-        copy.start()
+    pairs = [(lat_hbm, lat_ref), (lon_hbm, lon_ref)] + [(tracer_hbm.at[t], tracer_ref.at[t]) for t in range(tracer_count)]
+    copies = start_copies(pairs, sems)
 
     def beside(values, side):
         return jnp.concatenate([values[:, :whole], values[:, whole:], side[:, sector - whole :]], axis=1)
@@ -128,14 +158,15 @@
             base_ref[t, r] = value
 
 
-def physics_kernel(levels, sector, owner_count, first_ref, *refs):
-    base_ref, north_ref, low_ref, high_ref, courant_ref, surface_ref, mixing_ref, decay_ref, owner_ref, energy_in_ref = refs[:10]
-    physics_refs, energy_ref = refs[10:-1], refs[-1]
+def physics_kernel(levels, sector, owner_count, first_ref, even_ref, *refs):
+    base_ref, north_ref, inner_ref, outer_ref, top_ref, courant_ref, surface_ref, mixing_ref, decay_ref, owner_ref = refs[:10]
+    energy_in_ref, physics_refs, energy_ref = refs[10], refs[11:-1], refs[-1]
     if len(physics_refs) == 1:
         physics_refs = [physics_refs[0].at[i] for i in range(physics_refs[0].shape[0])]
     rows, width = base_ref.shape[1], base_ref.shape[-1]
     courant = [courant_ref[r] for r in range(rows)]
-    top = high_ref[high_ref.shape[0] - levels // 2 :, :]
+    even = even_ref[0] == 1
+    top = top_ref[...]
     top = jnp.concatenate([top[:, :width], second_half(top, sector)], axis=0)
     mix_high, mix_low = split_high_low(mixing_ref[...])
     mix = jnp.concatenate([mix_high, mix_high, mix_low, mix_low], axis=1)
@@ -145,7 +176,8 @@
     for i, physics_ref in enumerate(physics_refs):
         t = first_ref[0] + i
         place = pl.ds(pl.multiple_of(levels * t, levels), levels)
-        low, high = low_ref[place, :], high_ref[place, :]
+        inner, outer = inner_ref[place, :], outer_ref[place, :]
+        low, high = jnp.where(even, outer, inner), jnp.where(even, inner, outer)
         low_a, low_b = low[:, :width], second_half(low, sector)
         high_a, high_b = high[:, :width], second_half(high, sector)
         south = courant[0] * (NEAR * low_b - FAR * low_a)
@@ -329,39 +361,44 @@
     length = 2 * sector
     width = -(-sector // LANES) * LANES
     radix = length // LANES
-    upward = [(i, i + 1) for i in range(lat_count - 1)]
     downward = [(i + 1, i) for i in range(lat_count - 1)]
     swap = [(0, 1), (1, 0)]
 
     whole = pl.BlockSpec(memory_space=pltpu.VMEM)
     in_hbm = pl.BlockSpec(memory_space=pltpu.HBM)
     scalars = pl.BlockSpec(memory_space=pltpu.SMEM)
-    up, down = pl.pallas_call(
-        functools.partial(pack_kernel, rows, levels),
-        in_specs=[in_hbm, in_hbm],
-        out_specs=[whole, whole],
-        out_shape=[
-            jax.ShapeDtypeStruct((levels * tracer_count, length), f32),
-            jax.ShapeDtypeStruct((levels * tracer_count + levels // 2, length), f32),
-        ],
-        scratch_shapes=[
-            pltpu.VMEM(tracers.shape, f32),
-            pltpu.VMEM(courant_lat.shape, f32),
-            pltpu.SemaphoreType.DMA((tracer_count + 1,)),
-        ],
+    even = (1 - lat % 2).reshape(1)
+    inside = [pair for i in range(0, lat_count - 1, 2) for pair in ((i, i + 1), (i + 1, i))]
+    across = [pair for i in range(1, lat_count - 1, 2) for pair in ((i, i + 1), (i + 1, i))]
+    fields = [pltpu.with_memory_space_constraint(array, pltpu.HBM) for array in (tracers, courant_lat, courant_lon)]
+    field_buffers = [pltpu.VMEM(array.shape, f32) for array in (tracers, courant_lat, courant_lon)]
+    inner, outer, courant_row = pl.pallas_call(
+        pack_kernel,
+        in_specs=[scalars] + [in_hbm] * 2,
+        out_specs=[whole] * 3,
+        out_shape=[pltpu.VMEM((levels * tracer_count, length), f32)] * 2 + [pltpu.VMEM((levels // 2, length), f32)],
+        scratch_shapes=field_buffers[:2] + [pltpu.SemaphoreType.DMA((tracer_count + 1,))],
         compiler_params=params(),
         cost_estimate=cost(0, 600_000),
         name="pack",
-    )(*(pltpu.with_memory_space_constraint(array, pltpu.HBM) for array in (tracers, courant_lat)))
-    from_north = lax.ppermute(down, "lat", downward)
-    from_south = lax.ppermute(up, "lat", upward)
-    tracers, courant_lat, courant_lon, up, down = lax.optimization_barrier((tracers, courant_lat, courant_lon, up, down))
-
-    ends = [jnp.concatenate([tracers[..., -2:], tracers[..., :2]], axis=-1), jnp.pad(courant_lon[None, ..., :1], ((0, 0),) * 3 + ((2, 1),))]
-    sides = lax.ppermute(jnp.concatenate(ends, axis=0), "lon", swap)
-    sides = jnp.transpose(sides, (0, 2, 1, 3))
-    gap = jnp.zeros(sides.shape[:-1] + (width - sector - 4,), f32)
-    sides = jnp.concatenate([jnp.zeros(sides.shape[:-1] + (LANES + sector - width,), f32), sides[..., 2:], gap, sides[..., :2]], axis=-1)
+    )(even, *fields[:2])
+    from_inside = lax.ppermute(inner, "lat", inside)
+    from_across = lax.ppermute(outer, "lat", across)
+    top = lax.ppermute(courant_row, "lat", downward)
+
+    fields, inner = lax.optimization_barrier((fields, inner))
+    fields = [pltpu.with_memory_space_constraint(array, pltpu.HBM) for array in fields]
+    sides = pl.pallas_call(
+        side_kernel,
+        in_specs=[in_hbm] * 2,
+        out_specs=whole,
+        out_shape=jax.ShapeDtypeStruct((tracer_count + 1, rows, levels, LANES), f32),
+        scratch_shapes=[field_buffers[0], field_buffers[2], pltpu.SemaphoreType.DMA((tracer_count + 1,))],
+        compiler_params=params(),
+        cost_estimate=cost(0, 0),
+        name="side",
+    )(fields[0], fields[2])
+    sides = lax.ppermute(sides, "lon", swap)
     not_pole = (lat > 0).astype(f32).reshape(1)
     base, north, lat_courant = pl.pallas_call(
         functools.partial(base_kernel, width),
@@ -372,16 +409,11 @@
             jax.ShapeDtypeStruct((tracer_count, levels, width), f32),
             jax.ShapeDtypeStruct((rows, levels, width), f32),
         ],
-        scratch_shapes=[
-            pltpu.VMEM(tracers.shape, f32),
-            pltpu.VMEM(courant_lat.shape, f32),
-            pltpu.VMEM(courant_lon.shape, f32),
-            pltpu.SemaphoreType.DMA((tracer_count + 2,)),
-        ],
+        scratch_shapes=field_buffers + [pltpu.SemaphoreType.DMA((tracer_count + 2,))],
         compiler_params=params(),
-        cost_estimate=cost(0, 3_000_000),
+        cost_estimate=cost(0, 0),
         name="base",
-    )(not_pole, *(pltpu.with_memory_space_constraint(array, pltpu.HBM) for array in (tracers, courant_lat, courant_lon)), sides)
+    )(not_pole, *fields, sides)
 
     surface = jnp.pad(surface_flux, ((0, 0), (0, 0), (0, width - sector)))
     decay = decay_rate[:, :, None]
@@ -411,13 +443,13 @@
         shapes = shapes + [jax.ShapeDtypeStruct((1, LANES) if last else energy.shape, f32)]
         *results, energy = pl.pallas_call(
             functools.partial(physics_kernel, levels, sector, lat_count if last else 0),
-            in_specs=[scalars] + [whole] * 10,
+            in_specs=[scalars] * 2 + [whole] * 11,
             out_specs=[whole] * len(shapes),
             out_shape=shapes,
             compiler_params=params(),
             cost_estimate=cost(50_000_000, 2_000_000),
             name="physics",
-        )(first, base, north, from_south, from_north, lat_courant, surface, mixing, decay, owner_of, energy)
+        )(first, even, base, north, from_inside, from_across, top, lat_courant, surface, mixing, decay, owner_of, energy)
         return results, energy
 
     (given,), energy = run_physics(give, jnp.zeros((rows, 8, width), f32), [circles], False)

time: 50.3 us -> 51.2 us (1.018)
  local copies, waits for them, and re-layouts: 5.45 us -> 2.09 us
  starting transfers between devices: 13.6 us -> 15.6 us
  Pallas kernels: 12 us -> 13.9 us
  waiting for transfers between devices: 16.9 us -> 17.6 us
    optimization_barrier x1 -> x0, local copies, waits for them, and re-layouts: 3.5 us -> none  [on_device(): lax.optimization_barrier((tracers, courant_lat, courant_lon, up, down))]
    pallas_call x1 -> x2, Pallas kernels: 2.63 us -> 4.61 us  [the longest x1 2.83 us: on_device(): pl.pallas_call(pack_kernel, in_specs=[scalars] + [in_hbm] * 2, out_specs=...]
    unnamed x34 -> x36, local copies, waits for them, and re-layouts: 0.1 us -> 1.81 us
    slice x5 -> x0, local copies, waits for them, and re-layouts: 1.21 us -> none  [the longest x1 0.94 us: on_device(): tracers[..., -2:]]
    ppermute x3 -> x4, starting transfers between devices: 6.98 us -> 7.94 us  [the longest x1 5.76 us: on_device(): from_inside = lax.ppermute(inner, 'lat', inside)]
    ppermute x3, starting transfers between devices: 6.56 us -> 7.48 us  [send_energy(): lax.ppermute(energy, 'lat', [(i, i ^ distance) for i in range(lat_count)])]
    ppermute x3 -> x4, waiting for transfers between devices: 15.8 us -> 16.7 us  [the longest x1 11.2 us: on_device(): from_inside = lax.ppermute(inner, 'lat', inside)]
  transfers between devices with their start and end apart: 8 -> 9, of which waited for: 5 -> 5; matrix products, arithmetic and copies ran while one was open for 12% -> 1% of each run, Pallas kernels for 18% -> 21%
where the time goes in v3:
time: 51.2 us; the launch traced here: 50.9 us
  waiting for transfers between devices  17.6 us (34%)
  starting transfers between devices  15.6 us (30%)
  Pallas kernels  13.9 us (27%)
  local copies, waits for them, and re-layouts  2.09 us (4%)
  between operations  0.98 us (2%)
  other arithmetic  0.73 us (1%)
    ppermute x1, waiting for transfers between devices, on_device(): from_inside = lax.ppermute(inner, 'lat', inside)  11.2 us
    ppermute x3, starting transfers between devices, send_energy(): lax.ppermute(energy, 'lat', [(i, i ^ distance) for i in range(lat_count)])  7.48 us
    ppermute x1, starting transfers between devices, on_device(): from_inside = lax.ppermute(inner, 'lat', inside)  5.76 us
    ppermute x1, waiting for transfers between devices, on_device(): top = lax.ppermute(courant_row, 'lat', downward)  4.24 us
    pallas_call x1, Pallas kernels, on_device(): pl.pallas_call(functools.partial(base_kernel, width), in_specs=[scalars,...  3.98 us
    pallas_call x1, Pallas kernels, on_device(): pl.pallas_call(pack_kernel, in_specs=[scalars] + [in_hbm] * 2, out_specs=...  2.83 us
    pallas_call x1, Pallas kernels, on_device(): pl.pallas_call(functools.partial(inverse_kernel, radix, half), in_specs=[...  1.82 us
    unnamed x36, local copies, waits for them, and re-layouts  1.81 us
  transfers between devices with their start and end apart: 9, of which 5 were waited for; matrix products, arithmetic and copies ran while one was open for 1% of the time, Pallas kernels for 21%

profile of v3, /device:TPU:0, one launch (start us, length us, event | category | flops | bytes accessed | tf_op | source)
XLA Modules:
  0.0 50.9 jit_solution(8780944085923452417)
XLA Ops:
  0.6 2.8 %pack.1 = (f32[128,1152]{1,0:T(8,128)}, f32[128,1152]{1,0:T(8,128)}, f32[16,1152]{1,0:T(8,128)S(1)}) custom-call(s32[1]{0:T(128)} %bitcast.1.even_ref, f32[4,32,4,576]{3,2,1,0:T(4,128)} %tracer_hbm.3, f32[32,4,576]{2,1,0:T(4,128)} %lat_hbm.2), custom_call_target="tpu_custom_call" | custom-call | bytes 600000 | tf_op jit(solution)/shard_map/pack/pallas_call | solution.py:375
  3.5 0.0 copy-start.13
  3.5 0.0 copy-start.14
  3.5 0.0 copy-start.16
  3.5 0.0 copy-start.17
  3.5 0.0 copy-start.12
  3.5 0.8 %collective-permute-start.2 = (f32[128,1152]{1,0:T(8,128)}, f32[128,1152]{1,0:T(8,128)S(1)}, u32[]{:S(2)}, u32[]{:S(2)}) collective-permute-start(f32[128,1152]{1,0:T(8,128)} %get-tuple-element.43), channel_id=1, source_target_pairs={{2,4},{4,2},{6,8},{8,6},{10,12},{12,10},{3,5},{5,3},{7,9},{9,7},{1... | collective-permute-start | bytes 1769480 | tf_op jit(solution)/shard_map/ppermute | solution.py:386
  4.4 5.8 %collective-permute-start.1 = (f32[128,1152]{1,0:T(8,128)}, f32[128,1152]{1,0:T(8,128)S(1)}, u32[]{:S(2)}, u32[]{:S(2)}) collective-permute-start(f32[128,1152]{1,0:T(8,128)} %get-tuple-element.36), channel_id=1, source_target_pairs={{0,2},{2,0},{4,6},{6,4},{8,10},{10,8},{12,14},{14,12},{1,3},{3,1},... | collective-permute-start | bytes 1769480 | tf_op jit(solution)/shard_map/ppermute | solution.py:385
  10.1 1.3 %collective-permute-start.3 = (f32[16,1152]{1,0:T(8,128)S(1)}, f32[16,1152]{1,0:T(8,128)S(1)}, u32[]{:S(2)}, u32[]{:S(2)}) collective-permute-start(f32[16,1152]{1,0:T(8,128)S(1)} %get-tuple-element.44), channel_id=1, source_target_pairs={{2,0},{4,2},{6,4},{8,6},{10,8},{12,10},{14,12},{3,1},{5,3},{7,5},{... | collective-permute-start | bytes 221192 | tf_op jit(solution)/shard_map/ppermute | solution.py:387
  11.4 1.8 %side.1 = f32[5,4,32,128]{3,2,1,0:T(8,128)S(1)} custom-call(f32[4,32,4,576]{3,2,1,0:T(4,128)} %tracer_hbm.3, f32[32,4,576]{2,1,0:T(4,128)} %lon_hbm.1), custom_call_target="tpu_custom_call" | custom-call | tf_op jit(solution)/shard_map/side/pallas_call | solution.py:391
  13.2 0.0 copy-start.15
  13.2 0.1 collective-permute-start
  13.4 0.0 copy-done.13
  13.4 0.0 copy-done.14
  13.4 0.0 copy-done.16
  13.4 0.1 select_multiply_fusion.refs_7_
  13.5 0.0 copy-done.17
  13.5 0.1 broadcast_in_dim.27
  13.6 0.1 reshape_reshape.3
  13.7 0.0 copy-done.12
  13.7 1.2 %collective-permute-done.side_ref = f32[5,4,32,128]{3,2,1,0:T(8,128)S(1)} collective-permute-done((f32[5,4,32,128]{3,2,1,0:T(8,128)S(1)}, f32[5,4,32,128]{3,2,1,0:T(8,128)S(1)}, u32[]{:S(2)}, u32[]{:S(2)}) %collective-permute-start) | collective-permute-done | bytes 327712 | tf_op jit(solution)/shard_map/ppermute | solution.py:401
  14.9 0.7 %copy-done = f32[5,4,32,128]{3,2,1,0:T(8,128)} copy-done((f32[5,4,32,128]{3,2,1,0:T(8,128)}, f32[5,4,32,128]{3,2,1,0:T(8,128)S(1)}, u32[]{:S(2)}) %copy-start) | copy-done | bytes 327704
  15.7 1.0 %copy-done.1 = f32[5,4,32,128]{3,2,1,0:T(8,128)S(1)} copy-done((f32[5,4,32,128]{3,2,1,0:T(8,128)S(1)}, f32[5,4,32,128]{3,2,1,0:T(8,128)}, u32[]{:S(2)}) %copy-start.1) | copy-done | bytes 327704
  16.6 4.0 %base.1 = (f32[4,4,32,640]{3,2,1,0:T(8,128)S(1)}, f32[4,32,640]{2,1,0:T(8,128)S(1)}, f32[4,32,640]{2,1,0:T(8,128)S(1)}) custom-call(f32[1]{0:T(128)} %bitcast.2.not_pole_ref, f32[4,32,4,576]{3,2,1,0:T(4,128)} %tracer_hbm.3, f32[32,4,576]{2,1,0:T(4,128)} %lat_hbm.2, f32[32,4,576]{2,1,0:T(4,128)} %lon_hbm.1, f32[5,4,32,128]{3,2,1,0:T(8,128)S(1)} %copy-done.1), custom_call_target="tpu_custom_call" | custom-call | tf_op jit(solution)/shard_map/base/pallas_call | solution.py:403
  20.6 0.0 copy-done.15
  20.6 0.1 copy.22.refs_8_
  20.7 4.2 %collective-permute-done.3.refs_4_ = f32[16,1152]{1,0:T(8,128)S(1)} collective-permute-done((f32[16,1152]{1,0:T(8,128)S(1)}, f32[16,1152]{1,0:T(8,128)S(1)}, u32[]{:S(2)}, u32[]{:S(2)}) %collective-permute-start.3) | collective-permute-done | bytes 73760 | tf_op jit(solution)/shard_map/ppermute | solution.py:387
  25.0 0.0 collective-permute-done.2.refs_3_
  25.0 11.2 %collective-permute-done.1.refs_2_ = f32[128,1152]{1,0:T(8,128)S(1)} collective-permute-done((f32[128,1152]{1,0:T(8,128)}, f32[128,1152]{1,0:T(8,128)S(1)}, u32[]{:S(2)}, u32[]{:S(2)}) %collective-permute-start.1) | collective-permute-done | bytes 589856 | tf_op jit(solution)/shard_map/ppermute | solution.py:385
  36.2 0.0 copy-done.2
  36.2 0.5 physics.2
  36.7 0.1 collective-permute-start.5
  36.8 0.0 copy-start.6
  36.8 0.0 copy-start.7
  36.8 0.0 copy-start.10
  36.9 0.0 copy-start.11
  36.9 0.7 %physics.3 = (f32[4,32,640]{2,1,0:T(8,128)S(1)}, f32[4,32,640]{2,1,0:T(8,128)S(1)}, f32[1,128]{1,0:T(1,128)S(1)}) custom-call(s32[1]{0:T(128)} %bitcast.first_ref.keep_ref, s32[1]{0:T(128)} %bitcast.1.even_ref, f32[4,4,32,640]{3,2,1,0:T(8,128)S(1)} %get-tuple-element.41.refs_0_, f32[4,32,640]{2,1,0:T(8,128)S(1)} %get-tuple-element.42.refs_1_, ...), custom_call_target="tpu_custom_call" | custom-call | flops 50000000 | bytes 2000000 | tf_op jit(solution)/shard_map/physics/pallas_call | solution.py:444
  37.5 2.4 %collective-permute-start.4 = (f32[1,128]{1,0:T(1,128)S(1)}, f32[1,128]{1,0:T(1,128)S(1)}, u32[]{:S(2)}, u32[]{:S(2)}) collective-permute-start(f32[1,128]{1,0:T(1,128)S(1)} %get-tuple-element.50), channel_id=1, source_target_pairs={{0,2},{2,0},{4,6},{6,4},{8,10},{10,8},{12,14},{14,12},{1,3},{3,1},... | collective-permute-start | bytes 1544 | tf_op jit(solution)/shard_map/ppermute | solution.py:464
  39.9 0.0 collective-permute-done.5.refs_2_
  39.9 0.0 copy-done.6
  39.9 0.0 copy-done.7
  39.9 0.0 copy-done.10
  39.9 0.0 copy-done.11
  39.9 0.0 copy-start.3
  40.0 0.0 copy-start.4
  40.0 0.0 copy-start.5
  40.0 0.0 copy-start.8
  40.0 0.0 copy-start.9
  40.0 1.2 %forward.1 = (bf16[256,1152]{1,0:T(8,128)(2,1)S(1)}, bf16[256,1152]{1,0:T(8,128)(2,1)S(1)}) custom-call(f32[4,32,640]{2,1,0:T(8,128)S(1)} %get-tuple-element.51.refs_0_, f32[4,32,640]{2,1,0:T(8,128)S(1)} %get-tuple-element.52.refs_1_, f32[2,4,32,640]{3,2,1,0:T(8,128)S(1)} %collective-permute-done.5.refs_2_, bf16[1024,256]{1,0:T(8,128)(2,1)S(1)} %copy-done.7, ...), custom_call_target="tpu_custom_call" | custom-call | flops 2000000000 | bytes 6000000 | tf_op jit(solution)/shard_map/forward/pallas_call | solution.py:467
  41.2 0.2 collective-permute-done.4
  41.4 2.4 %collective-permute-start.6 = (f32[1,128]{1,0:T(1,128)S(1)}, f32[1,128]{1,0:T(1,128)S(1)}, u32[]{:S(2)}, u32[]{:S(2)}) collective-permute-start(f32[1,128]{1,0:T(1,128)S(1)} %add.49), channel_id=1, source_target_pairs={{0,4},{2,6},{4,0},{6,2},{8,12},{10,14},{12,8},{14,10},{1,5},{3,7},... | collective-permute-start | bytes 1544 | tf_op jit(solution)/shard_map/ppermute | solution.py:464
  43.9 0.0 copy-done.3
  43.9 0.0 copy-done.4
  43.9 0.0 copy-done.5
  43.9 0.0 copy-done.8
  43.9 0.0 copy-done.9
  43.9 1.8 %inverse.1 = (f32[32,4,576]{2,1,0:T(4,128)S(1)}, f32[32,4,576]{2,1,0:T(4,128)S(1)}, f32[2,4,32,640]{3,2,1,0:T(8,128)S(1)}) custom-call(s32[4]{0:T(128)S(1)} %copy-done.3, f32[4,32,640]{2,1,0:T(8,128)S(1)} %get-tuple-element.51.refs_0_, f32[4,32,640]{2,1,0:T(8,128)S(1)} %get-tuple-element.52.refs_1_, f32[2,4,32,640]{3,2,1,0:T(8,128)S(1)} %collective-permute-done.5.refs_2_, ...), custom_call_target="tpu_custom_call" | custom-call | flops 2000000000 | bytes 6000000 | tf_op jit(solution)/shard_map/inverse/pallas_call | solution.py:482
  45.7 0.0 collective-permute-done.6
  45.7 0.1 collective-permute-start.8
  45.8 2.7 %collective-permute-start.7 = (f32[1,128]{1,0:T(1,128)S(1)}, f32[1,128]{1,0:T(1,128)S(1)}, u32[]{:S(2)}, u32[]{:S(2)}) collective-permute-start(f32[1,128]{1,0:T(1,128)S(1)} %add.50), channel_id=1, source_target_pairs={{0,8},{2,10},{4,12},{6,14},{8,0},{10,2},{12,4},{14,6},{1,9},{3,11}... | collective-permute-start | bytes 1544 | tf_op jit(solution)/shard_map/ppermute | solution.py:464
  48.5 0.0 collective-permute-done.8.refs_2_
  48.5 1.2 %finish.1 = f32[4,32,4,576]{3,2,1,0:T(4,128)} custom-call(s32[1]{0:T(128)} %bitcast.first_ref.keep_ref, s32[1]{0:T(128)S(6)} %sub.7.first_ref.give_ref, f32[32,4,576]{2,1,0:T(4,128)S(1)} %get-tuple-element.65.refs_0_, f32[32,4,576]{2,1,0:T(4,128)S(1)} %get-tuple-element.66.refs_1_, f32[2,4,32,640]{3,2,1,0:T(8,128)S(1)} %collective-permute-done.8.refs_2_), custom_call_target="tpu_custom_call" | custom-call | bytes 3000000 | tf_op jit(solution)/shard_map/finish/pallas_call | solution.py:498
  49.7 0.7 %collective-permute-done.7 = f32[1,128]{1,0:T(1,128)S(1)} collective-permute-done((f32[1,128]{1,0:T(1,128)S(1)}, f32[1,128]{1,0:T(1,128)S(1)}, u32[]{:S(2)}, u32[]{:S(2)}) %collective-permute-start.7) | collective-permute-done | bytes 544 | tf_op jit(solution)/shard_map/ppermute | solution.py:464
  50.3 0.6 %fusion = f32[1,1]{1,0:T(1,128)} fusion(f32[1,128]{1,0:T(1,128)S(1)} %add.51, s32[]{:T(128)S(6)} %select_n.16), kind=kLoop, calls=%fused_computation.3 | loop fusion | flops 1 | bytes 12 | tf_op jit(solution)/shard_map/div | solution.py:516
  (10 shorter events, 0.1 us)
Async XLA Ops:
  3.5 9.9 %copy-start.13 = (f32[1152]{0:T(1024)S(1)}, f32[1152]{0:T(1024)}, u32[]{:S(2)}) copy-start(f32[1152]{0:T(1024)} %constant.73.clone) | copy-start | bytes 13828
  3.5 9.9 %copy-start.14 = (f32[1152]{0:T(1024)S(1)}, f32[1152]{0:T(1024)}, u32[]{:S(2)}) copy-start(f32[1152]{0:T(1024)} %constant.71.clone) | copy-start | bytes 13828
  3.5 9.9 %copy-start.16 = (pred[1152]{0:T(1024)(128)(4,1)S(1)}, pred[1152]{0:T(1024)(128)(4,1)}, u32[]{:S(2)}) copy-start(pred[1152]{0:T(1024)(128)(4,1)} %constant.72.clone) | copy-start | bytes 3460
  3.5 10.0 %copy-start.17 = (s32[1,1,18,1]{2,3,1,0:T(1,128)S(1)}, s32[1,1,18,1]{2,3,1,0:T(1,128)}, u32[]{:S(2)}) copy-start(s32[1,1,18,1]{2,3,1,0:T(1,128)} %param.25) | copy-start | bytes 220
  3.5 10.1 %copy-start.12 = (f32[4,4,576]{2,1,0:T(4,128)S(1)}, f32[4,4,576]{2,1,0:T(4,128)}, u32[]{:S(2)}) copy-start(f32[4,4,576]{2,1,0:T(4,128)} %param.22) | copy-start | bytes 110596
  3.5 21.4 %collective-permute-start.2 = (f32[128,1152]{1,0:T(8,128)}, f32[128,1152]{1,0:T(8,128)S(1)}, u32[]{:S(2)}, u32[]{:S(2)}) collective-permute-start(f32[128,1152]{1,0:T(8,128)} %get-tuple-element.43), channel_id=1, source_target_pairs={{2,4},{4,2},{6,8},{8,6},{10,12},{12,10},{3,5},{5,3},{7,9},{9,7},{1... | collective-permute-start | bytes 1769480 | tf_op jit(solution)/shard_map/ppermute | solution.py:386
  4.4 31.8 %collective-permute-start.1 = (f32[128,1152]{1,0:T(8,128)}, f32[128,1152]{1,0:T(8,128)S(1)}, u32[]{:S(2)}, u32[]{:S(2)}) collective-permute-start(f32[128,1152]{1,0:T(8,128)} %get-tuple-element.36), channel_id=1, source_target_pairs={{0,2},{2,0},{4,6},{6,4},{8,10},{10,8},{12,14},{14,12},{1,3},{3,1},... | collective-permute-start | bytes 1769480 | tf_op jit(solution)/shard_map/ppermute | solution.py:385
  10.1 14.8 %collective-permute-start.3 = (f32[16,1152]{1,0:T(8,128)S(1)}, f32[16,1152]{1,0:T(8,128)S(1)}, u32[]{:S(2)}, u32[]{:S(2)}) collective-permute-start(f32[16,1152]{1,0:T(8,128)S(1)} %get-tuple-element.44), channel_id=1, source_target_pairs={{2,0},{4,2},{6,4},{8,6},{10,8},{12,10},{14,12},{3,1},{5,3},{7,5},{... | collective-permute-start | bytes 221192 | tf_op jit(solution)/shard_map/ppermute | solution.py:387
  13.2 7.4 %copy-start.15 = (f32[4,32]{1,0:T(4,128)S(1)}, f32[4,32]{1,0:T(4,128)}, u32[]{:S(2)}) copy-start(f32[4,32]{1,0:T(4,128)} %param.24) | copy-start | bytes 1540
  13.2 1.7 %collective-permute-start = (f32[5,4,32,128]{3,2,1,0:T(8,128)S(1)}, f32[5,4,32,128]{3,2,1,0:T(8,128)S(1)}, u32[]{:S(2)}, u32[]{:S(2)}) collective-permute-start(f32[5,4,32,128]{3,2,1,0:T(8,128)S(1)} %side.1), channel_id=1, source_target_pairs={{0,1},{1,0},{2,3},{3,2},{4,5},{5,4},{6,7},{7,6},{8,9},{9,8},{10,11... | collective-permute-start | bytes 983048 | tf_op jit(solution)/shard_map/ppermute | solution.py:401
  13.5 22.8 %copy-start.2 = (f32[32,32]{1,0:T(8,128)S(1)}, f32[32,32]{1,0:T(8,128)}, u32[]{:S(2)}) copy-start(f32[32,32]{1,0:T(8,128)} %refs_7_.4) | copy-start | bytes 12292
  14.9 0.7 %copy-start = (f32[5,4,32,128]{3,2,1,0:T(8,128)}, f32[5,4,32,128]{3,2,1,0:T(8,128)S(1)}, u32[]{:S(2)}) copy-start(f32[5,4,32,128]{3,2,1,0:T(8,128)S(1)} %collective-permute-done.side_ref) | copy-start | bytes 983044
  15.7 1.0 %copy-start.1 = (f32[5,4,32,128]{3,2,1,0:T(8,128)S(1)}, f32[5,4,32,128]{3,2,1,0:T(8,128)}, u32[]{:S(2)}) copy-start(f32[5,4,32,128]{3,2,1,0:T(8,128)} %copy-done) | copy-start | bytes 983044
  36.7 3.2 %collective-permute-start.5 = (f32[2,4,32,640]{3,2,1,0:T(8,128)S(1)}, f32[2,4,32,640]{3,2,1,0:T(8,128)S(1)}, u32[]{:S(2)}, u32[]{:S(2)}) collective-permute-start(f32[2,4,32,640]{3,2,1,0:T(8,128)S(1)} %get-tuple-element.53), channel_id=1, source_target_pairs={{0,1},{1,0},{2,3},{3,2},{4,5},{5,4},{6,7},{7,6},{8,9},{9,8},{10,11... | collective-permute-start | bytes 1966088 | tf_op jit(solution)/shard_map/ppermute | solution.py:456
  36.8 3.1 %copy-start.6 = (bf16[1024,256]{1,0:T(8,128)(2,1)S(1)}, bf16[1024,256]{1,0:T(8,128)(2,1)}, u32[]{:S(2)}) copy-start(bf16[1024,256]{1,0:T(8,128)(2,1)} %constant.75.clone.refs_4_) | copy-start | bytes 1572868
  36.8 3.1 %copy-start.7 = (bf16[1024,256]{1,0:T(8,128)(2,1)S(1)}, bf16[1024,256]{1,0:T(8,128)(2,1)}, u32[]{:S(2)}) copy-start(bf16[1024,256]{1,0:T(8,128)(2,1)} %constant.74.clone.refs_3_) | copy-start | bytes 1572868
  36.8 3.1 %copy-start.10 = (bf16[128,128]{1,0:T(8,128)(2,1)S(1)}, bf16[128,128]{1,0:T(8,128)(2,1)}, u32[]{:S(2)}) copy-start(bf16[128,128]{1,0:T(8,128)(2,1)} %constant.77.clone.refs_6_) | copy-start | bytes 98308
  36.9 3.1 %copy-start.11 = (bf16[128,128]{1,0:T(8,128)(2,1)S(1)}, bf16[128,128]{1,0:T(8,128)(2,1)}, u32[]{:S(2)}) copy-start(bf16[128,128]{1,0:T(8,128)(2,1)} %constant.76.clone.refs_5_) | copy-start | bytes 98308
  37.5 3.9 %collective-permute-start.4 = (f32[1,128]{1,0:T(1,128)S(1)}, f32[1,128]{1,0:T(1,128)S(1)}, u32[]{:S(2)}, u32[]{:S(2)}) collective-permute-start(f32[1,128]{1,0:T(1,128)S(1)} %get-tuple-element.50), channel_id=1, source_target_pairs={{0,2},{2,0},{4,6},{6,4},{8,10},{10,8},{12,14},{14,12},{1,3},{3,1},... | collective-permute-start | bytes 1544 | tf_op jit(solution)/shard_map/ppermute | solution.py:464
  39.9 3.9 %copy-start.3 = (s32[4]{0:T(128)S(1)}, s32[4]{0:T(128)}, u32[]{:S(2)}) copy-start(s32[4]{0:T(128)} %mask_ref.1) | copy-start | bytes 52
  40.0 3.9 %copy-start.4 = (bf16[1024,256]{1,0:T(8,128)(2,1)S(1)}, bf16[1024,256]{1,0:T(8,128)(2,1)}, u32[]{:S(2)}) copy-start(bf16[1024,256]{1,0:T(8,128)(2,1)} %constant.79.clone.refs_6_) | copy-start | bytes 1572868
  40.0 3.9 %copy-start.5 = (bf16[1024,256]{1,0:T(8,128)(2,1)S(1)}, bf16[1024,256]{1,0:T(8,128)(2,1)}, u32[]{:S(2)}) copy-start(bf16[1024,256]{1,0:T(8,128)(2,1)} %constant.78.clone.refs_5_) | copy-start | bytes 1572868
  40.0 3.9 %copy-start.8 = (bf16[128,128]{1,0:T(8,128)(2,1)S(1)}, bf16[128,128]{1,0:T(8,128)(2,1)}, u32[]{:S(2)}) copy-start(bf16[128,128]{1,0:T(8,128)(2,1)} %constant.81.clone.refs_8_) | copy-start | bytes 98308
  40.0 3.9 %copy-start.9 = (bf16[128,128]{1,0:T(8,128)(2,1)S(1)}, bf16[128,128]{1,0:T(8,128)(2,1)}, u32[]{:S(2)}) copy-start(bf16[128,128]{1,0:T(8,128)(2,1)} %constant.80.clone.refs_7_) | copy-start | bytes 98308
  41.4 4.3 %collective-permute-start.6 = (f32[1,128]{1,0:T(1,128)S(1)}, f32[1,128]{1,0:T(1,128)S(1)}, u32[]{:S(2)}, u32[]{:S(2)}) collective-permute-start(f32[1,128]{1,0:T(1,128)S(1)} %add.49), channel_id=1, source_target_pairs={{0,4},{2,6},{4,0},{6,2},{8,12},{10,14},{12,8},{14,10},{1,5},{3,7},... | collective-permute-start | bytes 1544 | tf_op jit(solution)/shard_map/ppermute | solution.py:464
  45.7 2.7 %collective-permute-start.8 = (f32[2,4,32,640]{3,2,1,0:T(8,128)S(1)}, f32[2,4,32,640]{3,2,1,0:T(8,128)S(1)}, u32[]{:S(2)}, u32[]{:S(2)}) collective-permute-start(f32[2,4,32,640]{3,2,1,0:T(8,128)S(1)} %get-tuple-element.67), channel_id=1, source_target_pairs={{0,1},{1,0},{2,3},{3,2},{4,5},{5,4},{6,7},{7,6},{8,9},{9,8},{10,11... | collective-permute-start | bytes 1966088 | tf_op jit(solution)/shard_map/ppermute | solution.py:495
  45.8 4.5 %collective-permute-start.7 = (f32[1,128]{1,0:T(1,128)S(1)}, f32[1,128]{1,0:T(1,128)S(1)}, u32[]{:S(2)}, u32[]{:S(2)}) collective-permute-start(f32[1,128]{1,0:T(1,128)S(1)} %add.50), channel_id=1, source_target_pairs={{0,8},{2,10},{4,12},{6,14},{8,0},{10,2},{12,4},{14,6},{1,9},{3,11}... | collective-permute-start | bytes 1544 | tf_op jit(solution)/shard_map/ppermute | solution.py:464

commit v4 on v3

--- a/solution.py
+++ b/solution.py
@@ -12,7 +12,7 @@
 LANES = 128
 BLOCK = 128
 VMEM_BYTES = 6 * 1024 * 1024
-RESULT_PIECES = 4
+PIECES = 4
 NEAR = 7.0 / 12.0
 FAR = 1.0 / 12.0
 
@@ -82,9 +82,9 @@
     return copies
 
 
-def pack_halo(tracer_ref, t, out_ref, upward):
+def pack_halo(tracer_ref, t, out_ref, slot, upward):
     levels, rows = tracer_ref.shape[1:3]
-    place = slice(levels * t, levels * (t + 1))
+    place = slice(levels * slot, levels * (slot + 1))
 
     @pl.when(upward)
     def _():
@@ -95,27 +95,39 @@
         out_ref[place, :] = pack_rows(tracer_ref[t, :, 0, :], tracer_ref[t, :, 1, :])
 
 
-def pack_kernel(even_ref, tracer_hbm, lat_hbm, inner_ref, outer_ref, courant_ref, tracer_ref, lat_ref, sems):
+def copies_in_pieces(source, target, sems, pieces):
+    size = target.shape[0] // pieces
+    spans = [pl.ds(size * i, size) for i in range(pieces)]
+    copies = [pltpu.make_async_copy(source.at[span], target.at[span], sems.at[i]) for i, span in enumerate(spans)]
+    for copy in copies:
+        copy.start()
+    return copies
+
+
+def pack_kernel(even_ref, tracer_hbm, *refs):
+    inner_ref, outer_refs, (tracer_ref, sems) = refs[0], refs[1:-2], refs[-2:]
     count = tracer_ref.shape[0]
-    levels = tracer_ref.shape[1]
-    copies = start_copies([(tracer_hbm.at[t], tracer_ref.at[t]) for t in range(count)] + [(lat_hbm, lat_ref)], sems)
+    copies = [copies_in_pieces(tracer_hbm.at[t], tracer_ref.at[t], sems.at[t], PIECES) for t in range(count)]
     even = even_ref[0] == 1
+    share = count // len(outer_refs)
     for t in range(count):
-        copies[t].wait()
-        pack_halo(tracer_ref, t, inner_ref, even)
-        pack_halo(tracer_ref, t, outer_ref, jnp.logical_not(even))
-    copies[count].wait()
+        for copy in copies[t]:
+            copy.wait()
+        pack_halo(tracer_ref, t, inner_ref, t, even)
+        pack_halo(tracer_ref, t, outer_refs[t // share], t % share, jnp.logical_not(even))
+
+
+def side_kernel(tracer_hbm, lat_hbm, lon_hbm, side_ref, courant_ref, tracer_ref, lat_ref, lon_ref, sems):
+    count, levels, rows, sector = tracer_ref.shape
+    pairs = [(lat_hbm, lat_ref)] + [(tracer_hbm.at[t], tracer_ref.at[t]) for t in range(count)] + [(lon_hbm, lon_ref)]
+    copies = start_copies(pairs, sems)
+    shift, whole = sector % LANES, sector // LANES * LANES
+    lane = lax.broadcasted_iota(jnp.int32, (levels, LANES), 1)
+    copies[0].wait()
     courant = lat_ref[:, 0, :]
     courant_ref[...] = pack_rows(courant[: levels // 2], courant[levels // 2 :])
-
-
-def side_kernel(tracer_hbm, lon_hbm, side_ref, tracer_ref, lon_ref, sems):
-    count, levels, rows, sector = tracer_ref.shape
-    copies = start_copies([(tracer_hbm.at[t], tracer_ref.at[t]) for t in range(count)] + [(lon_hbm, lon_ref)], sems)
-    shift, whole = sector % LANES, sector // LANES * LANES
-    lane = lax.broadcasted_iota(jnp.int32, (levels, LANES), 1)
     for i in range(count + 1):
-        copies[i].wait()
+        copies[i + 1].wait()
         for r in range(rows):
             values = tracer_ref[i, :, r, :] if i < count else lon_ref[:, r, :]
             first = pltpu.roll(values[:, :LANES], shift, 1)
@@ -159,8 +171,9 @@
 
 
 def physics_kernel(levels, sector, owner_count, first_ref, even_ref, *refs):
-    base_ref, north_ref, inner_ref, outer_ref, top_ref, courant_ref, surface_ref, mixing_ref, decay_ref, owner_ref = refs[:10]
-    energy_in_ref, physics_refs, energy_ref = refs[10], refs[11:-1], refs[-1]
+    base_ref, north_ref, inner_ref, *outer_refs = refs[:5]
+    top_ref, courant_ref, surface_ref, mixing_ref, decay_ref, owner_ref, energy_in_ref = refs[5:12]
+    physics_refs, energy_ref = refs[12:-1], refs[-1]
     if len(physics_refs) == 1:
         physics_refs = [physics_refs[0].at[i] for i in range(physics_refs[0].shape[0])]
     rows, width = base_ref.shape[1], base_ref.shape[-1]
@@ -175,8 +188,9 @@
     energies = [energy_in_ref[r] for r in range(rows)]
     for i, physics_ref in enumerate(physics_refs):
         t = first_ref[0] + i
-        place = pl.ds(pl.multiple_of(levels * t, levels), levels)
-        inner, outer = inner_ref[place, :], outer_ref[place, :]
+        inner = inner_ref[pl.ds(pl.multiple_of(levels * t, levels), levels), :]
+        outer = [outer_ref[levels * i : levels * (i + 1), :] for outer_ref in outer_refs]
+        outer = jnp.where(first_ref[0] == 0, *outer)
         low, high = jnp.where(even, outer, inner), jnp.where(even, inner, outer)
         low_a, low_b = low[:, :width], second_half(low, sector)
         high_a, high_b = high[:, :width], second_half(high, sector)
@@ -217,9 +231,9 @@
 
 
 def send_result(result_ref, out_hbm, tracer, sems):
-    piece = result_ref.shape[0] // RESULT_PIECES
+    piece = result_ref.shape[0] // PIECES
     copies = []
-    for part in range(RESULT_PIECES):
+    for part in range(PIECES):
         span = pl.ds(piece * part, piece)
         copies.append(pltpu.make_async_copy(result_ref.at[span], out_hbm.at[tracer, span], sems.at[part]))
         copies[-1].start()
@@ -334,11 +348,11 @@
     result_refs, (received_ref, out_hbm, turned_ref, sems) = refs[:-4], refs[-4:]
     count, rows, levels, width = received_ref.shape
     sector = out_hbm.shape[-1]
-    piece = levels // RESULT_PIECES
+    piece = levels // PIECES
     copies = []
 
     def send(source_ref, tracer, slot):
-        for part in range(RESULT_PIECES):
+        for part in range(PIECES):
             span = pl.ds(piece * part, piece)
             copies.append(pltpu.make_async_copy(source_ref.at[span], out_hbm.at[tracer, span], sems.at[slot, part]))
             copies[-1].start()
@@ -372,32 +386,36 @@
     across = [pair for i in range(1, lat_count - 1, 2) for pair in ((i, i + 1), (i + 1, i))]
     fields = [pltpu.with_memory_space_constraint(array, pltpu.HBM) for array in (tracers, courant_lat, courant_lon)]
     field_buffers = [pltpu.VMEM(array.shape, f32) for array in (tracers, courant_lat, courant_lon)]
-    inner, outer, courant_row = pl.pallas_call(
+    half = tracer_count // 2
+    inner, *outer = pl.pallas_call(
         pack_kernel,
-        in_specs=[scalars] + [in_hbm] * 2,
+        in_specs=[scalars, in_hbm],
         out_specs=[whole] * 3,
-        out_shape=[pltpu.VMEM((levels * tracer_count, length), f32)] * 2 + [pltpu.VMEM((levels // 2, length), f32)],
-        scratch_shapes=field_buffers[:2] + [pltpu.SemaphoreType.DMA((tracer_count + 1,))],
+        out_shape=[pltpu.VMEM((levels * count, length), f32) for count in (tracer_count, half, half)],
+        scratch_shapes=[field_buffers[0], pltpu.SemaphoreType.DMA((tracer_count, PIECES))],
         compiler_params=params(),
         cost_estimate=cost(0, 600_000),
         name="pack",
-    )(even, *fields[:2])
+    )(even, fields[0])
     from_inside = lax.ppermute(inner, "lat", inside)
-    from_across = lax.ppermute(outer, "lat", across)
-    top = lax.ppermute(courant_row, "lat", downward)
+    from_across = [lax.ppermute(part, "lat", across) for part in outer]
 
     fields, inner = lax.optimization_barrier((fields, inner))
     fields = [pltpu.with_memory_space_constraint(array, pltpu.HBM) for array in fields]
-    sides = pl.pallas_call(
+    sides, courant_row = pl.pallas_call(
         side_kernel,
-        in_specs=[in_hbm] * 2,
-        out_specs=whole,
-        out_shape=jax.ShapeDtypeStruct((tracer_count + 1, rows, levels, LANES), f32),
-        scratch_shapes=[field_buffers[0], field_buffers[2], pltpu.SemaphoreType.DMA((tracer_count + 1,))],
+        in_specs=[in_hbm] * 3,
+        out_specs=[whole] * 2,
+        out_shape=[
+            jax.ShapeDtypeStruct((tracer_count + 1, rows, levels, LANES), f32),
+            jax.ShapeDtypeStruct((levels // 2, length), f32),
+        ],
+        scratch_shapes=field_buffers + [pltpu.SemaphoreType.DMA((tracer_count + 2,))],
         compiler_params=params(),
         cost_estimate=cost(0, 0),
         name="side",
-    )(fields[0], fields[2])
+    )(*fields)
+    top = lax.ppermute(courant_row, "lat", downward)
     sides = lax.ppermute(sides, "lon", swap)
     not_pole = (lat > 0).astype(f32).reshape(1)
     base, north, lat_courant = pl.pallas_call(
@@ -431,7 +449,6 @@
 
     base, scale, owner_of, surface, decay = lax.optimization_barrier((base, scale, owner_of, surface, decay))
 
-    half = tracer_count // 2
     keep = (half * lax.axis_index("lon")).reshape(1)
     give = half - keep
     circles = jax.ShapeDtypeStruct((half, rows, levels, width), f32)
@@ -443,13 +460,13 @@
         shapes = shapes + [jax.ShapeDtypeStruct((1, LANES) if last else energy.shape, f32)]
         *results, energy = pl.pallas_call(
             functools.partial(physics_kernel, levels, sector, lat_count if last else 0),
-            in_specs=[scalars] * 2 + [whole] * 11,
+            in_specs=[scalars] * 2 + [whole] * 12,
             out_specs=[whole] * len(shapes),
             out_shape=shapes,
             compiler_params=params(),
             cost_estimate=cost(50_000_000, 2_000_000),
             name="physics",
-        )(first, even, base, north, from_inside, from_across, top, lat_courant, surface, mixing, decay, owner_of, energy)
+        )(first, even, base, north, from_inside, *from_across, top, lat_courant, surface, mixing, decay, owner_of, energy)
         return results, energy
 
     (given,), energy = run_physics(give, jnp.zeros((rows, 8, width), f32), [circles], False)
@@ -502,7 +519,7 @@
         out_shape=out_shape,
         scratch_shapes=[
             pltpu.VMEM((half,) + result_shape.shape, f32),
-            pltpu.SemaphoreType.DMA((2 * half, RESULT_PIECES)),
+            pltpu.SemaphoreType.DMA((2 * half, PIECES)),
         ],
         compiler_params=params(),
         cost_estimate=cost(0, 3_000_000),

time: 51.2 us -> 48.5 us (0.947)
  starting transfers between devices: 15.6 us -> 13 us
    ppermute x1, starting transfers between devices: 5.76 us -> 2.74 us  [on_device(): from_inside = lax.ppermute(inner, 'lat', inside)]
    ppermute x1, waiting for transfers between devices: 4.24 us -> 3.04 us  [on_device(): top = lax.ppermute(courant_row, 'lat', downward)]
    ppermute x1, waiting for transfers between devices: 11.2 us -> 12 us  [on_device(): from_inside = lax.ppermute(inner, 'lat', inside)]
    ppermute x1 -> x2, starting transfers between devices: 0.83 us -> 1.35 us  [on_device(): from_across = [lax.ppermute(part, 'lat', across) for part in outer]]
  transfers between devices with their start and end apart: 9 -> 10, of which waited for: 5 -> 5; matrix products, arithmetic and copies ran while one was open for 1% -> 1% of each run, Pallas kernels for 21% -> 22%
where the time goes in v4:
time: 48.5 us; the launch traced here: 48.2 us
  waiting for transfers between devices  17.2 us (35%)
  Pallas kernels  14.2 us (29%)
  starting transfers between devices  13 us (27%)
  local copies, waits for them, and re-layouts  2.09 us (4%)
  between operations  1 us (2%)
  other arithmetic  0.73 us (2%)
    ppermute x1, waiting for transfers between devices, on_device(): from_inside = lax.ppermute(inner, 'lat', inside)  12 us
    ppermute x3, starting transfers between devices, send_energy(): lax.ppermute(energy, 'lat', [(i, i ^ distance) for i in range(lat_count)])  7.46 us
    pallas_call x1, Pallas kernels, on_device(): pl.pallas_call(functools.partial(base_kernel, width), in_specs=[scalars,...  3.98 us
    ppermute x1, waiting for transfers between devices, on_device(): top = lax.ppermute(courant_row, 'lat', downward)  3.04 us
    pallas_call x1, Pallas kernels, on_device(): pl.pallas_call(pack_kernel, in_specs=[scalars, in_hbm], out_specs=[whole]...  2.96 us
    ppermute x1, starting transfers between devices, on_device(): from_inside = lax.ppermute(inner, 'lat', inside)  2.74 us
    pallas_call x1, Pallas kernels, on_device(): pl.pallas_call(side_kernel, in_specs=[in_hbm] * 3, out_specs=[whole] * 2,...  1.89 us
    pallas_call x1, Pallas kernels, on_device(): pl.pallas_call(functools.partial(inverse_kernel, radix, half), in_specs=[...  1.82 us
  transfers between devices with their start and end apart: 10, of which 5 were waited for; matrix products, arithmetic and copies ran while one was open for 1% of the time, Pallas kernels for 22%

profile of v4, /device:TPU:0, one launch (start us, length us, event | category | flops | bytes accessed | tf_op | source)
XLA Modules:
  0.0 48.2 jit_solution(15138073891307468978)
XLA Ops:
  0.6 3.0 %pack.1 = (f32[128,1152]{1,0:T(8,128)}, f32[64,1152]{1,0:T(8,128)}, f32[64,1152]{1,0:T(8,128)}) custom-call(s32[1]{0:T(128)} %bitcast.1.even_ref, f32[4,32,4,576]{3,2,1,0:T(4,128)} %tracer_hbm.3), custom_call_target="tpu_custom_call" | custom-call | bytes 600000 | tf_op jit(solution)/shard_map/pack/pallas_call | solution.py:390
  3.6 0.0 copy-start.13
  3.6 0.0 copy-start.14
  3.6 0.0 copy-start.16
  3.6 0.0 copy-start.17
  3.7 0.0 copy-start.12
  3.7 2.7 %collective-permute-start.1 = (f32[128,1152]{1,0:T(8,128)}, f32[128,1152]{1,0:T(8,128)S(1)}, u32[]{:S(2)}, u32[]{:S(2)}) collective-permute-start(f32[128,1152]{1,0:T(8,128)} %get-tuple-element.38), channel_id=1, source_target_pairs={{0,2},{2,0},{4,6},{6,4},{8,10},{10,8},{12,14},{14,12},{1,3},{3,1},... | collective-permute-start | bytes 1769480 | tf_op jit(solution)/shard_map/ppermute | solution.py:400
  6.4 0.7 %collective-permute-start.2 = (f32[64,1152]{1,0:T(8,128)}, f32[64,1152]{1,0:T(8,128)S(1)}, u32[]{:S(2)}, u32[]{:S(2)}) collective-permute-start(f32[64,1152]{1,0:T(8,128)} %get-tuple-element.46), channel_id=1, source_target_pairs={{2,4},{4,2},{6,8},{8,6},{10,12},{12,10},{3,5},{5,3},{7,9},{9,7},{1... | collective-permute-start | bytes 884744 | tf_op jit(solution)/shard_map/ppermute | solution.py:401
  7.1 0.7 %collective-permute-start.3 = (f32[64,1152]{1,0:T(8,128)}, f32[64,1152]{1,0:T(8,128)S(1)}, u32[]{:S(2)}, u32[]{:S(2)}) collective-permute-start(f32[64,1152]{1,0:T(8,128)} %get-tuple-element.47), channel_id=1, source_target_pairs={{2,4},{4,2},{6,8},{8,6},{10,12},{12,10},{3,5},{5,3},{7,9},{9,7},{1... | collective-permute-start | bytes 884744 | tf_op jit(solution)/shard_map/ppermute | solution.py:401
  7.8 1.9 %side.1 = (f32[5,4,32,128]{3,2,1,0:T(8,128)S(1)}, f32[16,1152]{1,0:T(8,128)S(1)}) custom-call(f32[4,32,4,576]{3,2,1,0:T(4,128)} %tracer_hbm.3, f32[32,4,576]{2,1,0:T(4,128)} %lat_hbm.1, f32[32,4,576]{2,1,0:T(4,128)} %lon_hbm.1), custom_call_target="tpu_custom_call" | custom-call | tf_op jit(solution)/shard_map/side/pallas_call | solution.py:405
  9.7 0.0 copy-start.15
  9.7 1.3 %collective-permute-start.4 = (f32[16,1152]{1,0:T(8,128)S(1)}, f32[16,1152]{1,0:T(8,128)S(1)}, u32[]{:S(2)}, u32[]{:S(2)}) collective-permute-start(f32[16,1152]{1,0:T(8,128)S(1)} %get-tuple-element.48), channel_id=1, source_target_pairs={{2,0},{4,2},{6,4},{8,6},{10,8},{12,10},{14,12},{3,1},{5,3},{7,5},{... | collective-permute-start | bytes 221192 | tf_op jit(solution)/shard_map/ppermute | solution.py:418
  11.0 0.1 collective-permute-start
  11.1 0.0 copy-done.13
  11.1 0.0 copy-done.14
  11.1 0.0 copy-done.16
  11.1 0.1 select_multiply_fusion.refs_7_
  11.2 0.0 copy-done.17
  11.2 0.1 broadcast_in_dim.27
  11.3 0.1 reshape_reshape.3
  11.4 0.0 copy-done.12
  11.4 1.2 %collective-permute-done.side_ref = f32[5,4,32,128]{3,2,1,0:T(8,128)S(1)} collective-permute-done((f32[5,4,32,128]{3,2,1,0:T(8,128)S(1)}, f32[5,4,32,128]{3,2,1,0:T(8,128)S(1)}, u32[]{:S(2)}, u32[]{:S(2)}) %collective-permute-start) | collective-permute-done | bytes 327712 | tf_op jit(solution)/shard_map/ppermute | solution.py:419
  12.7 0.7 %copy-done = f32[5,4,32,128]{3,2,1,0:T(8,128)} copy-done((f32[5,4,32,128]{3,2,1,0:T(8,128)}, f32[5,4,32,128]{3,2,1,0:T(8,128)S(1)}, u32[]{:S(2)}) %copy-start) | copy-done | bytes 327704
  13.4 1.0 %copy-done.1 = f32[5,4,32,128]{3,2,1,0:T(8,128)S(1)} copy-done((f32[5,4,32,128]{3,2,1,0:T(8,128)S(1)}, f32[5,4,32,128]{3,2,1,0:T(8,128)}, u32[]{:S(2)}) %copy-start.1) | copy-done | bytes 327704
  14.4 4.0 %base.1 = (f32[4,4,32,640]{3,2,1,0:T(8,128)S(1)}, f32[4,32,640]{2,1,0:T(8,128)S(1)}, f32[4,32,640]{2,1,0:T(8,128)S(1)}) custom-call(f32[1]{0:T(128)} %bitcast.2.not_pole_ref, f32[4,32,4,576]{3,2,1,0:T(4,128)} %tracer_hbm.3, f32[32,4,576]{2,1,0:T(4,128)} %lat_hbm.1, f32[32,4,576]{2,1,0:T(4,128)} %lon_hbm.1, f32[5,4,32,128]{3,2,1,0:T(8,128)S(1)} %copy-done.1), custom_call_target="tpu_custom_call" | custom-call | tf_op jit(solution)/shard_map/base/pallas_call | solution.py:421
  18.4 0.0 copy-done.15
  18.4 0.1 copy.22.refs_9_
  18.5 3.0 %collective-permute-done.4.refs_5_ = f32[16,1152]{1,0:T(8,128)S(1)} collective-permute-done((f32[16,1152]{1,0:T(8,128)S(1)}, f32[16,1152]{1,0:T(8,128)S(1)}, u32[]{:S(2)}, u32[]{:S(2)}) %collective-permute-start.4) | collective-permute-done | bytes 73760 | tf_op jit(solution)/shard_map/ppermute | solution.py:418
  21.5 0.0 collective-permute-done.2.refs_3_
  21.5 0.0 collective-permute-done.3.refs_4_
  21.5 12.0 %collective-permute-done.1.refs_2_ = f32[128,1152]{1,0:T(8,128)S(1)} collective-permute-done((f32[128,1152]{1,0:T(8,128)}, f32[128,1152]{1,0:T(8,128)S(1)}, u32[]{:S(2)}, u32[]{:S(2)}) %collective-permute-start.1) | collective-permute-done | bytes 589856 | tf_op jit(solution)/shard_map/ppermute | solution.py:400
  33.5 0.0 copy-done.2
  33.5 0.5 %physics.2 = (f32[2,4,32,640]{3,2,1,0:T(8,128)S(1)}, f32[4,8,640]{2,1,0:T(8,128)S(1)}) custom-call(s32[1]{0:T(128)S(6)} %sub.7.first_ref.give_ref, s32[1]{0:T(128)} %bitcast.1.even_ref, f32[4,4,32,640]{3,2,1,0:T(8,128)S(1)} %get-tuple-element.44.refs_0_, f32[4,32,640]{2,1,0:T(8,128)S(1)} %get-tuple-element.45.refs_1_, ...), custom_call_target="tpu_custom_call" | custom-call | flops 50000000 | bytes 2000000 | tf_op jit(solution)/shard_map/physics/pallas_call | solution.py:461
  34.0 0.1 collective-permute-start.6
  34.1 0.0 copy-start.6
  34.1 0.0 copy-start.7
  34.1 0.0 copy-start.10
  34.2 0.0 copy-start.11
  34.2 0.7 %physics.3 = (f32[4,32,640]{2,1,0:T(8,128)S(1)}, f32[4,32,640]{2,1,0:T(8,128)S(1)}, f32[1,128]{1,0:T(1,128)S(1)}) custom-call(s32[1]{0:T(128)} %bitcast.first_ref.keep_ref, s32[1]{0:T(128)} %bitcast.1.even_ref, f32[4,4,32,640]{3,2,1,0:T(8,128)S(1)} %get-tuple-element.44.refs_0_, f32[4,32,640]{2,1,0:T(8,128)S(1)} %get-tuple-element.45.refs_1_, ...), custom_call_target="tpu_custom_call" | custom-call | flops 50000000 | bytes 2000000 | tf_op jit(solution)/shard_map/physics/pallas_call | solution.py:461
  34.8 2.4 %collective-permute-start.5 = (f32[1,128]{1,0:T(1,128)S(1)}, f32[1,128]{1,0:T(1,128)S(1)}, u32[]{:S(2)}, u32[]{:S(2)}) collective-permute-start(f32[1,128]{1,0:T(1,128)S(1)} %get-tuple-element.54), channel_id=1, source_target_pairs={{0,2},{2,0},{4,6},{6,4},{8,10},{10,8},{12,14},{14,12},{1,3},{3,1},... | collective-permute-start | bytes 1544 | tf_op jit(solution)/shard_map/ppermute | solution.py:481
  37.2 0.0 collective-permute-done.6.refs_2_
  37.2 0.0 copy-done.6
  37.2 0.0 copy-done.7
  37.2 0.0 copy-done.10
  37.3 0.0 copy-done.11
  37.3 0.0 copy-start.3
  37.3 0.0 copy-start.4
  37.3 0.0 copy-start.5
  37.3 0.0 copy-start.8
  37.3 0.0 copy-start.9
  37.3 1.2 %forward.1 = (bf16[256,1152]{1,0:T(8,128)(2,1)S(1)}, bf16[256,1152]{1,0:T(8,128)(2,1)S(1)}) custom-call(f32[4,32,640]{2,1,0:T(8,128)S(1)} %get-tuple-element.55.refs_0_, f32[4,32,640]{2,1,0:T(8,128)S(1)} %get-tuple-element.56.refs_1_, f32[2,4,32,640]{3,2,1,0:T(8,128)S(1)} %collective-permute-done.6.refs_2_, bf16[1024,256]{1,0:T(8,128)(2,1)S(1)} %copy-done.7, ...), custom_call_target="tpu_custom_call" | custom-call | flops 2000000000 | bytes 6000000 | tf_op jit(solution)/shard_map/forward/pallas_call | solution.py:484
  38.5 0.2 collective-permute-done.5
  38.8 2.4 %collective-permute-start.7 = (f32[1,128]{1,0:T(1,128)S(1)}, f32[1,128]{1,0:T(1,128)S(1)}, u32[]{:S(2)}, u32[]{:S(2)}) collective-permute-start(f32[1,128]{1,0:T(1,128)S(1)} %add.49), channel_id=1, source_target_pairs={{0,4},{2,6},{4,0},{6,2},{8,12},{10,14},{12,8},{14,10},{1,5},{3,7},... | collective-permute-start | bytes 1544 | tf_op jit(solution)/shard_map/ppermute | solution.py:481
  41.2 0.0 copy-done.3
  41.2 0.0 copy-done.4
  41.2 0.0 copy-done.5
  41.2 1.8 %inverse.1 = (f32[32,4,576]{2,1,0:T(4,128)S(1)}, f32[32,4,576]{2,1,0:T(4,128)S(1)}, f32[2,4,32,640]{3,2,1,0:T(8,128)S(1)}) custom-call(s32[4]{0:T(128)S(1)} %copy-done.3, f32[4,32,640]{2,1,0:T(8,128)S(1)} %get-tuple-element.55.refs_0_, f32[4,32,640]{2,1,0:T(8,128)S(1)} %get-tuple-element.56.refs_1_, f32[2,4,32,640]{3,2,1,0:T(8,128)S(1)} %collective-permute-done.6.refs_2_, ...), custom_call_target="tpu_custom_call" | custom-call | flops 2000000000 | bytes 6000000 | tf_op jit(solution)/shard_map/inverse/pallas_call | solution.py:499
  43.0 0.0 collective-permute-done.7
  43.0 0.1 collective-permute-start.9
  43.1 2.7 %collective-permute-start.8 = (f32[1,128]{1,0:T(1,128)S(1)}, f32[1,128]{1,0:T(1,128)S(1)}, u32[]{:S(2)}, u32[]{:S(2)}) collective-permute-start(f32[1,128]{1,0:T(1,128)S(1)} %add.50), channel_id=1, source_target_pairs={{0,8},{2,10},{4,12},{6,14},{8,0},{10,2},{12,4},{14,6},{1,9},{3,11}... | collective-permute-start | bytes 1544 | tf_op jit(solution)/shard_map/ppermute | solution.py:481
  45.8 0.0 collective-permute-done.9.refs_2_
  45.8 1.2 %finish.1 = f32[4,32,4,576]{3,2,1,0:T(4,128)} custom-call(s32[1]{0:T(128)} %bitcast.first_ref.keep_ref, s32[1]{0:T(128)S(6)} %sub.7.first_ref.give_ref, f32[32,4,576]{2,1,0:T(4,128)S(1)} %get-tuple-element.69.refs_0_, f32[32,4,576]{2,1,0:T(4,128)S(1)} %get-tuple-element.70.refs_1_, f32[2,4,32,640]{3,2,1,0:T(8,128)S(1)} %collective-permute-done.9.refs_2_), custom_call_target="tpu_custom_call" | custom-call | bytes 3000000 | tf_op jit(solution)/shard_map/finish/pallas_call | solution.py:515
  47.0 0.6 %collective-permute-done.8 = f32[1,128]{1,0:T(1,128)S(1)} collective-permute-done((f32[1,128]{1,0:T(1,128)S(1)}, f32[1,128]{1,0:T(1,128)S(1)}, u32[]{:S(2)}, u32[]{:S(2)}) %collective-permute-start.8) | collective-permute-done | bytes 544 | tf_op jit(solution)/shard_map/ppermute | solution.py:481
  47.6 0.6 %fusion = f32[1,1]{1,0:T(1,128)} fusion(f32[1,128]{1,0:T(1,128)S(1)} %add.51, s32[]{:T(128)S(6)} %select_n.16), kind=kLoop, calls=%fused_computation.3 | loop fusion | flops 1 | bytes 12 | tf_op jit(solution)/shard_map/div | solution.py:533
  (12 shorter events, 0.1 us)
Async XLA Ops:
  3.6 7.5 %copy-start.13 = (f32[1152]{0:T(1024)S(1)}, f32[1152]{0:T(1024)}, u32[]{:S(2)}) copy-start(f32[1152]{0:T(1024)} %constant.73.clone) | copy-start | bytes 13828
  3.6 7.5 %copy-start.14 = (f32[1152]{0:T(1024)S(1)}, f32[1152]{0:T(1024)}, u32[]{:S(2)}) copy-start(f32[1152]{0:T(1024)} %constant.71.clone) | copy-start | bytes 13828
  3.6 7.5 %copy-start.16 = (pred[1152]{0:T(1024)(128)(4,1)S(1)}, pred[1152]{0:T(1024)(128)(4,1)}, u32[]{:S(2)}) copy-start(pred[1152]{0:T(1024)(128)(4,1)} %constant.72.clone) | copy-start | bytes 3460
  3.6 7.6 %copy-start.17 = (s32[1,1,18,1]{2,3,1,0:T(1,128)S(1)}, s32[1,1,18,1]{2,3,1,0:T(1,128)}, u32[]{:S(2)}) copy-start(s32[1,1,18,1]{2,3,1,0:T(1,128)} %param.25) | copy-start | bytes 220
  3.7 7.8 %copy-start.12 = (f32[4,4,576]{2,1,0:T(4,128)S(1)}, f32[4,4,576]{2,1,0:T(4,128)}, u32[]{:S(2)}) copy-start(f32[4,4,576]{2,1,0:T(4,128)} %param.22) | copy-start | bytes 110596
  3.7 29.9 %collective-permute-start.1 = (f32[128,1152]{1,0:T(8,128)}, f32[128,1152]{1,0:T(8,128)S(1)}, u32[]{:S(2)}, u32[]{:S(2)}) collective-permute-start(f32[128,1152]{1,0:T(8,128)} %get-tuple-element.38), channel_id=1, source_target_pairs={{0,2},{2,0},{4,6},{6,4},{8,10},{10,8},{12,14},{14,12},{1,3},{3,1},... | collective-permute-start | bytes 1769480 | tf_op jit(solution)/shard_map/ppermute | solution.py:400
  6.4 15.1 %collective-permute-start.2 = (f32[64,1152]{1,0:T(8,128)}, f32[64,1152]{1,0:T(8,128)S(1)}, u32[]{:S(2)}, u32[]{:S(2)}) collective-permute-start(f32[64,1152]{1,0:T(8,128)} %get-tuple-element.46), channel_id=1, source_target_pairs={{2,4},{4,2},{6,8},{8,6},{10,12},{12,10},{3,5},{5,3},{7,9},{9,7},{1... | collective-permute-start | bytes 884744 | tf_op jit(solution)/shard_map/ppermute | solution.py:401
  7.1 14.4 %collective-permute-start.3 = (f32[64,1152]{1,0:T(8,128)}, f32[64,1152]{1,0:T(8,128)S(1)}, u32[]{:S(2)}, u32[]{:S(2)}) collective-permute-start(f32[64,1152]{1,0:T(8,128)} %get-tuple-element.47), channel_id=1, source_target_pairs={{2,4},{4,2},{6,8},{8,6},{10,12},{12,10},{3,5},{5,3},{7,9},{9,7},{1... | collective-permute-start | bytes 884744 | tf_op jit(solution)/shard_map/ppermute | solution.py:401
  9.7 8.7 %copy-start.15 = (f32[4,32]{1,0:T(4,128)S(1)}, f32[4,32]{1,0:T(4,128)}, u32[]{:S(2)}) copy-start(f32[4,32]{1,0:T(4,128)} %param.24) | copy-start | bytes 1540
  9.7 11.8 %collective-permute-start.4 = (f32[16,1152]{1,0:T(8,128)S(1)}, f32[16,1152]{1,0:T(8,128)S(1)}, u32[]{:S(2)}, u32[]{:S(2)}) collective-permute-start(f32[16,1152]{1,0:T(8,128)S(1)} %get-tuple-element.48), channel_id=1, source_target_pairs={{2,0},{4,2},{6,4},{8,6},{10,8},{12,10},{14,12},{3,1},{5,3},{7,5},{... | collective-permute-start | bytes 221192 | tf_op jit(solution)/shard_map/ppermute | solution.py:418
  11.0 1.7 %collective-permute-start = (f32[5,4,32,128]{3,2,1,0:T(8,128)S(1)}, f32[5,4,32,128]{3,2,1,0:T(8,128)S(1)}, u32[]{:S(2)}, u32[]{:S(2)}) collective-permute-start(f32[5,4,32,128]{3,2,1,0:T(8,128)S(1)} %get-tuple-element.42), channel_id=1, source_target_pairs={{0,1},{1,0},{2,3},{3,2},{4,5},{5,4},{6,7},{7,6},{8,9},{9,8},{10,11... | collective-permute-start | bytes 983048 | tf_op jit(solution)/shard_map/ppermute | solution.py:419
  11.2 22.3 %copy-start.2 = (f32[32,32]{1,0:T(8,128)S(1)}, f32[32,32]{1,0:T(8,128)}, u32[]{:S(2)}) copy-start(f32[32,32]{1,0:T(8,128)} %refs_8_.4) | copy-start | bytes 12292
  12.7 0.7 %copy-start = (f32[5,4,32,128]{3,2,1,0:T(8,128)}, f32[5,4,32,128]{3,2,1,0:T(8,128)S(1)}, u32[]{:S(2)}) copy-start(f32[5,4,32,128]{3,2,1,0:T(8,128)S(1)} %collective-permute-done.side_ref) | copy-start | bytes 983044
  13.4 1.0 %copy-start.1 = (f32[5,4,32,128]{3,2,1,0:T(8,128)S(1)}, f32[5,4,32,128]{3,2,1,0:T(8,128)}, u32[]{:S(2)}) copy-start(f32[5,4,32,128]{3,2,1,0:T(8,128)} %copy-done) | copy-start | bytes 983044
  34.0 3.2 %collective-permute-start.6 = (f32[2,4,32,640]{3,2,1,0:T(8,128)S(1)}, f32[2,4,32,640]{3,2,1,0:T(8,128)S(1)}, u32[]{:S(2)}, u32[]{:S(2)}) collective-permute-start(f32[2,4,32,640]{3,2,1,0:T(8,128)S(1)} %get-tuple-element.57), channel_id=1, source_target_pairs={{0,1},{1,0},{2,3},{3,2},{4,5},{5,4},{6,7},{7,6},{8,9},{9,8},{10,11... | collective-permute-start | bytes 1966088 | tf_op jit(solution)/shard_map/ppermute | solution.py:473
  34.1 3.1 %copy-start.6 = (bf16[1024,256]{1,0:T(8,128)(2,1)S(1)}, bf16[1024,256]{1,0:T(8,128)(2,1)}, u32[]{:S(2)}) copy-start(bf16[1024,256]{1,0:T(8,128)(2,1)} %constant.75.clone.refs_4_) | copy-start | bytes 1572868
  34.1 3.1 %copy-start.7 = (bf16[1024,256]{1,0:T(8,128)(2,1)S(1)}, bf16[1024,256]{1,0:T(8,128)(2,1)}, u32[]{:S(2)}) copy-start(bf16[1024,256]{1,0:T(8,128)(2,1)} %constant.74.clone.refs_3_) | copy-start | bytes 1572868
  34.1 3.1 %copy-start.10 = (bf16[128,128]{1,0:T(8,128)(2,1)S(1)}, bf16[128,128]{1,0:T(8,128)(2,1)}, u32[]{:S(2)}) copy-start(bf16[128,128]{1,0:T(8,128)(2,1)} %constant.77.clone.refs_6_) | copy-start | bytes 98308
  34.2 3.1 %copy-start.11 = (bf16[128,128]{1,0:T(8,128)(2,1)S(1)}, bf16[128,128]{1,0:T(8,128)(2,1)}, u32[]{:S(2)}) copy-start(bf16[128,128]{1,0:T(8,128)(2,1)} %constant.76.clone.refs_5_) | copy-start | bytes 98308
  34.8 3.9 %collective-permute-start.5 = (f32[1,128]{1,0:T(1,128)S(1)}, f32[1,128]{1,0:T(1,128)S(1)}, u32[]{:S(2)}, u32[]{:S(2)}) collective-permute-start(f32[1,128]{1,0:T(1,128)S(1)} %get-tuple-element.54), channel_id=1, source_target_pairs={{0,2},{2,0},{4,6},{6,4},{8,10},{10,8},{12,14},{14,12},{1,3},{3,1},... | collective-permute-start | bytes 1544 | tf_op jit(solution)/shard_map/ppermute | solution.py:481
  37.3 3.9 %copy-start.3 = (s32[4]{0:T(128)S(1)}, s32[4]{0:T(128)}, u32[]{:S(2)}) copy-start(s32[4]{0:T(128)} %mask_ref.1) | copy-start | bytes 52
  37.3 3.9 %copy-start.4 = (bf16[1024,256]{1,0:T(8,128)(2,1)S(1)}, bf16[1024,256]{1,0:T(8,128)(2,1)}, u32[]{:S(2)}) copy-start(bf16[1024,256]{1,0:T(8,128)(2,1)} %constant.79.clone.refs_6_) | copy-start | bytes 1572868
  37.3 3.9 %copy-start.5 = (bf16[1024,256]{1,0:T(8,128)(2,1)S(1)}, bf16[1024,256]{1,0:T(8,128)(2,1)}, u32[]{:S(2)}) copy-start(bf16[1024,256]{1,0:T(8,128)(2,1)} %constant.78.clone.refs_5_) | copy-start | bytes 1572868
  37.3 3.9 %copy-start.8 = (bf16[128,128]{1,0:T(8,128)(2,1)S(1)}, bf16[128,128]{1,0:T(8,128)(2,1)}, u32[]{:S(2)}) copy-start(bf16[128,128]{1,0:T(8,128)(2,1)} %constant.81.clone.refs_8_) | copy-start | bytes 98308
  37.3 3.9 %copy-start.9 = (bf16[128,128]{1,0:T(8,128)(2,1)S(1)}, bf16[128,128]{1,0:T(8,128)(2,1)}, u32[]{:S(2)}) copy-start(bf16[128,128]{1,0:T(8,128)(2,1)} %constant.80.clone.refs_7_) | copy-start | bytes 98308
  38.8 4.2 %collective-permute-start.7 = (f32[1,128]{1,0:T(1,128)S(1)}, f32[1,128]{1,0:T(1,128)S(1)}, u32[]{:S(2)}, u32[]{:S(2)}) collective-permute-start(f32[1,128]{1,0:T(1,128)S(1)} %add.49), channel_id=1, source_target_pairs={{0,4},{2,6},{4,0},{6,2},{8,12},{10,14},{12,8},{14,10},{1,5},{3,7},... | collective-permute-start | bytes 1544 | tf_op jit(solution)/shard_map/ppermute | solution.py:481
  43.0 2.7 %collective-permute-start.9 = (f32[2,4,32,640]{3,2,1,0:T(8,128)S(1)}, f32[2,4,32,640]{3,2,1,0:T(8,128)S(1)}, u32[]{:S(2)}, u32[]{:S(2)}) collective-permute-start(f32[2,4,32,640]{3,2,1,0:T(8,128)S(1)} %get-tuple-element.71), channel_id=1, source_target_pairs={{0,1},{1,0},{2,3},{3,2},{4,5},{5,4},{6,7},{7,6},{8,9},{9,8},{10,11... | collective-permute-start | bytes 1966088 | tf_op jit(solution)/shard_map/ppermute | solution.py:512
  43.1 4.5 %collective-permute-start.8 = (f32[1,128]{1,0:T(1,128)S(1)}, f32[1,128]{1,0:T(1,128)S(1)}, u32[]{:S(2)}, u32[]{:S(2)}) collective-permute-start(f32[1,128]{1,0:T(1,128)S(1)} %add.50), channel_id=1, source_target_pairs={{0,8},{2,10},{4,12},{6,14},{8,0},{10,2},{12,4},{14,6},{1,9},{3,11}... | collective-permute-start | bytes 1544 | tf_op jit(solution)/shard_map/ppermute | solution.py:481

commit v5 on v4

--- a/solution.py
+++ b/solution.py
@@ -82,57 +82,46 @@
     return copies
 
 
-def pack_halo(tracer_ref, t, out_ref, slot, upward):
-    levels, rows = tracer_ref.shape[1:3]
-    place = slice(levels * slot, levels * (slot + 1))
-
-    @pl.when(upward)
-    def _():
-        out_ref[place, :] = pack_rows(tracer_ref[t, :, rows - 2, :], tracer_ref[t, :, rows - 1, :])
-
-    @pl.when(jnp.logical_not(upward))
-    def _():
-        out_ref[place, :] = pack_rows(tracer_ref[t, :, 0, :], tracer_ref[t, :, 1, :])
-
-
-def copies_in_pieces(source, target, sems, pieces):
-    size = target.shape[0] // pieces
-    spans = [pl.ds(size * i, size) for i in range(pieces)]
-    copies = [pltpu.make_async_copy(source.at[span], target.at[span], sems.at[i]) for i, span in enumerate(spans)]
-    for copy in copies:
-        copy.start()
-    return copies
-
-
-def pack_kernel(even_ref, tracer_hbm, *refs):
-    inner_ref, outer_refs, (tracer_ref, sems) = refs[0], refs[1:-2], refs[-2:]
-    count = tracer_ref.shape[0]
-    copies = [copies_in_pieces(tracer_hbm.at[t], tracer_ref.at[t], sems.at[t], PIECES) for t in range(count)]
-    even = even_ref[0] == 1
-    share = count // len(outer_refs)
+def pack_kernel(even_ref, tracer_hbm, out_ref, row_ref, sems):
+    count, levels = row_ref.shape[:2]
+    first_row = pl.multiple_of(jnp.where(even_ref[0] == 1, tracer_hbm.shape[2] - 2, 0), 2)
+    sources = [tracer_hbm.at[t, :, pl.ds(first_row, 2), :] for t in range(count)]
+    copies = start_copies([(sources[t], row_ref.at[t]) for t in range(count)], sems)
     for t in range(count):
-        for copy in copies[t]:
-            copy.wait()
-        pack_halo(tracer_ref, t, inner_ref, t, even)
-        pack_halo(tracer_ref, t, outer_refs[t // share], t % share, jnp.logical_not(even))
-
-
-def side_kernel(tracer_hbm, lat_hbm, lon_hbm, side_ref, courant_ref, tracer_ref, lat_ref, lon_ref, sems):
+        copies[t].wait()
+        out_ref[levels * t : levels * (t + 1), :] = pack_rows(row_ref[t, :, 0, :], row_ref[t, :, 1, :])
+
+
+def rest_kernel(even_ref, tracer_hbm, lat_hbm, lon_hbm, *refs):
+    courant_ref, side_ref, tracer_ref, lat_ref, lon_ref, sems = refs[-6:]
+    outer_refs = refs[:-6]
     count, levels, rows, sector = tracer_ref.shape
-    pairs = [(lat_hbm, lat_ref)] + [(tracer_hbm.at[t], tracer_ref.at[t]) for t in range(count)] + [(lon_hbm, lon_ref)]
+    pairs = [(tracer_hbm.at[t], tracer_ref.at[t]) for t in range(count)] + [(lat_hbm, lat_ref), (lon_hbm, lon_ref)]
     copies = start_copies(pairs, sems)
     shift, whole = sector % LANES, sector // LANES * LANES
     lane = lax.broadcasted_iota(jnp.int32, (levels, LANES), 1)
-    copies[0].wait()
+    even = even_ref[0] == 1
+
+    def store_side(i, r, values):
+        first = pltpu.roll(values[:, :LANES], shift, 1)
+        last = jnp.concatenate([values[:, whole:], values[:, whole:]], axis=1)
+        side_ref[i, r] = jnp.where(lane < LANES - 2, first, last)
+
+    for t in range(count):
+        copies[t].wait()
+        row = [tracer_ref[t, :, r, :] for r in range(rows)]
+        slot = t // len(outer_refs)
+        outer_refs[t % len(outer_refs)][levels * slot : levels * (slot + 1), :] = pack_rows(
+            jnp.where(even, row[0], row[rows - 2]), jnp.where(even, row[1], row[rows - 1])
+        )
+        for r in range(rows):
+            store_side(t, r, row[r])
+    copies[count].wait()
     courant = lat_ref[:, 0, :]
     courant_ref[...] = pack_rows(courant[: levels // 2], courant[levels // 2 :])
-    for i in range(count + 1):
-        copies[i + 1].wait()
-        for r in range(rows):
-            values = tracer_ref[i, :, r, :] if i < count else lon_ref[:, r, :]
-            first = pltpu.roll(values[:, :LANES], shift, 1)
-            last = jnp.concatenate([values[:, whole:], values[:, whole:]], axis=1)
-            side_ref[i, r] = jnp.where(lane < LANES - 2, first, last)
+    copies[count + 1].wait()
+    for r in range(rows):
+        store_side(count, r, lon_ref[:, r, :])
 
 
 def base_kernel(width, not_pole_ref, tracer_hbm, lat_hbm, lon_hbm, side_ref, base_ref, north_ref, courant_ref, *scratch):
@@ -170,12 +159,12 @@
             base_ref[t, r] = value
 
 
-def physics_kernel(levels, sector, owner_count, first_ref, even_ref, *refs):
-    base_ref, north_ref, inner_ref, *outer_refs = refs[:5]
-    top_ref, courant_ref, surface_ref, mixing_ref, decay_ref, owner_ref, energy_in_ref = refs[5:12]
-    physics_refs, energy_ref = refs[12:-1], refs[-1]
-    if len(physics_refs) == 1:
-        physics_refs = [physics_refs[0].at[i] for i in range(physics_refs[0].shape[0])]
+def physics_kernel(levels, sector, owner_count, chunk, even_ref, *refs):
+    count = len(refs) - 12 >> 1
+    first_refs, refs = refs[:count], refs[count:]
+    base_ref, north_ref, inner_ref, outer_ref = refs[:4]
+    top_ref, courant_ref, surface_ref, mixing_ref, decay_ref, owner_ref, energy_in_ref = refs[4:11]
+    physics_refs, energy_ref = refs[11:-1], refs[-1]
     rows, width = base_ref.shape[1], base_ref.shape[-1]
     courant = [courant_ref[r] for r in range(rows)]
     even = even_ref[0] == 1
@@ -186,11 +175,10 @@
     level = lax.broadcasted_iota(jnp.int32, (8, width), 0)
     lane = lax.broadcasted_iota(jnp.int32, (8, width), 1)
     energies = [energy_in_ref[r] for r in range(rows)]
-    for i, physics_ref in enumerate(physics_refs):
-        t = first_ref[0] + i
+    for first_ref, physics_ref in zip(first_refs, physics_refs):
+        t = first_ref[0] + chunk
         inner = inner_ref[pl.ds(pl.multiple_of(levels * t, levels), levels), :]
-        outer = [outer_ref[levels * i : levels * (i + 1), :] for outer_ref in outer_refs]
-        outer = jnp.where(first_ref[0] == 0, *outer)
+        outer = jnp.where(first_ref[0] == 0, outer_ref[:levels, :], outer_ref[levels:, :])
         low, high = jnp.where(even, outer, inner), jnp.where(even, inner, outer)
         low_a, low_b = low[:, :width], second_half(low, sector)
         high_a, high_b = high[:, :width], second_half(high, sector)
@@ -247,6 +235,10 @@
     return pairs, cosine, sine
 
 
+def row_of(piece_refs, r):
+    return piece_refs[0].at[r] if len(piece_refs) == 1 else piece_refs[r].at[0]
+
+
 def stacked_table(high_ref, low_ref, begin, size):
     high = high_ref[begin : begin + size, :]
     return jnp.concatenate([high, high, low_ref[begin : begin + size, :]], axis=0)
@@ -258,11 +250,11 @@
     return jnp.dot(stacked, table, preferred_element_type=jnp.float32)
 
 
-def forward_kernel(radix, count, *refs):
-    own_refs, refs = refs[:count], refs[count:]
-    other_ref, table_high_ref, table_low_ref, first_high_ref, first_low_ref, scale_ref = refs[:6]
-    out_high_ref, out_low_ref, high_ref, low_ref = refs[6:]
-    rows, levels, width = own_refs[0].shape
+def forward_kernel(radix, pieces, own_ref, *refs):
+    other_refs, refs = refs[:pieces], refs[pieces:]
+    table_high_ref, table_low_ref, first_high_ref, first_low_ref, scale_ref, *refs = refs
+    out_high_ref, out_low_ref, high_ref, low_ref = refs
+    rows, levels, width = own_ref.shape
     pairs, cosine, sine = waves_of(radix)
     segments = width // LANES
     shift = radix * LANES // 2 % LANES
@@ -271,29 +263,29 @@
     def store(place, column, wave):
         high_ref[place, column : column + LANES], low_ref[place, column : column + LANES] = split_high_low(wave)
 
-    for i, own_ref in enumerate(own_refs):
-        for r in range(rows):
-            place = slice(levels * (rows * i + r), levels * (rows * i + r + 1))
-            own = [own_ref[r, :, LANES * n : LANES * (n + 1)] for n in range(segments)]
-            turned = [pltpu.roll(other_ref[i, r, :, LANES * n : LANES * (n + 1)], shift, 1) for n in range(segments)]
-            joined = own[:-1] + [jnp.where(lane < shift, own[-1], turned[0])]
-            joined += [jnp.where(lane < shift, turned[n], turned[n + 1]) for n in range(segments - 1)]
-            plus = [joined[n] + joined[radix - n] for n in range(1, pairs + 1)]
-            minus = [joined[radix - n] - joined[n] for n in range(1, pairs + 1)]
-            store(place, 0, sum(plus, joined[0]))
-            for k in range(1, pairs + 1):
-                real = sum((cosine(k, n) * plus[n - 1] for n in range(1, pairs + 1)), joined[0])
-                imaginary = sine(k, 1) * minus[0]
-                for n in range(2, pairs + 1):
-                    imaginary = imaginary + sine(k, n) * minus[n - 1]
-                store(place, LANES * (2 * k - 1), real)
-                store(place, LANES * 2 * k, imaginary)
+    for r in range(rows):
+        place = slice(levels * r, levels * (r + 1))
+        other_ref = row_of(other_refs, r)
+        own = [own_ref[r, :, LANES * n : LANES * (n + 1)] for n in range(segments)]
+        turned = [pltpu.roll(other_ref[:, LANES * n : LANES * (n + 1)], shift, 1) for n in range(segments)]
+        joined = own[:-1] + [jnp.where(lane < shift, own[-1], turned[0])]
+        joined += [jnp.where(lane < shift, turned[n], turned[n + 1]) for n in range(segments - 1)]
+        plus = [joined[n] + joined[radix - n] for n in range(1, pairs + 1)]
+        minus = [joined[radix - n] - joined[n] for n in range(1, pairs + 1)]
+        store(place, 0, sum(plus, joined[0]))
+        for k in range(1, pairs + 1):
+            real = sum((cosine(k, n) * plus[n - 1] for n in range(1, pairs + 1)), joined[0])
+            imaginary = sine(k, 1) * minus[0]
+            for n in range(2, pairs + 1):
+                imaginary = imaginary + sine(k, n) * minus[n - 1]
+            store(place, LANES * (2 * k - 1), real)
+            store(place, LANES * 2 * k, imaginary)
 
     def transform(begin, size, table):
         spectrum = product_of(high_ref, low_ref, begin, size, table)
-        for i in range(count * rows):
-            place = slice(levels * i, levels * (i + 1))
-            damped = spectrum[place] * scale_ref[i % rows : i % rows + 1, begin : begin + size]
+        for r in range(rows):
+            place = slice(levels * r, levels * (r + 1))
+            damped = spectrum[place] * scale_ref[r : r + 1, begin : begin + size]
             out_high_ref[place, begin : begin + size], out_low_ref[place, begin : begin + size] = split_high_low(damped)
 
     transform(0, LANES, stacked_table(first_high_ref, first_low_ref, 0, LANES))
@@ -301,12 +293,12 @@
         transform(LANES * (2 * k + 1), 2 * LANES, stacked_table(table_high_ref, table_low_ref, 2 * LANES * k, 2 * LANES))
 
 
-def inverse_kernel(radix, count, mask_ref, *refs):
-    own_refs, refs = refs[:count], refs[count:]
-    other_ref, high_ref, low_ref, table_high_ref, table_low_ref, first_high_ref, first_low_ref = refs[:7]
-    result_refs, back_ref, wave_ref = refs[7 : 7 + count], refs[7 + count], refs[8 + count]
-    rows, levels, width = own_refs[0].shape
-    sector = result_refs[0].shape[-1]
+def inverse_kernel(radix, pieces, mask_ref, own_ref, *refs):
+    other_refs, refs = refs[:pieces], refs[pieces:]
+    high_ref, low_ref, table_high_ref, table_low_ref, first_high_ref, first_low_ref, *refs = refs
+    result_ref, back_ref, wave_ref = refs
+    rows, levels, width = own_ref.shape
+    sector = result_ref.shape[-1]
     pairs, cosine, sine = waves_of(radix)
     segments = width // LANES
     shift = radix * LANES // 2 % LANES
@@ -319,34 +311,34 @@
     for k in range(pairs):
         transform(LANES * (2 * k + 1), 2 * LANES, stacked_table(table_high_ref, table_low_ref, 2 * LANES * k, 2 * LANES))
 
-    for i, (own_ref, result_ref) in enumerate(zip(own_refs, result_refs)):
-        for r in range(rows):
-            place = slice(levels * (rows * i + r), levels * (rows * i + r + 1))
-            waves = [wave_ref[place, LANES * n : LANES * (n + 1)] for n in range(radix)]
-            results = [None] * radix
-            results[0] = sum((waves[2 * k - 1] for k in range(1, pairs + 1)), waves[0])
-            for n in range(1, pairs + 1):
-                even = sum((cosine(k, n) * waves[2 * k - 1] for k in range(1, pairs + 1)), waves[0])
-                odd = sine(1, n) * waves[2]
-                for k in range(2, pairs + 1):
-                    odd = odd + sine(k, n) * waves[2 * k]
-                results[n], results[radix - n] = even - odd, even + odd
-            filtered_row = mask_ref[r] == 1
-            turned = [pltpu.roll(result, LANES - shift, 1) for result in results[segments - 1 :]]
-            for n in range(segments):
-                begin = LANES * n
-                size = min(LANES, sector - begin)
-                value = jnp.where(filtered_row, results[n], own_ref[r, :, begin : begin + LANES])
-                result_ref[:, r, begin : begin + size] = value[:, :size]
-                value = jnp.where(lane < LANES - shift, turned[n], turned[min(n + 1, segments - 1)])
-                back_ref[i, r, :, begin : begin + LANES] = jnp.where(
-                    filtered_row, value, other_ref[i, r, :, begin : begin + LANES]
-                )
+    for r in range(rows):
+        place = slice(levels * r, levels * (r + 1))
+        other_ref = row_of(other_refs, r)
+        waves = [wave_ref[place, LANES * n : LANES * (n + 1)] for n in range(radix)]
+        results = [None] * radix
+        results[0] = sum((waves[2 * k - 1] for k in range(1, pairs + 1)), waves[0])
+        for n in range(1, pairs + 1):
+            even = sum((cosine(k, n) * waves[2 * k - 1] for k in range(1, pairs + 1)), waves[0])
+            odd = sine(1, n) * waves[2]
+            for k in range(2, pairs + 1):
+                odd = odd + sine(k, n) * waves[2 * k]
+            results[n], results[radix - n] = even - odd, even + odd
+        filtered_row = mask_ref[r] == 1
+        turned = [pltpu.roll(result, LANES - shift, 1) for result in results[segments - 1 :]]
+        for n in range(segments):
+            begin = LANES * n
+            size = min(LANES, sector - begin)
+            value = jnp.where(filtered_row, results[n], own_ref[r, :, begin : begin + LANES])
+            result_ref[:, r, begin : begin + size] = value[:, :size]
+            value = jnp.where(lane < LANES - shift, turned[n], turned[min(n + 1, segments - 1)])
+            back_ref[r, :, begin : begin + LANES] = jnp.where(filtered_row, value, other_ref[:, begin : begin + LANES])
 
 
 def finish_kernel(keep_ref, give_ref, *refs):
-    result_refs, (received_ref, out_hbm, turned_ref, sems) = refs[:-4], refs[-4:]
-    count, rows, levels, width = received_ref.shape
+    out_hbm, turned_ref, sems = refs[-3:]
+    count = turned_ref.shape[0]
+    result_refs, received_refs = refs[:count], refs[count : 2 * count]
+    rows, levels, width = received_refs[0].shape
     sector = out_hbm.shape[-1]
     piece = levels // PIECES
     copies = []
@@ -361,7 +353,7 @@
         send(result_ref, keep_ref[0] + i, i)
     for i in range(count):
         for r in range(rows):
-            turned_ref[i, :, r, :] = received_ref[i, r, :, :sector]
+            turned_ref[i, :, r, :] = received_refs[i][r, :, :sector]
         send(turned_ref.at[i], give_ref[0] + i, count + i)
     for copy in copies:
         copy.wait()
@@ -387,35 +379,35 @@
     fields = [pltpu.with_memory_space_constraint(array, pltpu.HBM) for array in (tracers, courant_lat, courant_lon)]
     field_buffers = [pltpu.VMEM(array.shape, f32) for array in (tracers, courant_lat, courant_lon)]
     half = tracer_count // 2
-    inner, *outer = pl.pallas_call(
+    inner = pl.pallas_call(
         pack_kernel,
         in_specs=[scalars, in_hbm],
-        out_specs=[whole] * 3,
-        out_shape=[pltpu.VMEM((levels * count, length), f32) for count in (tracer_count, half, half)],
-        scratch_shapes=[field_buffers[0], pltpu.SemaphoreType.DMA((tracer_count, PIECES))],
+        out_specs=whole,
+        out_shape=pltpu.VMEM((levels * tracer_count, length), f32),
+        scratch_shapes=[pltpu.VMEM((tracer_count, levels, 2, sector), f32), pltpu.SemaphoreType.DMA((tracer_count,))],
         compiler_params=params(),
         cost_estimate=cost(0, 600_000),
         name="pack",
     )(even, fields[0])
     from_inside = lax.ppermute(inner, "lat", inside)
-    from_across = [lax.ppermute(part, "lat", across) for part in outer]
-
-    fields, inner = lax.optimization_barrier((fields, inner))
-    fields = [pltpu.with_memory_space_constraint(array, pltpu.HBM) for array in fields]
-    sides, courant_row = pl.pallas_call(
-        side_kernel,
-        in_specs=[in_hbm] * 3,
-        out_specs=[whole] * 2,
-        out_shape=[
+    even_rest, inner = lax.optimization_barrier((even, inner))
+    *outer, courant_row, sides = pl.pallas_call(
+        rest_kernel,
+        in_specs=[scalars] + [in_hbm] * 3,
+        out_specs=[whole] * (half + 2),
+        out_shape=[pltpu.VMEM((levels * 2, length), f32)] * half
+        + [
+            jax.ShapeDtypeStruct((levels // 2, length), f32),
             jax.ShapeDtypeStruct((tracer_count + 1, rows, levels, LANES), f32),
-            jax.ShapeDtypeStruct((levels // 2, length), f32),
         ],
         scratch_shapes=field_buffers + [pltpu.SemaphoreType.DMA((tracer_count + 2,))],
         compiler_params=params(),
         cost_estimate=cost(0, 0),
-        name="side",
-    )(*fields)
+        name="rest",
+    )(even_rest, *fields)
+    from_across = [lax.ppermute(part, "lat", across) for part in outer[:-1]]
     top = lax.ppermute(courant_row, "lat", downward)
+
     sides = lax.ppermute(sides, "lon", swap)
     not_pole = (lat > 0).astype(f32).reshape(1)
     base, north, lat_courant = pl.pallas_call(
@@ -449,72 +441,96 @@
 
     base, scale, owner_of, surface, decay = lax.optimization_barrier((base, scale, owner_of, surface, decay))
 
+    base, outer = lax.optimization_barrier((base, outer))
+    from_across.append(lax.ppermute(outer[-1], "lat", across))
+
     keep = (half * lax.axis_index("lon")).reshape(1)
     give = half - keep
     circles = jax.ShapeDtypeStruct((half, rows, levels, width), f32)
     result_shape = jax.ShapeDtypeStruct((levels, rows, sector), f32)
-    spectra = jax.ShapeDtypeStruct((half * rows * levels, length), jnp.bfloat16)
     out_shape = jax.ShapeDtypeStruct(tracers.shape, f32)
 
-    def run_physics(first, energy, shapes, last):
-        shapes = shapes + [jax.ShapeDtypeStruct((1, LANES) if last else energy.shape, f32)]
+    def run_physics(chunk, firsts, energy, last=False):
+        shapes = [jax.ShapeDtypeStruct(circles.shape[1:], f32)] * len(firsts)
+        shapes.append(jax.ShapeDtypeStruct((1, LANES) if last else energy.shape, f32))
         *results, energy = pl.pallas_call(
-            functools.partial(physics_kernel, levels, sector, lat_count if last else 0),
-            in_specs=[scalars] * 2 + [whole] * 12,
+            functools.partial(physics_kernel, levels, sector, lat_count if last else 0, chunk),
+            in_specs=[scalars] * (1 + len(firsts)) + [whole] * 11,
             out_specs=[whole] * len(shapes),
             out_shape=shapes,
             compiler_params=params(),
-            cost_estimate=cost(50_000_000, 2_000_000),
+            cost_estimate=cost(0, 0),
             name="physics",
-        )(first, even, base, north, from_inside, *from_across, top, lat_courant, surface, mixing, decay, owner_of, energy)
+        )(even, *firsts, base, north, from_inside, from_across[chunk], top, lat_courant, surface, mixing, decay, owner_of, energy)
         return results, energy
 
-    (given,), energy = run_physics(give, jnp.zeros((rows, 8, width), f32), [circles], False)
-    other = lax.ppermute(given, "lon", swap)
-    kept, energy = run_physics(keep, energy, [jax.ShapeDtypeStruct(circles.shape[1:], f32)] * half, True)
-
     forward, inverse = ([jnp.asarray(part) for table in tables for part in split_table(table)] for tables in (forward, inverse))
+    circle = jax.ShapeDtypeStruct(circles.shape[1:], f32)
+    spectra = jax.ShapeDtypeStruct((rows * levels, length), jnp.bfloat16)
+
+    def run_forward(own, other):
+        return pl.pallas_call(
+            functools.partial(forward_kernel, radix, len(other)),
+            in_specs=[whole] * (6 + len(other)),
+            out_specs=[whole] * 2,
+            out_shape=[spectra] * 2,
+            scratch_shapes=[pltpu.VMEM(spectra.shape, jnp.bfloat16)] * 2,
+            compiler_params=params(),
+            cost_estimate=cost(0, 0),
+            name="forward",
+        )(own, *other, *forward, scale)
+
+    def run_inverse(own, other, high, low):
+        return pl.pallas_call(
+            functools.partial(inverse_kernel, radix, len(other)),
+            in_specs=[scalars] + [whole] * (7 + len(other)),
+            out_specs=[whole] * 2,
+            out_shape=[result_shape, circle],
+            scratch_shapes=[pltpu.VMEM(spectra.shape, f32)],
+            compiler_params=params(),
+            cost_estimate=cost(0, 0),
+            name="inverse",
+        )(polar_mask, own, *other, high, low, *inverse)
+
+    energy = jnp.zeros((rows, 8, width), f32)
+    results, received = [], []
+    for chunk in range(half - 1):
+        (given, own), energy = run_physics(chunk, [give, keep], energy)
+        other = [lax.ppermute(given[r : r + 1], "lon", swap) for r in range(rows)]
+        spectrum = run_forward(own, other)
+        result, back = run_inverse(own, other, *spectrum)
+        results.append(result)
+        received.append(lax.ppermute(back, "lon", swap))
+        energy, back = lax.optimization_barrier((energy, back))
+
     distances = [1 << i for i in range(lat_count.bit_length() - 1)]
 
     def send_energy(energy):
         distance = distances.pop(0)
         return lax.ppermute(energy, "lat", [(i, i ^ distance) for i in range(lat_count)])
 
+    (given,), energy = run_physics(half - 1, [give], energy)
+    other = [lax.ppermute(given, "lon", swap)]
+    (own,), energy = run_physics(half - 1, [keep], energy, True)
+
     coming = send_energy(energy)
-    high, low = pl.pallas_call(
-        functools.partial(forward_kernel, radix, half),
-        in_specs=[whole] * (half + 6),
-        out_specs=[whole] * 2,
-        out_shape=[spectra] * 2,
-        scratch_shapes=[pltpu.VMEM(spectra.shape, jnp.bfloat16)] * 2,
-        compiler_params=params(),
-        cost_estimate=cost(2_000_000_000, 6_000_000),
-        name="forward",
-    )(*kept, other, *forward, scale)
+    high, low = run_forward(own, other)
     coming, high = lax.optimization_barrier((coming, high))
     energy = energy + coming
     energy, high = lax.optimization_barrier((energy, high))
 
     coming = send_energy(energy)
-    *results, back = pl.pallas_call(
-        functools.partial(inverse_kernel, radix, half),
-        in_specs=[scalars] + [whole] * (half + 7),
-        out_specs=[whole] * (half + 1),
-        out_shape=[result_shape] * half + [circles],
-        scratch_shapes=[pltpu.VMEM(spectra.shape, f32)],
-        compiler_params=params(),
-        cost_estimate=cost(2_000_000_000, 6_000_000),
-        name="inverse",
-    )(polar_mask, *kept, other, high, low, *inverse)
+    result, back = run_inverse(own, other, high, low)
     coming, back = lax.optimization_barrier((coming, back))
     energy = energy + coming
     energy, back = lax.optimization_barrier((energy, back))
-    received = lax.ppermute(back, "lon", swap)
+    results.append(result)
+    received.append(lax.ppermute(back, "lon", swap))
 
     coming = send_energy(energy)
     out = pl.pallas_call(
         finish_kernel,
-        in_specs=[scalars] * 2 + [whole] * (half + 1),
+        in_specs=[scalars] * 2 + [whole] * (2 * half),
         out_specs=in_hbm,
         out_shape=out_shape,
         scratch_shapes=[
@@ -524,7 +540,7 @@
         compiler_params=params(),
         cost_estimate=cost(0, 3_000_000),
         name="finish",
-    )(keep, give, *results, received)
+    )(keep, give, *results, *received)
     coming, out = lax.optimization_barrier((coming, out))
     energy = energy + coming
     while distances:

time: 48.5 us -> 47 us (0.969)
  waiting for transfers between devices: 17.2 us -> 10.1 us
  starting transfers between devices: 13 us -> 16 us
  Pallas kernels: 14.2 us -> 16 us
  local copies, waits for them, and re-layouts: 2.09 us -> 2.82 us
    ppermute x1, waiting for transfers between devices: 12 us -> 5.58 us  [on_device(): from_inside = lax.ppermute(inner, 'lat', inside)]
    ppermute x4 -> x9, starting transfers between devices: 1.49 us -> 3.91 us  [the longest x1 1.4 us: on_device(): from_across = [lax.ppermute(part, 'lat', across) for part in outer[:-1]]]
    ppermute x1, waiting for transfers between devices: 3.04 us -> 0.73 us  [on_device(): top = lax.ppermute(courant_row, 'lat', downward)]
    pallas_call x2 -> x3, Pallas kernels: 1.16 us -> 2.39 us  [run_physics(): pl.pallas_call(functools.partial(physics_kernel, levels, sector, lat_coun...]
    ppermute x4 -> x9, waiting for transfers between devices: 0.01 us -> 0.93 us  [the longest x4 0.92 us: on_device(): other = [lax.ppermute(given[r:r + 1], 'lon', swap) for r in range(rows)]]
    ppermute x3, waiting for transfers between devices: 0.9 us -> 1.61 us  [send_energy(): lax.ppermute(energy, 'lat', [(i, i ^ distance) for i in range(lat_count)])]
    unnamed x36 -> x38, local copies, waits for them, and re-layouts: 1.81 us -> 2.51 us
    pallas_call x5 -> x7, Pallas kernels: 9.01 us -> 9.7 us  [the longest x2 3.24 us: run_inverse(): pl.pallas_call(functools.partial(inverse_kernel, radix, len(other)), in_s...]
  transfers between devices with their start and end apart: 10 -> 15, of which waited for: 5 -> 10; matrix products, arithmetic and copies ran while one was open for 1% -> 1% of each run, Pallas kernels for 22% -> 31%
where the time goes in v5:
time: 47 us; the launch traced here: 46.7 us
  Pallas kernels  16 us (34%)
  starting transfers between devices  16 us (34%)
  waiting for transfers between devices  10.1 us (21%)
  local copies, waits for them, and re-layouts  2.82 us (6%)
  between operations  1 us (2%)
  other arithmetic  0.72 us (2%)
    ppermute x3, starting transfers between devices, send_energy(): lax.ppermute(energy, 'lat', [(i, i ^ distance) for i in range(lat_count)])  7.67 us
    ppermute x1, waiting for transfers between devices, on_device(): from_inside = lax.ppermute(inner, 'lat', inside)  5.58 us
    pallas_call x1, Pallas kernels, on_device(): pl.pallas_call(functools.partial(base_kernel, width), in_specs=[scalars,...  3.95 us
    pallas_call x2, Pallas kernels, run_inverse(): pl.pallas_call(functools.partial(inverse_kernel, radix, len(other)), in_s...  3.24 us
    ppermute x1, starting transfers between devices, on_device(): from_inside = lax.ppermute(inner, 'lat', inside)  3 us
    pallas_call x1, Pallas kernels, on_device(): pl.pallas_call(rest_kernel, in_specs=[scalars] + [in_hbm] * 3, out_specs=...  2.54 us
    unnamed x38, local copies, waits for them, and re-layouts  2.51 us
    pallas_call x3, Pallas kernels, run_physics(): pl.pallas_call(functools.partial(physics_kernel, levels, sector, lat_coun...  2.39 us
  transfers between devices with their start and end apart: 15, of which 10 were waited for; matrix products, arithmetic and copies ran while one was open for 1% of the time, Pallas kernels for 31%

profile of v5, /device:TPU:0, one launch (start us, length us, event | category | flops | bytes accessed | tf_op | source)
XLA Modules:
  0.0 46.7 jit_solution(14898885017395820630)
XLA Ops:
  0.6 1.3 %pack.1 = f32[128,1152]{1,0:T(8,128)S(1)} custom-call(s32[1]{0:T(128)} %bitcast.even_ref, f32[4,32,4,576]{3,2,1,0:T(4,128)} %tracer_hbm.5), custom_call_target="tpu_custom_call" | custom-call | bytes 600000 | tf_op jit(solution)/shard_map/pack/pallas_call | solution.py:382
  2.0 0.0 copy-start.14
  2.0 0.0 copy-start.15
  2.0 0.0 copy-start.17
  2.0 0.0 copy-start.18
  2.0 0.0 copy-start.13
  2.1 3.0 %collective-permute-start.1 = (f32[128,1152]{1,0:T(8,128)S(1)}, f32[128,1152]{1,0:T(8,128)S(1)}, u32[]{:S(2)}, u32[]{:S(2)}) collective-permute-start(f32[128,1152]{1,0:T(8,128)S(1)} %pack.1), channel_id=1, source_target_pairs={{0,2},{2,0},{4,6},{6,4},{8,10},{10,8},{12,14},{14,12},{1,3},{3,1},... | collective-permute-start | bytes 1769480 | tf_op jit(solution)/shard_map/ppermute | solution.py:392
  5.1 2.5 %rest.1 = (f32[64,1152]{1,0:T(8,128)}, f32[64,1152]{1,0:T(8,128)S(1)}, f32[16,1152]{1,0:T(8,128)S(1)}, f32[5,4,32,128]{3,2,1,0:T(8,128)S(1)}) custom-call(s32[1]{0:T(128)} %bitcast.even_ref, f32[4,32,4,576]{3,2,1,0:T(4,128)} %tracer_hbm.5, f32[32,4,576]{2,1,0:T(4,128)} %lat_hbm.3, f32[32,4,576]{2,1,0:T(4,128)} %lon_hbm.3), custom_call_target="tpu_custom_call" | custom-call | tf_op jit(solution)/shard_map/rest/pallas_call | solution.py:394
  7.6 0.7 %copy-done.12 = f32[64,1152]{1,0:T(8,128)} copy-done((f32[64,1152]{1,0:T(8,128)}, f32[64,1152]{1,0:T(8,128)S(1)}, u32[]{:S(2)}) %copy-start.12) | copy-done | bytes 294936
  8.3 1.4 %collective-permute-start.3 = (f32[16,1152]{1,0:T(8,128)S(1)}, f32[16,1152]{1,0:T(8,128)S(1)}, u32[]{:S(2)}, u32[]{:S(2)}) collective-permute-start(f32[16,1152]{1,0:T(8,128)S(1)} %get-tuple-element.52), channel_id=1, source_target_pairs={{2,0},{4,2},{6,4},{8,6},{10,8},{12,10},{14,12},{3,1},{5,3},{7,5},{... | collective-permute-start | bytes 221192 | tf_op jit(solution)/shard_map/ppermute | solution.py:409
  9.8 1.4 %collective-permute-start.4 = (f32[64,1152]{1,0:T(8,128)}, f32[64,1152]{1,0:T(8,128)}, u32[]{:S(2)}, u32[]{:S(2)}) collective-permute-start(f32[64,1152]{1,0:T(8,128)} %get-tuple-element.47), channel_id=1, source_target_pairs={{2,4},{4,2},{6,8},{8,6},{10,12},{12,10},{3,5},{5,3},{7,9},{9,7},{1... | collective-permute-start | bytes 884744 | tf_op jit(solution)/shard_map/ppermute | solution.py:408
  11.2 0.0 collective-permute-start
  11.2 0.1 select_multiply_fusion.refs_8_.refs_5_
  11.3 0.0 copy-done.18
  11.3 0.1 broadcast_in_dim.27
  11.4 0.1 reshape_reshape.3
  11.5 1.2 %collective-permute-done.side_ref = f32[5,4,32,128]{3,2,1,0:T(8,128)S(1)} collective-permute-done((f32[5,4,32,128]{3,2,1,0:T(8,128)S(1)}, f32[5,4,32,128]{3,2,1,0:T(8,128)S(1)}, u32[]{:S(2)}, u32[]{:S(2)}) %collective-permute-start) | collective-permute-done | bytes 327712 | tf_op jit(solution)/shard_map/ppermute | solution.py:411
  12.8 0.7 %copy-done.4 = f32[5,4,32,128]{3,2,1,0:T(8,128)} copy-done((f32[5,4,32,128]{3,2,1,0:T(8,128)}, f32[5,4,32,128]{3,2,1,0:T(8,128)S(1)}, u32[]{:S(2)}) %copy-start.4) | copy-done | bytes 327704
  13.5 1.0 %copy-done.5 = f32[5,4,32,128]{3,2,1,0:T(8,128)S(1)} copy-done((f32[5,4,32,128]{3,2,1,0:T(8,128)S(1)}, f32[5,4,32,128]{3,2,1,0:T(8,128)}, u32[]{:S(2)}) %copy-start.5) | copy-done | bytes 327704
  14.5 4.0 %base.1 = (f32[4,4,32,640]{3,2,1,0:T(8,128)S(1)}, f32[4,32,640]{2,1,0:T(8,128)S(1)}, f32[4,32,640]{2,1,0:T(8,128)S(1)}) custom-call(f32[1]{0:T(128)} %bitcast.2.not_pole_ref, f32[4,32,4,576]{3,2,1,0:T(4,128)} %tracer_hbm.5, f32[32,4,576]{2,1,0:T(4,128)} %lat_hbm.3, f32[32,4,576]{2,1,0:T(4,128)} %lon_hbm.3, f32[5,4,32,128]{3,2,1,0:T(8,128)S(1)} %copy-done.5), custom_call_target="tpu_custom_call" | custom-call | tf_op jit(solution)/shard_map/base/pallas_call | solution.py:413
  18.4 0.1 copy.23.refs_10_.refs_9_
  18.6 0.7 %collective-permute-start.2 = (f32[64,1152]{1,0:T(8,128)}, f32[64,1152]{1,0:T(8,128)S(1)}, u32[]{:S(2)}, u32[]{:S(2)}) collective-permute-start(f32[64,1152]{1,0:T(8,128)} %copy-done.12), channel_id=1, source_target_pairs={{2,4},{4,2},{6,8},{8,6},{10,12},{12,10},{3,5},{5,3},{7,9},{9,7},{1... | collective-permute-start | bytes 884744 | tf_op jit(solution)/shard_map/ppermute | solution.py:445
  19.2 0.7 %collective-permute-done.3.refs_6_.refs_5_ = f32[16,1152]{1,0:T(8,128)S(1)} collective-permute-done((f32[16,1152]{1,0:T(8,128)S(1)}, f32[16,1152]{1,0:T(8,128)S(1)}, u32[]{:S(2)}, u32[]{:S(2)}) %collective-permute-start.3) | collective-permute-done | bytes 73760 | tf_op jit(solution)/shard_map/ppermute | solution.py:409
  20.0 0.0 collective-permute-done.4.refs_5_
  20.0 5.6 %collective-permute-done.1.refs_4_.refs_3_ = f32[128,1152]{1,0:T(8,128)S(1)} collective-permute-done((f32[128,1152]{1,0:T(8,128)S(1)}, f32[128,1152]{1,0:T(8,128)S(1)}, u32[]{:S(2)}, u32[]{:S(2)}) %collective-permute-start.1) | collective-permute-done | bytes 589856 | tf_op jit(solution)/shard_map/ppermute | solution.py:392
  25.6 0.0 copy-start.2
  25.6 0.0 copy-start.3
  25.6 0.0 copy-start.9
  25.6 0.0 copy-start.10
  25.6 1.5 %physics.3 = (f32[4,32,640]{2,1,0:T(8,128)S(1)}, f32[4,32,640]{2,1,0:T(8,128)S(1)}, f32[4,8,640]{2,1,0:T(8,128)S(1)}) custom-call(s32[1]{0:T(128)} %bitcast.even_ref, s32[1]{0:T(128)S(6)} %sub.7.refs_0_.give_ref, s32[1]{0:T(128)} %bitcast.1.refs_1_.refs_0_.keep_ref, f32[4,4,32,640]{3,2,1,0:T(8,128)S(1)} %get-tuple-element.49.refs_2_.refs_1_, ...), custom_call_target="tpu_custom_call" | custom-call | tf_op jit(solution)/shard_map/physics/pallas_call | solution.py:456
  27.2 0.0 copy-start
  27.2 0.0 copy-start.1
  27.2 0.0 copy-start.7
  27.2 0.0 copy-start.8
  27.2 0.0 copy-start.11
  27.2 0.1 collective-permute-start.8
  27.3 0.5 %collective-permute-start.7 = (f32[1,32,640]{2,1,0:T(8,128)S(1)}, f32[1,32,640]{2,1,0:T(8,128)S(1)}, u32[]{:S(2)}, u32[]{:S(2)}) collective-permute-start(f32[1,32,640]{2,1,0:T(8,128)S(1)} %get-tuple-element.85), channel_id=1, source_target_pairs={{0,1},{1,0},{2,3},{3,2},{4,5},{5,4},{6,7},{7,6},{8,9},{9,8},{10,11... | collective-permute-start | bytes 245768 | tf_op jit(solution)/shard_map/ppermute | solution.py:499
  27.8 0.1 collective-permute-start.6
  27.9 0.4 collective-permute-start.5
  28.3 0.3 collective-permute-done.8.refs_3_
  28.6 0.2 collective-permute-done.7.refs_2_
  28.7 0.4 collective-permute-done.6.refs_1_
  29.1 0.2 collective-permute-done.5.refs_0_
  29.3 0.7 %forward.2 = (bf16[128,1152]{1,0:T(8,128)(2,1)S(1)}, bf16[128,1152]{1,0:T(8,128)(2,1)S(1)}) custom-call(f32[4,32,640]{2,1,0:T(8,128)S(1)} %get-tuple-element.58.own_ref, f32[1,32,640]{2,1,0:T(8,128)S(1)} %collective-permute-done.5.refs_0_, f32[1,32,640]{2,1,0:T(8,128)S(1)} %collective-permute-done.6.refs_1_, ...), custom_call_target="tpu_custom_call" | custom-call | tf_op jit(solution)/shard_map/forward/pallas_call | solution.py:472
  30.0 2.0 %inverse.2 = (f32[32,4,576]{2,1,0:T(4,128)S(1)}, f32[4,32,640]{2,1,0:T(8,128)}) custom-call(s32[4]{0:T(128)S(1)} %copy-done.11, f32[4,32,640]{2,1,0:T(8,128)S(1)} %get-tuple-element.58.own_ref, f32[1,32,640]{2,1,0:T(8,128)S(1)} %collective-permute-done.5.refs_0_, f32[1,32,640]{2,1,0:T(8,128)S(1)} %collective-permute-done.6.refs_1_, ...), custom_call_target="tpu_custom_call" | custom-call | tf_op jit(solution)/shard_map/inverse/pallas_call | solution.py:484
  32.0 0.0 collective-permute-done.2.refs_4_
  32.0 0.3 physics.4
  32.4 0.4 collective-permute-start.10
  32.8 0.5 %physics.5 = (f32[4,32,640]{2,1,0:T(8,128)S(1)}, f32[1,128]{1,0:T(1,128)S(1)}) custom-call(s32[1]{0:T(128)} %bitcast.even_ref, s32[1]{0:T(128)} %bitcast.1.refs_1_.refs_0_.keep_ref, f32[4,4,32,640]{3,2,1,0:T(8,128)S(1)} %get-tuple-element.49.refs_2_.refs_1_, f32[4,32,640]{2,1,0:T(8,128)S(1)} %get-tuple-element.50.refs_3_.refs_2_, ...), custom_call_target="tpu_custom_call" | custom-call | tf_op jit(solution)/shard_map/physics/pallas_call | solution.py:456
  33.3 2.5 %collective-permute-start.9 = (f32[1,128]{1,0:T(1,128)S(1)}, f32[1,128]{1,0:T(1,128)S(1)}, u32[]{:S(2)}, u32[]{:S(2)}) collective-permute-start(f32[1,128]{1,0:T(1,128)S(1)} %get-tuple-element.66), channel_id=1, source_target_pairs={{0,2},{2,0},{4,6},{6,4},{8,10},{10,8},{12,14},{14,12},{1,3},{3,1},... | collective-permute-start | bytes 1544 | tf_op jit(solution)/shard_map/ppermute | solution.py:510
  35.8 0.0 collective-permute-done.10.refs_0_
  35.8 0.7 %forward.3 = (bf16[128,1152]{1,0:T(8,128)(2,1)S(1)}, bf16[128,1152]{1,0:T(8,128)(2,1)S(1)}) custom-call(f32[4,32,640]{2,1,0:T(8,128)S(1)} %get-tuple-element.67.own_ref, f32[4,32,640]{2,1,0:T(8,128)S(1)} %collective-permute-done.10.refs_0_, bf16[1024,256]{1,0:T(8,128)(2,1)S(1)} %copy-done.3, bf16[1024,256]{1,0:T(8,128)(2,1)S(1)} %copy-done.2, ...), custom_call_target="tpu_custom_call" | custom-call | tf_op jit(solution)/shard_map/forward/pallas_call | solution.py:472
  36.5 0.8 %collective-permute-done.9 = f32[1,128]{1,0:T(1,128)S(1)} collective-permute-done((f32[1,128]{1,0:T(1,128)S(1)}, f32[1,128]{1,0:T(1,128)S(1)}, u32[]{:S(2)}, u32[]{:S(2)}) %collective-permute-start.9) | collective-permute-done | bytes 544 | tf_op jit(solution)/shard_map/ppermute | solution.py:510
  37.3 2.5 %collective-permute-start.11 = (f32[1,128]{1,0:T(1,128)S(1)}, f32[1,128]{1,0:T(1,128)S(1)}, u32[]{:S(2)}, u32[]{:S(2)}) collective-permute-start(f32[1,128]{1,0:T(1,128)S(1)} %add.49), channel_id=1, source_target_pairs={{0,4},{2,6},{4,0},{6,2},{8,12},{10,14},{12,8},{14,10},{1,5},{3,7},... | collective-permute-start | bytes 1544 | tf_op jit(solution)/shard_map/ppermute | solution.py:510
  39.8 0.0 collective-permute-start.13
  39.8 1.3 %inverse.3 = (f32[32,4,576]{2,1,0:T(4,128)S(1)}, f32[4,32,640]{2,1,0:T(8,128)S(1)}) custom-call(s32[4]{0:T(128)S(1)} %copy-done.11, f32[4,32,640]{2,1,0:T(8,128)S(1)} %get-tuple-element.67.own_ref, f32[4,32,640]{2,1,0:T(8,128)S(1)} %collective-permute-done.10.refs_0_, bf16[128,1152]{1,0:T(8,128)(2,1)S(1)} %get-tuple-element.73.refs_1_, ...), custom_call_target="tpu_custom_call" | custom-call | tf_op jit(solution)/shard_map/inverse/pallas_call | solution.py:484
  41.1 0.3 collective-permute-done.11
  41.3 0.3 collective-permute-start.14
  41.7 2.7 %collective-permute-start.12 = (f32[1,128]{1,0:T(1,128)S(1)}, f32[1,128]{1,0:T(1,128)S(1)}, u32[]{:S(2)}, u32[]{:S(2)}) collective-permute-start(f32[1,128]{1,0:T(1,128)S(1)} %add.50), channel_id=1, source_target_pairs={{0,8},{2,10},{4,12},{6,14},{8,0},{10,2},{12,4},{14,6},{1,9},{3,11}... | collective-permute-start | bytes 1544 | tf_op jit(solution)/shard_map/ppermute | solution.py:510
  44.4 0.0 collective-permute-done.13.refs_2_
  44.4 0.0 collective-permute-done.14.refs_3_
  44.4 1.2 %finish.1 = f32[4,32,4,576]{3,2,1,0:T(4,128)} custom-call(s32[1]{0:T(128)} %bitcast.1.refs_1_.refs_0_.keep_ref, s32[1]{0:T(128)S(6)} %sub.7.refs_0_.give_ref, f32[32,4,576]{2,1,0:T(4,128)S(1)} %get-tuple-element.79.refs_0_, f32[32,4,576]{2,1,0:T(4,128)S(1)} %get-tuple-element.80.refs_1_, f32[4,32,640]{2,1,0:T(8,128)S(1)} %collective-permute-done.13.refs_2_, ...), custom_call_target="tpu_custom_call" | custom-call | bytes 3000000 | tf_op jit(solution)/shard_map/finish/pallas_call | solution.py:531
  45.6 0.5 %collective-permute-done.12 = f32[1,128]{1,0:T(1,128)S(1)} collective-permute-done((f32[1,128]{1,0:T(1,128)S(1)}, f32[1,128]{1,0:T(1,128)S(1)}, u32[]{:S(2)}, u32[]{:S(2)}) %collective-permute-start.12) | collective-permute-done | bytes 544 | tf_op jit(solution)/shard_map/ppermute | solution.py:510
  46.1 0.6 %fusion.1 = f32[1,1]{1,0:T(1,128)} fusion(f32[1,128]{1,0:T(1,128)S(1)} %add.51, s32[]{:T(128)S(6)} %select_n.16), kind=kLoop, calls=%fused_computation.4 | loop fusion | flops 1 | bytes 12 | tf_op jit(solution)/shard_map/div | solution.py:549
  (28 shorter events, 0.1 us)
Async XLA Ops:
  2.0 9.2 %copy-start.14 = (f32[1152]{0:T(1024)S(1)}, f32[1152]{0:T(1024)}, u32[]{:S(2)}) copy-start(f32[1152]{0:T(1024)} %constant.73.clone) | copy-start | bytes 13828
  2.0 9.2 %copy-start.15 = (f32[1152]{0:T(1024)S(1)}, f32[1152]{0:T(1024)}, u32[]{:S(2)}) copy-start(f32[1152]{0:T(1024)} %constant.71.clone) | copy-start | bytes 13828
  2.0 9.2 %copy-start.17 = (pred[1152]{0:T(1024)(128)(4,1)S(1)}, pred[1152]{0:T(1024)(128)(4,1)}, u32[]{:S(2)}) copy-start(pred[1152]{0:T(1024)(128)(4,1)} %constant.72.clone) | copy-start | bytes 3460
  2.0 9.3 %copy-start.18 = (s32[1,1,18,1]{2,3,1,0:T(1,128)S(1)}, s32[1,1,18,1]{2,3,1,0:T(1,128)}, u32[]{:S(2)}) copy-start(s32[1,1,18,1]{2,3,1,0:T(1,128)} %param.25) | copy-start | bytes 220
  2.0 9.5 %copy-start.13 = (f32[4,4,576]{2,1,0:T(4,128)S(1)}, f32[4,4,576]{2,1,0:T(4,128)}, u32[]{:S(2)}) copy-start(f32[4,4,576]{2,1,0:T(4,128)} %param.22) | copy-start | bytes 110596
  2.1 23.5 %collective-permute-start.1 = (f32[128,1152]{1,0:T(8,128)S(1)}, f32[128,1152]{1,0:T(8,128)S(1)}, u32[]{:S(2)}, u32[]{:S(2)}) collective-permute-start(f32[128,1152]{1,0:T(8,128)S(1)} %pack.1), channel_id=1, source_target_pairs={{0,2},{2,0},{4,6},{6,4},{8,10},{10,8},{12,14},{14,12},{1,3},{3,1},... | collective-permute-start | bytes 1769480 | tf_op jit(solution)/shard_map/ppermute | solution.py:392
  7.6 0.7 %copy-start.12 = (f32[64,1152]{1,0:T(8,128)}, f32[64,1152]{1,0:T(8,128)S(1)}, u32[]{:S(2)}) copy-start(f32[64,1152]{1,0:T(8,128)S(1)} %get-tuple-element.51) | copy-start | bytes 884740
  8.3 10.1 %copy-start.16 = (f32[4,32]{1,0:T(4,128)S(1)}, f32[4,32]{1,0:T(4,128)}, u32[]{:S(2)}) copy-start(f32[4,32]{1,0:T(4,128)} %param.24) | copy-start | bytes 1540
  8.3 11.6 %collective-permute-start.3 = (f32[16,1152]{1,0:T(8,128)S(1)}, f32[16,1152]{1,0:T(8,128)S(1)}, u32[]{:S(2)}, u32[]{:S(2)}) collective-permute-start(f32[16,1152]{1,0:T(8,128)S(1)} %get-tuple-element.52), channel_id=1, source_target_pairs={{2,0},{4,2},{6,4},{8,6},{10,8},{12,10},{14,12},{3,1},{5,3},{7,5},{... | collective-permute-start | bytes 221192 | tf_op jit(solution)/shard_map/ppermute | solution.py:409
  9.8 10.2 %collective-permute-start.4 = (f32[64,1152]{1,0:T(8,128)}, f32[64,1152]{1,0:T(8,128)}, u32[]{:S(2)}, u32[]{:S(2)}) collective-permute-start(f32[64,1152]{1,0:T(8,128)} %get-tuple-element.47), channel_id=1, source_target_pairs={{2,4},{4,2},{6,8},{8,6},{10,12},{12,10},{3,5},{5,3},{7,9},{9,7},{1... | collective-permute-start | bytes 884744 | tf_op jit(solution)/shard_map/ppermute | solution.py:408
  11.2 1.6 %collective-permute-start = (f32[5,4,32,128]{3,2,1,0:T(8,128)S(1)}, f32[5,4,32,128]{3,2,1,0:T(8,128)S(1)}, u32[]{:S(2)}, u32[]{:S(2)}) collective-permute-start(f32[5,4,32,128]{3,2,1,0:T(8,128)S(1)} %get-tuple-element.44), channel_id=1, source_target_pairs={{0,1},{1,0},{2,3},{3,2},{4,5},{5,4},{6,7},{7,6},{8,9},{9,8},{10,11... | collective-permute-start | bytes 983048 | tf_op jit(solution)/shard_map/ppermute | solution.py:411
  11.3 14.2 %copy-start.6 = (f32[32,32]{1,0:T(8,128)S(1)}, f32[32,32]{1,0:T(8,128)}, u32[]{:S(2)}) copy-start(f32[32,32]{1,0:T(8,128)} %refs_8_.4) | copy-start | bytes 12292
  12.8 0.7 %copy-start.4 = (f32[5,4,32,128]{3,2,1,0:T(8,128)}, f32[5,4,32,128]{3,2,1,0:T(8,128)S(1)}, u32[]{:S(2)}) copy-start(f32[5,4,32,128]{3,2,1,0:T(8,128)S(1)} %collective-permute-done.side_ref) | copy-start | bytes 983044
  13.5 1.0 %copy-start.5 = (f32[5,4,32,128]{3,2,1,0:T(8,128)S(1)}, f32[5,4,32,128]{3,2,1,0:T(8,128)}, u32[]{:S(2)}) copy-start(f32[5,4,32,128]{3,2,1,0:T(8,128)} %copy-done.4) | copy-start | bytes 983044
  18.6 13.5 %collective-permute-start.2 = (f32[64,1152]{1,0:T(8,128)}, f32[64,1152]{1,0:T(8,128)S(1)}, u32[]{:S(2)}, u32[]{:S(2)}) collective-permute-start(f32[64,1152]{1,0:T(8,128)} %copy-done.12), channel_id=1, source_target_pairs={{2,4},{4,2},{6,8},{8,6},{10,12},{12,10},{3,5},{5,3},{7,9},{9,7},{1... | collective-permute-start | bytes 884744 | tf_op jit(solution)/shard_map/ppermute | solution.py:445
  25.6 3.7 %copy-start.2 = (bf16[1024,256]{1,0:T(8,128)(2,1)S(1)}, bf16[1024,256]{1,0:T(8,128)(2,1)}, u32[]{:S(2)}) copy-start(bf16[1024,256]{1,0:T(8,128)(2,1)} %constant.75.clone.refs_5_.refs_2_) | copy-start | bytes 1572868
  25.6 3.7 %copy-start.3 = (bf16[1024,256]{1,0:T(8,128)(2,1)S(1)}, bf16[1024,256]{1,0:T(8,128)(2,1)}, u32[]{:S(2)}) copy-start(bf16[1024,256]{1,0:T(8,128)(2,1)} %constant.74.clone.refs_4_.refs_1_) | copy-start | bytes 1572868
  25.6 3.7 %copy-start.9 = (bf16[128,128]{1,0:T(8,128)(2,1)S(1)}, bf16[128,128]{1,0:T(8,128)(2,1)}, u32[]{:S(2)}) copy-start(bf16[128,128]{1,0:T(8,128)(2,1)} %constant.77.clone.refs_7_.refs_4_) | copy-start | bytes 98308
  25.6 3.7 %copy-start.10 = (bf16[128,128]{1,0:T(8,128)(2,1)S(1)}, bf16[128,128]{1,0:T(8,128)(2,1)}, u32[]{:S(2)}) copy-start(bf16[128,128]{1,0:T(8,128)(2,1)} %constant.76.clone.refs_6_.refs_3_) | copy-start | bytes 98308
  27.2 2.8 %copy-start = (bf16[1024,256]{1,0:T(8,128)(2,1)S(1)}, bf16[1024,256]{1,0:T(8,128)(2,1)}, u32[]{:S(2)}) copy-start(bf16[1024,256]{1,0:T(8,128)(2,1)} %constant.79.clone.refs_7_.refs_4_) | copy-start | bytes 1572868
  27.2 2.8 %copy-start.1 = (bf16[1024,256]{1,0:T(8,128)(2,1)S(1)}, bf16[1024,256]{1,0:T(8,128)(2,1)}, u32[]{:S(2)}) copy-start(bf16[1024,256]{1,0:T(8,128)(2,1)} %constant.78.clone.refs_6_.refs_3_) | copy-start | bytes 1572868
  27.2 2.8 %copy-start.7 = (bf16[128,128]{1,0:T(8,128)(2,1)S(1)}, bf16[128,128]{1,0:T(8,128)(2,1)}, u32[]{:S(2)}) copy-start(bf16[128,128]{1,0:T(8,128)(2,1)} %constant.81.clone.refs_9_.refs_6_) | copy-start | bytes 98308
  27.2 2.8 %copy-start.8 = (bf16[128,128]{1,0:T(8,128)(2,1)S(1)}, bf16[128,128]{1,0:T(8,128)(2,1)}, u32[]{:S(2)}) copy-start(bf16[128,128]{1,0:T(8,128)(2,1)} %constant.80.clone.refs_8_.refs_5_) | copy-start | bytes 98308
  27.2 2.8 %copy-start.11 = (s32[4]{0:T(128)S(1)}, s32[4]{0:T(128)}, u32[]{:S(2)}) copy-start(s32[4]{0:T(128)} %mask_ref.3) | copy-start | bytes 52
  27.2 1.3 %collective-permute-start.8 = (f32[1,32,640]{2,1,0:T(8,128)S(1)}, f32[1,32,640]{2,1,0:T(8,128)S(1)}, u32[]{:S(2)}, u32[]{:S(2)}) collective-permute-start(f32[1,32,640]{2,1,0:T(8,128)S(1)} %get-tuple-element.84), channel_id=1, source_target_pairs={{0,1},{1,0},{2,3},{3,2},{4,5},{5,4},{6,7},{7,6},{8,9},{9,8},{10,11... | collective-permute-start | bytes 245768 | tf_op jit(solution)/shard_map/ppermute | solution.py:499
  27.3 1.4 %collective-permute-start.7 = (f32[1,32,640]{2,1,0:T(8,128)S(1)}, f32[1,32,640]{2,1,0:T(8,128)S(1)}, u32[]{:S(2)}, u32[]{:S(2)}) collective-permute-start(f32[1,32,640]{2,1,0:T(8,128)S(1)} %get-tuple-element.85), channel_id=1, source_target_pairs={{0,1},{1,0},{2,3},{3,2},{4,5},{5,4},{6,7},{7,6},{8,9},{9,8},{10,11... | collective-permute-start | bytes 245768 | tf_op jit(solution)/shard_map/ppermute | solution.py:499
  27.8 1.3 %collective-permute-start.6 = (f32[1,32,640]{2,1,0:T(8,128)S(1)}, f32[1,32,640]{2,1,0:T(8,128)S(1)}, u32[]{:S(2)}, u32[]{:S(2)}) collective-permute-start(f32[1,32,640]{2,1,0:T(8,128)S(1)} %get-tuple-element.86), channel_id=1, source_target_pairs={{0,1},{1,0},{2,3},{3,2},{4,5},{5,4},{6,7},{7,6},{8,9},{9,8},{10,11... | collective-permute-start | bytes 245768 | tf_op jit(solution)/shard_map/ppermute | solution.py:499
  27.9 1.4 %collective-permute-start.5 = (f32[1,32,640]{2,1,0:T(8,128)S(1)}, f32[1,32,640]{2,1,0:T(8,128)S(1)}, u32[]{:S(2)}, u32[]{:S(2)}) collective-permute-start(f32[1,32,640]{2,1,0:T(8,128)S(1)} %get-tuple-element.87), channel_id=1, source_target_pairs={{0,1},{1,0},{2,3},{3,2},{4,5},{5,4},{6,7},{7,6},{8,9},{9,8},{10,11... | collective-permute-start | bytes 245768 | tf_op jit(solution)/shard_map/ppermute | solution.py:499
  32.4 3.5 %collective-permute-start.10 = (f32[4,32,640]{2,1,0:T(8,128)S(1)}, f32[4,32,640]{2,1,0:T(8,128)S(1)}, u32[]{:S(2)}, u32[]{:S(2)}) collective-permute-start(f32[4,32,640]{2,1,0:T(8,128)S(1)} %get-tuple-element.68), channel_id=1, source_target_pairs={{0,1},{1,0},{2,3},{3,2},{4,5},{5,4},{6,7},{7,6},{8,9},{9,8},{10,11... | collective-permute-start | bytes 983048 | tf_op jit(solution)/shard_map/ppermute | solution.py:513
  33.3 4.0 %collective-permute-start.9 = (f32[1,128]{1,0:T(1,128)S(1)}, f32[1,128]{1,0:T(1,128)S(1)}, u32[]{:S(2)}, u32[]{:S(2)}) collective-permute-start(f32[1,128]{1,0:T(1,128)S(1)} %get-tuple-element.66), channel_id=1, source_target_pairs={{0,2},{2,0},{4,6},{6,4},{8,10},{10,8},{12,14},{14,12},{1,3},{3,1},... | collective-permute-start | bytes 1544 | tf_op jit(solution)/shard_map/ppermute | solution.py:510
  37.3 4.0 %collective-permute-start.11 = (f32[1,128]{1,0:T(1,128)S(1)}, f32[1,128]{1,0:T(1,128)S(1)}, u32[]{:S(2)}, u32[]{:S(2)}) collective-permute-start(f32[1,128]{1,0:T(1,128)S(1)} %add.49), channel_id=1, source_target_pairs={{0,4},{2,6},{4,0},{6,2},{8,12},{10,14},{12,8},{14,10},{1,5},{3,7},... | collective-permute-start | bytes 1544 | tf_op jit(solution)/shard_map/ppermute | solution.py:510
  39.8 4.6 %collective-permute-start.13 = (f32[4,32,640]{2,1,0:T(8,128)}, f32[4,32,640]{2,1,0:T(8,128)S(1)}, u32[]{:S(2)}, u32[]{:S(2)}) collective-permute-start(f32[4,32,640]{2,1,0:T(8,128)} %get-tuple-element.63), channel_id=1, source_target_pairs={{0,1},{1,0},{2,3},{3,2},{4,5},{5,4},{6,7},{7,6},{8,9},{9,8},{10,11... | collective-permute-start | bytes 983048 | tf_op jit(solution)/shard_map/ppermute | solution.py:503
  41.3 3.0 %collective-permute-start.14 = (f32[4,32,640]{2,1,0:T(8,128)S(1)}, f32[4,32,640]{2,1,0:T(8,128)S(1)}, u32[]{:S(2)}, u32[]{:S(2)}) collective-permute-start(f32[4,32,640]{2,1,0:T(8,128)S(1)} %get-tuple-element.81), channel_id=1, source_target_pairs={{0,1},{1,0},{2,3},{3,2},{4,5},{5,4},{6,7},{7,6},{8,9},{9,8},{10,11... | collective-permute-start | bytes 983048 | tf_op jit(solution)/shard_map/ppermute | solution.py:528
  41.7 4.4 %collective-permute-start.12 = (f32[1,128]{1,0:T(1,128)S(1)}, f32[1,128]{1,0:T(1,128)S(1)}, u32[]{:S(2)}, u32[]{:S(2)}) collective-permute-start(f32[1,128]{1,0:T(1,128)S(1)} %add.50), channel_id=1, source_target_pairs={{0,8},{2,10},{4,12},{6,14},{8,0},{10,2},{12,4},{14,6},{1,9},{3,11}... | collective-permute-start | bytes 1544 | tf_op jit(solution)/shard_map/ppermute | solution.py:510

commit v6 on v5

--- a/solution.py
+++ b/solution.py
@@ -216,16 +216,6 @@
         total = jnp.sum(jnp.sum(chosen, axis=0, keepdims=True), axis=1, keepdims=True)
         result = jnp.where(spot == owner, total, result)
     energy_ref[...] = result
-
-
-def send_result(result_ref, out_hbm, tracer, sems):
-    piece = result_ref.shape[0] // PIECES
-    copies = []
-    for part in range(PIECES):
-        span = pl.ds(piece * part, piece)
-        copies.append(pltpu.make_async_copy(result_ref.at[span], out_hbm.at[tracer, span], sems.at[part]))
-        copies[-1].start()
-    return copies
 
 
 def waves_of(radix):
@@ -509,9 +499,8 @@
         distance = distances.pop(0)
         return lax.ppermute(energy, "lat", [(i, i ^ distance) for i in range(lat_count)])
 
-    (given,), energy = run_physics(half - 1, [give], energy)
+    (given, own), energy = run_physics(half - 1, [give, keep], energy, True)
     other = [lax.ppermute(given, "lon", swap)]
-    (own,), energy = run_physics(half - 1, [keep], energy, True)
 
     coming = send_energy(energy)
     high, low = run_forward(own, other)

time: 47 us -> 52.2 us (1.11)
  waiting for transfers between devices: 10.1 us -> 15.5 us
  local copies, waits for them, and re-layouts: 2.82 us -> 2.11 us
  starting transfers between devices: 16 us -> 16.7 us
    ppermute x3, waiting for transfers between devices: 1.61 us -> 4.71 us  [send_energy(): lax.ppermute(energy, 'lat', [(i, i ^ distance) for i in range(lat_count)])]
    ppermute x2, waiting for transfers between devices: 0.01 us -> 1.61 us  [on_device(): received.append(lax.ppermute(back, 'lon', swap))]
    ppermute x3, starting transfers between devices: 7.67 us -> 8.74 us  [send_energy(): lax.ppermute(energy, 'lat', [(i, i ^ distance) for i in range(lat_count)])]
    unnamed x38, local copies, waits for them, and re-layouts: 2.51 us -> 1.8 us
    ppermute x1, waiting for transfers between devices: 0.73 us -> 1.37 us  [on_device(): top = lax.ppermute(courant_row, 'lat', downward)]
    pallas_call x3 -> x2, Pallas kernels: 2.39 us -> 2.2 us  [run_physics(): pl.pallas_call(functools.partial(physics_kernel, levels, sector, lat_coun...]
  transfers between devices with their start and end apart: 15 -> 15, of which waited for: 10 -> 11; matrix products, arithmetic and copies ran while one was open for 1% -> 1% of each run, Pallas kernels for 31% -> 27%
where the time goes in v6:
time: 52.2 us; the launch traced here: 52 us
  starting transfers between devices  16.7 us (32%)
  Pallas kernels  15.9 us (30%)
  waiting for transfers between devices  15.5 us (30%)
  local copies, waits for them, and re-layouts  2.11 us (4%)
  between operations  1.02 us (2%)
  other arithmetic  0.72 us (1%)
    ppermute x3, starting transfers between devices, send_energy(): lax.ppermute(energy, 'lat', [(i, i ^ distance) for i in range(lat_count)])  8.74 us
    ppermute x1, waiting for transfers between devices, on_device(): from_inside = lax.ppermute(inner, 'lat', inside)  5.65 us
    ppermute x3, waiting for transfers between devices, send_energy(): lax.ppermute(energy, 'lat', [(i, i ^ distance) for i in range(lat_count)])  4.71 us
    pallas_call x1, Pallas kernels, on_device(): pl.pallas_call(functools.partial(base_kernel, width), in_specs=[scalars,...  3.98 us
    pallas_call x2, Pallas kernels, run_inverse(): pl.pallas_call(functools.partial(inverse_kernel, radix, len(other)), in_s...  3.24 us
    ppermute x1, starting transfers between devices, on_device(): from_inside = lax.ppermute(inner, 'lat', inside)  3 us
    pallas_call x1, Pallas kernels, on_device(): pl.pallas_call(rest_kernel, in_specs=[scalars] + [in_hbm] * 3, out_specs=...  2.55 us
    pallas_call x2, Pallas kernels, run_physics(): pl.pallas_call(functools.partial(physics_kernel, levels, sector, lat_coun...  2.2 us
  transfers between devices with their start and end apart: 15, of which 11 were waited for; matrix products, arithmetic and copies ran while one was open for 1% of the time, Pallas kernels for 27%

profile of v6, /device:TPU:0, one launch (start us, length us, event | category | flops | bytes accessed | tf_op | source)
XLA Modules:
  0.0 52.0 jit_solution(8866959804986916890)
XLA Ops:
  0.6 1.3 %pack.1 = f32[128,1152]{1,0:T(8,128)S(1)} custom-call(s32[1]{0:T(128)} %bitcast.even_ref, f32[4,32,4,576]{3,2,1,0:T(4,128)} %tracer_hbm.5), custom_call_target="tpu_custom_call" | custom-call | bytes 600000 | tf_op jit(solution)/shard_map/pack/pallas_call | solution.py:372
  2.0 0.0 copy-start.14
  2.0 0.0 copy-start.15
  2.0 0.0 copy-start.17
  2.0 0.0 copy-start.18
  2.0 0.0 copy-start.13
  2.1 3.0 %collective-permute-start.1 = (f32[128,1152]{1,0:T(8,128)S(1)}, f32[128,1152]{1,0:T(8,128)S(1)}, u32[]{:S(2)}, u32[]{:S(2)}) collective-permute-start(f32[128,1152]{1,0:T(8,128)S(1)} %pack.1), channel_id=1, source_target_pairs={{0,2},{2,0},{4,6},{6,4},{8,10},{10,8},{12,14},{14,12},{1,3},{3,1},... | collective-permute-start | bytes 1769480 | tf_op jit(solution)/shard_map/ppermute | solution.py:382
  5.1 2.5 %rest.1 = (f32[64,1152]{1,0:T(8,128)}, f32[64,1152]{1,0:T(8,128)S(1)}, f32[16,1152]{1,0:T(8,128)S(1)}, f32[5,4,32,128]{3,2,1,0:T(8,128)S(1)}) custom-call(s32[1]{0:T(128)} %bitcast.even_ref, f32[4,32,4,576]{3,2,1,0:T(4,128)} %tracer_hbm.5, f32[32,4,576]{2,1,0:T(4,128)} %lat_hbm.3, f32[32,4,576]{2,1,0:T(4,128)} %lon_hbm.3), custom_call_target="tpu_custom_call" | custom-call | tf_op jit(solution)/shard_map/rest/pallas_call | solution.py:384
  7.6 0.0 copy-start.12
  7.6 0.0 copy-start.16
  7.6 1.4 %collective-permute-start.3 = (f32[16,1152]{1,0:T(8,128)S(1)}, f32[16,1152]{1,0:T(8,128)S(1)}, u32[]{:S(2)}, u32[]{:S(2)}) collective-permute-start(f32[16,1152]{1,0:T(8,128)S(1)} %get-tuple-element.51), channel_id=1, source_target_pairs={{2,0},{4,2},{6,4},{8,6},{10,8},{12,10},{14,12},{3,1},{5,3},{7,5},{... | collective-permute-start | bytes 221192 | tf_op jit(solution)/shard_map/ppermute | solution.py:399
  9.1 1.4 %collective-permute-start.4 = (f32[64,1152]{1,0:T(8,128)}, f32[64,1152]{1,0:T(8,128)}, u32[]{:S(2)}, u32[]{:S(2)}) collective-permute-start(f32[64,1152]{1,0:T(8,128)} %get-tuple-element.46), channel_id=1, source_target_pairs={{2,4},{4,2},{6,8},{8,6},{10,12},{12,10},{3,5},{5,3},{7,9},{9,7},{1... | collective-permute-start | bytes 884744 | tf_op jit(solution)/shard_map/ppermute | solution.py:398
  10.5 0.0 copy-done.12
  10.5 0.0 collective-permute-start
  10.6 0.1 select_multiply_fusion.refs_8_.refs_5_
  10.7 0.1 broadcast_in_dim.27
  10.7 0.1 reshape_reshape.3
  10.9 1.2 %collective-permute-done.side_ref = f32[5,4,32,128]{3,2,1,0:T(8,128)S(1)} collective-permute-done((f32[5,4,32,128]{3,2,1,0:T(8,128)S(1)}, f32[5,4,32,128]{3,2,1,0:T(8,128)S(1)}, u32[]{:S(2)}, u32[]{:S(2)}) %collective-permute-start) | collective-permute-done | bytes 327712 | tf_op jit(solution)/shard_map/ppermute | solution.py:401
  12.1 0.7 %copy-done.4 = f32[5,4,32,128]{3,2,1,0:T(8,128)} copy-done((f32[5,4,32,128]{3,2,1,0:T(8,128)}, f32[5,4,32,128]{3,2,1,0:T(8,128)S(1)}, u32[]{:S(2)}) %copy-start.4) | copy-done | bytes 327704
  12.8 1.0 %copy-done.5 = f32[5,4,32,128]{3,2,1,0:T(8,128)S(1)} copy-done((f32[5,4,32,128]{3,2,1,0:T(8,128)S(1)}, f32[5,4,32,128]{3,2,1,0:T(8,128)}, u32[]{:S(2)}) %copy-start.5) | copy-done | bytes 327704
  13.8 4.0 %base.1 = (f32[4,4,32,640]{3,2,1,0:T(8,128)S(1)}, f32[4,32,640]{2,1,0:T(8,128)S(1)}, f32[4,32,640]{2,1,0:T(8,128)S(1)}) custom-call(f32[1]{0:T(128)} %bitcast.2.not_pole_ref, f32[4,32,4,576]{3,2,1,0:T(4,128)} %tracer_hbm.5, f32[32,4,576]{2,1,0:T(4,128)} %lat_hbm.3, f32[32,4,576]{2,1,0:T(4,128)} %lon_hbm.3, f32[5,4,32,128]{3,2,1,0:T(8,128)S(1)} %copy-done.5), custom_call_target="tpu_custom_call" | custom-call | tf_op jit(solution)/shard_map/base/pallas_call | solution.py:403
  17.8 0.1 copy.22.refs_10_
  17.9 0.7 %collective-permute-start.2 = (f32[64,1152]{1,0:T(8,128)}, f32[64,1152]{1,0:T(8,128)S(1)}, u32[]{:S(2)}, u32[]{:S(2)}) collective-permute-start(f32[64,1152]{1,0:T(8,128)} %copy-done.12), channel_id=1, source_target_pairs={{2,4},{4,2},{6,8},{8,6},{10,12},{12,10},{3,5},{5,3},{7,9},{9,7},{1... | collective-permute-start | bytes 884744 | tf_op jit(solution)/shard_map/ppermute | solution.py:435
  18.6 1.4 %collective-permute-done.3.refs_6_ = f32[16,1152]{1,0:T(8,128)S(1)} collective-permute-done((f32[16,1152]{1,0:T(8,128)S(1)}, f32[16,1152]{1,0:T(8,128)S(1)}, u32[]{:S(2)}, u32[]{:S(2)}) %collective-permute-start.3) | collective-permute-done | bytes 73760 | tf_op jit(solution)/shard_map/ppermute | solution.py:399
  20.0 0.0 collective-permute-done.4.refs_5_
  20.0 5.6 %collective-permute-done.1.refs_4_ = f32[128,1152]{1,0:T(8,128)S(1)} collective-permute-done((f32[128,1152]{1,0:T(8,128)S(1)}, f32[128,1152]{1,0:T(8,128)S(1)}, u32[]{:S(2)}, u32[]{:S(2)}) %collective-permute-start.1) | collective-permute-done | bytes 589856 | tf_op jit(solution)/shard_map/ppermute | solution.py:382
  25.6 0.0 copy-start.2
  25.6 0.0 copy-start.3
  25.7 0.0 copy-start.8
  25.7 0.0 copy-start.9
  25.7 1.5 %physics.2 = (f32[4,32,640]{2,1,0:T(8,128)S(1)}, f32[4,32,640]{2,1,0:T(8,128)S(1)}, f32[4,8,640]{2,1,0:T(8,128)S(1)}) custom-call(s32[1]{0:T(128)} %bitcast.even_ref, s32[1]{0:T(128)S(6)} %sub.7.refs_0_.give_ref, s32[1]{0:T(128)} %bitcast.1.refs_1_.keep_ref, f32[4,4,32,640]{3,2,1,0:T(8,128)S(1)} %get-tuple-element.48.refs_2_, ...), custom_call_target="tpu_custom_call" | custom-call | tf_op jit(solution)/shard_map/physics/pallas_call | solution.py:446
  27.2 0.0 copy-start
  27.2 0.0 copy-start.1
  27.2 0.0 copy-start.6
  27.3 0.0 copy-start.7
  27.3 0.0 copy-start.11
  27.3 0.1 collective-permute-start.8
  27.4 0.5 collective-permute-start.7
  27.9 0.1 collective-permute-start.6
  28.0 0.4 collective-permute-start.5
  28.4 0.3 collective-permute-done.8.refs_3_
  28.7 0.2 collective-permute-done.7.refs_2_
  28.8 0.4 collective-permute-done.6.refs_1_
  29.2 0.2 collective-permute-done.5.refs_0_
  29.3 0.7 %forward.2 = (bf16[128,1152]{1,0:T(8,128)(2,1)S(1)}, bf16[128,1152]{1,0:T(8,128)(2,1)S(1)}) custom-call(f32[4,32,640]{2,1,0:T(8,128)S(1)} %get-tuple-element.57.own_ref, f32[1,32,640]{2,1,0:T(8,128)S(1)} %collective-permute-done.5.refs_0_, f32[1,32,640]{2,1,0:T(8,128)S(1)} %collective-permute-done.6.refs_1_, ...), custom_call_target="tpu_custom_call" | custom-call | tf_op jit(solution)/shard_map/forward/pallas_call | solution.py:462
  30.1 2.0 %inverse.2 = (f32[32,4,576]{2,1,0:T(4,128)S(1)}, f32[4,32,640]{2,1,0:T(8,128)}) custom-call(s32[4]{0:T(128)S(1)} %copy-done.11, f32[4,32,640]{2,1,0:T(8,128)S(1)} %get-tuple-element.57.own_ref, f32[1,32,640]{2,1,0:T(8,128)S(1)} %collective-permute-done.5.refs_0_, f32[1,32,640]{2,1,0:T(8,128)S(1)} %collective-permute-done.6.refs_1_, ...), custom_call_target="tpu_custom_call" | custom-call | tf_op jit(solution)/shard_map/inverse/pallas_call | solution.py:474
  32.1 0.0 collective-permute-done.2.refs_5_
  32.1 0.7 %physics.3 = (f32[4,32,640]{2,1,0:T(8,128)S(1)}, f32[4,32,640]{2,1,0:T(8,128)S(1)}, f32[1,128]{1,0:T(1,128)S(1)}) custom-call(s32[1]{0:T(128)} %bitcast.even_ref, s32[1]{0:T(128)S(6)} %sub.7.refs_0_.give_ref, s32[1]{0:T(128)} %bitcast.1.refs_1_.keep_ref, f32[4,4,32,640]{3,2,1,0:T(8,128)S(1)} %get-tuple-element.48.refs_2_, ...), custom_call_target="tpu_custom_call" | custom-call | tf_op jit(solution)/shard_map/physics/pallas_call | solution.py:446
  32.7 0.4 collective-permute-start.10
  33.1 8.7 %collective-permute-start.9 = (f32[1,128]{1,0:T(1,128)S(1)}, f32[1,128]{1,0:T(1,128)S(1)}, u32[]{:S(2)}, u32[]{:S(2)}) collective-permute-start(f32[1,128]{1,0:T(1,128)S(1)} %get-tuple-element.64), channel_id=1, source_target_pairs={{0,2},{2,0},{4,6},{6,4},{8,10},{10,8},{12,14},{14,12},{1,3},{3,1},... | collective-permute-start | bytes 1544 | tf_op jit(solution)/shard_map/ppermute | solution.py:500
  41.9 0.0 collective-permute-done.10.refs_0_
  41.9 0.7 %forward.3 = (bf16[128,1152]{1,0:T(8,128)(2,1)S(1)}, bf16[128,1152]{1,0:T(8,128)(2,1)S(1)}) custom-call(f32[4,32,640]{2,1,0:T(8,128)S(1)} %get-tuple-element.65.own_ref, f32[4,32,640]{2,1,0:T(8,128)S(1)} %collective-permute-done.10.refs_0_, bf16[1024,256]{1,0:T(8,128)(2,1)S(1)} %copy-done.3, bf16[1024,256]{1,0:T(8,128)(2,1)S(1)} %copy-done.2, ...), custom_call_target="tpu_custom_call" | custom-call | tf_op jit(solution)/shard_map/forward/pallas_call | solution.py:462
  42.6 0.8 %collective-permute-done.9 = f32[1,128]{1,0:T(1,128)S(1)} collective-permute-done((f32[1,128]{1,0:T(1,128)S(1)}, f32[1,128]{1,0:T(1,128)S(1)}, u32[]{:S(2)}, u32[]{:S(2)}) %collective-permute-start.9) | collective-permute-done | bytes 544 | tf_op jit(solution)/shard_map/ppermute | solution.py:500
  43.4 0.0 collective-permute-start.11
  43.4 0.0 collective-permute-start.13
  43.4 1.3 %inverse.3 = (f32[32,4,576]{2,1,0:T(4,128)S(1)}, f32[4,32,640]{2,1,0:T(8,128)S(1)}) custom-call(s32[4]{0:T(128)S(1)} %copy-done.11, f32[4,32,640]{2,1,0:T(8,128)S(1)} %get-tuple-element.65.own_ref, f32[4,32,640]{2,1,0:T(8,128)S(1)} %collective-permute-done.10.refs_0_, bf16[128,1152]{1,0:T(8,128)(2,1)S(1)} %get-tuple-element.71.refs_1_, ...), custom_call_target="tpu_custom_call" | custom-call | tf_op jit(solution)/shard_map/inverse/pallas_call | solution.py:474
  44.6 2.3 %collective-permute-done.11 = f32[1,128]{1,0:T(1,128)S(1)} collective-permute-done((f32[1,128]{1,0:T(1,128)S(1)}, f32[1,128]{1,0:T(1,128)S(1)}, u32[]{:S(2)}, u32[]{:S(2)}) %collective-permute-start.11) | collective-permute-done | bytes 544 | tf_op jit(solution)/shard_map/ppermute | solution.py:500
  46.9 0.0 collective-permute-start.14
  46.9 0.0 collective-permute-start.12
  46.9 0.0 collective-permute-done.13.refs_2_
  46.9 1.6 %collective-permute-done.14.refs_3_ = f32[4,32,640]{2,1,0:T(8,128)S(1)} collective-permute-done((f32[4,32,640]{2,1,0:T(8,128)S(1)}, f32[4,32,640]{2,1,0:T(8,128)S(1)}, u32[]{:S(2)}, u32[]{:S(2)}) %collective-permute-start.14) | collective-permute-done | bytes 327712 | tf_op jit(solution)/shard_map/ppermute | solution.py:517
  48.5 1.2 %finish.1 = f32[4,32,4,576]{3,2,1,0:T(4,128)} custom-call(s32[1]{0:T(128)} %bitcast.1.refs_1_.keep_ref, s32[1]{0:T(128)S(6)} %sub.7.refs_0_.give_ref, f32[32,4,576]{2,1,0:T(4,128)S(1)} %get-tuple-element.77.refs_0_, f32[32,4,576]{2,1,0:T(4,128)S(1)} %get-tuple-element.78.refs_1_, f32[4,32,640]{2,1,0:T(8,128)S(1)} %collective-permute-done.13.refs_2_, ...), custom_call_target="tpu_custom_call" | custom-call | bytes 3000000 | tf_op jit(solution)/shard_map/finish/pallas_call | solution.py:520
  49.7 1.6 %collective-permute-done.12 = f32[1,128]{1,0:T(1,128)S(1)} collective-permute-done((f32[1,128]{1,0:T(1,128)S(1)}, f32[1,128]{1,0:T(1,128)S(1)}, u32[]{:S(2)}, u32[]{:S(2)}) %collective-permute-start.12) | collective-permute-done | bytes 544 | tf_op jit(solution)/shard_map/ppermute | solution.py:500
  51.4 0.6 %fusion.1 = f32[1,1]{1,0:T(1,128)} fusion(f32[1,128]{1,0:T(1,128)S(1)} %add.51, s32[]{:T(128)S(6)} %select_n.16), kind=kLoop, calls=%fused_computation.4 | loop fusion | flops 1 | bytes 12 | tf_op jit(solution)/shard_map/div | solution.py:538
  (27 shorter events, 0.1 us)
Async XLA Ops:
  2.0 8.5 %copy-start.14 = (f32[1152]{0:T(1024)S(1)}, f32[1152]{0:T(1024)}, u32[]{:S(2)}) copy-start(f32[1152]{0:T(1024)} %constant.73.clone) | copy-start | bytes 13828
  2.0 8.5 %copy-start.15 = (f32[1152]{0:T(1024)S(1)}, f32[1152]{0:T(1024)}, u32[]{:S(2)}) copy-start(f32[1152]{0:T(1024)} %constant.71.clone) | copy-start | bytes 13828
  2.0 8.5 %copy-start.17 = (pred[1152]{0:T(1024)(128)(4,1)S(1)}, pred[1152]{0:T(1024)(128)(4,1)}, u32[]{:S(2)}) copy-start(pred[1152]{0:T(1024)(128)(4,1)} %constant.72.clone) | copy-start | bytes 3460
  2.0 8.6 %copy-start.18 = (s32[1,1,18,1]{2,3,1,0:T(1,128)S(1)}, s32[1,1,18,1]{2,3,1,0:T(1,128)}, u32[]{:S(2)}) copy-start(s32[1,1,18,1]{2,3,1,0:T(1,128)} %param.25) | copy-start | bytes 220
  2.0 8.8 %copy-start.13 = (f32[4,4,576]{2,1,0:T(4,128)S(1)}, f32[4,4,576]{2,1,0:T(4,128)}, u32[]{:S(2)}) copy-start(f32[4,4,576]{2,1,0:T(4,128)} %param.22) | copy-start | bytes 110596
  2.1 23.6 %collective-permute-start.1 = (f32[128,1152]{1,0:T(8,128)S(1)}, f32[128,1152]{1,0:T(8,128)S(1)}, u32[]{:S(2)}, u32[]{:S(2)}) collective-permute-start(f32[128,1152]{1,0:T(8,128)S(1)} %pack.1), channel_id=1, source_target_pairs={{0,2},{2,0},{4,6},{6,4},{8,10},{10,8},{12,14},{14,12},{1,3},{3,1},... | collective-permute-start | bytes 1769480 | tf_op jit(solution)/shard_map/ppermute | solution.py:382
  7.6 2.9 %copy-start.12 = (f32[64,1152]{1,0:T(8,128)}, f32[64,1152]{1,0:T(8,128)S(1)}, u32[]{:S(2)}) copy-start(f32[64,1152]{1,0:T(8,128)S(1)} %get-tuple-element.50) | copy-start | bytes 884740
  7.6 10.2 %copy-start.16 = (f32[4,32]{1,0:T(4,128)S(1)}, f32[4,32]{1,0:T(4,128)}, u32[]{:S(2)}) copy-start(f32[4,32]{1,0:T(4,128)} %param.24) | copy-start | bytes 1540
  7.6 12.3 %collective-permute-start.3 = (f32[16,1152]{1,0:T(8,128)S(1)}, f32[16,1152]{1,0:T(8,128)S(1)}, u32[]{:S(2)}, u32[]{:S(2)}) collective-permute-start(f32[16,1152]{1,0:T(8,128)S(1)} %get-tuple-element.51), channel_id=1, source_target_pairs={{2,0},{4,2},{6,4},{8,6},{10,8},{12,10},{14,12},{3,1},{5,3},{7,5},{... | collective-permute-start | bytes 221192 | tf_op jit(solution)/shard_map/ppermute | solution.py:399
  9.1 10.9 %collective-permute-start.4 = (f32[64,1152]{1,0:T(8,128)}, f32[64,1152]{1,0:T(8,128)}, u32[]{:S(2)}, u32[]{:S(2)}) collective-permute-start(f32[64,1152]{1,0:T(8,128)} %get-tuple-element.46), channel_id=1, source_target_pairs={{2,4},{4,2},{6,8},{8,6},{10,12},{12,10},{3,5},{5,3},{7,9},{9,7},{1... | collective-permute-start | bytes 884744 | tf_op jit(solution)/shard_map/ppermute | solution.py:398
  10.5 1.6 %collective-permute-start = (f32[5,4,32,128]{3,2,1,0:T(8,128)S(1)}, f32[5,4,32,128]{3,2,1,0:T(8,128)S(1)}, u32[]{:S(2)}, u32[]{:S(2)}) collective-permute-start(f32[5,4,32,128]{3,2,1,0:T(8,128)S(1)} %get-tuple-element.43), channel_id=1, source_target_pairs={{0,1},{1,0},{2,3},{3,2},{4,5},{5,4},{6,7},{7,6},{8,9},{9,8},{10,11... | collective-permute-start | bytes 983048 | tf_op jit(solution)/shard_map/ppermute | solution.py:401
  10.6 15.0 %copy-start.10 = (f32[32,32]{1,0:T(8,128)S(1)}, f32[32,32]{1,0:T(8,128)}, u32[]{:S(2)}) copy-start(f32[32,32]{1,0:T(8,128)} %refs_9_.4) | copy-start | bytes 12292
  12.1 0.7 %copy-start.4 = (f32[5,4,32,128]{3,2,1,0:T(8,128)}, f32[5,4,32,128]{3,2,1,0:T(8,128)S(1)}, u32[]{:S(2)}) copy-start(f32[5,4,32,128]{3,2,1,0:T(8,128)S(1)} %collective-permute-done.side_ref) | copy-start | bytes 983044
  12.8 1.0 %copy-start.5 = (f32[5,4,32,128]{3,2,1,0:T(8,128)S(1)}, f32[5,4,32,128]{3,2,1,0:T(8,128)}, u32[]{:S(2)}) copy-start(f32[5,4,32,128]{3,2,1,0:T(8,128)} %copy-done.4) | copy-start | bytes 983044
  17.9 14.2 %collective-permute-start.2 = (f32[64,1152]{1,0:T(8,128)}, f32[64,1152]{1,0:T(8,128)S(1)}, u32[]{:S(2)}, u32[]{:S(2)}) collective-permute-start(f32[64,1152]{1,0:T(8,128)} %copy-done.12), channel_id=1, source_target_pairs={{2,4},{4,2},{6,8},{8,6},{10,12},{12,10},{3,5},{5,3},{7,9},{9,7},{1... | collective-permute-start | bytes 884744 | tf_op jit(solution)/shard_map/ppermute | solution.py:435
  25.6 3.7 %copy-start.2 = (bf16[1024,256]{1,0:T(8,128)(2,1)S(1)}, bf16[1024,256]{1,0:T(8,128)(2,1)}, u32[]{:S(2)}) copy-start(bf16[1024,256]{1,0:T(8,128)(2,1)} %constant.75.clone.refs_5_.refs_2_) | copy-start | bytes 1572868
  25.6 3.7 %copy-start.3 = (bf16[1024,256]{1,0:T(8,128)(2,1)S(1)}, bf16[1024,256]{1,0:T(8,128)(2,1)}, u32[]{:S(2)}) copy-start(bf16[1024,256]{1,0:T(8,128)(2,1)} %constant.74.clone.refs_4_.refs_1_) | copy-start | bytes 1572868
  25.7 3.7 %copy-start.8 = (bf16[128,128]{1,0:T(8,128)(2,1)S(1)}, bf16[128,128]{1,0:T(8,128)(2,1)}, u32[]{:S(2)}) copy-start(bf16[128,128]{1,0:T(8,128)(2,1)} %constant.77.clone.refs_7_.refs_4_) | copy-start | bytes 98308
  25.7 3.7 %copy-start.9 = (bf16[128,128]{1,0:T(8,128)(2,1)S(1)}, bf16[128,128]{1,0:T(8,128)(2,1)}, u32[]{:S(2)}) copy-start(bf16[128,128]{1,0:T(8,128)(2,1)} %constant.76.clone.refs_6_.refs_3_) | copy-start | bytes 98308
  27.2 2.8 %copy-start = (bf16[1024,256]{1,0:T(8,128)(2,1)S(1)}, bf16[1024,256]{1,0:T(8,128)(2,1)}, u32[]{:S(2)}) copy-start(bf16[1024,256]{1,0:T(8,128)(2,1)} %constant.79.clone.refs_7_.refs_4_) | copy-start | bytes 1572868
  27.2 2.8 %copy-start.1 = (bf16[1024,256]{1,0:T(8,128)(2,1)S(1)}, bf16[1024,256]{1,0:T(8,128)(2,1)}, u32[]{:S(2)}) copy-start(bf16[1024,256]{1,0:T(8,128)(2,1)} %constant.78.clone.refs_6_.refs_3_) | copy-start | bytes 1572868
  27.2 2.8 %copy-start.6 = (bf16[128,128]{1,0:T(8,128)(2,1)S(1)}, bf16[128,128]{1,0:T(8,128)(2,1)}, u32[]{:S(2)}) copy-start(bf16[128,128]{1,0:T(8,128)(2,1)} %constant.81.clone.refs_9_.refs_6_) | copy-start | bytes 98308
  27.3 2.8 %copy-start.7 = (bf16[128,128]{1,0:T(8,128)(2,1)S(1)}, bf16[128,128]{1,0:T(8,128)(2,1)}, u32[]{:S(2)}) copy-start(bf16[128,128]{1,0:T(8,128)(2,1)} %constant.80.clone.refs_8_.refs_5_) | copy-start | bytes 98308
  27.3 2.8 %copy-start.11 = (s32[4]{0:T(128)S(1)}, s32[4]{0:T(128)}, u32[]{:S(2)}) copy-start(s32[4]{0:T(128)} %mask_ref.3) | copy-start | bytes 52
  27.3 1.3 %collective-permute-start.8 = (f32[1,32,640]{2,1,0:T(8,128)S(1)}, f32[1,32,640]{2,1,0:T(8,128)S(1)}, u32[]{:S(2)}, u32[]{:S(2)}) collective-permute-start(f32[1,32,640]{2,1,0:T(8,128)S(1)} %get-tuple-element.82), channel_id=1, source_target_pairs={{0,1},{1,0},{2,3},{3,2},{4,5},{5,4},{6,7},{7,6},{8,9},{9,8},{10,11... | collective-permute-start | bytes 245768 | tf_op jit(solution)/shard_map/ppermute | solution.py:489
  27.4 1.4 %collective-permute-start.7 = (f32[1,32,640]{2,1,0:T(8,128)S(1)}, f32[1,32,640]{2,1,0:T(8,128)S(1)}, u32[]{:S(2)}, u32[]{:S(2)}) collective-permute-start(f32[1,32,640]{2,1,0:T(8,128)S(1)} %get-tuple-element.83), channel_id=1, source_target_pairs={{0,1},{1,0},{2,3},{3,2},{4,5},{5,4},{6,7},{7,6},{8,9},{9,8},{10,11... | collective-permute-start | bytes 245768 | tf_op jit(solution)/shard_map/ppermute | solution.py:489
  27.9 1.3 %collective-permute-start.6 = (f32[1,32,640]{2,1,0:T(8,128)S(1)}, f32[1,32,640]{2,1,0:T(8,128)S(1)}, u32[]{:S(2)}, u32[]{:S(2)}) collective-permute-start(f32[1,32,640]{2,1,0:T(8,128)S(1)} %get-tuple-element.84), channel_id=1, source_target_pairs={{0,1},{1,0},{2,3},{3,2},{4,5},{5,4},{6,7},{7,6},{8,9},{9,8},{10,11... | collective-permute-start | bytes 245768 | tf_op jit(solution)/shard_map/ppermute | solution.py:489
  28.0 1.4 %collective-permute-start.5 = (f32[1,32,640]{2,1,0:T(8,128)S(1)}, f32[1,32,640]{2,1,0:T(8,128)S(1)}, u32[]{:S(2)}, u32[]{:S(2)}) collective-permute-start(f32[1,32,640]{2,1,0:T(8,128)S(1)} %get-tuple-element.85), channel_id=1, source_target_pairs={{0,1},{1,0},{2,3},{3,2},{4,5},{5,4},{6,7},{7,6},{8,9},{9,8},{10,11... | collective-permute-start | bytes 245768 | tf_op jit(solution)/shard_map/ppermute | solution.py:489
  32.7 9.1 %collective-permute-start.10 = (f32[4,32,640]{2,1,0:T(8,128)S(1)}, f32[4,32,640]{2,1,0:T(8,128)S(1)}, u32[]{:S(2)}, u32[]{:S(2)}) collective-permute-start(f32[4,32,640]{2,1,0:T(8,128)S(1)} %get-tuple-element.66), channel_id=1, source_target_pairs={{0,1},{1,0},{2,3},{3,2},{4,5},{5,4},{6,7},{7,6},{8,9},{9,8},{10,11... | collective-permute-start | bytes 983048 | tf_op jit(solution)/shard_map/ppermute | solution.py:503
  33.1 10.2 %collective-permute-start.9 = (f32[1,128]{1,0:T(1,128)S(1)}, f32[1,128]{1,0:T(1,128)S(1)}, u32[]{:S(2)}, u32[]{:S(2)}) collective-permute-start(f32[1,128]{1,0:T(1,128)S(1)} %get-tuple-element.64), channel_id=1, source_target_pairs={{0,2},{2,0},{4,6},{6,4},{8,10},{10,8},{12,14},{14,12},{1,3},{3,1},... | collective-permute-start | bytes 1544 | tf_op jit(solution)/shard_map/ppermute | solution.py:500
  43.4 3.5 %collective-permute-start.11 = (f32[1,128]{1,0:T(1,128)S(1)}, f32[1,128]{1,0:T(1,128)S(1)}, u32[]{:S(2)}, u32[]{:S(2)}) collective-permute-start(f32[1,128]{1,0:T(1,128)S(1)} %add.49), channel_id=1, source_target_pairs={{0,4},{2,6},{4,0},{6,2},{8,12},{10,14},{12,8},{14,10},{1,5},{3,7},... | collective-permute-start | bytes 1544 | tf_op jit(solution)/shard_map/ppermute | solution.py:500
  43.4 3.6 %collective-permute-start.13 = (f32[4,32,640]{2,1,0:T(8,128)}, f32[4,32,640]{2,1,0:T(8,128)S(1)}, u32[]{:S(2)}, u32[]{:S(2)}) collective-permute-start(f32[4,32,640]{2,1,0:T(8,128)} %get-tuple-element.62), channel_id=1, source_target_pairs={{0,1},{1,0},{2,3},{3,2},{4,5},{5,4},{6,7},{7,6},{8,9},{9,8},{10,11... | collective-permute-start | bytes 983048 | tf_op jit(solution)/shard_map/ppermute | solution.py:493
  46.9 1.6 %collective-permute-start.14 = (f32[4,32,640]{2,1,0:T(8,128)S(1)}, f32[4,32,640]{2,1,0:T(8,128)S(1)}, u32[]{:S(2)}, u32[]{:S(2)}) collective-permute-start(f32[4,32,640]{2,1,0:T(8,128)S(1)} %get-tuple-element.79), channel_id=1, source_target_pairs={{0,1},{1,0},{2,3},{3,2},{4,5},{5,4},{6,7},{7,6},{8,9},{9,8},{10,11... | collective-permute-start | bytes 983048 | tf_op jit(solution)/shard_map/ppermute | solution.py:517
  46.9 4.4 %collective-permute-start.12 = (f32[1,128]{1,0:T(1,128)S(1)}, f32[1,128]{1,0:T(1,128)S(1)}, u32[]{:S(2)}, u32[]{:S(2)}) collective-permute-start(f32[1,128]{1,0:T(1,128)S(1)} %add.50), channel_id=1, source_target_pairs={{0,8},{2,10},{4,12},{6,14},{8,0},{10,2},{12,4},{14,6},{1,9},{3,11}... | collective-permute-start | bytes 1544 | tf_op jit(solution)/shard_map/ppermute | solution.py:500

commit v7 on v6

--- a/solution.py
+++ b/solution.py
@@ -395,7 +395,6 @@
         cost_estimate=cost(0, 0),
         name="rest",
     )(even_rest, *fields)
-    from_across = [lax.ppermute(part, "lat", across) for part in outer[:-1]]
     top = lax.ppermute(courant_row, "lat", downward)
 
     sides = lax.ppermute(sides, "lon", swap)
@@ -432,7 +431,7 @@
     base, scale, owner_of, surface, decay = lax.optimization_barrier((base, scale, owner_of, surface, decay))
 
     base, outer = lax.optimization_barrier((base, outer))
-    from_across.append(lax.ppermute(outer[-1], "lat", across))
+    from_across = [lax.ppermute(part, "lat", across) for part in outer]
 
     keep = (half * lax.axis_index("lon")).reshape(1)
     give = half - keep

time: 52.2 us -> 55.4 us (1.061)
  starting transfers between devices: 16.7 us -> 25.2 us
  waiting for transfers between devices: 15.5 us -> 9.5 us
  local copies, waits for them, and re-layouts: 2.11 us -> 2.8 us
    ppermute x3, starting transfers between devices: 8.74 us -> 17.1 us  [send_energy(): lax.ppermute(energy, 'lat', [(i, i ^ distance) for i in range(lat_count)])]
    ppermute x1, waiting for transfers between devices: 5.65 us -> 0.01 us  [on_device(): from_inside = lax.ppermute(inner, 'lat', inside)]
    ppermute x1, waiting for transfers between devices: 1.37 us -> 5.69 us  [on_device(): top = lax.ppermute(courant_row, 'lat', downward)]
    ppermute x3, waiting for transfers between devices: 4.71 us -> 1.61 us  [send_energy(): lax.ppermute(energy, 'lat', [(i, i ^ distance) for i in range(lat_count)])]
    ppermute x2, waiting for transfers between devices: 1.61 us -> 0.01 us  [on_device(): received.append(lax.ppermute(back, 'lon', swap))]
    unnamed x38, local copies, waits for them, and re-layouts: 1.8 us -> 2.5 us
  transfers between devices with their start and end apart: 15 -> 15, of which waited for: 11 -> 9; matrix products, arithmetic and copies ran while one was open for 1% -> 1% of each run, Pallas kernels for 27% -> 25%
where the time goes in v7:
time: 55.4 us; the launch traced here: 55.1 us
  starting transfers between devices  25.2 us (45%)
  Pallas kernels  15.9 us (29%)
  waiting for transfers between devices  9.5 us (17%)
  local copies, waits for them, and re-layouts  2.8 us (5%)
  between operations  0.99 us (2%)
  other arithmetic  0.72 us (1%)
    ppermute x3, starting transfers between devices, send_energy(): lax.ppermute(energy, 'lat', [(i, i ^ distance) for i in range(lat_count)])  17.1 us
    ppermute x1, waiting for transfers between devices, on_device(): top = lax.ppermute(courant_row, 'lat', downward)  5.69 us
    pallas_call x1, Pallas kernels, on_device(): pl.pallas_call(functools.partial(base_kernel, width), in_specs=[scalars,...  3.98 us
    pallas_call x2, Pallas kernels, run_inverse(): pl.pallas_call(functools.partial(inverse_kernel, radix, len(other)), in_s...  3.24 us
    ppermute x1, starting transfers between devices, on_device(): from_inside = lax.ppermute(inner, 'lat', inside)  3 us
    pallas_call x1, Pallas kernels, on_device(): pl.pallas_call(rest_kernel, in_specs=[scalars] + [in_hbm] * 3, out_specs=...  2.55 us
    unnamed x38, local copies, waits for them, and re-layouts  2.5 us
    pallas_call x2, Pallas kernels, run_physics(): pl.pallas_call(functools.partial(physics_kernel, levels, sector, lat_coun...  2.2 us
  transfers between devices with their start and end apart: 15, of which 9 were waited for; matrix products, arithmetic and copies ran while one was open for 1% of the time, Pallas kernels for 25%

profile of v7, /device:TPU:0, one launch (start us, length us, event | category | flops | bytes accessed | tf_op | source)
XLA Modules:
  0.0 55.1 jit_solution(7901750419116485954)
XLA Ops:
  0.6 1.3 %pack.1 = f32[128,1152]{1,0:T(8,128)S(1)} custom-call(s32[1]{0:T(128)} %bitcast.even_ref, f32[4,32,4,576]{3,2,1,0:T(4,128)} %tracer_hbm.5), custom_call_target="tpu_custom_call" | custom-call | bytes 600000 | tf_op jit(solution)/shard_map/pack/pallas_call | solution.py:372
  2.0 0.0 copy-start.18
  2.0 0.0 copy-start.13
  2.0 0.0 copy-start.14
  2.0 0.0 copy-start.15
  2.0 0.0 copy-start.17
  2.1 3.0 %collective-permute-start.1 = (f32[128,1152]{1,0:T(8,128)S(1)}, f32[128,1152]{1,0:T(8,128)S(1)}, u32[]{:S(2)}, u32[]{:S(2)}) collective-permute-start(f32[128,1152]{1,0:T(8,128)S(1)} %pack.1), channel_id=1, source_target_pairs={{0,2},{2,0},{4,6},{6,4},{8,10},{10,8},{12,14},{14,12},{1,3},{3,1},... | collective-permute-start | bytes 1769480 | tf_op jit(solution)/shard_map/ppermute | solution.py:382
  5.1 2.5 %rest.1 = (f32[64,1152]{1,0:T(8,128)}, f32[64,1152]{1,0:T(8,128)S(1)}, f32[16,1152]{1,0:T(8,128)S(1)}, f32[5,4,32,128]{3,2,1,0:T(8,128)S(1)}) custom-call(s32[1]{0:T(128)} %bitcast.even_ref, f32[4,32,4,576]{3,2,1,0:T(4,128)} %tracer_hbm.5, f32[32,4,576]{2,1,0:T(4,128)} %lat_hbm.3, f32[32,4,576]{2,1,0:T(4,128)} %lon_hbm.3), custom_call_target="tpu_custom_call" | custom-call | tf_op jit(solution)/shard_map/rest/pallas_call | solution.py:384
  7.6 0.7 %copy-done.12 = f32[64,1152]{1,0:T(8,128)} copy-done((f32[64,1152]{1,0:T(8,128)}, f32[64,1152]{1,0:T(8,128)S(1)}, u32[]{:S(2)}) %copy-start.12) | copy-done | bytes 294936
  8.3 0.0 collective-permute-start
  8.4 0.1 broadcast_in_dim.27
  8.5 0.1 reshape_reshape.3
  8.5 0.0 copy-done.13
  8.6 0.0 copy-done.14
  8.6 0.1 select_multiply_fusion.refs_8_.refs_5_
  8.7 1.3 %collective-permute-done.side_ref = f32[5,4,32,128]{3,2,1,0:T(8,128)S(1)} collective-permute-done((f32[5,4,32,128]{3,2,1,0:T(8,128)S(1)}, f32[5,4,32,128]{3,2,1,0:T(8,128)S(1)}, u32[]{:S(2)}, u32[]{:S(2)}) %collective-permute-start) | collective-permute-done | bytes 327712 | tf_op jit(solution)/shard_map/ppermute | solution.py:400
  10.0 0.7 %copy-done.4 = f32[5,4,32,128]{3,2,1,0:T(8,128)} copy-done((f32[5,4,32,128]{3,2,1,0:T(8,128)}, f32[5,4,32,128]{3,2,1,0:T(8,128)S(1)}, u32[]{:S(2)}) %copy-start.4) | copy-done | bytes 327704
  10.7 1.0 %copy-done.5 = f32[5,4,32,128]{3,2,1,0:T(8,128)S(1)} copy-done((f32[5,4,32,128]{3,2,1,0:T(8,128)S(1)}, f32[5,4,32,128]{3,2,1,0:T(8,128)}, u32[]{:S(2)}) %copy-start.5) | copy-done | bytes 327704
  11.6 4.0 %base.1 = (f32[4,4,32,640]{3,2,1,0:T(8,128)S(1)}, f32[4,32,640]{2,1,0:T(8,128)S(1)}, f32[4,32,640]{2,1,0:T(8,128)S(1)}) custom-call(f32[1]{0:T(128)} %bitcast.2.not_pole_ref, f32[4,32,4,576]{3,2,1,0:T(4,128)} %tracer_hbm.5, f32[32,4,576]{2,1,0:T(4,128)} %lat_hbm.3, f32[32,4,576]{2,1,0:T(4,128)} %lon_hbm.3, f32[5,4,32,128]{3,2,1,0:T(8,128)S(1)} %copy-done.5), custom_call_target="tpu_custom_call" | custom-call | tf_op jit(solution)/shard_map/base/pallas_call | solution.py:402
  15.6 1.4 %collective-permute-start.4 = (f32[64,1152]{1,0:T(8,128)}, f32[64,1152]{1,0:T(8,128)}, u32[]{:S(2)}, u32[]{:S(2)}) collective-permute-start(f32[64,1152]{1,0:T(8,128)} %get-tuple-element.57), channel_id=1, source_target_pairs={{2,4},{4,2},{6,8},{8,6},{10,12},{12,10},{3,5},{5,3},{7,9},{9,7},{1... | collective-permute-start | bytes 884744 | tf_op jit(solution)/shard_map/ppermute | solution.py:434
  17.0 1.3 %collective-permute-start.3 = (f32[16,1152]{1,0:T(8,128)S(1)}, f32[16,1152]{1,0:T(8,128)S(1)}, u32[]{:S(2)}, u32[]{:S(2)}) collective-permute-start(f32[16,1152]{1,0:T(8,128)S(1)} %get-tuple-element.52), channel_id=1, source_target_pairs={{2,0},{4,2},{6,4},{8,6},{10,8},{12,10},{14,12},{3,1},{5,3},{7,5},{... | collective-permute-start | bytes 221192 | tf_op jit(solution)/shard_map/ppermute | solution.py:398
  18.4 0.1 copy.22.refs_10_
  18.5 0.7 %collective-permute-start.2 = (f32[64,1152]{1,0:T(8,128)}, f32[64,1152]{1,0:T(8,128)S(1)}, u32[]{:S(2)}, u32[]{:S(2)}) collective-permute-start(f32[64,1152]{1,0:T(8,128)} %copy-done.12), channel_id=1, source_target_pairs={{2,4},{4,2},{6,8},{8,6},{10,12},{12,10},{3,5},{5,3},{7,9},{9,7},{1... | collective-permute-start | bytes 884744 | tf_op jit(solution)/shard_map/ppermute | solution.py:434
  19.1 5.7 %collective-permute-done.3.refs_6_ = f32[16,1152]{1,0:T(8,128)S(1)} collective-permute-done((f32[16,1152]{1,0:T(8,128)S(1)}, f32[16,1152]{1,0:T(8,128)S(1)}, u32[]{:S(2)}, u32[]{:S(2)}) %collective-permute-start.3) | collective-permute-done | bytes 73760 | tf_op jit(solution)/shard_map/ppermute | solution.py:398
  24.8 0.0 collective-permute-done.1.refs_4_
  24.8 0.0 collective-permute-done.4.refs_5_
  24.9 0.0 copy-start.2
  24.9 0.0 copy-start.3
  24.9 0.0 copy-start.8
  24.9 0.0 copy-start.9
  24.9 1.5 %physics.2 = (f32[4,32,640]{2,1,0:T(8,128)S(1)}, f32[4,32,640]{2,1,0:T(8,128)S(1)}, f32[4,8,640]{2,1,0:T(8,128)S(1)}) custom-call(s32[1]{0:T(128)} %bitcast.even_ref, s32[1]{0:T(128)S(6)} %sub.7.refs_0_.give_ref, s32[1]{0:T(128)} %bitcast.1.refs_1_.keep_ref, f32[4,4,32,640]{3,2,1,0:T(8,128)S(1)} %get-tuple-element.49.refs_2_, ...), custom_call_target="tpu_custom_call" | custom-call | tf_op jit(solution)/shard_map/physics/pallas_call | solution.py:445
  26.5 0.0 copy-start
  26.5 0.0 copy-start.1
  26.5 0.0 copy-start.6
  26.5 0.0 copy-start.7
  26.5 0.0 copy-start.11
  26.5 0.1 collective-permute-start.8
  26.6 0.5 collective-permute-start.7
  27.1 0.1 collective-permute-start.6
  27.2 0.4 collective-permute-start.5
  27.6 0.3 collective-permute-done.8.refs_3_
  27.9 0.2 collective-permute-done.7.refs_2_
  28.0 0.4 collective-permute-done.6.refs_1_
  28.4 0.2 collective-permute-done.5.refs_0_
  28.6 0.7 %forward.2 = (bf16[128,1152]{1,0:T(8,128)(2,1)S(1)}, bf16[128,1152]{1,0:T(8,128)(2,1)S(1)}) custom-call(f32[4,32,640]{2,1,0:T(8,128)S(1)} %get-tuple-element.59.own_ref, f32[1,32,640]{2,1,0:T(8,128)S(1)} %collective-permute-done.5.refs_0_, f32[1,32,640]{2,1,0:T(8,128)S(1)} %collective-permute-done.6.refs_1_, ...), custom_call_target="tpu_custom_call" | custom-call | tf_op jit(solution)/shard_map/forward/pallas_call | solution.py:461
  29.3 2.0 %inverse.2 = (f32[32,4,576]{2,1,0:T(4,128)S(1)}, f32[4,32,640]{2,1,0:T(8,128)}) custom-call(s32[4]{0:T(128)S(1)} %copy-done.11, f32[4,32,640]{2,1,0:T(8,128)S(1)} %get-tuple-element.59.own_ref, f32[1,32,640]{2,1,0:T(8,128)S(1)} %collective-permute-done.5.refs_0_, f32[1,32,640]{2,1,0:T(8,128)S(1)} %collective-permute-done.6.refs_1_, ...), custom_call_target="tpu_custom_call" | custom-call | tf_op jit(solution)/shard_map/inverse/pallas_call | solution.py:473
  31.3 0.0 collective-permute-done.2.refs_5_
  31.3 0.7 %physics.3 = (f32[4,32,640]{2,1,0:T(8,128)S(1)}, f32[4,32,640]{2,1,0:T(8,128)S(1)}, f32[1,128]{1,0:T(1,128)S(1)}) custom-call(s32[1]{0:T(128)} %bitcast.even_ref, s32[1]{0:T(128)S(6)} %sub.7.refs_0_.give_ref, s32[1]{0:T(128)} %bitcast.1.refs_1_.keep_ref, f32[4,4,32,640]{3,2,1,0:T(8,128)S(1)} %get-tuple-element.49.refs_2_, ...), custom_call_target="tpu_custom_call" | custom-call | tf_op jit(solution)/shard_map/physics/pallas_call | solution.py:445
  32.0 0.4 collective-permute-start.10
  32.4 5.3 %collective-permute-start.9 = (f32[1,128]{1,0:T(1,128)S(1)}, f32[1,128]{1,0:T(1,128)S(1)}, u32[]{:S(2)}, u32[]{:S(2)}) collective-permute-start(f32[1,128]{1,0:T(1,128)S(1)} %get-tuple-element.66), channel_id=1, source_target_pairs={{0,2},{2,0},{4,6},{6,4},{8,10},{10,8},{12,14},{14,12},{1,3},{3,1},... | collective-permute-start | bytes 1544 | tf_op jit(solution)/shard_map/ppermute | solution.py:499
  37.7 0.0 collective-permute-done.10.refs_0_
  37.7 0.7 %forward.3 = (bf16[128,1152]{1,0:T(8,128)(2,1)S(1)}, bf16[128,1152]{1,0:T(8,128)(2,1)S(1)}) custom-call(f32[4,32,640]{2,1,0:T(8,128)S(1)} %get-tuple-element.67.own_ref, f32[4,32,640]{2,1,0:T(8,128)S(1)} %collective-permute-done.10.refs_0_, bf16[1024,256]{1,0:T(8,128)(2,1)S(1)} %copy-done.3, bf16[1024,256]{1,0:T(8,128)(2,1)S(1)} %copy-done.2, ...), custom_call_target="tpu_custom_call" | custom-call | tf_op jit(solution)/shard_map/forward/pallas_call | solution.py:461
  38.4 0.8 %collective-permute-done.9 = f32[1,128]{1,0:T(1,128)S(1)} collective-permute-done((f32[1,128]{1,0:T(1,128)S(1)}, f32[1,128]{1,0:T(1,128)S(1)}, u32[]{:S(2)}, u32[]{:S(2)}) %collective-permute-start.9) | collective-permute-done | bytes 544 | tf_op jit(solution)/shard_map/ppermute | solution.py:499
  39.2 9.0 %collective-permute-start.11 = (f32[1,128]{1,0:T(1,128)S(1)}, f32[1,128]{1,0:T(1,128)S(1)}, u32[]{:S(2)}, u32[]{:S(2)}) collective-permute-start(f32[1,128]{1,0:T(1,128)S(1)} %add.49), channel_id=1, source_target_pairs={{0,4},{2,6},{4,0},{6,2},{8,12},{10,14},{12,8},{14,10},{1,5},{3,7},... | collective-permute-start | bytes 1544 | tf_op jit(solution)/shard_map/ppermute | solution.py:499
  48.2 0.0 collective-permute-start.13
  48.2 1.3 %inverse.3 = (f32[32,4,576]{2,1,0:T(4,128)S(1)}, f32[4,32,640]{2,1,0:T(8,128)S(1)}) custom-call(s32[4]{0:T(128)S(1)} %copy-done.11, f32[4,32,640]{2,1,0:T(8,128)S(1)} %get-tuple-element.67.own_ref, f32[4,32,640]{2,1,0:T(8,128)S(1)} %collective-permute-done.10.refs_0_, bf16[128,1152]{1,0:T(8,128)(2,1)S(1)} %get-tuple-element.73.refs_1_, ...), custom_call_target="tpu_custom_call" | custom-call | tf_op jit(solution)/shard_map/inverse/pallas_call | solution.py:473
  49.5 0.3 collective-permute-done.11
  49.8 0.3 collective-permute-start.14
  50.1 2.7 %collective-permute-start.12 = (f32[1,128]{1,0:T(1,128)S(1)}, f32[1,128]{1,0:T(1,128)S(1)}, u32[]{:S(2)}, u32[]{:S(2)}) collective-permute-start(f32[1,128]{1,0:T(1,128)S(1)} %add.50), channel_id=1, source_target_pairs={{0,8},{2,10},{4,12},{6,14},{8,0},{10,2},{12,4},{14,6},{1,9},{3,11}... | collective-permute-start | bytes 1544 | tf_op jit(solution)/shard_map/ppermute | solution.py:499
  52.8 0.0 collective-permute-done.13.refs_2_
  52.8 0.0 collective-permute-done.14.refs_3_
  52.8 1.2 %finish.1 = f32[4,32,4,576]{3,2,1,0:T(4,128)} custom-call(s32[1]{0:T(128)} %bitcast.1.refs_1_.keep_ref, s32[1]{0:T(128)S(6)} %sub.7.refs_0_.give_ref, f32[32,4,576]{2,1,0:T(4,128)S(1)} %get-tuple-element.79.refs_0_, f32[32,4,576]{2,1,0:T(4,128)S(1)} %get-tuple-element.80.refs_1_, f32[4,32,640]{2,1,0:T(8,128)S(1)} %collective-permute-done.13.refs_2_, ...), custom_call_target="tpu_custom_call" | custom-call | bytes 3000000 | tf_op jit(solution)/shard_map/finish/pallas_call | solution.py:519
  54.0 0.5 collective-permute-done.12
  54.5 0.6 %fusion.1 = f32[1,1]{1,0:T(1,128)} fusion(f32[1,128]{1,0:T(1,128)S(1)} %add.51, s32[]{:T(128)S(6)} %select_n.16), kind=kLoop, calls=%fused_computation.4 | loop fusion | flops 1 | bytes 12 | tf_op jit(solution)/shard_map/div | solution.py:537
  (27 shorter events, 0.1 us)
Async XLA Ops:
  2.0 6.4 %copy-start.18 = (s32[1,1,18,1]{2,3,1,0:T(1,128)S(1)}, s32[1,1,18,1]{2,3,1,0:T(1,128)}, u32[]{:S(2)}) copy-start(s32[1,1,18,1]{2,3,1,0:T(1,128)} %param.25) | copy-start | bytes 220
  2.0 6.5 %copy-start.13 = (f32[4,4,576]{2,1,0:T(4,128)S(1)}, f32[4,4,576]{2,1,0:T(4,128)}, u32[]{:S(2)}) copy-start(f32[4,4,576]{2,1,0:T(4,128)} %param.22) | copy-start | bytes 110596
  2.0 6.6 %copy-start.14 = (f32[1152]{0:T(1024)S(1)}, f32[1152]{0:T(1024)}, u32[]{:S(2)}) copy-start(f32[1152]{0:T(1024)} %constant.73.clone) | copy-start | bytes 13828
  2.0 6.6 %copy-start.15 = (f32[1152]{0:T(1024)S(1)}, f32[1152]{0:T(1024)}, u32[]{:S(2)}) copy-start(f32[1152]{0:T(1024)} %constant.71.clone) | copy-start | bytes 13828
  2.0 6.6 %copy-start.17 = (pred[1152]{0:T(1024)(128)(4,1)S(1)}, pred[1152]{0:T(1024)(128)(4,1)}, u32[]{:S(2)}) copy-start(pred[1152]{0:T(1024)(128)(4,1)} %constant.72.clone) | copy-start | bytes 3460
  2.1 22.8 %collective-permute-start.1 = (f32[128,1152]{1,0:T(8,128)S(1)}, f32[128,1152]{1,0:T(8,128)S(1)}, u32[]{:S(2)}, u32[]{:S(2)}) collective-permute-start(f32[128,1152]{1,0:T(8,128)S(1)} %pack.1), channel_id=1, source_target_pairs={{0,2},{2,0},{4,6},{6,4},{8,10},{10,8},{12,14},{14,12},{1,3},{3,1},... | collective-permute-start | bytes 1769480 | tf_op jit(solution)/shard_map/ppermute | solution.py:382
  7.6 0.7 %copy-start.12 = (f32[64,1152]{1,0:T(8,128)}, f32[64,1152]{1,0:T(8,128)S(1)}, u32[]{:S(2)}) copy-start(f32[64,1152]{1,0:T(8,128)S(1)} %get-tuple-element.51) | copy-start | bytes 884740
  8.3 10.0 %copy-start.16 = (f32[4,32]{1,0:T(4,128)S(1)}, f32[4,32]{1,0:T(4,128)}, u32[]{:S(2)}) copy-start(f32[4,32]{1,0:T(4,128)} %param.24) | copy-start | bytes 1540
  8.3 1.6 %collective-permute-start = (f32[5,4,32,128]{3,2,1,0:T(8,128)S(1)}, f32[5,4,32,128]{3,2,1,0:T(8,128)S(1)}, u32[]{:S(2)}, u32[]{:S(2)}) collective-permute-start(f32[5,4,32,128]{3,2,1,0:T(8,128)S(1)} %get-tuple-element.44), channel_id=1, source_target_pairs={{0,1},{1,0},{2,3},{3,2},{4,5},{5,4},{6,7},{7,6},{8,9},{9,8},{10,11... | collective-permute-start | bytes 983048 | tf_op jit(solution)/shard_map/ppermute | solution.py:400
  8.5 16.3 %copy-start.10 = (f32[32,32]{1,0:T(8,128)S(1)}, f32[32,32]{1,0:T(8,128)}, u32[]{:S(2)}) copy-start(f32[32,32]{1,0:T(8,128)} %refs_9_.4) | copy-start | bytes 12292
  10.0 0.7 %copy-start.4 = (f32[5,4,32,128]{3,2,1,0:T(8,128)}, f32[5,4,32,128]{3,2,1,0:T(8,128)S(1)}, u32[]{:S(2)}) copy-start(f32[5,4,32,128]{3,2,1,0:T(8,128)S(1)} %collective-permute-done.side_ref) | copy-start | bytes 983044
  10.7 1.0 %copy-start.5 = (f32[5,4,32,128]{3,2,1,0:T(8,128)S(1)}, f32[5,4,32,128]{3,2,1,0:T(8,128)}, u32[]{:S(2)}) copy-start(f32[5,4,32,128]{3,2,1,0:T(8,128)} %copy-done.4) | copy-start | bytes 983044
  15.6 9.2 %collective-permute-start.4 = (f32[64,1152]{1,0:T(8,128)}, f32[64,1152]{1,0:T(8,128)}, u32[]{:S(2)}, u32[]{:S(2)}) collective-permute-start(f32[64,1152]{1,0:T(8,128)} %get-tuple-element.57), channel_id=1, source_target_pairs={{2,4},{4,2},{6,8},{8,6},{10,12},{12,10},{3,5},{5,3},{7,9},{9,7},{1... | collective-permute-start | bytes 884744 | tf_op jit(solution)/shard_map/ppermute | solution.py:434
  17.0 7.8 %collective-permute-start.3 = (f32[16,1152]{1,0:T(8,128)S(1)}, f32[16,1152]{1,0:T(8,128)S(1)}, u32[]{:S(2)}, u32[]{:S(2)}) collective-permute-start(f32[16,1152]{1,0:T(8,128)S(1)} %get-tuple-element.52), channel_id=1, source_target_pairs={{2,0},{4,2},{6,4},{8,6},{10,8},{12,10},{14,12},{3,1},{5,3},{7,5},{... | collective-permute-start | bytes 221192 | tf_op jit(solution)/shard_map/ppermute | solution.py:398
  18.5 12.8 %collective-permute-start.2 = (f32[64,1152]{1,0:T(8,128)}, f32[64,1152]{1,0:T(8,128)S(1)}, u32[]{:S(2)}, u32[]{:S(2)}) collective-permute-start(f32[64,1152]{1,0:T(8,128)} %copy-done.12), channel_id=1, source_target_pairs={{2,4},{4,2},{6,8},{8,6},{10,12},{12,10},{3,5},{5,3},{7,9},{9,7},{1... | collective-permute-start | bytes 884744 | tf_op jit(solution)/shard_map/ppermute | solution.py:434
  24.9 3.7 %copy-start.2 = (bf16[1024,256]{1,0:T(8,128)(2,1)S(1)}, bf16[1024,256]{1,0:T(8,128)(2,1)}, u32[]{:S(2)}) copy-start(bf16[1024,256]{1,0:T(8,128)(2,1)} %constant.75.clone.refs_5_.refs_2_) | copy-start | bytes 1572868
  24.9 3.7 %copy-start.3 = (bf16[1024,256]{1,0:T(8,128)(2,1)S(1)}, bf16[1024,256]{1,0:T(8,128)(2,1)}, u32[]{:S(2)}) copy-start(bf16[1024,256]{1,0:T(8,128)(2,1)} %constant.74.clone.refs_4_.refs_1_) | copy-start | bytes 1572868
  24.9 3.7 %copy-start.8 = (bf16[128,128]{1,0:T(8,128)(2,1)S(1)}, bf16[128,128]{1,0:T(8,128)(2,1)}, u32[]{:S(2)}) copy-start(bf16[128,128]{1,0:T(8,128)(2,1)} %constant.77.clone.refs_7_.refs_4_) | copy-start | bytes 98308
  24.9 3.7 %copy-start.9 = (bf16[128,128]{1,0:T(8,128)(2,1)S(1)}, bf16[128,128]{1,0:T(8,128)(2,1)}, u32[]{:S(2)}) copy-start(bf16[128,128]{1,0:T(8,128)(2,1)} %constant.76.clone.refs_6_.refs_3_) | copy-start | bytes 98308
  26.5 2.8 %copy-start = (bf16[1024,256]{1,0:T(8,128)(2,1)S(1)}, bf16[1024,256]{1,0:T(8,128)(2,1)}, u32[]{:S(2)}) copy-start(bf16[1024,256]{1,0:T(8,128)(2,1)} %constant.79.clone.refs_7_.refs_4_) | copy-start | bytes 1572868
  26.5 2.8 %copy-start.1 = (bf16[1024,256]{1,0:T(8,128)(2,1)S(1)}, bf16[1024,256]{1,0:T(8,128)(2,1)}, u32[]{:S(2)}) copy-start(bf16[1024,256]{1,0:T(8,128)(2,1)} %constant.78.clone.refs_6_.refs_3_) | copy-start | bytes 1572868
  26.5 2.8 %copy-start.6 = (bf16[128,128]{1,0:T(8,128)(2,1)S(1)}, bf16[128,128]{1,0:T(8,128)(2,1)}, u32[]{:S(2)}) copy-start(bf16[128,128]{1,0:T(8,128)(2,1)} %constant.81.clone.refs_9_.refs_6_) | copy-start | bytes 98308
  26.5 2.8 %copy-start.7 = (bf16[128,128]{1,0:T(8,128)(2,1)S(1)}, bf16[128,128]{1,0:T(8,128)(2,1)}, u32[]{:S(2)}) copy-start(bf16[128,128]{1,0:T(8,128)(2,1)} %constant.80.clone.refs_8_.refs_5_) | copy-start | bytes 98308
  26.5 2.8 %copy-start.11 = (s32[4]{0:T(128)S(1)}, s32[4]{0:T(128)}, u32[]{:S(2)}) copy-start(s32[4]{0:T(128)} %mask_ref.3) | copy-start | bytes 52
  26.5 1.3 %collective-permute-start.8 = (f32[1,32,640]{2,1,0:T(8,128)S(1)}, f32[1,32,640]{2,1,0:T(8,128)S(1)}, u32[]{:S(2)}, u32[]{:S(2)}) collective-permute-start(f32[1,32,640]{2,1,0:T(8,128)S(1)} %get-tuple-element.84), channel_id=1, source_target_pairs={{0,1},{1,0},{2,3},{3,2},{4,5},{5,4},{6,7},{7,6},{8,9},{9,8},{10,11... | collective-permute-start | bytes 245768 | tf_op jit(solution)/shard_map/ppermute | solution.py:488
  26.6 1.4 %collective-permute-start.7 = (f32[1,32,640]{2,1,0:T(8,128)S(1)}, f32[1,32,640]{2,1,0:T(8,128)S(1)}, u32[]{:S(2)}, u32[]{:S(2)}) collective-permute-start(f32[1,32,640]{2,1,0:T(8,128)S(1)} %get-tuple-element.85), channel_id=1, source_target_pairs={{0,1},{1,0},{2,3},{3,2},{4,5},{5,4},{6,7},{7,6},{8,9},{9,8},{10,11... | collective-permute-start | bytes 245768 | tf_op jit(solution)/shard_map/ppermute | solution.py:488
  27.1 1.3 %collective-permute-start.6 = (f32[1,32,640]{2,1,0:T(8,128)S(1)}, f32[1,32,640]{2,1,0:T(8,128)S(1)}, u32[]{:S(2)}, u32[]{:S(2)}) collective-permute-start(f32[1,32,640]{2,1,0:T(8,128)S(1)} %get-tuple-element.86), channel_id=1, source_target_pairs={{0,1},{1,0},{2,3},{3,2},{4,5},{5,4},{6,7},{7,6},{8,9},{9,8},{10,11... | collective-permute-start | bytes 245768 | tf_op jit(solution)/shard_map/ppermute | solution.py:488
  27.2 1.4 %collective-permute-start.5 = (f32[1,32,640]{2,1,0:T(8,128)S(1)}, f32[1,32,640]{2,1,0:T(8,128)S(1)}, u32[]{:S(2)}, u32[]{:S(2)}) collective-permute-start(f32[1,32,640]{2,1,0:T(8,128)S(1)} %get-tuple-element.87), channel_id=1, source_target_pairs={{0,1},{1,0},{2,3},{3,2},{4,5},{5,4},{6,7},{7,6},{8,9},{9,8},{10,11... | collective-permute-start | bytes 245768 | tf_op jit(solution)/shard_map/ppermute | solution.py:488
  32.0 5.7 %collective-permute-start.10 = (f32[4,32,640]{2,1,0:T(8,128)S(1)}, f32[4,32,640]{2,1,0:T(8,128)S(1)}, u32[]{:S(2)}, u32[]{:S(2)}) collective-permute-start(f32[4,32,640]{2,1,0:T(8,128)S(1)} %get-tuple-element.68), channel_id=1, source_target_pairs={{0,1},{1,0},{2,3},{3,2},{4,5},{5,4},{6,7},{7,6},{8,9},{9,8},{10,11... | collective-permute-start | bytes 983048 | tf_op jit(solution)/shard_map/ppermute | solution.py:502
  32.4 6.8 %collective-permute-start.9 = (f32[1,128]{1,0:T(1,128)S(1)}, f32[1,128]{1,0:T(1,128)S(1)}, u32[]{:S(2)}, u32[]{:S(2)}) collective-permute-start(f32[1,128]{1,0:T(1,128)S(1)} %get-tuple-element.66), channel_id=1, source_target_pairs={{0,2},{2,0},{4,6},{6,4},{8,10},{10,8},{12,14},{14,12},{1,3},{3,1},... | collective-permute-start | bytes 1544 | tf_op jit(solution)/shard_map/ppermute | solution.py:499
  39.2 10.6 %collective-permute-start.11 = (f32[1,128]{1,0:T(1,128)S(1)}, f32[1,128]{1,0:T(1,128)S(1)}, u32[]{:S(2)}, u32[]{:S(2)}) collective-permute-start(f32[1,128]{1,0:T(1,128)S(1)} %add.49), channel_id=1, source_target_pairs={{0,4},{2,6},{4,0},{6,2},{8,12},{10,14},{12,8},{14,10},{1,5},{3,7},... | collective-permute-start | bytes 1544 | tf_op jit(solution)/shard_map/ppermute | solution.py:499
  48.2 4.6 %collective-permute-start.13 = (f32[4,32,640]{2,1,0:T(8,128)}, f32[4,32,640]{2,1,0:T(8,128)S(1)}, u32[]{:S(2)}, u32[]{:S(2)}) collective-permute-start(f32[4,32,640]{2,1,0:T(8,128)} %get-tuple-element.64), channel_id=1, source_target_pairs={{0,1},{1,0},{2,3},{3,2},{4,5},{5,4},{6,7},{7,6},{8,9},{9,8},{10,11... | collective-permute-start | bytes 983048 | tf_op jit(solution)/shard_map/ppermute | solution.py:492
  49.8 3.0 %collective-permute-start.14 = (f32[4,32,640]{2,1,0:T(8,128)S(1)}, f32[4,32,640]{2,1,0:T(8,128)S(1)}, u32[]{:S(2)}, u32[]{:S(2)}) collective-permute-start(f32[4,32,640]{2,1,0:T(8,128)S(1)} %get-tuple-element.81), channel_id=1, source_target_pairs={{0,1},{1,0},{2,3},{3,2},{4,5},{5,4},{6,7},{7,6},{8,9},{9,8},{10,11... | collective-permute-start | bytes 983048 | tf_op jit(solution)/shard_map/ppermute | solution.py:516
  50.1 4.4 %collective-permute-start.12 = (f32[1,128]{1,0:T(1,128)S(1)}, f32[1,128]{1,0:T(1,128)S(1)}, u32[]{:S(2)}, u32[]{:S(2)}) collective-permute-start(f32[1,128]{1,0:T(1,128)S(1)} %add.50), channel_id=1, source_target_pairs={{0,8},{2,10},{4,12},{6,14},{8,0},{10,2},{12,4},{14,6},{1,9},{3,11}... | collective-permute-start | bytes 1544 | tf_op jit(solution)/shard_map/ppermute | solution.py:499

commit v8 on v6

--- a/solution.py
+++ b/solution.py
@@ -107,8 +107,9 @@
         last = jnp.concatenate([values[:, whole:], values[:, whole:]], axis=1)
         side_ref[i, r] = jnp.where(lane < LANES - 2, first, last)
 
+    for copy in copies:
+        copy.wait()
     for t in range(count):
-        copies[t].wait()
         row = [tracer_ref[t, :, r, :] for r in range(rows)]
         slot = t // len(outer_refs)
         outer_refs[t % len(outer_refs)][levels * slot : levels * (slot + 1), :] = pack_rows(
@@ -116,10 +117,8 @@
         )
         for r in range(rows):
             store_side(t, r, row[r])
-    copies[count].wait()
     courant = lat_ref[:, 0, :]
     courant_ref[...] = pack_rows(courant[: levels // 2], courant[levels // 2 :])
-    copies[count + 1].wait()
     for r in range(rows):
         store_side(count, r, lon_ref[:, r, :])
 

time: 52.2 us -> 46.4 us (0.89)
  waiting for transfers between devices: 15.5 us -> 10.6 us
  starting transfers between devices: 16.7 us -> 15.6 us
    ppermute x3, waiting for transfers between devices: 4.71 us -> 1.61 us  [send_energy(): lax.ppermute(energy, 'lat', [(i, i ^ distance) for i in range(lat_count)])]
    ppermute x2, waiting for transfers between devices: 1.61 us -> 0.01 us  [on_device(): received.append(lax.ppermute(back, 'lon', swap))]
    ppermute x3, starting transfers between devices: 8.74 us -> 7.31 us  [send_energy(): lax.ppermute(energy, 'lat', [(i, i ^ distance) for i in range(lat_count)])]
  transfers between devices with their start and end apart: 15 -> 15, of which waited for: 11 -> 10; matrix products, arithmetic and copies ran while one was open for 1% -> 1% of each run, Pallas kernels for 27% -> 30%
where the time goes in v8:
time: 46.4 us; the launch traced here: 46.1 us
  Pallas kernels  16 us (34%)
  starting transfers between devices  15.6 us (34%)
  waiting for transfers between devices  10.6 us (23%)
  local copies, waits for them, and re-layouts  2.11 us (5%)
  between operations  1 us (2%)
  other arithmetic  0.72 us (2%)
    ppermute x3, starting transfers between devices, send_energy(): lax.ppermute(energy, 'lat', [(i, i ^ distance) for i in range(lat_count)])  7.31 us
    ppermute x1, waiting for transfers between devices, on_device(): from_inside = lax.ppermute(inner, 'lat', inside)  5.58 us
    pallas_call x1, Pallas kernels, on_device(): pl.pallas_call(functools.partial(base_kernel, width), in_specs=[scalars,...  3.98 us
    pallas_call x2, Pallas kernels, run_inverse(): pl.pallas_call(functools.partial(inverse_kernel, radix, len(other)), in_s...  3.24 us
    ppermute x1, starting transfers between devices, on_device(): from_inside = lax.ppermute(inner, 'lat', inside)  3 us
    pallas_call x1, Pallas kernels, on_device(): pl.pallas_call(rest_kernel, in_specs=[scalars] + [in_hbm] * 3, out_specs=...  2.68 us
    pallas_call x2, Pallas kernels, run_physics(): pl.pallas_call(functools.partial(physics_kernel, levels, sector, lat_coun...  2.2 us
    unnamed x38, local copies, waits for them, and re-layouts  1.8 us
  transfers between devices with their start and end apart: 15, of which 10 were waited for; matrix products, arithmetic and copies ran while one was open for 1% of the time, Pallas kernels for 30%

profile of v8, /device:TPU:0, one launch (start us, length us, event | category | flops | bytes accessed | tf_op | source)
XLA Modules:
  0.0 46.1 jit_solution(9466957869591057343)
XLA Ops:
  0.6 1.3 %pack.1 = f32[128,1152]{1,0:T(8,128)S(1)} custom-call(s32[1]{0:T(128)} %bitcast.even_ref, f32[4,32,4,576]{3,2,1,0:T(4,128)} %tracer_hbm.5), custom_call_target="tpu_custom_call" | custom-call | bytes 600000 | tf_op jit(solution)/shard_map/pack/pallas_call | solution.py:371
  2.0 0.0 copy-start.14
  2.0 0.0 copy-start.15
  2.0 0.0 copy-start.17
  2.0 0.0 copy-start.18
  2.0 0.0 copy-start.13
  2.1 3.0 %collective-permute-start.1 = (f32[128,1152]{1,0:T(8,128)S(1)}, f32[128,1152]{1,0:T(8,128)S(1)}, u32[]{:S(2)}, u32[]{:S(2)}) collective-permute-start(f32[128,1152]{1,0:T(8,128)S(1)} %pack.1), channel_id=1, source_target_pairs={{0,2},{2,0},{4,6},{6,4},{8,10},{10,8},{12,14},{14,12},{1,3},{3,1},... | collective-permute-start | bytes 1769480 | tf_op jit(solution)/shard_map/ppermute | solution.py:381
  5.1 2.7 %rest.1 = (f32[64,1152]{1,0:T(8,128)}, f32[64,1152]{1,0:T(8,128)S(1)}, f32[16,1152]{1,0:T(8,128)S(1)}, f32[5,4,32,128]{3,2,1,0:T(8,128)S(1)}) custom-call(s32[1]{0:T(128)} %bitcast.even_ref, f32[4,32,4,576]{3,2,1,0:T(4,128)} %tracer_hbm.5, f32[32,4,576]{2,1,0:T(4,128)} %lat_hbm.3, f32[32,4,576]{2,1,0:T(4,128)} %lon_hbm.3), custom_call_target="tpu_custom_call" | custom-call | tf_op jit(solution)/shard_map/rest/pallas_call | solution.py:383
  7.8 0.0 copy-start.16
  7.8 1.4 %collective-permute-start.3 = (f32[16,1152]{1,0:T(8,128)S(1)}, f32[16,1152]{1,0:T(8,128)S(1)}, u32[]{:S(2)}, u32[]{:S(2)}) collective-permute-start(f32[16,1152]{1,0:T(8,128)S(1)} %get-tuple-element.51), channel_id=1, source_target_pairs={{2,0},{4,2},{6,4},{8,6},{10,8},{12,10},{14,12},{3,1},{5,3},{7,5},{... | collective-permute-start | bytes 221192 | tf_op jit(solution)/shard_map/ppermute | solution.py:398
  9.2 1.4 %collective-permute-start.4 = (f32[64,1152]{1,0:T(8,128)}, f32[64,1152]{1,0:T(8,128)}, u32[]{:S(2)}, u32[]{:S(2)}) collective-permute-start(f32[64,1152]{1,0:T(8,128)} %get-tuple-element.46), channel_id=1, source_target_pairs={{2,4},{4,2},{6,8},{8,6},{10,12},{12,10},{3,5},{5,3},{7,9},{9,7},{1... | collective-permute-start | bytes 884744 | tf_op jit(solution)/shard_map/ppermute | solution.py:397
  10.6 0.0 copy-done.12
  10.6 0.0 collective-permute-start
  10.7 0.1 select_multiply_fusion.refs_8_.refs_5_
  10.8 0.0 copy-done.18
  10.8 0.1 broadcast_in_dim.27
  10.9 0.1 reshape_reshape.3
  11.0 1.2 %collective-permute-done.side_ref = f32[5,4,32,128]{3,2,1,0:T(8,128)S(1)} collective-permute-done((f32[5,4,32,128]{3,2,1,0:T(8,128)S(1)}, f32[5,4,32,128]{3,2,1,0:T(8,128)S(1)}, u32[]{:S(2)}, u32[]{:S(2)}) %collective-permute-start) | collective-permute-done | bytes 327712 | tf_op jit(solution)/shard_map/ppermute | solution.py:400
  12.2 0.7 %copy-done.4 = f32[5,4,32,128]{3,2,1,0:T(8,128)} copy-done((f32[5,4,32,128]{3,2,1,0:T(8,128)}, f32[5,4,32,128]{3,2,1,0:T(8,128)S(1)}, u32[]{:S(2)}) %copy-start.4) | copy-done | bytes 327704
  13.0 1.0 %copy-done.5 = f32[5,4,32,128]{3,2,1,0:T(8,128)S(1)} copy-done((f32[5,4,32,128]{3,2,1,0:T(8,128)S(1)}, f32[5,4,32,128]{3,2,1,0:T(8,128)}, u32[]{:S(2)}) %copy-start.5) | copy-done | bytes 327704
  13.9 4.0 %base.1 = (f32[4,4,32,640]{3,2,1,0:T(8,128)S(1)}, f32[4,32,640]{2,1,0:T(8,128)S(1)}, f32[4,32,640]{2,1,0:T(8,128)S(1)}) custom-call(f32[1]{0:T(128)} %bitcast.2.not_pole_ref, f32[4,32,4,576]{3,2,1,0:T(4,128)} %tracer_hbm.5, f32[32,4,576]{2,1,0:T(4,128)} %lat_hbm.3, f32[32,4,576]{2,1,0:T(4,128)} %lon_hbm.3, f32[5,4,32,128]{3,2,1,0:T(8,128)S(1)} %copy-done.5), custom_call_target="tpu_custom_call" | custom-call | tf_op jit(solution)/shard_map/base/pallas_call | solution.py:402
  17.9 0.1 copy.22.refs_10_
  18.0 0.7 %collective-permute-start.2 = (f32[64,1152]{1,0:T(8,128)}, f32[64,1152]{1,0:T(8,128)S(1)}, u32[]{:S(2)}, u32[]{:S(2)}) collective-permute-start(f32[64,1152]{1,0:T(8,128)} %copy-done.12), channel_id=1, source_target_pairs={{2,4},{4,2},{6,8},{8,6},{10,12},{12,10},{3,5},{5,3},{7,9},{9,7},{1... | collective-permute-start | bytes 884744 | tf_op jit(solution)/shard_map/ppermute | solution.py:434
  18.7 1.2 %collective-permute-done.3.refs_6_ = f32[16,1152]{1,0:T(8,128)S(1)} collective-permute-done((f32[16,1152]{1,0:T(8,128)S(1)}, f32[16,1152]{1,0:T(8,128)S(1)}, u32[]{:S(2)}, u32[]{:S(2)}) %collective-permute-start.3) | collective-permute-done | bytes 73760 | tf_op jit(solution)/shard_map/ppermute | solution.py:398
  20.0 0.0 collective-permute-done.4.refs_5_
  20.0 5.6 %collective-permute-done.1.refs_4_ = f32[128,1152]{1,0:T(8,128)S(1)} collective-permute-done((f32[128,1152]{1,0:T(8,128)S(1)}, f32[128,1152]{1,0:T(8,128)S(1)}, u32[]{:S(2)}, u32[]{:S(2)}) %collective-permute-start.1) | collective-permute-done | bytes 589856 | tf_op jit(solution)/shard_map/ppermute | solution.py:381
  25.6 0.0 copy-start.2
  25.6 0.0 copy-start.3
  25.6 0.0 copy-start.8
  25.6 0.0 copy-start.9
  25.6 1.5 %physics.2 = (f32[4,32,640]{2,1,0:T(8,128)S(1)}, f32[4,32,640]{2,1,0:T(8,128)S(1)}, f32[4,8,640]{2,1,0:T(8,128)S(1)}) custom-call(s32[1]{0:T(128)} %bitcast.even_ref, s32[1]{0:T(128)S(6)} %sub.7.refs_0_.give_ref, s32[1]{0:T(128)} %bitcast.1.refs_1_.keep_ref, f32[4,4,32,640]{3,2,1,0:T(8,128)S(1)} %get-tuple-element.48.refs_2_, ...), custom_call_target="tpu_custom_call" | custom-call | tf_op jit(solution)/shard_map/physics/pallas_call | solution.py:445
  27.2 0.0 copy-start
  27.2 0.0 copy-start.1
  27.2 0.0 copy-start.6
  27.2 0.0 copy-start.7
  27.2 0.0 copy-start.11
  27.2 0.1 collective-permute-start.8
  27.3 0.5 %collective-permute-start.7 = (f32[1,32,640]{2,1,0:T(8,128)S(1)}, f32[1,32,640]{2,1,0:T(8,128)S(1)}, u32[]{:S(2)}, u32[]{:S(2)}) collective-permute-start(f32[1,32,640]{2,1,0:T(8,128)S(1)} %get-tuple-element.83), channel_id=1, source_target_pairs={{0,1},{1,0},{2,3},{3,2},{4,5},{5,4},{6,7},{7,6},{8,9},{9,8},{10,11... | collective-permute-start | bytes 245768 | tf_op jit(solution)/shard_map/ppermute | solution.py:488
  27.8 0.1 collective-permute-start.6
  27.9 0.4 collective-permute-start.5
  28.3 0.3 collective-permute-done.8.refs_3_
  28.6 0.2 collective-permute-done.7.refs_2_
  28.7 0.4 collective-permute-done.6.refs_1_
  29.1 0.2 collective-permute-done.5.refs_0_
  29.3 0.7 %forward.2 = (bf16[128,1152]{1,0:T(8,128)(2,1)S(1)}, bf16[128,1152]{1,0:T(8,128)(2,1)S(1)}) custom-call(f32[4,32,640]{2,1,0:T(8,128)S(1)} %get-tuple-element.57.own_ref, f32[1,32,640]{2,1,0:T(8,128)S(1)} %collective-permute-done.5.refs_0_, f32[1,32,640]{2,1,0:T(8,128)S(1)} %collective-permute-done.6.refs_1_, ...), custom_call_target="tpu_custom_call" | custom-call | tf_op jit(solution)/shard_map/forward/pallas_call | solution.py:461
  30.0 2.0 %inverse.2 = (f32[32,4,576]{2,1,0:T(4,128)S(1)}, f32[4,32,640]{2,1,0:T(8,128)}) custom-call(s32[4]{0:T(128)S(1)} %copy-done.11, f32[4,32,640]{2,1,0:T(8,128)S(1)} %get-tuple-element.57.own_ref, f32[1,32,640]{2,1,0:T(8,128)S(1)} %collective-permute-done.5.refs_0_, f32[1,32,640]{2,1,0:T(8,128)S(1)} %collective-permute-done.6.refs_1_, ...), custom_call_target="tpu_custom_call" | custom-call | tf_op jit(solution)/shard_map/inverse/pallas_call | solution.py:473
  32.0 0.0 collective-permute-done.2.refs_5_
  32.0 0.7 %physics.3 = (f32[4,32,640]{2,1,0:T(8,128)S(1)}, f32[4,32,640]{2,1,0:T(8,128)S(1)}, f32[1,128]{1,0:T(1,128)S(1)}) custom-call(s32[1]{0:T(128)} %bitcast.even_ref, s32[1]{0:T(128)S(6)} %sub.7.refs_0_.give_ref, s32[1]{0:T(128)} %bitcast.1.refs_1_.keep_ref, f32[4,4,32,640]{3,2,1,0:T(8,128)S(1)} %get-tuple-element.48.refs_2_, ...), custom_call_target="tpu_custom_call" | custom-call | tf_op jit(solution)/shard_map/physics/pallas_call | solution.py:445
  32.7 0.4 collective-permute-start.10
  33.1 2.5 %collective-permute-start.9 = (f32[1,128]{1,0:T(1,128)S(1)}, f32[1,128]{1,0:T(1,128)S(1)}, u32[]{:S(2)}, u32[]{:S(2)}) collective-permute-start(f32[1,128]{1,0:T(1,128)S(1)} %get-tuple-element.64), channel_id=1, source_target_pairs={{0,2},{2,0},{4,6},{6,4},{8,10},{10,8},{12,14},{14,12},{1,3},{3,1},... | collective-permute-start | bytes 1544 | tf_op jit(solution)/shard_map/ppermute | solution.py:499
  35.5 0.0 collective-permute-done.10.refs_0_
  35.5 0.7 %forward.3 = (bf16[128,1152]{1,0:T(8,128)(2,1)S(1)}, bf16[128,1152]{1,0:T(8,128)(2,1)S(1)}) custom-call(f32[4,32,640]{2,1,0:T(8,128)S(1)} %get-tuple-element.65.own_ref, f32[4,32,640]{2,1,0:T(8,128)S(1)} %collective-permute-done.10.refs_0_, bf16[1024,256]{1,0:T(8,128)(2,1)S(1)} %copy-done.3, bf16[1024,256]{1,0:T(8,128)(2,1)S(1)} %copy-done.2, ...), custom_call_target="tpu_custom_call" | custom-call | tf_op jit(solution)/shard_map/forward/pallas_call | solution.py:461
  36.2 0.8 %collective-permute-done.9 = f32[1,128]{1,0:T(1,128)S(1)} collective-permute-done((f32[1,128]{1,0:T(1,128)S(1)}, f32[1,128]{1,0:T(1,128)S(1)}, u32[]{:S(2)}, u32[]{:S(2)}) %collective-permute-start.9) | collective-permute-done | bytes 544 | tf_op jit(solution)/shard_map/ppermute | solution.py:499
  37.1 2.1 %collective-permute-start.11 = (f32[1,128]{1,0:T(1,128)S(1)}, f32[1,128]{1,0:T(1,128)S(1)}, u32[]{:S(2)}, u32[]{:S(2)}) collective-permute-start(f32[1,128]{1,0:T(1,128)S(1)} %add.49), channel_id=1, source_target_pairs={{0,4},{2,6},{4,0},{6,2},{8,12},{10,14},{12,8},{14,10},{1,5},{3,7},... | collective-permute-start | bytes 1544 | tf_op jit(solution)/shard_map/ppermute | solution.py:499
  39.2 0.0 collective-permute-start.13
  39.2 1.3 %inverse.3 = (f32[32,4,576]{2,1,0:T(4,128)S(1)}, f32[4,32,640]{2,1,0:T(8,128)S(1)}) custom-call(s32[4]{0:T(128)S(1)} %copy-done.11, f32[4,32,640]{2,1,0:T(8,128)S(1)} %get-tuple-element.65.own_ref, f32[4,32,640]{2,1,0:T(8,128)S(1)} %collective-permute-done.10.refs_0_, bf16[128,1152]{1,0:T(8,128)(2,1)S(1)} %get-tuple-element.71.refs_1_, ...), custom_call_target="tpu_custom_call" | custom-call | tf_op jit(solution)/shard_map/inverse/pallas_call | solution.py:473
  40.4 0.3 collective-permute-done.11
  40.7 0.3 collective-permute-start.14
  41.0 2.7 %collective-permute-start.12 = (f32[1,128]{1,0:T(1,128)S(1)}, f32[1,128]{1,0:T(1,128)S(1)}, u32[]{:S(2)}, u32[]{:S(2)}) collective-permute-start(f32[1,128]{1,0:T(1,128)S(1)} %add.50), channel_id=1, source_target_pairs={{0,8},{2,10},{4,12},{6,14},{8,0},{10,2},{12,4},{14,6},{1,9},{3,11}... | collective-permute-start | bytes 1544 | tf_op jit(solution)/shard_map/ppermute | solution.py:499
  43.7 0.0 collective-permute-done.13.refs_2_
  43.7 0.0 collective-permute-done.14.refs_3_
  43.7 1.2 %finish.1 = f32[4,32,4,576]{3,2,1,0:T(4,128)} custom-call(s32[1]{0:T(128)} %bitcast.1.refs_1_.keep_ref, s32[1]{0:T(128)S(6)} %sub.7.refs_0_.give_ref, f32[32,4,576]{2,1,0:T(4,128)S(1)} %get-tuple-element.77.refs_0_, f32[32,4,576]{2,1,0:T(4,128)S(1)} %get-tuple-element.78.refs_1_, f32[4,32,640]{2,1,0:T(8,128)S(1)} %collective-permute-done.13.refs_2_, ...), custom_call_target="tpu_custom_call" | custom-call | bytes 3000000 | tf_op jit(solution)/shard_map/finish/pallas_call | solution.py:519
  44.9 0.5 %collective-permute-done.12 = f32[1,128]{1,0:T(1,128)S(1)} collective-permute-done((f32[1,128]{1,0:T(1,128)S(1)}, f32[1,128]{1,0:T(1,128)S(1)}, u32[]{:S(2)}, u32[]{:S(2)}) %collective-permute-start.12) | collective-permute-done | bytes 544 | tf_op jit(solution)/shard_map/ppermute | solution.py:499
  45.5 0.6 %fusion.1 = f32[1,1]{1,0:T(1,128)} fusion(f32[1,128]{1,0:T(1,128)S(1)} %add.51, s32[]{:T(128)S(6)} %select_n.16), kind=kLoop, calls=%fused_computation.4 | loop fusion | flops 1 | bytes 12 | tf_op jit(solution)/shard_map/div | solution.py:537
  (27 shorter events, 0.1 us)
Async XLA Ops:
  2.0 8.7 %copy-start.14 = (f32[1152]{0:T(1024)S(1)}, f32[1152]{0:T(1024)}, u32[]{:S(2)}) copy-start(f32[1152]{0:T(1024)} %constant.73.clone) | copy-start | bytes 13828
  2.0 8.7 %copy-start.15 = (f32[1152]{0:T(1024)S(1)}, f32[1152]{0:T(1024)}, u32[]{:S(2)}) copy-start(f32[1152]{0:T(1024)} %constant.71.clone) | copy-start | bytes 13828
  2.0 8.7 %copy-start.17 = (pred[1152]{0:T(1024)(128)(4,1)S(1)}, pred[1152]{0:T(1024)(128)(4,1)}, u32[]{:S(2)}) copy-start(pred[1152]{0:T(1024)(128)(4,1)} %constant.72.clone) | copy-start | bytes 3460
  2.0 8.8 %copy-start.18 = (s32[1,1,18,1]{2,3,1,0:T(1,128)S(1)}, s32[1,1,18,1]{2,3,1,0:T(1,128)}, u32[]{:S(2)}) copy-start(s32[1,1,18,1]{2,3,1,0:T(1,128)} %param.25) | copy-start | bytes 220
  2.0 8.9 %copy-start.13 = (f32[4,4,576]{2,1,0:T(4,128)S(1)}, f32[4,4,576]{2,1,0:T(4,128)}, u32[]{:S(2)}) copy-start(f32[4,4,576]{2,1,0:T(4,128)} %param.22) | copy-start | bytes 110596
  2.1 23.5 %collective-permute-start.1 = (f32[128,1152]{1,0:T(8,128)S(1)}, f32[128,1152]{1,0:T(8,128)S(1)}, u32[]{:S(2)}, u32[]{:S(2)}) collective-permute-start(f32[128,1152]{1,0:T(8,128)S(1)} %pack.1), channel_id=1, source_target_pairs={{0,2},{2,0},{4,6},{6,4},{8,10},{10,8},{12,14},{14,12},{1,3},{3,1},... | collective-permute-start | bytes 1769480 | tf_op jit(solution)/shard_map/ppermute | solution.py:381
  7.7 2.9 %copy-start.12 = (f32[64,1152]{1,0:T(8,128)}, f32[64,1152]{1,0:T(8,128)S(1)}, u32[]{:S(2)}) copy-start(f32[64,1152]{1,0:T(8,128)S(1)} %get-tuple-element.50) | copy-start | bytes 884740
  7.8 10.2 %copy-start.16 = (f32[4,32]{1,0:T(4,128)S(1)}, f32[4,32]{1,0:T(4,128)}, u32[]{:S(2)}) copy-start(f32[4,32]{1,0:T(4,128)} %param.24) | copy-start | bytes 1540
  7.8 12.2 %collective-permute-start.3 = (f32[16,1152]{1,0:T(8,128)S(1)}, f32[16,1152]{1,0:T(8,128)S(1)}, u32[]{:S(2)}, u32[]{:S(2)}) collective-permute-start(f32[16,1152]{1,0:T(8,128)S(1)} %get-tuple-element.51), channel_id=1, source_target_pairs={{2,0},{4,2},{6,4},{8,6},{10,8},{12,10},{14,12},{3,1},{5,3},{7,5},{... | collective-permute-start | bytes 221192 | tf_op jit(solution)/shard_map/ppermute | solution.py:398
  9.2 10.8 %collective-permute-start.4 = (f32[64,1152]{1,0:T(8,128)}, f32[64,1152]{1,0:T(8,128)}, u32[]{:S(2)}, u32[]{:S(2)}) collective-permute-start(f32[64,1152]{1,0:T(8,128)} %get-tuple-element.46), channel_id=1, source_target_pairs={{2,4},{4,2},{6,8},{8,6},{10,12},{12,10},{3,5},{5,3},{7,9},{9,7},{1... | collective-permute-start | bytes 884744 | tf_op jit(solution)/shard_map/ppermute | solution.py:397
  10.6 1.6 %collective-permute-start = (f32[5,4,32,128]{3,2,1,0:T(8,128)S(1)}, f32[5,4,32,128]{3,2,1,0:T(8,128)S(1)}, u32[]{:S(2)}, u32[]{:S(2)}) collective-permute-start(f32[5,4,32,128]{3,2,1,0:T(8,128)S(1)} %get-tuple-element.43), channel_id=1, source_target_pairs={{0,1},{1,0},{2,3},{3,2},{4,5},{5,4},{6,7},{7,6},{8,9},{9,8},{10,11... | collective-permute-start | bytes 983048 | tf_op jit(solution)/shard_map/ppermute | solution.py:400
  10.8 14.8 %copy-start.10 = (f32[32,32]{1,0:T(8,128)S(1)}, f32[32,32]{1,0:T(8,128)}, u32[]{:S(2)}) copy-start(f32[32,32]{1,0:T(8,128)} %refs_9_.4) | copy-start | bytes 12292
  12.2 0.7 %copy-start.4 = (f32[5,4,32,128]{3,2,1,0:T(8,128)}, f32[5,4,32,128]{3,2,1,0:T(8,128)S(1)}, u32[]{:S(2)}) copy-start(f32[5,4,32,128]{3,2,1,0:T(8,128)S(1)} %collective-permute-done.side_ref) | copy-start | bytes 983044
  13.0 1.0 %copy-start.5 = (f32[5,4,32,128]{3,2,1,0:T(8,128)S(1)}, f32[5,4,32,128]{3,2,1,0:T(8,128)}, u32[]{:S(2)}) copy-start(f32[5,4,32,128]{3,2,1,0:T(8,128)} %copy-done.4) | copy-start | bytes 983044
  18.0 14.0 %collective-permute-start.2 = (f32[64,1152]{1,0:T(8,128)}, f32[64,1152]{1,0:T(8,128)S(1)}, u32[]{:S(2)}, u32[]{:S(2)}) collective-permute-start(f32[64,1152]{1,0:T(8,128)} %copy-done.12), channel_id=1, source_target_pairs={{2,4},{4,2},{6,8},{8,6},{10,12},{12,10},{3,5},{5,3},{7,9},{9,7},{1... | collective-permute-start | bytes 884744 | tf_op jit(solution)/shard_map/ppermute | solution.py:434
  25.6 3.7 %copy-start.2 = (bf16[1024,256]{1,0:T(8,128)(2,1)S(1)}, bf16[1024,256]{1,0:T(8,128)(2,1)}, u32[]{:S(2)}) copy-start(bf16[1024,256]{1,0:T(8,128)(2,1)} %constant.75.clone.refs_5_.refs_2_) | copy-start | bytes 1572868
  25.6 3.7 %copy-start.3 = (bf16[1024,256]{1,0:T(8,128)(2,1)S(1)}, bf16[1024,256]{1,0:T(8,128)(2,1)}, u32[]{:S(2)}) copy-start(bf16[1024,256]{1,0:T(8,128)(2,1)} %constant.74.clone.refs_4_.refs_1_) | copy-start | bytes 1572868
  25.6 3.7 %copy-start.8 = (bf16[128,128]{1,0:T(8,128)(2,1)S(1)}, bf16[128,128]{1,0:T(8,128)(2,1)}, u32[]{:S(2)}) copy-start(bf16[128,128]{1,0:T(8,128)(2,1)} %constant.77.clone.refs_7_.refs_4_) | copy-start | bytes 98308
  25.6 3.7 %copy-start.9 = (bf16[128,128]{1,0:T(8,128)(2,1)S(1)}, bf16[128,128]{1,0:T(8,128)(2,1)}, u32[]{:S(2)}) copy-start(bf16[128,128]{1,0:T(8,128)(2,1)} %constant.76.clone.refs_6_.refs_3_) | copy-start | bytes 98308
  27.2 2.8 %copy-start = (bf16[1024,256]{1,0:T(8,128)(2,1)S(1)}, bf16[1024,256]{1,0:T(8,128)(2,1)}, u32[]{:S(2)}) copy-start(bf16[1024,256]{1,0:T(8,128)(2,1)} %constant.79.clone.refs_7_.refs_4_) | copy-start | bytes 1572868
  27.2 2.8 %copy-start.1 = (bf16[1024,256]{1,0:T(8,128)(2,1)S(1)}, bf16[1024,256]{1,0:T(8,128)(2,1)}, u32[]{:S(2)}) copy-start(bf16[1024,256]{1,0:T(8,128)(2,1)} %constant.78.clone.refs_6_.refs_3_) | copy-start | bytes 1572868
  27.2 2.8 %copy-start.6 = (bf16[128,128]{1,0:T(8,128)(2,1)S(1)}, bf16[128,128]{1,0:T(8,128)(2,1)}, u32[]{:S(2)}) copy-start(bf16[128,128]{1,0:T(8,128)(2,1)} %constant.81.clone.refs_9_.refs_6_) | copy-start | bytes 98308
  27.2 2.8 %copy-start.7 = (bf16[128,128]{1,0:T(8,128)(2,1)S(1)}, bf16[128,128]{1,0:T(8,128)(2,1)}, u32[]{:S(2)}) copy-start(bf16[128,128]{1,0:T(8,128)(2,1)} %constant.80.clone.refs_8_.refs_5_) | copy-start | bytes 98308
  27.2 2.8 %copy-start.11 = (s32[4]{0:T(128)S(1)}, s32[4]{0:T(128)}, u32[]{:S(2)}) copy-start(s32[4]{0:T(128)} %mask_ref.3) | copy-start | bytes 52
  27.2 1.3 %collective-permute-start.8 = (f32[1,32,640]{2,1,0:T(8,128)S(1)}, f32[1,32,640]{2,1,0:T(8,128)S(1)}, u32[]{:S(2)}, u32[]{:S(2)}) collective-permute-start(f32[1,32,640]{2,1,0:T(8,128)S(1)} %get-tuple-element.82), channel_id=1, source_target_pairs={{0,1},{1,0},{2,3},{3,2},{4,5},{5,4},{6,7},{7,6},{8,9},{9,8},{10,11... | collective-permute-start | bytes 245768 | tf_op jit(solution)/shard_map/ppermute | solution.py:488
  27.3 1.4 %collective-permute-start.7 = (f32[1,32,640]{2,1,0:T(8,128)S(1)}, f32[1,32,640]{2,1,0:T(8,128)S(1)}, u32[]{:S(2)}, u32[]{:S(2)}) collective-permute-start(f32[1,32,640]{2,1,0:T(8,128)S(1)} %get-tuple-element.83), channel_id=1, source_target_pairs={{0,1},{1,0},{2,3},{3,2},{4,5},{5,4},{6,7},{7,6},{8,9},{9,8},{10,11... | collective-permute-start | bytes 245768 | tf_op jit(solution)/shard_map/ppermute | solution.py:488
  27.8 1.3 %collective-permute-start.6 = (f32[1,32,640]{2,1,0:T(8,128)S(1)}, f32[1,32,640]{2,1,0:T(8,128)S(1)}, u32[]{:S(2)}, u32[]{:S(2)}) collective-permute-start(f32[1,32,640]{2,1,0:T(8,128)S(1)} %get-tuple-element.84), channel_id=1, source_target_pairs={{0,1},{1,0},{2,3},{3,2},{4,5},{5,4},{6,7},{7,6},{8,9},{9,8},{10,11... | collective-permute-start | bytes 245768 | tf_op jit(solution)/shard_map/ppermute | solution.py:488
  27.9 1.4 %collective-permute-start.5 = (f32[1,32,640]{2,1,0:T(8,128)S(1)}, f32[1,32,640]{2,1,0:T(8,128)S(1)}, u32[]{:S(2)}, u32[]{:S(2)}) collective-permute-start(f32[1,32,640]{2,1,0:T(8,128)S(1)} %get-tuple-element.85), channel_id=1, source_target_pairs={{0,1},{1,0},{2,3},{3,2},{4,5},{5,4},{6,7},{7,6},{8,9},{9,8},{10,11... | collective-permute-start | bytes 245768 | tf_op jit(solution)/shard_map/ppermute | solution.py:488
  32.7 2.9 %collective-permute-start.10 = (f32[4,32,640]{2,1,0:T(8,128)S(1)}, f32[4,32,640]{2,1,0:T(8,128)S(1)}, u32[]{:S(2)}, u32[]{:S(2)}) collective-permute-start(f32[4,32,640]{2,1,0:T(8,128)S(1)} %get-tuple-element.66), channel_id=1, source_target_pairs={{0,1},{1,0},{2,3},{3,2},{4,5},{5,4},{6,7},{7,6},{8,9},{9,8},{10,11... | collective-permute-start | bytes 983048 | tf_op jit(solution)/shard_map/ppermute | solution.py:502
  33.1 4.0 %collective-permute-start.9 = (f32[1,128]{1,0:T(1,128)S(1)}, f32[1,128]{1,0:T(1,128)S(1)}, u32[]{:S(2)}, u32[]{:S(2)}) collective-permute-start(f32[1,128]{1,0:T(1,128)S(1)} %get-tuple-element.64), channel_id=1, source_target_pairs={{0,2},{2,0},{4,6},{6,4},{8,10},{10,8},{12,14},{14,12},{1,3},{3,1},... | collective-permute-start | bytes 1544 | tf_op jit(solution)/shard_map/ppermute | solution.py:499
  37.1 3.6 %collective-permute-start.11 = (f32[1,128]{1,0:T(1,128)S(1)}, f32[1,128]{1,0:T(1,128)S(1)}, u32[]{:S(2)}, u32[]{:S(2)}) collective-permute-start(f32[1,128]{1,0:T(1,128)S(1)} %add.49), channel_id=1, source_target_pairs={{0,4},{2,6},{4,0},{6,2},{8,12},{10,14},{12,8},{14,10},{1,5},{3,7},... | collective-permute-start | bytes 1544 | tf_op jit(solution)/shard_map/ppermute | solution.py:499
  39.2 4.6 %collective-permute-start.13 = (f32[4,32,640]{2,1,0:T(8,128)}, f32[4,32,640]{2,1,0:T(8,128)S(1)}, u32[]{:S(2)}, u32[]{:S(2)}) collective-permute-start(f32[4,32,640]{2,1,0:T(8,128)} %get-tuple-element.62), channel_id=1, source_target_pairs={{0,1},{1,0},{2,3},{3,2},{4,5},{5,4},{6,7},{7,6},{8,9},{9,8},{10,11... | collective-permute-start | bytes 983048 | tf_op jit(solution)/shard_map/ppermute | solution.py:492
  40.7 3.0 %collective-permute-start.14 = (f32[4,32,640]{2,1,0:T(8,128)S(1)}, f32[4,32,640]{2,1,0:T(8,128)S(1)}, u32[]{:S(2)}, u32[]{:S(2)}) collective-permute-start(f32[4,32,640]{2,1,0:T(8,128)S(1)} %get-tuple-element.79), channel_id=1, source_target_pairs={{0,1},{1,0},{2,3},{3,2},{4,5},{5,4},{6,7},{7,6},{8,9},{9,8},{10,11... | collective-permute-start | bytes 983048 | tf_op jit(solution)/shard_map/ppermute | solution.py:516
  41.0 4.4 %collective-permute-start.12 = (f32[1,128]{1,0:T(1,128)S(1)}, f32[1,128]{1,0:T(1,128)S(1)}, u32[]{:S(2)}, u32[]{:S(2)}) collective-permute-start(f32[1,128]{1,0:T(1,128)S(1)} %add.50), channel_id=1, source_target_pairs={{0,8},{2,10},{4,12},{6,14},{8,0},{10,2},{12,4},{14,6},{1,9},{3,11}... | collective-permute-start | bytes 1544 | tf_op jit(solution)/shard_map/ppermute | solution.py:499

commit v9 on v8

--- a/solution.py
+++ b/solution.py
@@ -450,7 +450,10 @@
             compiler_params=params(),
             cost_estimate=cost(0, 0),
             name="physics",
-        )(even, *firsts, base, north, from_inside, from_across[chunk], top, lat_courant, surface, mixing, decay, owner_of, energy)
+        )(
+            even, *firsts, base, north, from_inside, pltpu.with_memory_space_constraint(from_across[chunk], pltpu.VMEM), top,
+            lat_courant, surface, mixing, decay, owner_of, energy,
+        )
         return results, energy
 
     forward, inverse = ([jnp.asarray(part) for table in tables for part in split_table(table)] for tables in (forward, inverse))

time: 46.4 us -> 46.4 us (level)
  no operation moved by 1% of the time
where the time goes in v9:
time: 46.4 us; the launch traced here: 46.1 us
  Pallas kernels  16 us (34%)
  starting transfers between devices  15.6 us (34%)
  waiting for transfers between devices  10.6 us (23%)
  local copies, waits for them, and re-layouts  2.11 us (5%)
  between operations  1 us (2%)
  other arithmetic  0.72 us (2%)
    ppermute x3, starting transfers between devices, send_energy(): lax.ppermute(energy, 'lat', [(i, i ^ distance) for i in range(lat_count)])  7.31 us
    ppermute x1, waiting for transfers between devices, on_device(): from_inside = lax.ppermute(inner, 'lat', inside)  5.58 us
    pallas_call x1, Pallas kernels, on_device(): pl.pallas_call(functools.partial(base_kernel, width), in_specs=[scalars,...  3.98 us
    pallas_call x2, Pallas kernels, run_inverse(): pl.pallas_call(functools.partial(inverse_kernel, radix, len(other)), in_s...  3.24 us
    ppermute x1, starting transfers between devices, on_device(): from_inside = lax.ppermute(inner, 'lat', inside)  3 us
    pallas_call x1, Pallas kernels, on_device(): pl.pallas_call(rest_kernel, in_specs=[scalars] + [in_hbm] * 3, out_specs=...  2.68 us
    pallas_call x2, Pallas kernels, run_physics(): pl.pallas_call(functools.partial(physics_kernel, levels, sector, lat_coun...  2.2 us
    unnamed x38, local copies, waits for them, and re-layouts  1.8 us
  transfers between devices with their start and end apart: 15, of which 10 were waited for; matrix products, arithmetic and copies ran while one was open for 1% of the time, Pallas kernels for 30%

profile of v9, /device:TPU:0, one launch (start us, length us, event | category | flops | bytes accessed | tf_op | source)
XLA Modules:
  0.0 46.1 jit_solution(9466957869591057343)
XLA Ops:
  0.6 1.3 %pack.1 = f32[128,1152]{1,0:T(8,128)S(1)} custom-call(s32[1]{0:T(128)} %bitcast.even_ref, f32[4,32,4,576]{3,2,1,0:T(4,128)} %tracer_hbm.5), custom_call_target="tpu_custom_call" | custom-call | bytes 600000 | tf_op jit(solution)/shard_map/pack/pallas_call | solution.py:371
  2.0 0.0 copy-start.14
  2.0 0.0 copy-start.15
  2.0 0.0 copy-start.17
  2.0 0.0 copy-start.18
  2.0 0.0 copy-start.13
  2.1 3.0 %collective-permute-start.1 = (f32[128,1152]{1,0:T(8,128)S(1)}, f32[128,1152]{1,0:T(8,128)S(1)}, u32[]{:S(2)}, u32[]{:S(2)}) collective-permute-start(f32[128,1152]{1,0:T(8,128)S(1)} %pack.1), channel_id=1, source_target_pairs={{0,2},{2,0},{4,6},{6,4},{8,10},{10,8},{12,14},{14,12},{1,3},{3,1},... | collective-permute-start | bytes 1769480 | tf_op jit(solution)/shard_map/ppermute | solution.py:381
  5.1 2.7 %rest.1 = (f32[64,1152]{1,0:T(8,128)}, f32[64,1152]{1,0:T(8,128)S(1)}, f32[16,1152]{1,0:T(8,128)S(1)}, f32[5,4,32,128]{3,2,1,0:T(8,128)S(1)}) custom-call(s32[1]{0:T(128)} %bitcast.even_ref, f32[4,32,4,576]{3,2,1,0:T(4,128)} %tracer_hbm.5, f32[32,4,576]{2,1,0:T(4,128)} %lat_hbm.3, f32[32,4,576]{2,1,0:T(4,128)} %lon_hbm.3), custom_call_target="tpu_custom_call" | custom-call | tf_op jit(solution)/shard_map/rest/pallas_call | solution.py:383
  7.8 0.0 copy-start.16
  7.8 1.4 %collective-permute-start.3 = (f32[16,1152]{1,0:T(8,128)S(1)}, f32[16,1152]{1,0:T(8,128)S(1)}, u32[]{:S(2)}, u32[]{:S(2)}) collective-permute-start(f32[16,1152]{1,0:T(8,128)S(1)} %get-tuple-element.51), channel_id=1, source_target_pairs={{2,0},{4,2},{6,4},{8,6},{10,8},{12,10},{14,12},{3,1},{5,3},{7,5},{... | collective-permute-start | bytes 221192 | tf_op jit(solution)/shard_map/ppermute | solution.py:398
  9.2 1.4 %collective-permute-start.4 = (f32[64,1152]{1,0:T(8,128)}, f32[64,1152]{1,0:T(8,128)}, u32[]{:S(2)}, u32[]{:S(2)}) collective-permute-start(f32[64,1152]{1,0:T(8,128)} %get-tuple-element.46), channel_id=1, source_target_pairs={{2,4},{4,2},{6,8},{8,6},{10,12},{12,10},{3,5},{5,3},{7,9},{9,7},{1... | collective-permute-start | bytes 884744 | tf_op jit(solution)/shard_map/ppermute | solution.py:397
  10.6 0.0 copy-done.12
  10.6 0.0 collective-permute-start
  10.7 0.1 select_multiply_fusion.refs_8_.refs_5_
  10.8 0.0 copy-done.18
  10.8 0.1 broadcast_in_dim.27
  10.9 0.1 reshape_reshape.3
  11.0 1.2 %collective-permute-done.side_ref = f32[5,4,32,128]{3,2,1,0:T(8,128)S(1)} collective-permute-done((f32[5,4,32,128]{3,2,1,0:T(8,128)S(1)}, f32[5,4,32,128]{3,2,1,0:T(8,128)S(1)}, u32[]{:S(2)}, u32[]{:S(2)}) %collective-permute-start) | collective-permute-done | bytes 327712 | tf_op jit(solution)/shard_map/ppermute | solution.py:400
  12.2 0.7 %copy-done.4 = f32[5,4,32,128]{3,2,1,0:T(8,128)} copy-done((f32[5,4,32,128]{3,2,1,0:T(8,128)}, f32[5,4,32,128]{3,2,1,0:T(8,128)S(1)}, u32[]{:S(2)}) %copy-start.4) | copy-done | bytes 327704
  13.0 1.0 %copy-done.5 = f32[5,4,32,128]{3,2,1,0:T(8,128)S(1)} copy-done((f32[5,4,32,128]{3,2,1,0:T(8,128)S(1)}, f32[5,4,32,128]{3,2,1,0:T(8,128)}, u32[]{:S(2)}) %copy-start.5) | copy-done | bytes 327704
  13.9 4.0 %base.1 = (f32[4,4,32,640]{3,2,1,0:T(8,128)S(1)}, f32[4,32,640]{2,1,0:T(8,128)S(1)}, f32[4,32,640]{2,1,0:T(8,128)S(1)}) custom-call(f32[1]{0:T(128)} %bitcast.2.not_pole_ref, f32[4,32,4,576]{3,2,1,0:T(4,128)} %tracer_hbm.5, f32[32,4,576]{2,1,0:T(4,128)} %lat_hbm.3, f32[32,4,576]{2,1,0:T(4,128)} %lon_hbm.3, f32[5,4,32,128]{3,2,1,0:T(8,128)S(1)} %copy-done.5), custom_call_target="tpu_custom_call" | custom-call | tf_op jit(solution)/shard_map/base/pallas_call | solution.py:402
  17.9 0.1 copy.22.refs_10_
  18.0 0.7 %collective-permute-start.2 = (f32[64,1152]{1,0:T(8,128)}, f32[64,1152]{1,0:T(8,128)S(1)}, u32[]{:S(2)}, u32[]{:S(2)}) collective-permute-start(f32[64,1152]{1,0:T(8,128)} %copy-done.12), channel_id=1, source_target_pairs={{2,4},{4,2},{6,8},{8,6},{10,12},{12,10},{3,5},{5,3},{7,9},{9,7},{1... | collective-permute-start | bytes 884744 | tf_op jit(solution)/shard_map/ppermute | solution.py:434
  18.7 1.2 %collective-permute-done.3.refs_6_ = f32[16,1152]{1,0:T(8,128)S(1)} collective-permute-done((f32[16,1152]{1,0:T(8,128)S(1)}, f32[16,1152]{1,0:T(8,128)S(1)}, u32[]{:S(2)}, u32[]{:S(2)}) %collective-permute-start.3) | collective-permute-done | bytes 73760 | tf_op jit(solution)/shard_map/ppermute | solution.py:398
  20.0 0.0 collective-permute-done.4.refs_5_
  20.0 5.6 %collective-permute-done.1.refs_4_ = f32[128,1152]{1,0:T(8,128)S(1)} collective-permute-done((f32[128,1152]{1,0:T(8,128)S(1)}, f32[128,1152]{1,0:T(8,128)S(1)}, u32[]{:S(2)}, u32[]{:S(2)}) %collective-permute-start.1) | collective-permute-done | bytes 589856 | tf_op jit(solution)/shard_map/ppermute | solution.py:381
  25.6 0.0 copy-start.2
  25.6 0.0 copy-start.3
  25.6 0.0 copy-start.8
  25.6 0.0 copy-start.9
  25.6 1.5 %physics.2 = (f32[4,32,640]{2,1,0:T(8,128)S(1)}, f32[4,32,640]{2,1,0:T(8,128)S(1)}, f32[4,8,640]{2,1,0:T(8,128)S(1)}) custom-call(s32[1]{0:T(128)} %bitcast.even_ref, s32[1]{0:T(128)S(6)} %sub.7.refs_0_.give_ref, s32[1]{0:T(128)} %bitcast.1.refs_1_.keep_ref, f32[4,4,32,640]{3,2,1,0:T(8,128)S(1)} %get-tuple-element.48.refs_2_, ...), custom_call_target="tpu_custom_call" | custom-call | tf_op jit(solution)/shard_map/physics/pallas_call | solution.py:445
  27.2 0.0 copy-start
  27.2 0.0 copy-start.1
  27.2 0.0 copy-start.6
  27.2 0.0 copy-start.7
  27.2 0.0 copy-start.11
  27.2 0.1 collective-permute-start.8
  27.3 0.5 %collective-permute-start.7 = (f32[1,32,640]{2,1,0:T(8,128)S(1)}, f32[1,32,640]{2,1,0:T(8,128)S(1)}, u32[]{:S(2)}, u32[]{:S(2)}) collective-permute-start(f32[1,32,640]{2,1,0:T(8,128)S(1)} %get-tuple-element.83), channel_id=1, source_target_pairs={{0,1},{1,0},{2,3},{3,2},{4,5},{5,4},{6,7},{7,6},{8,9},{9,8},{10,11... | collective-permute-start | bytes 245768 | tf_op jit(solution)/shard_map/ppermute | solution.py:491
  27.8 0.1 collective-permute-start.6
  27.9 0.4 collective-permute-start.5
  28.3 0.3 collective-permute-done.8.refs_3_
  28.6 0.2 collective-permute-done.7.refs_2_
  28.7 0.4 collective-permute-done.6.refs_1_
  29.1 0.2 collective-permute-done.5.refs_0_
  29.3 0.7 %forward.2 = (bf16[128,1152]{1,0:T(8,128)(2,1)S(1)}, bf16[128,1152]{1,0:T(8,128)(2,1)S(1)}) custom-call(f32[4,32,640]{2,1,0:T(8,128)S(1)} %get-tuple-element.57.own_ref, f32[1,32,640]{2,1,0:T(8,128)S(1)} %collective-permute-done.5.refs_0_, f32[1,32,640]{2,1,0:T(8,128)S(1)} %collective-permute-done.6.refs_1_, ...), custom_call_target="tpu_custom_call" | custom-call | tf_op jit(solution)/shard_map/forward/pallas_call | solution.py:464
  30.0 2.0 %inverse.2 = (f32[32,4,576]{2,1,0:T(4,128)S(1)}, f32[4,32,640]{2,1,0:T(8,128)}) custom-call(s32[4]{0:T(128)S(1)} %copy-done.11, f32[4,32,640]{2,1,0:T(8,128)S(1)} %get-tuple-element.57.own_ref, f32[1,32,640]{2,1,0:T(8,128)S(1)} %collective-permute-done.5.refs_0_, f32[1,32,640]{2,1,0:T(8,128)S(1)} %collective-permute-done.6.refs_1_, ...), custom_call_target="tpu_custom_call" | custom-call | tf_op jit(solution)/shard_map/inverse/pallas_call | solution.py:476
  32.0 0.0 collective-permute-done.2.refs_5_
  32.0 0.7 %physics.3 = (f32[4,32,640]{2,1,0:T(8,128)S(1)}, f32[4,32,640]{2,1,0:T(8,128)S(1)}, f32[1,128]{1,0:T(1,128)S(1)}) custom-call(s32[1]{0:T(128)} %bitcast.even_ref, s32[1]{0:T(128)S(6)} %sub.7.refs_0_.give_ref, s32[1]{0:T(128)} %bitcast.1.refs_1_.keep_ref, f32[4,4,32,640]{3,2,1,0:T(8,128)S(1)} %get-tuple-element.48.refs_2_, ...), custom_call_target="tpu_custom_call" | custom-call | tf_op jit(solution)/shard_map/physics/pallas_call | solution.py:445
  32.7 0.4 collective-permute-start.10
  33.1 2.5 %collective-permute-start.9 = (f32[1,128]{1,0:T(1,128)S(1)}, f32[1,128]{1,0:T(1,128)S(1)}, u32[]{:S(2)}, u32[]{:S(2)}) collective-permute-start(f32[1,128]{1,0:T(1,128)S(1)} %get-tuple-element.64), channel_id=1, source_target_pairs={{0,2},{2,0},{4,6},{6,4},{8,10},{10,8},{12,14},{14,12},{1,3},{3,1},... | collective-permute-start | bytes 1544 | tf_op jit(solution)/shard_map/ppermute | solution.py:502
  35.5 0.0 collective-permute-done.10.refs_0_
  35.5 0.7 %forward.3 = (bf16[128,1152]{1,0:T(8,128)(2,1)S(1)}, bf16[128,1152]{1,0:T(8,128)(2,1)S(1)}) custom-call(f32[4,32,640]{2,1,0:T(8,128)S(1)} %get-tuple-element.65.own_ref, f32[4,32,640]{2,1,0:T(8,128)S(1)} %collective-permute-done.10.refs_0_, bf16[1024,256]{1,0:T(8,128)(2,1)S(1)} %copy-done.3, bf16[1024,256]{1,0:T(8,128)(2,1)S(1)} %copy-done.2, ...), custom_call_target="tpu_custom_call" | custom-call | tf_op jit(solution)/shard_map/forward/pallas_call | solution.py:464
  36.2 0.8 %collective-permute-done.9 = f32[1,128]{1,0:T(1,128)S(1)} collective-permute-done((f32[1,128]{1,0:T(1,128)S(1)}, f32[1,128]{1,0:T(1,128)S(1)}, u32[]{:S(2)}, u32[]{:S(2)}) %collective-permute-start.9) | collective-permute-done | bytes 544 | tf_op jit(solution)/shard_map/ppermute | solution.py:502
  37.1 2.1 %collective-permute-start.11 = (f32[1,128]{1,0:T(1,128)S(1)}, f32[1,128]{1,0:T(1,128)S(1)}, u32[]{:S(2)}, u32[]{:S(2)}) collective-permute-start(f32[1,128]{1,0:T(1,128)S(1)} %add.49), channel_id=1, source_target_pairs={{0,4},{2,6},{4,0},{6,2},{8,12},{10,14},{12,8},{14,10},{1,5},{3,7},... | collective-permute-start | bytes 1544 | tf_op jit(solution)/shard_map/ppermute | solution.py:502
  39.2 0.0 collective-permute-start.13
  39.2 1.3 %inverse.3 = (f32[32,4,576]{2,1,0:T(4,128)S(1)}, f32[4,32,640]{2,1,0:T(8,128)S(1)}) custom-call(s32[4]{0:T(128)S(1)} %copy-done.11, f32[4,32,640]{2,1,0:T(8,128)S(1)} %get-tuple-element.65.own_ref, f32[4,32,640]{2,1,0:T(8,128)S(1)} %collective-permute-done.10.refs_0_, bf16[128,1152]{1,0:T(8,128)(2,1)S(1)} %get-tuple-element.71.refs_1_, ...), custom_call_target="tpu_custom_call" | custom-call | tf_op jit(solution)/shard_map/inverse/pallas_call | solution.py:476
  40.4 0.3 collective-permute-done.11
  40.7 0.3 collective-permute-start.14
  41.0 2.7 %collective-permute-start.12 = (f32[1,128]{1,0:T(1,128)S(1)}, f32[1,128]{1,0:T(1,128)S(1)}, u32[]{:S(2)}, u32[]{:S(2)}) collective-permute-start(f32[1,128]{1,0:T(1,128)S(1)} %add.50), channel_id=1, source_target_pairs={{0,8},{2,10},{4,12},{6,14},{8,0},{10,2},{12,4},{14,6},{1,9},{3,11}... | collective-permute-start | bytes 1544 | tf_op jit(solution)/shard_map/ppermute | solution.py:502
  43.7 0.0 collective-permute-done.13.refs_2_
  43.7 0.0 collective-permute-done.14.refs_3_
  43.7 1.2 %finish.1 = f32[4,32,4,576]{3,2,1,0:T(4,128)} custom-call(s32[1]{0:T(128)} %bitcast.1.refs_1_.keep_ref, s32[1]{0:T(128)S(6)} %sub.7.refs_0_.give_ref, f32[32,4,576]{2,1,0:T(4,128)S(1)} %get-tuple-element.77.refs_0_, f32[32,4,576]{2,1,0:T(4,128)S(1)} %get-tuple-element.78.refs_1_, f32[4,32,640]{2,1,0:T(8,128)S(1)} %collective-permute-done.13.refs_2_, ...), custom_call_target="tpu_custom_call" | custom-call | bytes 3000000 | tf_op jit(solution)/shard_map/finish/pallas_call | solution.py:522
  44.9 0.5 %collective-permute-done.12 = f32[1,128]{1,0:T(1,128)S(1)} collective-permute-done((f32[1,128]{1,0:T(1,128)S(1)}, f32[1,128]{1,0:T(1,128)S(1)}, u32[]{:S(2)}, u32[]{:S(2)}) %collective-permute-start.12) | collective-permute-done | bytes 544 | tf_op jit(solution)/shard_map/ppermute | solution.py:502
  45.5 0.6 %fusion.1 = f32[1,1]{1,0:T(1,128)} fusion(f32[1,128]{1,0:T(1,128)S(1)} %add.51, s32[]{:T(128)S(6)} %select_n.16), kind=kLoop, calls=%fused_computation.4 | loop fusion | flops 1 | bytes 12 | tf_op jit(solution)/shard_map/div | solution.py:540
  (27 shorter events, 0.1 us)
Async XLA Ops:
  2.0 8.7 %copy-start.14 = (f32[1152]{0:T(1024)S(1)}, f32[1152]{0:T(1024)}, u32[]{:S(2)}) copy-start(f32[1152]{0:T(1024)} %constant.73.clone) | copy-start | bytes 13828
  2.0 8.7 %copy-start.15 = (f32[1152]{0:T(1024)S(1)}, f32[1152]{0:T(1024)}, u32[]{:S(2)}) copy-start(f32[1152]{0:T(1024)} %constant.71.clone) | copy-start | bytes 13828
  2.0 8.7 %copy-start.17 = (pred[1152]{0:T(1024)(128)(4,1)S(1)}, pred[1152]{0:T(1024)(128)(4,1)}, u32[]{:S(2)}) copy-start(pred[1152]{0:T(1024)(128)(4,1)} %constant.72.clone) | copy-start | bytes 3460
  2.0 8.8 %copy-start.18 = (s32[1,1,18,1]{2,3,1,0:T(1,128)S(1)}, s32[1,1,18,1]{2,3,1,0:T(1,128)}, u32[]{:S(2)}) copy-start(s32[1,1,18,1]{2,3,1,0:T(1,128)} %param.25) | copy-start | bytes 220
  2.0 8.9 %copy-start.13 = (f32[4,4,576]{2,1,0:T(4,128)S(1)}, f32[4,4,576]{2,1,0:T(4,128)}, u32[]{:S(2)}) copy-start(f32[4,4,576]{2,1,0:T(4,128)} %param.22) | copy-start | bytes 110596
  2.1 23.5 %collective-permute-start.1 = (f32[128,1152]{1,0:T(8,128)S(1)}, f32[128,1152]{1,0:T(8,128)S(1)}, u32[]{:S(2)}, u32[]{:S(2)}) collective-permute-start(f32[128,1152]{1,0:T(8,128)S(1)} %pack.1), channel_id=1, source_target_pairs={{0,2},{2,0},{4,6},{6,4},{8,10},{10,8},{12,14},{14,12},{1,3},{3,1},... | collective-permute-start | bytes 1769480 | tf_op jit(solution)/shard_map/ppermute | solution.py:381
  7.7 2.9 %copy-start.12 = (f32[64,1152]{1,0:T(8,128)}, f32[64,1152]{1,0:T(8,128)S(1)}, u32[]{:S(2)}) copy-start(f32[64,1152]{1,0:T(8,128)S(1)} %get-tuple-element.50) | copy-start | bytes 884740
  7.8 10.2 %copy-start.16 = (f32[4,32]{1,0:T(4,128)S(1)}, f32[4,32]{1,0:T(4,128)}, u32[]{:S(2)}) copy-start(f32[4,32]{1,0:T(4,128)} %param.24) | copy-start | bytes 1540
  7.8 12.2 %collective-permute-start.3 = (f32[16,1152]{1,0:T(8,128)S(1)}, f32[16,1152]{1,0:T(8,128)S(1)}, u32[]{:S(2)}, u32[]{:S(2)}) collective-permute-start(f32[16,1152]{1,0:T(8,128)S(1)} %get-tuple-element.51), channel_id=1, source_target_pairs={{2,0},{4,2},{6,4},{8,6},{10,8},{12,10},{14,12},{3,1},{5,3},{7,5},{... | collective-permute-start | bytes 221192 | tf_op jit(solution)/shard_map/ppermute | solution.py:398
  9.2 10.8 %collective-permute-start.4 = (f32[64,1152]{1,0:T(8,128)}, f32[64,1152]{1,0:T(8,128)}, u32[]{:S(2)}, u32[]{:S(2)}) collective-permute-start(f32[64,1152]{1,0:T(8,128)} %get-tuple-element.46), channel_id=1, source_target_pairs={{2,4},{4,2},{6,8},{8,6},{10,12},{12,10},{3,5},{5,3},{7,9},{9,7},{1... | collective-permute-start | bytes 884744 | tf_op jit(solution)/shard_map/ppermute | solution.py:397
  10.6 1.6 %collective-permute-start = (f32[5,4,32,128]{3,2,1,0:T(8,128)S(1)}, f32[5,4,32,128]{3,2,1,0:T(8,128)S(1)}, u32[]{:S(2)}, u32[]{:S(2)}) collective-permute-start(f32[5,4,32,128]{3,2,1,0:T(8,128)S(1)} %get-tuple-element.43), channel_id=1, source_target_pairs={{0,1},{1,0},{2,3},{3,2},{4,5},{5,4},{6,7},{7,6},{8,9},{9,8},{10,11... | collective-permute-start | bytes 983048 | tf_op jit(solution)/shard_map/ppermute | solution.py:400
  10.8 14.8 %copy-start.10 = (f32[32,32]{1,0:T(8,128)S(1)}, f32[32,32]{1,0:T(8,128)}, u32[]{:S(2)}) copy-start(f32[32,32]{1,0:T(8,128)} %refs_9_.4) | copy-start | bytes 12292
  12.2 0.7 %copy-start.4 = (f32[5,4,32,128]{3,2,1,0:T(8,128)}, f32[5,4,32,128]{3,2,1,0:T(8,128)S(1)}, u32[]{:S(2)}) copy-start(f32[5,4,32,128]{3,2,1,0:T(8,128)S(1)} %collective-permute-done.side_ref) | copy-start | bytes 983044
  13.0 1.0 %copy-start.5 = (f32[5,4,32,128]{3,2,1,0:T(8,128)S(1)}, f32[5,4,32,128]{3,2,1,0:T(8,128)}, u32[]{:S(2)}) copy-start(f32[5,4,32,128]{3,2,1,0:T(8,128)} %copy-done.4) | copy-start | bytes 983044
  18.0 14.0 %collective-permute-start.2 = (f32[64,1152]{1,0:T(8,128)}, f32[64,1152]{1,0:T(8,128)S(1)}, u32[]{:S(2)}, u32[]{:S(2)}) collective-permute-start(f32[64,1152]{1,0:T(8,128)} %copy-done.12), channel_id=1, source_target_pairs={{2,4},{4,2},{6,8},{8,6},{10,12},{12,10},{3,5},{5,3},{7,9},{9,7},{1... | collective-permute-start | bytes 884744 | tf_op jit(solution)/shard_map/ppermute | solution.py:434
  25.6 3.7 %copy-start.2 = (bf16[1024,256]{1,0:T(8,128)(2,1)S(1)}, bf16[1024,256]{1,0:T(8,128)(2,1)}, u32[]{:S(2)}) copy-start(bf16[1024,256]{1,0:T(8,128)(2,1)} %constant.75.clone.refs_5_.refs_2_) | copy-start | bytes 1572868
  25.6 3.7 %copy-start.3 = (bf16[1024,256]{1,0:T(8,128)(2,1)S(1)}, bf16[1024,256]{1,0:T(8,128)(2,1)}, u32[]{:S(2)}) copy-start(bf16[1024,256]{1,0:T(8,128)(2,1)} %constant.74.clone.refs_4_.refs_1_) | copy-start | bytes 1572868
  25.6 3.7 %copy-start.8 = (bf16[128,128]{1,0:T(8,128)(2,1)S(1)}, bf16[128,128]{1,0:T(8,128)(2,1)}, u32[]{:S(2)}) copy-start(bf16[128,128]{1,0:T(8,128)(2,1)} %constant.77.clone.refs_7_.refs_4_) | copy-start | bytes 98308
  25.6 3.7 %copy-start.9 = (bf16[128,128]{1,0:T(8,128)(2,1)S(1)}, bf16[128,128]{1,0:T(8,128)(2,1)}, u32[]{:S(2)}) copy-start(bf16[128,128]{1,0:T(8,128)(2,1)} %constant.76.clone.refs_6_.refs_3_) | copy-start | bytes 98308
  27.2 2.8 %copy-start = (bf16[1024,256]{1,0:T(8,128)(2,1)S(1)}, bf16[1024,256]{1,0:T(8,128)(2,1)}, u32[]{:S(2)}) copy-start(bf16[1024,256]{1,0:T(8,128)(2,1)} %constant.79.clone.refs_7_.refs_4_) | copy-start | bytes 1572868
  27.2 2.8 %copy-start.1 = (bf16[1024,256]{1,0:T(8,128)(2,1)S(1)}, bf16[1024,256]{1,0:T(8,128)(2,1)}, u32[]{:S(2)}) copy-start(bf16[1024,256]{1,0:T(8,128)(2,1)} %constant.78.clone.refs_6_.refs_3_) | copy-start | bytes 1572868
  27.2 2.8 %copy-start.6 = (bf16[128,128]{1,0:T(8,128)(2,1)S(1)}, bf16[128,128]{1,0:T(8,128)(2,1)}, u32[]{:S(2)}) copy-start(bf16[128,128]{1,0:T(8,128)(2,1)} %constant.81.clone.refs_9_.refs_6_) | copy-start | bytes 98308
  27.2 2.8 %copy-start.7 = (bf16[128,128]{1,0:T(8,128)(2,1)S(1)}, bf16[128,128]{1,0:T(8,128)(2,1)}, u32[]{:S(2)}) copy-start(bf16[128,128]{1,0:T(8,128)(2,1)} %constant.80.clone.refs_8_.refs_5_) | copy-start | bytes 98308
  27.2 2.8 %copy-start.11 = (s32[4]{0:T(128)S(1)}, s32[4]{0:T(128)}, u32[]{:S(2)}) copy-start(s32[4]{0:T(128)} %mask_ref.3) | copy-start | bytes 52
  27.2 1.3 %collective-permute-start.8 = (f32[1,32,640]{2,1,0:T(8,128)S(1)}, f32[1,32,640]{2,1,0:T(8,128)S(1)}, u32[]{:S(2)}, u32[]{:S(2)}) collective-permute-start(f32[1,32,640]{2,1,0:T(8,128)S(1)} %get-tuple-element.82), channel_id=1, source_target_pairs={{0,1},{1,0},{2,3},{3,2},{4,5},{5,4},{6,7},{7,6},{8,9},{9,8},{10,11... | collective-permute-start | bytes 245768 | tf_op jit(solution)/shard_map/ppermute | solution.py:491
  27.3 1.4 %collective-permute-start.7 = (f32[1,32,640]{2,1,0:T(8,128)S(1)}, f32[1,32,640]{2,1,0:T(8,128)S(1)}, u32[]{:S(2)}, u32[]{:S(2)}) collective-permute-start(f32[1,32,640]{2,1,0:T(8,128)S(1)} %get-tuple-element.83), channel_id=1, source_target_pairs={{0,1},{1,0},{2,3},{3,2},{4,5},{5,4},{6,7},{7,6},{8,9},{9,8},{10,11... | collective-permute-start | bytes 245768 | tf_op jit(solution)/shard_map/ppermute | solution.py:491
  27.8 1.3 %collective-permute-start.6 = (f32[1,32,640]{2,1,0:T(8,128)S(1)}, f32[1,32,640]{2,1,0:T(8,128)S(1)}, u32[]{:S(2)}, u32[]{:S(2)}) collective-permute-start(f32[1,32,640]{2,1,0:T(8,128)S(1)} %get-tuple-element.84), channel_id=1, source_target_pairs={{0,1},{1,0},{2,3},{3,2},{4,5},{5,4},{6,7},{7,6},{8,9},{9,8},{10,11... | collective-permute-start | bytes 245768 | tf_op jit(solution)/shard_map/ppermute | solution.py:491
  27.9 1.4 %collective-permute-start.5 = (f32[1,32,640]{2,1,0:T(8,128)S(1)}, f32[1,32,640]{2,1,0:T(8,128)S(1)}, u32[]{:S(2)}, u32[]{:S(2)}) collective-permute-start(f32[1,32,640]{2,1,0:T(8,128)S(1)} %get-tuple-element.85), channel_id=1, source_target_pairs={{0,1},{1,0},{2,3},{3,2},{4,5},{5,4},{6,7},{7,6},{8,9},{9,8},{10,11... | collective-permute-start | bytes 245768 | tf_op jit(solution)/shard_map/ppermute | solution.py:491
  32.7 2.9 %collective-permute-start.10 = (f32[4,32,640]{2,1,0:T(8,128)S(1)}, f32[4,32,640]{2,1,0:T(8,128)S(1)}, u32[]{:S(2)}, u32[]{:S(2)}) collective-permute-start(f32[4,32,640]{2,1,0:T(8,128)S(1)} %get-tuple-element.66), channel_id=1, source_target_pairs={{0,1},{1,0},{2,3},{3,2},{4,5},{5,4},{6,7},{7,6},{8,9},{9,8},{10,11... | collective-permute-start | bytes 983048 | tf_op jit(solution)/shard_map/ppermute | solution.py:505
  33.1 4.0 %collective-permute-start.9 = (f32[1,128]{1,0:T(1,128)S(1)}, f32[1,128]{1,0:T(1,128)S(1)}, u32[]{:S(2)}, u32[]{:S(2)}) collective-permute-start(f32[1,128]{1,0:T(1,128)S(1)} %get-tuple-element.64), channel_id=1, source_target_pairs={{0,2},{2,0},{4,6},{6,4},{8,10},{10,8},{12,14},{14,12},{1,3},{3,1},... | collective-permute-start | bytes 1544 | tf_op jit(solution)/shard_map/ppermute | solution.py:502
  37.1 3.6 %collective-permute-start.11 = (f32[1,128]{1,0:T(1,128)S(1)}, f32[1,128]{1,0:T(1,128)S(1)}, u32[]{:S(2)}, u32[]{:S(2)}) collective-permute-start(f32[1,128]{1,0:T(1,128)S(1)} %add.49), channel_id=1, source_target_pairs={{0,4},{2,6},{4,0},{6,2},{8,12},{10,14},{12,8},{14,10},{1,5},{3,7},... | collective-permute-start | bytes 1544 | tf_op jit(solution)/shard_map/ppermute | solution.py:502
  39.2 4.6 %collective-permute-start.13 = (f32[4,32,640]{2,1,0:T(8,128)}, f32[4,32,640]{2,1,0:T(8,128)S(1)}, u32[]{:S(2)}, u32[]{:S(2)}) collective-permute-start(f32[4,32,640]{2,1,0:T(8,128)} %get-tuple-element.62), channel_id=1, source_target_pairs={{0,1},{1,0},{2,3},{3,2},{4,5},{5,4},{6,7},{7,6},{8,9},{9,8},{10,11... | collective-permute-start | bytes 983048 | tf_op jit(solution)/shard_map/ppermute | solution.py:495
  40.7 3.0 %collective-permute-start.14 = (f32[4,32,640]{2,1,0:T(8,128)S(1)}, f32[4,32,640]{2,1,0:T(8,128)S(1)}, u32[]{:S(2)}, u32[]{:S(2)}) collective-permute-start(f32[4,32,640]{2,1,0:T(8,128)S(1)} %get-tuple-element.79), channel_id=1, source_target_pairs={{0,1},{1,0},{2,3},{3,2},{4,5},{5,4},{6,7},{7,6},{8,9},{9,8},{10,11... | collective-permute-start | bytes 983048 | tf_op jit(solution)/shard_map/ppermute | solution.py:519
  41.0 4.4 %collective-permute-start.12 = (f32[1,128]{1,0:T(1,128)S(1)}, f32[1,128]{1,0:T(1,128)S(1)}, u32[]{:S(2)}, u32[]{:S(2)}) collective-permute-start(f32[1,128]{1,0:T(1,128)S(1)} %add.50), channel_id=1, source_target_pairs={{0,8},{2,10},{4,12},{6,14},{8,0},{10,2},{12,4},{14,6},{1,9},{3,11}... | collective-permute-start | bytes 1544 | tf_op jit(solution)/shard_map/ppermute | solution.py:502

commit v10 on v8

--- a/solution.py
+++ b/solution.py
@@ -225,7 +225,8 @@
 
 
 def row_of(piece_refs, r):
-    return piece_refs[0].at[r] if len(piece_refs) == 1 else piece_refs[r].at[0]
+    share = piece_refs[0].shape[0]
+    return piece_refs[r // share].at[r % share]
 
 
 def stacked_table(high_ref, low_ref, begin, size):
@@ -485,7 +486,7 @@
     results, received = [], []
     for chunk in range(half - 1):
         (given, own), energy = run_physics(chunk, [give, keep], energy)
-        other = [lax.ppermute(given[r : r + 1], "lon", swap) for r in range(rows)]
+        other = [lax.ppermute(given[r : r + 2], "lon", swap) for r in range(0, rows, 2)]
         spectrum = run_forward(own, other)
         result, back = run_inverse(own, other, *spectrum)
         results.append(result)

time: 46.4 us -> 46.3 us (level)
    ppermute x4 -> x2, starting transfers between devices: 1.08 us -> 0.57 us  [on_device(): lax.ppermute(given[r:r + 2], 'lon', swap)]
    ppermute x4 -> x2, waiting for transfers between devices: 0.92 us -> 1.12 us  [on_device(): lax.ppermute(given[r:r + 2], 'lon', swap)]
  transfers between devices with their start and end apart: 15 -> 13, of which waited for: 10 -> 8; matrix products, arithmetic and copies ran while one was open for 1% -> 1% of each run, Pallas kernels for 30% -> 30%
where the time goes in v10:
time: 46.3 us; the launch traced here: 46 us
  Pallas kernels  16 us (35%)
  starting transfers between devices  15.3 us (33%)
  waiting for transfers between devices  10.8 us (23%)
  local copies, waits for them, and re-layouts  2.11 us (5%)
  between operations  1 us (2%)
  other arithmetic  0.72 us (2%)
    ppermute x3, starting transfers between devices, send_energy(): lax.ppermute(energy, 'lat', [(i, i ^ distance) for i in range(lat_count)])  7.62 us
    ppermute x1, waiting for transfers between devices, on_device(): from_inside = lax.ppermute(inner, 'lat', inside)  5.58 us
    pallas_call x1, Pallas kernels, on_device(): pl.pallas_call(functools.partial(base_kernel, width), in_specs=[scalars,...  3.98 us
    pallas_call x2, Pallas kernels, run_inverse(): pl.pallas_call(functools.partial(inverse_kernel, radix, len(other)), in_s...  3.23 us
    ppermute x1, starting transfers between devices, on_device(): from_inside = lax.ppermute(inner, 'lat', inside)  3 us
    pallas_call x1, Pallas kernels, on_device(): pl.pallas_call(rest_kernel, in_specs=[scalars] + [in_hbm] * 3, out_specs=...  2.67 us
    pallas_call x2, Pallas kernels, run_physics(): pl.pallas_call(functools.partial(physics_kernel, levels, sector, lat_coun...  2.2 us
    unnamed x38, local copies, waits for them, and re-layouts  1.8 us
  transfers between devices with their start and end apart: 13, of which 8 were waited for; matrix products, arithmetic and copies ran while one was open for 1% of the time, Pallas kernels for 30%

profile of v10, /device:TPU:0, one launch (start us, length us, event | category | flops | bytes accessed | tf_op | source)
XLA Modules:
  0.0 46.0 jit_solution(1927291555309783810)
XLA Ops:
  0.6 1.3 %pack.1 = f32[128,1152]{1,0:T(8,128)S(1)} custom-call(s32[1]{0:T(128)} %bitcast.even_ref, f32[4,32,4,576]{3,2,1,0:T(4,128)} %tracer_hbm.5), custom_call_target="tpu_custom_call" | custom-call | bytes 600000 | tf_op jit(solution)/shard_map/pack/pallas_call | solution.py:372
  2.0 0.0 copy-start.14
  2.0 0.0 copy-start.15
  2.0 0.0 copy-start.17
  2.0 0.0 copy-start.18
  2.0 0.0 copy-start.13
  2.1 3.0 %collective-permute-start.1 = (f32[128,1152]{1,0:T(8,128)S(1)}, f32[128,1152]{1,0:T(8,128)S(1)}, u32[]{:S(2)}, u32[]{:S(2)}) collective-permute-start(f32[128,1152]{1,0:T(8,128)S(1)} %pack.1), channel_id=1, source_target_pairs={{0,2},{2,0},{4,6},{6,4},{8,10},{10,8},{12,14},{14,12},{1,3},{3,1},... | collective-permute-start | bytes 1769480 | tf_op jit(solution)/shard_map/ppermute | solution.py:382
  5.1 2.7 %rest.1 = (f32[64,1152]{1,0:T(8,128)}, f32[64,1152]{1,0:T(8,128)S(1)}, f32[16,1152]{1,0:T(8,128)S(1)}, f32[5,4,32,128]{3,2,1,0:T(8,128)S(1)}) custom-call(s32[1]{0:T(128)} %bitcast.even_ref, f32[4,32,4,576]{3,2,1,0:T(4,128)} %tracer_hbm.5, f32[32,4,576]{2,1,0:T(4,128)} %lat_hbm.3, f32[32,4,576]{2,1,0:T(4,128)} %lon_hbm.3), custom_call_target="tpu_custom_call" | custom-call | tf_op jit(solution)/shard_map/rest/pallas_call | solution.py:384
  7.8 0.0 copy-start.16
  7.8 1.4 %collective-permute-start.3 = (f32[16,1152]{1,0:T(8,128)S(1)}, f32[16,1152]{1,0:T(8,128)S(1)}, u32[]{:S(2)}, u32[]{:S(2)}) collective-permute-start(f32[16,1152]{1,0:T(8,128)S(1)} %get-tuple-element.51), channel_id=1, source_target_pairs={{2,0},{4,2},{6,4},{8,6},{10,8},{12,10},{14,12},{3,1},{5,3},{7,5},{... | collective-permute-start | bytes 221192 | tf_op jit(solution)/shard_map/ppermute | solution.py:399
  9.2 1.4 %collective-permute-start.4 = (f32[64,1152]{1,0:T(8,128)}, f32[64,1152]{1,0:T(8,128)}, u32[]{:S(2)}, u32[]{:S(2)}) collective-permute-start(f32[64,1152]{1,0:T(8,128)} %get-tuple-element.46), channel_id=1, source_target_pairs={{2,4},{4,2},{6,8},{8,6},{10,12},{12,10},{3,5},{5,3},{7,9},{9,7},{1... | collective-permute-start | bytes 884744 | tf_op jit(solution)/shard_map/ppermute | solution.py:398
  10.6 0.0 collective-permute-start
  10.7 0.1 select_multiply_fusion.refs_6_.refs_5_
  10.8 0.0 copy-done.18
  10.8 0.1 broadcast_in_dim.27
  10.9 0.1 reshape_reshape.3
  11.0 1.2 %collective-permute-done.side_ref = f32[5,4,32,128]{3,2,1,0:T(8,128)S(1)} collective-permute-done((f32[5,4,32,128]{3,2,1,0:T(8,128)S(1)}, f32[5,4,32,128]{3,2,1,0:T(8,128)S(1)}, u32[]{:S(2)}, u32[]{:S(2)}) %collective-permute-start) | collective-permute-done | bytes 327712 | tf_op jit(solution)/shard_map/ppermute | solution.py:401
  12.2 0.7 %copy-done.4 = f32[5,4,32,128]{3,2,1,0:T(8,128)} copy-done((f32[5,4,32,128]{3,2,1,0:T(8,128)}, f32[5,4,32,128]{3,2,1,0:T(8,128)S(1)}, u32[]{:S(2)}) %copy-start.4) | copy-done | bytes 327704
  13.0 1.0 %copy-done.5 = f32[5,4,32,128]{3,2,1,0:T(8,128)S(1)} copy-done((f32[5,4,32,128]{3,2,1,0:T(8,128)S(1)}, f32[5,4,32,128]{3,2,1,0:T(8,128)}, u32[]{:S(2)}) %copy-start.5) | copy-done | bytes 327704
  13.9 4.0 %base.1 = (f32[4,4,32,640]{3,2,1,0:T(8,128)S(1)}, f32[4,32,640]{2,1,0:T(8,128)S(1)}, f32[4,32,640]{2,1,0:T(8,128)S(1)}) custom-call(f32[1]{0:T(128)} %bitcast.2.not_pole_ref, f32[4,32,4,576]{3,2,1,0:T(4,128)} %tracer_hbm.5, f32[32,4,576]{2,1,0:T(4,128)} %lat_hbm.3, f32[32,4,576]{2,1,0:T(4,128)} %lon_hbm.3, f32[5,4,32,128]{3,2,1,0:T(8,128)S(1)} %copy-done.5), custom_call_target="tpu_custom_call" | custom-call | tf_op jit(solution)/shard_map/base/pallas_call | solution.py:403
  17.9 0.1 copy.22.refs_10_
  18.0 0.7 %collective-permute-start.2 = (f32[64,1152]{1,0:T(8,128)}, f32[64,1152]{1,0:T(8,128)S(1)}, u32[]{:S(2)}, u32[]{:S(2)}) collective-permute-start(f32[64,1152]{1,0:T(8,128)} %copy-done.12), channel_id=1, source_target_pairs={{2,4},{4,2},{6,8},{8,6},{10,12},{12,10},{3,5},{5,3},{7,9},{9,7},{1... | collective-permute-start | bytes 884744 | tf_op jit(solution)/shard_map/ppermute | solution.py:435
  18.7 1.3 %collective-permute-done.3.refs_6_ = f32[16,1152]{1,0:T(8,128)S(1)} collective-permute-done((f32[16,1152]{1,0:T(8,128)S(1)}, f32[16,1152]{1,0:T(8,128)S(1)}, u32[]{:S(2)}, u32[]{:S(2)}) %collective-permute-start.3) | collective-permute-done | bytes 73760 | tf_op jit(solution)/shard_map/ppermute | solution.py:399
  20.0 0.0 collective-permute-done.4.refs_5_
  20.0 5.6 %collective-permute-done.1.refs_4_ = f32[128,1152]{1,0:T(8,128)S(1)} collective-permute-done((f32[128,1152]{1,0:T(8,128)S(1)}, f32[128,1152]{1,0:T(8,128)S(1)}, u32[]{:S(2)}, u32[]{:S(2)}) %collective-permute-start.1) | collective-permute-done | bytes 589856 | tf_op jit(solution)/shard_map/ppermute | solution.py:382
  25.6 0.0 copy-done.10
  25.6 0.0 copy-start.2
  25.6 0.0 copy-start.3
  25.6 0.0 copy-start.8
  25.6 0.0 copy-start.9
  25.6 1.5 %physics.2 = (f32[4,32,640]{2,1,0:T(8,128)S(1)}, f32[4,32,640]{2,1,0:T(8,128)S(1)}, f32[4,8,640]{2,1,0:T(8,128)S(1)}) custom-call(s32[1]{0:T(128)} %bitcast.even_ref, s32[1]{0:T(128)S(6)} %sub.7.refs_0_.give_ref, s32[1]{0:T(128)} %bitcast.1.refs_1_.keep_ref, f32[4,4,32,640]{3,2,1,0:T(8,128)S(1)} %get-tuple-element.48.refs_2_, ...), custom_call_target="tpu_custom_call" | custom-call | tf_op jit(solution)/shard_map/physics/pallas_call | solution.py:446
  27.2 0.0 copy-start
  27.2 0.0 copy-start.1
  27.2 0.0 copy-start.6
  27.2 0.0 copy-start.7
  27.2 0.0 copy-start.11
  27.2 0.1 collective-permute-start.6
  27.3 0.5 %collective-permute-start.5 = (f32[2,32,640]{2,1,0:T(8,128)S(1)}, f32[2,32,640]{2,1,0:T(8,128)S(1)}, u32[]{:S(2)}, u32[]{:S(2)}) collective-permute-start(f32[2,32,640]{2,1,0:T(8,128)S(1)} %get-tuple-element.83), channel_id=1, source_target_pairs={{0,1},{1,0},{2,3},{3,2},{4,5},{5,4},{6,7},{7,6},{8,9},{9,8},{10,11... | collective-permute-start | bytes 491528 | tf_op jit(solution)/shard_map/ppermute | solution.py:489
  27.8 0.9 %collective-permute-done.6.refs_1_ = f32[2,32,640]{2,1,0:T(8,128)S(1)} collective-permute-done((f32[2,32,640]{2,1,0:T(8,128)S(1)}, f32[2,32,640]{2,1,0:T(8,128)S(1)}, u32[]{:S(2)}, u32[]{:S(2)}) %collective-permute-start.6) | collective-permute-done | bytes 163872 | tf_op jit(solution)/shard_map/ppermute | solution.py:489
  28.7 0.2 collective-permute-done.5.refs_0_
  29.0 0.0 copy-done.9
  29.0 0.7 %forward.2 = (bf16[128,1152]{1,0:T(8,128)(2,1)S(1)}, bf16[128,1152]{1,0:T(8,128)(2,1)S(1)}) custom-call(f32[4,32,640]{2,1,0:T(8,128)S(1)} %get-tuple-element.57.own_ref, f32[2,32,640]{2,1,0:T(8,128)S(1)} %collective-permute-done.5.refs_0_, f32[2,32,640]{2,1,0:T(8,128)S(1)} %collective-permute-done.6.refs_1_, bf16[1024,256]{1,0:T(8,128)(2,1)S(1)} %copy-done.3, ...), custom_call_target="tpu_custom_call" | custom-call | tf_op jit(solution)/shard_map/forward/pallas_call | solution.py:462
  29.7 0.0 copy-done
  29.7 0.0 copy-done.1
  29.7 0.0 copy-done.6
  29.7 2.0 %inverse.2 = (f32[32,4,576]{2,1,0:T(4,128)S(1)}, f32[4,32,640]{2,1,0:T(8,128)}) custom-call(s32[4]{0:T(128)S(1)} %copy-done.11, f32[4,32,640]{2,1,0:T(8,128)S(1)} %get-tuple-element.57.own_ref, f32[2,32,640]{2,1,0:T(8,128)S(1)} %collective-permute-done.5.refs_0_, f32[2,32,640]{2,1,0:T(8,128)S(1)} %collective-permute-done.6.refs_1_, ...), custom_call_target="tpu_custom_call" | custom-call | tf_op jit(solution)/shard_map/inverse/pallas_call | solution.py:474
  31.7 0.0 collective-permute-done.2.refs_5_
  31.7 0.7 %physics.3 = (f32[4,32,640]{2,1,0:T(8,128)S(1)}, f32[4,32,640]{2,1,0:T(8,128)S(1)}, f32[1,128]{1,0:T(1,128)S(1)}) custom-call(s32[1]{0:T(128)} %bitcast.even_ref, s32[1]{0:T(128)S(6)} %sub.7.refs_0_.give_ref, s32[1]{0:T(128)} %bitcast.1.refs_1_.keep_ref, f32[4,4,32,640]{3,2,1,0:T(8,128)S(1)} %get-tuple-element.48.refs_2_, ...), custom_call_target="tpu_custom_call" | custom-call | tf_op jit(solution)/shard_map/physics/pallas_call | solution.py:446
  32.3 0.3 collective-permute-start.8
  32.6 2.5 %collective-permute-start.7 = (f32[1,128]{1,0:T(1,128)S(1)}, f32[1,128]{1,0:T(1,128)S(1)}, u32[]{:S(2)}, u32[]{:S(2)}) collective-permute-start(f32[1,128]{1,0:T(1,128)S(1)} %get-tuple-element.64), channel_id=1, source_target_pairs={{0,2},{2,0},{4,6},{6,4},{8,10},{10,8},{12,14},{14,12},{1,3},{3,1},... | collective-permute-start | bytes 1544 | tf_op jit(solution)/shard_map/ppermute | solution.py:500
  35.1 0.0 collective-permute-done.8.refs_0_
  35.1 0.7 %forward.3 = (bf16[128,1152]{1,0:T(8,128)(2,1)S(1)}, bf16[128,1152]{1,0:T(8,128)(2,1)S(1)}) custom-call(f32[4,32,640]{2,1,0:T(8,128)S(1)} %get-tuple-element.65.own_ref, f32[4,32,640]{2,1,0:T(8,128)S(1)} %collective-permute-done.8.refs_0_, bf16[1024,256]{1,0:T(8,128)(2,1)S(1)} %copy-done.3, bf16[1024,256]{1,0:T(8,128)(2,1)S(1)} %copy-done.2, ...), custom_call_target="tpu_custom_call" | custom-call | tf_op jit(solution)/shard_map/forward/pallas_call | solution.py:462
  35.8 0.8 %collective-permute-done.7 = f32[1,128]{1,0:T(1,128)S(1)} collective-permute-done((f32[1,128]{1,0:T(1,128)S(1)}, f32[1,128]{1,0:T(1,128)S(1)}, u32[]{:S(2)}, u32[]{:S(2)}) %collective-permute-start.7) | collective-permute-done | bytes 544 | tf_op jit(solution)/shard_map/ppermute | solution.py:500
  36.7 2.4 %collective-permute-start.9 = (f32[1,128]{1,0:T(1,128)S(1)}, f32[1,128]{1,0:T(1,128)S(1)}, u32[]{:S(2)}, u32[]{:S(2)}) collective-permute-start(f32[1,128]{1,0:T(1,128)S(1)} %add.49), channel_id=1, source_target_pairs={{0,4},{2,6},{4,0},{6,2},{8,12},{10,14},{12,8},{14,10},{1,5},{3,7},... | collective-permute-start | bytes 1544 | tf_op jit(solution)/shard_map/ppermute | solution.py:500
  39.1 0.0 collective-permute-start.11
  39.1 1.3 %inverse.3 = (f32[32,4,576]{2,1,0:T(4,128)S(1)}, f32[4,32,640]{2,1,0:T(8,128)S(1)}) custom-call(s32[4]{0:T(128)S(1)} %copy-done.11, f32[4,32,640]{2,1,0:T(8,128)S(1)} %get-tuple-element.65.own_ref, f32[4,32,640]{2,1,0:T(8,128)S(1)} %collective-permute-done.8.refs_0_, bf16[128,1152]{1,0:T(8,128)(2,1)S(1)} %get-tuple-element.71.refs_1_, ...), custom_call_target="tpu_custom_call" | custom-call | tf_op jit(solution)/shard_map/inverse/pallas_call | solution.py:474
  40.3 0.3 collective-permute-done.9
  40.6 0.3 collective-permute-start.12
  40.9 2.7 %collective-permute-start.10 = (f32[1,128]{1,0:T(1,128)S(1)}, f32[1,128]{1,0:T(1,128)S(1)}, u32[]{:S(2)}, u32[]{:S(2)}) collective-permute-start(f32[1,128]{1,0:T(1,128)S(1)} %add.50), channel_id=1, source_target_pairs={{0,8},{2,10},{4,12},{6,14},{8,0},{10,2},{12,4},{14,6},{1,9},{3,11}... | collective-permute-start | bytes 1544 | tf_op jit(solution)/shard_map/ppermute | solution.py:500
  43.6 0.0 collective-permute-done.11.refs_2_
  43.6 0.0 collective-permute-done.12.refs_3_
  43.6 1.2 %finish.1 = f32[4,32,4,576]{3,2,1,0:T(4,128)} custom-call(s32[1]{0:T(128)} %bitcast.1.refs_1_.keep_ref, s32[1]{0:T(128)S(6)} %sub.7.refs_0_.give_ref, f32[32,4,576]{2,1,0:T(4,128)S(1)} %get-tuple-element.77.refs_0_, f32[32,4,576]{2,1,0:T(4,128)S(1)} %get-tuple-element.78.refs_1_, f32[4,32,640]{2,1,0:T(8,128)S(1)} %collective-permute-done.11.refs_2_, ...), custom_call_target="tpu_custom_call" | custom-call | bytes 3000000 | tf_op jit(solution)/shard_map/finish/pallas_call | solution.py:520
  44.8 0.5 %collective-permute-done.10 = f32[1,128]{1,0:T(1,128)S(1)} collective-permute-done((f32[1,128]{1,0:T(1,128)S(1)}, f32[1,128]{1,0:T(1,128)S(1)}, u32[]{:S(2)}, u32[]{:S(2)}) %collective-permute-start.10) | collective-permute-done | bytes 544 | tf_op jit(solution)/shard_map/ppermute | solution.py:500
  45.4 0.6 %fusion.1 = f32[1,1]{1,0:T(1,128)} fusion(f32[1,128]{1,0:T(1,128)S(1)} %add.51, s32[]{:T(128)S(6)} %select_n.16), kind=kLoop, calls=%fused_computation.4 | loop fusion | flops 1 | bytes 12 | tf_op jit(solution)/shard_map/div | solution.py:538
  (23 shorter events, 0.1 us)
Async XLA Ops:
  2.0 8.7 %copy-start.14 = (f32[1152]{0:T(1024)S(1)}, f32[1152]{0:T(1024)}, u32[]{:S(2)}) copy-start(f32[1152]{0:T(1024)} %constant.73.clone) | copy-start | bytes 13828
  2.0 8.7 %copy-start.15 = (f32[1152]{0:T(1024)S(1)}, f32[1152]{0:T(1024)}, u32[]{:S(2)}) copy-start(f32[1152]{0:T(1024)} %constant.71.clone) | copy-start | bytes 13828
  2.0 8.7 %copy-start.17 = (pred[1152]{0:T(1024)(128)(4,1)S(1)}, pred[1152]{0:T(1024)(128)(4,1)}, u32[]{:S(2)}) copy-start(pred[1152]{0:T(1024)(128)(4,1)} %constant.72.clone) | copy-start | bytes 3460
  2.0 8.7 %copy-start.18 = (s32[1,1,18,1]{2,3,1,0:T(1,128)S(1)}, s32[1,1,18,1]{2,3,1,0:T(1,128)}, u32[]{:S(2)}) copy-start(s32[1,1,18,1]{2,3,1,0:T(1,128)} %param.25) | copy-start | bytes 220
  2.0 8.9 %copy-start.13 = (f32[4,4,576]{2,1,0:T(4,128)S(1)}, f32[4,4,576]{2,1,0:T(4,128)}, u32[]{:S(2)}) copy-start(f32[4,4,576]{2,1,0:T(4,128)} %param.22) | copy-start | bytes 110596
  2.1 23.5 %collective-permute-start.1 = (f32[128,1152]{1,0:T(8,128)S(1)}, f32[128,1152]{1,0:T(8,128)S(1)}, u32[]{:S(2)}, u32[]{:S(2)}) collective-permute-start(f32[128,1152]{1,0:T(8,128)S(1)} %pack.1), channel_id=1, source_target_pairs={{0,2},{2,0},{4,6},{6,4},{8,10},{10,8},{12,14},{14,12},{1,3},{3,1},... | collective-permute-start | bytes 1769480 | tf_op jit(solution)/shard_map/ppermute | solution.py:382
  7.7 2.9 %copy-start.12 = (f32[64,1152]{1,0:T(8,128)}, f32[64,1152]{1,0:T(8,128)S(1)}, u32[]{:S(2)}) copy-start(f32[64,1152]{1,0:T(8,128)S(1)} %get-tuple-element.50) | copy-start | bytes 884740
  7.8 10.2 %copy-start.16 = (f32[4,32]{1,0:T(4,128)S(1)}, f32[4,32]{1,0:T(4,128)}, u32[]{:S(2)}) copy-start(f32[4,32]{1,0:T(4,128)} %param.24) | copy-start | bytes 1540
  7.8 12.2 %collective-permute-start.3 = (f32[16,1152]{1,0:T(8,128)S(1)}, f32[16,1152]{1,0:T(8,128)S(1)}, u32[]{:S(2)}, u32[]{:S(2)}) collective-permute-start(f32[16,1152]{1,0:T(8,128)S(1)} %get-tuple-element.51), channel_id=1, source_target_pairs={{2,0},{4,2},{6,4},{8,6},{10,8},{12,10},{14,12},{3,1},{5,3},{7,5},{... | collective-permute-start | bytes 221192 | tf_op jit(solution)/shard_map/ppermute | solution.py:399
  9.2 10.8 %collective-permute-start.4 = (f32[64,1152]{1,0:T(8,128)}, f32[64,1152]{1,0:T(8,128)}, u32[]{:S(2)}, u32[]{:S(2)}) collective-permute-start(f32[64,1152]{1,0:T(8,128)} %get-tuple-element.46), channel_id=1, source_target_pairs={{2,4},{4,2},{6,8},{8,6},{10,12},{12,10},{3,5},{5,3},{7,9},{9,7},{1... | collective-permute-start | bytes 884744 | tf_op jit(solution)/shard_map/ppermute | solution.py:398
  10.6 1.6 %collective-permute-start = (f32[5,4,32,128]{3,2,1,0:T(8,128)S(1)}, f32[5,4,32,128]{3,2,1,0:T(8,128)S(1)}, u32[]{:S(2)}, u32[]{:S(2)}) collective-permute-start(f32[5,4,32,128]{3,2,1,0:T(8,128)S(1)} %get-tuple-element.43), channel_id=1, source_target_pairs={{0,1},{1,0},{2,3},{3,2},{4,5},{5,4},{6,7},{7,6},{8,9},{9,8},{10,11... | collective-permute-start | bytes 983048 | tf_op jit(solution)/shard_map/ppermute | solution.py:401
  10.8 14.8 %copy-start.10 = (f32[32,32]{1,0:T(8,128)S(1)}, f32[32,32]{1,0:T(8,128)}, u32[]{:S(2)}) copy-start(f32[32,32]{1,0:T(8,128)} %refs_9_.3) | copy-start | bytes 12292
  12.2 0.7 %copy-start.4 = (f32[5,4,32,128]{3,2,1,0:T(8,128)}, f32[5,4,32,128]{3,2,1,0:T(8,128)S(1)}, u32[]{:S(2)}) copy-start(f32[5,4,32,128]{3,2,1,0:T(8,128)S(1)} %collective-permute-done.side_ref) | copy-start | bytes 983044
  12.9 1.0 %copy-start.5 = (f32[5,4,32,128]{3,2,1,0:T(8,128)S(1)}, f32[5,4,32,128]{3,2,1,0:T(8,128)}, u32[]{:S(2)}) copy-start(f32[5,4,32,128]{3,2,1,0:T(8,128)} %copy-done.4) | copy-start | bytes 983044
  18.0 13.7 %collective-permute-start.2 = (f32[64,1152]{1,0:T(8,128)}, f32[64,1152]{1,0:T(8,128)S(1)}, u32[]{:S(2)}, u32[]{:S(2)}) collective-permute-start(f32[64,1152]{1,0:T(8,128)} %copy-done.12), channel_id=1, source_target_pairs={{2,4},{4,2},{6,8},{8,6},{10,12},{12,10},{3,5},{5,3},{7,9},{9,7},{1... | collective-permute-start | bytes 884744 | tf_op jit(solution)/shard_map/ppermute | solution.py:435
  25.6 3.4 %copy-start.2 = (bf16[1024,256]{1,0:T(8,128)(2,1)S(1)}, bf16[1024,256]{1,0:T(8,128)(2,1)}, u32[]{:S(2)}) copy-start(bf16[1024,256]{1,0:T(8,128)(2,1)} %constant.75.clone.refs_3_.refs_2_) | copy-start | bytes 1572868
  25.6 3.4 %copy-start.3 = (bf16[1024,256]{1,0:T(8,128)(2,1)S(1)}, bf16[1024,256]{1,0:T(8,128)(2,1)}, u32[]{:S(2)}) copy-start(bf16[1024,256]{1,0:T(8,128)(2,1)} %constant.74.clone.refs_2_.refs_1_) | copy-start | bytes 1572868
  25.6 3.4 %copy-start.8 = (bf16[128,128]{1,0:T(8,128)(2,1)S(1)}, bf16[128,128]{1,0:T(8,128)(2,1)}, u32[]{:S(2)}) copy-start(bf16[128,128]{1,0:T(8,128)(2,1)} %constant.77.clone.refs_5_.refs_4_) | copy-start | bytes 98308
  25.6 3.4 %copy-start.9 = (bf16[128,128]{1,0:T(8,128)(2,1)S(1)}, bf16[128,128]{1,0:T(8,128)(2,1)}, u32[]{:S(2)}) copy-start(bf16[128,128]{1,0:T(8,128)(2,1)} %constant.76.clone.refs_4_.refs_3_) | copy-start | bytes 98308
  27.2 2.5 %copy-start = (bf16[1024,256]{1,0:T(8,128)(2,1)S(1)}, bf16[1024,256]{1,0:T(8,128)(2,1)}, u32[]{:S(2)}) copy-start(bf16[1024,256]{1,0:T(8,128)(2,1)} %constant.79.clone.refs_5_.refs_4_) | copy-start | bytes 1572868
  27.2 2.5 %copy-start.1 = (bf16[1024,256]{1,0:T(8,128)(2,1)S(1)}, bf16[1024,256]{1,0:T(8,128)(2,1)}, u32[]{:S(2)}) copy-start(bf16[1024,256]{1,0:T(8,128)(2,1)} %constant.78.clone.refs_4_.refs_3_) | copy-start | bytes 1572868
  27.2 2.5 %copy-start.6 = (bf16[128,128]{1,0:T(8,128)(2,1)S(1)}, bf16[128,128]{1,0:T(8,128)(2,1)}, u32[]{:S(2)}) copy-start(bf16[128,128]{1,0:T(8,128)(2,1)} %constant.81.clone.refs_7_.refs_6_) | copy-start | bytes 98308
  27.2 2.5 %copy-start.7 = (bf16[128,128]{1,0:T(8,128)(2,1)S(1)}, bf16[128,128]{1,0:T(8,128)(2,1)}, u32[]{:S(2)}) copy-start(bf16[128,128]{1,0:T(8,128)(2,1)} %constant.80.clone.refs_6_.refs_5_) | copy-start | bytes 98308
  27.2 2.5 %copy-start.11 = (s32[4]{0:T(128)S(1)}, s32[4]{0:T(128)}, u32[]{:S(2)}) copy-start(s32[4]{0:T(128)} %mask_ref.3) | copy-start | bytes 52
  27.2 1.5 %collective-permute-start.6 = (f32[2,32,640]{2,1,0:T(8,128)S(1)}, f32[2,32,640]{2,1,0:T(8,128)S(1)}, u32[]{:S(2)}, u32[]{:S(2)}) collective-permute-start(f32[2,32,640]{2,1,0:T(8,128)S(1)} %get-tuple-element.82), channel_id=1, source_target_pairs={{0,1},{1,0},{2,3},{3,2},{4,5},{5,4},{6,7},{7,6},{8,9},{9,8},{10,11... | collective-permute-start | bytes 491528 | tf_op jit(solution)/shard_map/ppermute | solution.py:489
  27.3 1.6 %collective-permute-start.5 = (f32[2,32,640]{2,1,0:T(8,128)S(1)}, f32[2,32,640]{2,1,0:T(8,128)S(1)}, u32[]{:S(2)}, u32[]{:S(2)}) collective-permute-start(f32[2,32,640]{2,1,0:T(8,128)S(1)} %get-tuple-element.83), channel_id=1, source_target_pairs={{0,1},{1,0},{2,3},{3,2},{4,5},{5,4},{6,7},{7,6},{8,9},{9,8},{10,11... | collective-permute-start | bytes 491528 | tf_op jit(solution)/shard_map/ppermute | solution.py:489
  32.3 2.8 %collective-permute-start.8 = (f32[4,32,640]{2,1,0:T(8,128)S(1)}, f32[4,32,640]{2,1,0:T(8,128)S(1)}, u32[]{:S(2)}, u32[]{:S(2)}) collective-permute-start(f32[4,32,640]{2,1,0:T(8,128)S(1)} %get-tuple-element.66), channel_id=1, source_target_pairs={{0,1},{1,0},{2,3},{3,2},{4,5},{5,4},{6,7},{7,6},{8,9},{9,8},{10,11... | collective-permute-start | bytes 983048 | tf_op jit(solution)/shard_map/ppermute | solution.py:503
  32.6 4.0 %collective-permute-start.7 = (f32[1,128]{1,0:T(1,128)S(1)}, f32[1,128]{1,0:T(1,128)S(1)}, u32[]{:S(2)}, u32[]{:S(2)}) collective-permute-start(f32[1,128]{1,0:T(1,128)S(1)} %get-tuple-element.64), channel_id=1, source_target_pairs={{0,2},{2,0},{4,6},{6,4},{8,10},{10,8},{12,14},{14,12},{1,3},{3,1},... | collective-permute-start | bytes 1544 | tf_op jit(solution)/shard_map/ppermute | solution.py:500
  36.7 3.9 %collective-permute-start.9 = (f32[1,128]{1,0:T(1,128)S(1)}, f32[1,128]{1,0:T(1,128)S(1)}, u32[]{:S(2)}, u32[]{:S(2)}) collective-permute-start(f32[1,128]{1,0:T(1,128)S(1)} %add.49), channel_id=1, source_target_pairs={{0,4},{2,6},{4,0},{6,2},{8,12},{10,14},{12,8},{14,10},{1,5},{3,7},... | collective-permute-start | bytes 1544 | tf_op jit(solution)/shard_map/ppermute | solution.py:500
  39.1 4.6 %collective-permute-start.11 = (f32[4,32,640]{2,1,0:T(8,128)}, f32[4,32,640]{2,1,0:T(8,128)S(1)}, u32[]{:S(2)}, u32[]{:S(2)}) collective-permute-start(f32[4,32,640]{2,1,0:T(8,128)} %get-tuple-element.62), channel_id=1, source_target_pairs={{0,1},{1,0},{2,3},{3,2},{4,5},{5,4},{6,7},{7,6},{8,9},{9,8},{10,11... | collective-permute-start | bytes 983048 | tf_op jit(solution)/shard_map/ppermute | solution.py:493
  40.6 3.0 %collective-permute-start.12 = (f32[4,32,640]{2,1,0:T(8,128)S(1)}, f32[4,32,640]{2,1,0:T(8,128)S(1)}, u32[]{:S(2)}, u32[]{:S(2)}) collective-permute-start(f32[4,32,640]{2,1,0:T(8,128)S(1)} %get-tuple-element.79), channel_id=1, source_target_pairs={{0,1},{1,0},{2,3},{3,2},{4,5},{5,4},{6,7},{7,6},{8,9},{9,8},{10,11... | collective-permute-start | bytes 983048 | tf_op jit(solution)/shard_map/ppermute | solution.py:517
  40.9 4.4 %collective-permute-start.10 = (f32[1,128]{1,0:T(1,128)S(1)}, f32[1,128]{1,0:T(1,128)S(1)}, u32[]{:S(2)}, u32[]{:S(2)}) collective-permute-start(f32[1,128]{1,0:T(1,128)S(1)} %add.50), channel_id=1, source_target_pairs={{0,8},{2,10},{4,12},{6,14},{8,0},{10,2},{12,4},{14,6},{1,9},{3,11}... | collective-permute-start | bytes 1544 | tf_op jit(solution)/shard_map/ppermute | solution.py:500

commit v11 on v10

--- a/solution.py
+++ b/solution.py
@@ -60,6 +60,15 @@
     return forward, inverse, np.concatenate(numbers), np.concatenate(weights)
 
 
+def is_even():
+    return lax.axis_index("lat") % 2 == 0
+
+
+def first_of(half, tracer_count):
+    lon = lax.axis_index("lon")
+    return (tracer_count // 2) * (lon if half == "keep" else 1 - lon)
+
+
 def pack_rows(first, second):
     return jnp.concatenate([first, second], axis=1)
 
@@ -82,9 +91,9 @@
     return copies
 
 
-def pack_kernel(even_ref, tracer_hbm, out_ref, row_ref, sems):
+def pack_kernel(tracer_hbm, out_ref, row_ref, sems):
     count, levels = row_ref.shape[:2]
-    first_row = pl.multiple_of(jnp.where(even_ref[0] == 1, tracer_hbm.shape[2] - 2, 0), 2)
+    first_row = pl.multiple_of(jnp.where(is_even(), tracer_hbm.shape[2] - 2, 0), 2)
     sources = [tracer_hbm.at[t, :, pl.ds(first_row, 2), :] for t in range(count)]
     copies = start_copies([(sources[t], row_ref.at[t]) for t in range(count)], sems)
     for t in range(count):
@@ -92,7 +101,7 @@
         out_ref[levels * t : levels * (t + 1), :] = pack_rows(row_ref[t, :, 0, :], row_ref[t, :, 1, :])
 
 
-def rest_kernel(even_ref, tracer_hbm, lat_hbm, lon_hbm, *refs):
+def rest_kernel(tracer_hbm, lat_hbm, lon_hbm, *refs):
     courant_ref, side_ref, tracer_ref, lat_ref, lon_ref, sems = refs[-6:]
     outer_refs = refs[:-6]
     count, levels, rows, sector = tracer_ref.shape
@@ -100,7 +109,7 @@
     copies = start_copies(pairs, sems)
     shift, whole = sector % LANES, sector // LANES * LANES
     lane = lax.broadcasted_iota(jnp.int32, (levels, LANES), 1)
-    even = even_ref[0] == 1
+    even = is_even()
 
     def store_side(i, r, values):
         first = pltpu.roll(values[:, :LANES], shift, 1)
@@ -123,7 +132,7 @@
         store_side(count, r, lon_ref[:, r, :])
 
 
-def base_kernel(width, not_pole_ref, tracer_hbm, lat_hbm, lon_hbm, side_ref, base_ref, north_ref, courant_ref, *scratch):
+def base_kernel(width, tracer_hbm, lat_hbm, lon_hbm, side_ref, base_ref, north_ref, courant_ref, *scratch):
     tracer_ref, lat_ref, lon_ref, sems = scratch
     tracer_count, levels, rows, sector = tracer_ref.shape
     whole = sector // LANES * LANES
@@ -137,7 +146,7 @@
     copies[1].wait()
     nothing = jnp.zeros((levels, LANES), jnp.float32)
     for r in range(rows):
-        courant = lat_ref[:, r, :] if r else lat_ref[:, r, :] * not_pole_ref[0]
+        courant = lat_ref[:, r, :] if r else jnp.where(lax.axis_index("lat") > 0, lat_ref[:, r, :], 0.0)
         courant_ref[r] = beside(courant, nothing)
     for t in range(tracer_count):
         copies[t + 2].wait()
@@ -158,15 +167,13 @@
             base_ref[t, r] = value
 
 
-def physics_kernel(levels, sector, owner_count, chunk, even_ref, *refs):
-    count = len(refs) - 12 >> 1
-    first_refs, refs = refs[:count], refs[count:]
+def physics_kernel(levels, sector, owner_count, chunk, halves, *refs):
     base_ref, north_ref, inner_ref, outer_ref = refs[:4]
     top_ref, courant_ref, surface_ref, mixing_ref, decay_ref, owner_ref, energy_in_ref = refs[4:11]
     physics_refs, energy_ref = refs[11:-1], refs[-1]
     rows, width = base_ref.shape[1], base_ref.shape[-1]
     courant = [courant_ref[r] for r in range(rows)]
-    even = even_ref[0] == 1
+    even = is_even()
     top = top_ref[...]
     top = jnp.concatenate([top[:, :width], second_half(top, sector)], axis=0)
     mix_high, mix_low = split_high_low(mixing_ref[...])
@@ -174,10 +181,11 @@
     level = lax.broadcasted_iota(jnp.int32, (8, width), 0)
     lane = lax.broadcasted_iota(jnp.int32, (8, width), 1)
     energies = [energy_in_ref[r] for r in range(rows)]
-    for first_ref, physics_ref in zip(first_refs, physics_refs):
-        t = first_ref[0] + chunk
+    for half, physics_ref in zip(halves, physics_refs):
+        first = first_of(half, base_ref.shape[0])
+        t = first + chunk
         inner = inner_ref[pl.ds(pl.multiple_of(levels * t, levels), levels), :]
-        outer = jnp.where(first_ref[0] == 0, outer_ref[:levels, :], outer_ref[levels:, :])
+        outer = jnp.where(first == 0, outer_ref[:levels, :], outer_ref[levels:, :])
         low, high = jnp.where(even, outer, inner), jnp.where(even, inner, outer)
         low_a, low_b = low[:, :width], second_half(low, sector)
         high_a, high_b = high[:, :width], second_half(high, sector)
@@ -324,7 +332,7 @@
             back_ref[r, :, begin : begin + LANES] = jnp.where(filtered_row, value, other_ref[:, begin : begin + LANES])
 
 
-def finish_kernel(keep_ref, give_ref, *refs):
+def finish_kernel(*refs):
     out_hbm, turned_ref, sems = refs[-3:]
     count = turned_ref.shape[0]
     result_refs, received_refs = refs[:count], refs[count : 2 * count]
@@ -340,11 +348,11 @@
             copies[-1].start()
 
     for i, result_ref in enumerate(result_refs):
-        send(result_ref, keep_ref[0] + i, i)
+        send(result_ref, first_of("keep", 2 * count) + i, i)
     for i in range(count):
         for r in range(rows):
             turned_ref[i, :, r, :] = received_refs[i][r, :, :sector]
-        send(turned_ref.at[i], give_ref[0] + i, count + i)
+        send(turned_ref.at[i], first_of("give", 2 * count) + i, count + i)
     for copy in copies:
         copy.wait()
 
@@ -363,7 +371,6 @@
     whole = pl.BlockSpec(memory_space=pltpu.VMEM)
     in_hbm = pl.BlockSpec(memory_space=pltpu.HBM)
     scalars = pl.BlockSpec(memory_space=pltpu.SMEM)
-    even = (1 - lat % 2).reshape(1)
     inside = [pair for i in range(0, lat_count - 1, 2) for pair in ((i, i + 1), (i + 1, i))]
     across = [pair for i in range(1, lat_count - 1, 2) for pair in ((i, i + 1), (i + 1, i))]
     fields = [pltpu.with_memory_space_constraint(array, pltpu.HBM) for array in (tracers, courant_lat, courant_lon)]
@@ -371,19 +378,20 @@
     half = tracer_count // 2
     inner = pl.pallas_call(
         pack_kernel,
-        in_specs=[scalars, in_hbm],
+        in_specs=[in_hbm],
         out_specs=whole,
         out_shape=pltpu.VMEM((levels * tracer_count, length), f32),
         scratch_shapes=[pltpu.VMEM((tracer_count, levels, 2, sector), f32), pltpu.SemaphoreType.DMA((tracer_count,))],
         compiler_params=params(),
         cost_estimate=cost(0, 600_000),
         name="pack",
-    )(even, fields[0])
+    )(fields[0])
     from_inside = lax.ppermute(inner, "lat", inside)
-    even_rest, inner = lax.optimization_barrier((even, inner))
+    fields, inner = lax.optimization_barrier((fields, inner))
+    fields = [pltpu.with_memory_space_constraint(array, pltpu.HBM) for array in fields]
     *outer, courant_row, sides = pl.pallas_call(
         rest_kernel,
-        in_specs=[scalars] + [in_hbm] * 3,
+        in_specs=[in_hbm] * 3,
         out_specs=[whole] * (half + 2),
         out_shape=[pltpu.VMEM((levels * 2, length), f32)] * half
         + [
@@ -394,15 +402,14 @@
         compiler_params=params(),
         cost_estimate=cost(0, 0),
         name="rest",
-    )(even_rest, *fields)
+    )(*fields)
     from_across = [lax.ppermute(part, "lat", across) for part in outer[:-1]]
     top = lax.ppermute(courant_row, "lat", downward)
 
     sides = lax.ppermute(sides, "lon", swap)
-    not_pole = (lat > 0).astype(f32).reshape(1)
     base, north, lat_courant = pl.pallas_call(
         functools.partial(base_kernel, width),
-        in_specs=[scalars, in_hbm, in_hbm, in_hbm, whole],
+        in_specs=[in_hbm, in_hbm, in_hbm, whole],
         out_specs=[whole] * 3,
         out_shape=[
             jax.ShapeDtypeStruct((tracer_count, rows, levels, width), f32),
@@ -413,7 +420,7 @@
         compiler_params=params(),
         cost_estimate=cost(0, 0),
         name="base",
-    )(not_pole, *fields, sides)
+    )(*fields, sides)
 
     surface = jnp.pad(surface_flux, ((0, 0), (0, 0), (0, width - sector)))
     decay = decay_rate[:, :, None]
@@ -434,24 +441,22 @@
     base, outer = lax.optimization_barrier((base, outer))
     from_across.append(lax.ppermute(outer[-1], "lat", across))
 
-    keep = (half * lax.axis_index("lon")).reshape(1)
-    give = half - keep
     circles = jax.ShapeDtypeStruct((half, rows, levels, width), f32)
     result_shape = jax.ShapeDtypeStruct((levels, rows, sector), f32)
     out_shape = jax.ShapeDtypeStruct(tracers.shape, f32)
 
-    def run_physics(chunk, firsts, energy, last=False):
-        shapes = [jax.ShapeDtypeStruct(circles.shape[1:], f32)] * len(firsts)
+    def run_physics(chunk, energy, last=False):
+        shapes = [jax.ShapeDtypeStruct(circles.shape[1:], f32)] * 2
         shapes.append(jax.ShapeDtypeStruct((1, LANES) if last else energy.shape, f32))
         *results, energy = pl.pallas_call(
-            functools.partial(physics_kernel, levels, sector, lat_count if last else 0, chunk),
-            in_specs=[scalars] * (1 + len(firsts)) + [whole] * 11,
+            functools.partial(physics_kernel, levels, sector, lat_count if last else 0, chunk, ("give", "keep")),
+            in_specs=[whole] * 11,
             out_specs=[whole] * len(shapes),
             out_shape=shapes,
             compiler_params=params(),
             cost_estimate=cost(0, 0),
             name="physics",
-        )(even, *firsts, base, north, from_inside, from_across[chunk], top, lat_courant, surface, mixing, decay, owner_of, energy)
+        )(base, north, from_inside, from_across[chunk], top, lat_courant, surface, mixing, decay, owner_of, energy)
         return results, energy
 
     forward, inverse = ([jnp.asarray(part) for table in tables for part in split_table(table)] for tables in (forward, inverse))
@@ -485,7 +490,7 @@
     energy = jnp.zeros((rows, 8, width), f32)
     results, received = [], []
     for chunk in range(half - 1):
-        (given, own), energy = run_physics(chunk, [give, keep], energy)
+        (given, own), energy = run_physics(chunk, energy)
         other = [lax.ppermute(given[r : r + 2], "lon", swap) for r in range(0, rows, 2)]
         spectrum = run_forward(own, other)
         result, back = run_inverse(own, other, *spectrum)
@@ -499,7 +504,7 @@
         distance = distances.pop(0)
         return lax.ppermute(energy, "lat", [(i, i ^ distance) for i in range(lat_count)])
 
-    (given, own), energy = run_physics(half - 1, [give, keep], energy, True)
+    (given, own), energy = run_physics(half - 1, energy, True)
     other = [lax.ppermute(given, "lon", swap)]
 
     coming = send_energy(energy)
@@ -519,7 +524,7 @@
     coming = send_energy(energy)
     out = pl.pallas_call(
         finish_kernel,
-        in_specs=[scalars] * 2 + [whole] * (2 * half),
+        in_specs=[whole] * (2 * half),
         out_specs=in_hbm,
         out_shape=out_shape,
         scratch_shapes=[
@@ -529,7 +534,7 @@
         compiler_params=params(),
         cost_estimate=cost(0, 3_000_000),
         name="finish",
-    )(keep, give, *results, *received)
+    )(*results, *received)
     coming, out = lax.optimization_barrier((coming, out))
     energy = energy + coming
     while distances:

time: 46.3 us -> 46.2 us (level)
  no operation moved by 1% of the time
where the time goes in v11:
time: 46.2 us; the launch traced here: 45.9 us
  Pallas kernels  16 us (35%)
  starting transfers between devices  15.3 us (33%)
  waiting for transfers between devices  10.8 us (23%)
  local copies, waits for them, and re-layouts  2.11 us (5%)
  between operations  0.97 us (2%)
  other arithmetic  0.72 us (2%)
    ppermute x3, starting transfers between devices, send_energy(): lax.ppermute(energy, 'lat', [(i, i ^ distance) for i in range(lat_count)])  7.6 us
    ppermute x1, waiting for transfers between devices, on_device(): from_inside = lax.ppermute(inner, 'lat', inside)  5.58 us
    pallas_call x1, Pallas kernels, on_device(): pl.pallas_call(functools.partial(base_kernel, width), in_specs=[in_hbm, i...  3.95 us
    pallas_call x2, Pallas kernels, run_inverse(): pl.pallas_call(functools.partial(inverse_kernel, radix, len(other)), in_s...  3.23 us
    ppermute x1, starting transfers between devices, on_device(): from_inside = lax.ppermute(inner, 'lat', inside)  3 us
    pallas_call x1, Pallas kernels, on_device(): pl.pallas_call(rest_kernel, in_specs=[in_hbm] * 3, out_specs=[whole] * (h...  2.67 us
    pallas_call x2, Pallas kernels, run_physics(): pl.pallas_call(functools.partial(physics_kernel, levels, sector, lat_coun...  2.22 us
    unnamed x38, local copies, waits for them, and re-layouts  1.81 us
  transfers between devices with their start and end apart: 13, of which 8 were waited for; matrix products, arithmetic and copies ran while one was open for 1% of the time, Pallas kernels for 30%

profile of v11, /device:TPU:0, one launch (start us, length us, event | category | flops | bytes accessed | tf_op | source)
XLA Modules:
  0.0 45.9 jit_solution(6259795921912246838)
XLA Ops:
  0.6 1.4 %pack.1 = f32[128,1152]{1,0:T(8,128)S(1)} custom-call(f32[4,32,4,576]{3,2,1,0:T(4,128)} %tracer_hbm.3), custom_call_target="tpu_custom_call" | custom-call | bytes 600000 | tf_op jit(solution)/shard_map/pack/pallas_call | solution.py:379
  2.0 0.0 copy-start.14
  2.0 0.0 copy-start.15
  2.0 0.0 copy-start.17
  2.0 0.0 copy-start.18
  2.0 0.0 copy-start.13
  2.1 3.0 %collective-permute-start.1 = (f32[128,1152]{1,0:T(8,128)S(1)}, f32[128,1152]{1,0:T(8,128)S(1)}, u32[]{:S(2)}, u32[]{:S(2)}) collective-permute-start(f32[128,1152]{1,0:T(8,128)S(1)} %pack.1), channel_id=1, source_target_pairs={{0,2},{2,0},{4,6},{6,4},{8,10},{10,8},{12,14},{14,12},{1,3},{3,1},... | collective-permute-start | bytes 1769480 | tf_op jit(solution)/shard_map/ppermute | solution.py:389
  5.1 2.7 %rest.1 = (f32[64,1152]{1,0:T(8,128)}, f32[64,1152]{1,0:T(8,128)S(1)}, f32[16,1152]{1,0:T(8,128)S(1)}, f32[5,4,32,128]{3,2,1,0:T(8,128)S(1)}) custom-call(f32[4,32,4,576]{3,2,1,0:T(4,128)} %tracer_hbm.3, f32[32,4,576]{2,1,0:T(4,128)} %lat_hbm.1, f32[32,4,576]{2,1,0:T(4,128)} %lon_hbm.1), custom_call_target="tpu_custom_call" | custom-call | tf_op jit(solution)/shard_map/rest/pallas_call | solution.py:392
  7.7 0.0 copy-start.12
  7.7 0.0 copy-start.16
  7.8 1.4 %collective-permute-start.3 = (f32[16,1152]{1,0:T(8,128)S(1)}, f32[16,1152]{1,0:T(8,128)S(1)}, u32[]{:S(2)}, u32[]{:S(2)}) collective-permute-start(f32[16,1152]{1,0:T(8,128)S(1)} %get-tuple-element.55), channel_id=1, source_target_pairs={{2,0},{4,2},{6,4},{8,6},{10,8},{12,10},{14,12},{3,1},{5,3},{7,5},{... | collective-permute-start | bytes 221192 | tf_op jit(solution)/shard_map/ppermute | solution.py:407
  9.2 1.4 %collective-permute-start.4 = (f32[64,1152]{1,0:T(8,128)}, f32[64,1152]{1,0:T(8,128)}, u32[]{:S(2)}, u32[]{:S(2)}) collective-permute-start(f32[64,1152]{1,0:T(8,128)} %get-tuple-element.50), channel_id=1, source_target_pairs={{2,4},{4,2},{6,8},{8,6},{10,12},{12,10},{3,5},{5,3},{7,9},{9,7},{1... | collective-permute-start | bytes 884744 | tf_op jit(solution)/shard_map/ppermute | solution.py:406
  10.6 0.0 collective-permute-start
  10.6 0.0 copy-done.12
  10.7 0.0 copy-start.10
  10.7 0.1 select_multiply_fusion.refs_6_.refs_5_
  10.8 0.1 broadcast_in_dim.27
  10.8 0.1 reshape_reshape.3
  11.0 1.3 %collective-permute-done.side_ref = f32[5,4,32,128]{3,2,1,0:T(8,128)S(1)} collective-permute-done((f32[5,4,32,128]{3,2,1,0:T(8,128)S(1)}, f32[5,4,32,128]{3,2,1,0:T(8,128)S(1)}, u32[]{:S(2)}, u32[]{:S(2)}) %collective-permute-start) | collective-permute-done | bytes 327712 | tf_op jit(solution)/shard_map/ppermute | solution.py:409
  12.2 0.7 %copy-done.4 = f32[5,4,32,128]{3,2,1,0:T(8,128)} copy-done((f32[5,4,32,128]{3,2,1,0:T(8,128)}, f32[5,4,32,128]{3,2,1,0:T(8,128)S(1)}, u32[]{:S(2)}) %copy-start.4) | copy-done | bytes 327704
  12.9 1.0 %copy-done.5 = f32[5,4,32,128]{3,2,1,0:T(8,128)S(1)} copy-done((f32[5,4,32,128]{3,2,1,0:T(8,128)S(1)}, f32[5,4,32,128]{3,2,1,0:T(8,128)}, u32[]{:S(2)}) %copy-start.5) | copy-done | bytes 327704
  13.9 4.0 %base.1 = (f32[4,4,32,640]{3,2,1,0:T(8,128)S(1)}, f32[4,32,640]{2,1,0:T(8,128)S(1)}, f32[4,32,640]{2,1,0:T(8,128)S(1)}) custom-call(f32[4,32,4,576]{3,2,1,0:T(4,128)} %tracer_hbm.3, f32[32,4,576]{2,1,0:T(4,128)} %lat_hbm.1, f32[32,4,576]{2,1,0:T(4,128)} %lon_hbm.1, f32[5,4,32,128]{3,2,1,0:T(8,128)S(1)} %copy-done.5), custom_call_target="tpu_custom_call" | custom-call | tf_op jit(solution)/shard_map/base/pallas_call | solution.py:410
  17.9 0.0 copy-done.16
  17.9 0.1 copy.22.refs_8_
  18.0 0.7 %collective-permute-start.2 = (f32[64,1152]{1,0:T(8,128)}, f32[64,1152]{1,0:T(8,128)S(1)}, u32[]{:S(2)}, u32[]{:S(2)}) collective-permute-start(f32[64,1152]{1,0:T(8,128)} %copy-done.12), channel_id=1, source_target_pairs={{2,4},{4,2},{6,8},{8,6},{10,12},{12,10},{3,5},{5,3},{7,9},{9,7},{1... | collective-permute-start | bytes 884744 | tf_op jit(solution)/shard_map/ppermute | solution.py:442
  18.7 1.3 %collective-permute-done.3.refs_4_ = f32[16,1152]{1,0:T(8,128)S(1)} collective-permute-done((f32[16,1152]{1,0:T(8,128)S(1)}, f32[16,1152]{1,0:T(8,128)S(1)}, u32[]{:S(2)}, u32[]{:S(2)}) %collective-permute-start.3) | collective-permute-done | bytes 73760 | tf_op jit(solution)/shard_map/ppermute | solution.py:407
  20.0 0.0 collective-permute-done.4.refs_3_
  20.0 5.6 %collective-permute-done.1.refs_2_ = f32[128,1152]{1,0:T(8,128)S(1)} collective-permute-done((f32[128,1152]{1,0:T(8,128)S(1)}, f32[128,1152]{1,0:T(8,128)S(1)}, u32[]{:S(2)}, u32[]{:S(2)}) %collective-permute-start.1) | collective-permute-done | bytes 589856 | tf_op jit(solution)/shard_map/ppermute | solution.py:389
  25.6 0.0 copy-done.10
  25.6 0.0 copy-start.2
  25.6 0.0 copy-start.3
  25.6 0.0 copy-start.8
  25.6 0.0 copy-start.9
  25.6 1.5 %physics.2 = (f32[4,32,640]{2,1,0:T(8,128)S(1)}, f32[4,32,640]{2,1,0:T(8,128)S(1)}, f32[4,8,640]{2,1,0:T(8,128)S(1)}) custom-call(f32[4,4,32,640]{3,2,1,0:T(8,128)S(1)} %get-tuple-element.52.refs_0_, f32[4,32,640]{2,1,0:T(8,128)S(1)} %get-tuple-element.53.refs_1_, f32[128,1152]{1,0:T(8,128)S(1)} %collective-permute-done.1.refs_2_, ...), custom_call_target="tpu_custom_call" | custom-call | tf_op jit(solution)/shard_map/physics/pallas_call | solution.py:451
  27.2 0.0 copy-start
  27.2 0.0 copy-start.1
  27.2 0.0 copy-start.6
  27.2 0.0 copy-start.7
  27.2 0.0 copy-start.11
  27.3 0.1 collective-permute-start.6
  27.3 0.5 %collective-permute-start.5 = (f32[2,32,640]{2,1,0:T(8,128)S(1)}, f32[2,32,640]{2,1,0:T(8,128)S(1)}, u32[]{:S(2)}, u32[]{:S(2)}) collective-permute-start(f32[2,32,640]{2,1,0:T(8,128)S(1)} %get-tuple-element.87), channel_id=1, source_target_pairs={{0,1},{1,0},{2,3},{3,2},{4,5},{5,4},{6,7},{7,6},{8,9},{9,8},{10,11... | collective-permute-start | bytes 491528 | tf_op jit(solution)/shard_map/ppermute | solution.py:494
  27.8 0.9 %collective-permute-done.6.refs_1_ = f32[2,32,640]{2,1,0:T(8,128)S(1)} collective-permute-done((f32[2,32,640]{2,1,0:T(8,128)S(1)}, f32[2,32,640]{2,1,0:T(8,128)S(1)}, u32[]{:S(2)}, u32[]{:S(2)}) %collective-permute-start.6) | collective-permute-done | bytes 163872 | tf_op jit(solution)/shard_map/ppermute | solution.py:494
  28.7 0.2 collective-permute-done.5.refs_0_
  29.0 0.0 copy-done.3
  29.0 0.7 %forward.2 = (bf16[128,1152]{1,0:T(8,128)(2,1)S(1)}, bf16[128,1152]{1,0:T(8,128)(2,1)S(1)}) custom-call(f32[4,32,640]{2,1,0:T(8,128)S(1)} %get-tuple-element.61.own_ref, f32[2,32,640]{2,1,0:T(8,128)S(1)} %collective-permute-done.5.refs_0_, f32[2,32,640]{2,1,0:T(8,128)S(1)} %collective-permute-done.6.refs_1_, bf16[1024,256]{1,0:T(8,128)(2,1)S(1)} %copy-done.3, ...), custom_call_target="tpu_custom_call" | custom-call | tf_op jit(solution)/shard_map/forward/pallas_call | solution.py:467
  29.7 2.0 %inverse.2 = (f32[32,4,576]{2,1,0:T(4,128)S(1)}, f32[4,32,640]{2,1,0:T(8,128)}) custom-call(s32[4]{0:T(128)S(1)} %copy-done.11, f32[4,32,640]{2,1,0:T(8,128)S(1)} %get-tuple-element.61.own_ref, f32[2,32,640]{2,1,0:T(8,128)S(1)} %collective-permute-done.5.refs_0_, f32[2,32,640]{2,1,0:T(8,128)S(1)} %collective-permute-done.6.refs_1_, ...), custom_call_target="tpu_custom_call" | custom-call | tf_op jit(solution)/shard_map/inverse/pallas_call | solution.py:479
  31.7 0.0 collective-permute-done.2.refs_3_
  31.7 0.7 %physics.3 = (f32[4,32,640]{2,1,0:T(8,128)S(1)}, f32[4,32,640]{2,1,0:T(8,128)S(1)}, f32[1,128]{1,0:T(1,128)S(1)}) custom-call(f32[4,4,32,640]{3,2,1,0:T(8,128)S(1)} %get-tuple-element.52.refs_0_, f32[4,32,640]{2,1,0:T(8,128)S(1)} %get-tuple-element.53.refs_1_, f32[128,1152]{1,0:T(8,128)S(1)} %collective-permute-done.1.refs_2_, ...), custom_call_target="tpu_custom_call" | custom-call | tf_op jit(solution)/shard_map/physics/pallas_call | solution.py:451
  32.4 0.3 collective-permute-start.8
  32.7 2.5 %collective-permute-start.7 = (f32[1,128]{1,0:T(1,128)S(1)}, f32[1,128]{1,0:T(1,128)S(1)}, u32[]{:S(2)}, u32[]{:S(2)}) collective-permute-start(f32[1,128]{1,0:T(1,128)S(1)} %get-tuple-element.68), channel_id=1, source_target_pairs={{0,2},{2,0},{4,6},{6,4},{8,10},{10,8},{12,14},{14,12},{1,3},{3,1},... | collective-permute-start | bytes 1544 | tf_op jit(solution)/shard_map/ppermute | solution.py:505
  35.2 0.0 collective-permute-done.8.refs_0_
  35.2 0.7 %forward.3 = (bf16[128,1152]{1,0:T(8,128)(2,1)S(1)}, bf16[128,1152]{1,0:T(8,128)(2,1)S(1)}) custom-call(f32[4,32,640]{2,1,0:T(8,128)S(1)} %get-tuple-element.69.own_ref, f32[4,32,640]{2,1,0:T(8,128)S(1)} %collective-permute-done.8.refs_0_, bf16[1024,256]{1,0:T(8,128)(2,1)S(1)} %copy-done.3, bf16[1024,256]{1,0:T(8,128)(2,1)S(1)} %copy-done.2, ...), custom_call_target="tpu_custom_call" | custom-call | tf_op jit(solution)/shard_map/forward/pallas_call | solution.py:467
  35.9 0.8 %collective-permute-done.7 = f32[1,128]{1,0:T(1,128)S(1)} collective-permute-done((f32[1,128]{1,0:T(1,128)S(1)}, f32[1,128]{1,0:T(1,128)S(1)}, u32[]{:S(2)}, u32[]{:S(2)}) %collective-permute-start.7) | collective-permute-done | bytes 544 | tf_op jit(solution)/shard_map/ppermute | solution.py:505
  36.7 2.4 %collective-permute-start.9 = (f32[1,128]{1,0:T(1,128)S(1)}, f32[1,128]{1,0:T(1,128)S(1)}, u32[]{:S(2)}, u32[]{:S(2)}) collective-permute-start(f32[1,128]{1,0:T(1,128)S(1)} %add.44), channel_id=1, source_target_pairs={{0,4},{2,6},{4,0},{6,2},{8,12},{10,14},{12,8},{14,10},{1,5},{3,7},... | collective-permute-start | bytes 1544 | tf_op jit(solution)/shard_map/ppermute | solution.py:505
  39.1 0.0 collective-permute-start.11
  39.1 1.3 %inverse.3 = (f32[32,4,576]{2,1,0:T(4,128)S(1)}, f32[4,32,640]{2,1,0:T(8,128)S(1)}) custom-call(s32[4]{0:T(128)S(1)} %copy-done.11, f32[4,32,640]{2,1,0:T(8,128)S(1)} %get-tuple-element.69.own_ref, f32[4,32,640]{2,1,0:T(8,128)S(1)} %collective-permute-done.8.refs_0_, bf16[128,1152]{1,0:T(8,128)(2,1)S(1)} %get-tuple-element.75.refs_1_, ...), custom_call_target="tpu_custom_call" | custom-call | tf_op jit(solution)/shard_map/inverse/pallas_call | solution.py:479
  40.3 0.3 collective-permute-done.9
  40.6 0.3 collective-permute-start.12
  40.9 2.7 %collective-permute-start.10 = (f32[1,128]{1,0:T(1,128)S(1)}, f32[1,128]{1,0:T(1,128)S(1)}, u32[]{:S(2)}, u32[]{:S(2)}) collective-permute-start(f32[1,128]{1,0:T(1,128)S(1)} %add.45), channel_id=1, source_target_pairs={{0,8},{2,10},{4,12},{6,14},{8,0},{10,2},{12,4},{14,6},{1,9},{3,11}... | collective-permute-start | bytes 1544 | tf_op jit(solution)/shard_map/ppermute | solution.py:505
  43.6 0.0 collective-permute-done.11.refs_2_
  43.6 0.0 collective-permute-done.12.refs_3_
  43.6 1.2 %finish.1 = f32[4,32,4,576]{3,2,1,0:T(4,128)} custom-call(f32[32,4,576]{2,1,0:T(4,128)S(1)} %get-tuple-element.81.refs_0_, f32[32,4,576]{2,1,0:T(4,128)S(1)} %get-tuple-element.82.refs_1_, f32[4,32,640]{2,1,0:T(8,128)S(1)} %collective-permute-done.11.refs_2_, f32[4,32,640]{2,1,0:T(8,128)S(1)} %collective-permute-done.12.refs_3_), custom_call_target="tpu_custom_call" | custom-call | bytes 3000000 | tf_op jit(solution)/shard_map/finish/pallas_call | solution.py:525
  44.8 0.5 %collective-permute-done.10 = f32[1,128]{1,0:T(1,128)S(1)} collective-permute-done((f32[1,128]{1,0:T(1,128)S(1)}, f32[1,128]{1,0:T(1,128)S(1)}, u32[]{:S(2)}, u32[]{:S(2)}) %collective-permute-start.10) | collective-permute-done | bytes 544 | tf_op jit(solution)/shard_map/ppermute | solution.py:505
  45.3 0.6 %fusion.1 = f32[1,1]{1,0:T(1,128)} fusion(f32[1,128]{1,0:T(1,128)S(1)} %add.46, s32[]{:T(128)S(6)} %select_n.8), kind=kLoop, calls=%fused_computation.4 | loop fusion | flops 1 | bytes 12 | tf_op jit(solution)/shard_map/div | solution.py:543
  (23 shorter events, 0.1 us)
Async XLA Ops:
  2.0 8.7 %copy-start.14 = (f32[1152]{0:T(1024)S(1)}, f32[1152]{0:T(1024)}, u32[]{:S(2)}) copy-start(f32[1152]{0:T(1024)} %constant.56.clone) | copy-start | bytes 13828
  2.0 8.7 %copy-start.15 = (f32[1152]{0:T(1024)S(1)}, f32[1152]{0:T(1024)}, u32[]{:S(2)}) copy-start(f32[1152]{0:T(1024)} %constant.54.clone) | copy-start | bytes 13828
  2.0 8.7 %copy-start.17 = (pred[1152]{0:T(1024)(128)(4,1)S(1)}, pred[1152]{0:T(1024)(128)(4,1)}, u32[]{:S(2)}) copy-start(pred[1152]{0:T(1024)(128)(4,1)} %constant.55.clone) | copy-start | bytes 3460
  2.0 8.7 %copy-start.18 = (s32[1,1,18,1]{2,3,1,0:T(1,128)S(1)}, s32[1,1,18,1]{2,3,1,0:T(1,128)}, u32[]{:S(2)}) copy-start(s32[1,1,18,1]{2,3,1,0:T(1,128)} %param.25) | copy-start | bytes 220
  2.0 8.9 %copy-start.13 = (f32[4,4,576]{2,1,0:T(4,128)S(1)}, f32[4,4,576]{2,1,0:T(4,128)}, u32[]{:S(2)}) copy-start(f32[4,4,576]{2,1,0:T(4,128)} %param.22) | copy-start | bytes 110596
  2.1 23.5 %collective-permute-start.1 = (f32[128,1152]{1,0:T(8,128)S(1)}, f32[128,1152]{1,0:T(8,128)S(1)}, u32[]{:S(2)}, u32[]{:S(2)}) collective-permute-start(f32[128,1152]{1,0:T(8,128)S(1)} %pack.1), channel_id=1, source_target_pairs={{0,2},{2,0},{4,6},{6,4},{8,10},{10,8},{12,14},{14,12},{1,3},{3,1},... | collective-permute-start | bytes 1769480 | tf_op jit(solution)/shard_map/ppermute | solution.py:389
  7.7 2.9 %copy-start.12 = (f32[64,1152]{1,0:T(8,128)}, f32[64,1152]{1,0:T(8,128)S(1)}, u32[]{:S(2)}) copy-start(f32[64,1152]{1,0:T(8,128)S(1)} %get-tuple-element.54) | copy-start | bytes 884740
  7.7 10.1 %copy-start.16 = (f32[4,32]{1,0:T(4,128)S(1)}, f32[4,32]{1,0:T(4,128)}, u32[]{:S(2)}) copy-start(f32[4,32]{1,0:T(4,128)} %param.24) | copy-start | bytes 1540
  7.8 12.2 %collective-permute-start.3 = (f32[16,1152]{1,0:T(8,128)S(1)}, f32[16,1152]{1,0:T(8,128)S(1)}, u32[]{:S(2)}, u32[]{:S(2)}) collective-permute-start(f32[16,1152]{1,0:T(8,128)S(1)} %get-tuple-element.55), channel_id=1, source_target_pairs={{2,0},{4,2},{6,4},{8,6},{10,8},{12,10},{14,12},{3,1},{5,3},{7,5},{... | collective-permute-start | bytes 221192 | tf_op jit(solution)/shard_map/ppermute | solution.py:407
  9.2 10.8 %collective-permute-start.4 = (f32[64,1152]{1,0:T(8,128)}, f32[64,1152]{1,0:T(8,128)}, u32[]{:S(2)}, u32[]{:S(2)}) collective-permute-start(f32[64,1152]{1,0:T(8,128)} %get-tuple-element.50), channel_id=1, source_target_pairs={{2,4},{4,2},{6,8},{8,6},{10,12},{12,10},{3,5},{5,3},{7,9},{9,7},{1... | collective-permute-start | bytes 884744 | tf_op jit(solution)/shard_map/ppermute | solution.py:406
  10.6 1.6 %collective-permute-start = (f32[5,4,32,128]{3,2,1,0:T(8,128)S(1)}, f32[5,4,32,128]{3,2,1,0:T(8,128)S(1)}, u32[]{:S(2)}, u32[]{:S(2)}) collective-permute-start(f32[5,4,32,128]{3,2,1,0:T(8,128)S(1)} %get-tuple-element.47), channel_id=1, source_target_pairs={{0,1},{1,0},{2,3},{3,2},{4,5},{5,4},{6,7},{7,6},{8,9},{9,8},{10,11... | collective-permute-start | bytes 983048 | tf_op jit(solution)/shard_map/ppermute | solution.py:409
  10.7 14.9 %copy-start.10 = (f32[32,32]{1,0:T(8,128)S(1)}, f32[32,32]{1,0:T(8,128)}, u32[]{:S(2)}) copy-start(f32[32,32]{1,0:T(8,128)} %refs_7_.4) | copy-start | bytes 12292
  12.2 0.7 %copy-start.4 = (f32[5,4,32,128]{3,2,1,0:T(8,128)}, f32[5,4,32,128]{3,2,1,0:T(8,128)S(1)}, u32[]{:S(2)}) copy-start(f32[5,4,32,128]{3,2,1,0:T(8,128)S(1)} %collective-permute-done.side_ref) | copy-start | bytes 983044
  12.9 1.0 %copy-start.5 = (f32[5,4,32,128]{3,2,1,0:T(8,128)S(1)}, f32[5,4,32,128]{3,2,1,0:T(8,128)}, u32[]{:S(2)}) copy-start(f32[5,4,32,128]{3,2,1,0:T(8,128)} %copy-done.4) | copy-start | bytes 983044
  18.0 13.7 %collective-permute-start.2 = (f32[64,1152]{1,0:T(8,128)}, f32[64,1152]{1,0:T(8,128)S(1)}, u32[]{:S(2)}, u32[]{:S(2)}) collective-permute-start(f32[64,1152]{1,0:T(8,128)} %copy-done.12), channel_id=1, source_target_pairs={{2,4},{4,2},{6,8},{8,6},{10,12},{12,10},{3,5},{5,3},{7,9},{9,7},{1... | collective-permute-start | bytes 884744 | tf_op jit(solution)/shard_map/ppermute | solution.py:442
  25.6 3.4 %copy-start.2 = (bf16[1024,256]{1,0:T(8,128)(2,1)S(1)}, bf16[1024,256]{1,0:T(8,128)(2,1)}, u32[]{:S(2)}) copy-start(bf16[1024,256]{1,0:T(8,128)(2,1)} %constant.58.clone.refs_3_.refs_2_) | copy-start | bytes 1572868
  25.6 3.4 %copy-start.3 = (bf16[1024,256]{1,0:T(8,128)(2,1)S(1)}, bf16[1024,256]{1,0:T(8,128)(2,1)}, u32[]{:S(2)}) copy-start(bf16[1024,256]{1,0:T(8,128)(2,1)} %constant.57.clone.refs_2_.refs_1_) | copy-start | bytes 1572868
  25.6 3.4 %copy-start.8 = (bf16[128,128]{1,0:T(8,128)(2,1)S(1)}, bf16[128,128]{1,0:T(8,128)(2,1)}, u32[]{:S(2)}) copy-start(bf16[128,128]{1,0:T(8,128)(2,1)} %constant.60.clone.refs_5_.refs_4_) | copy-start | bytes 98308
  25.6 3.4 %copy-start.9 = (bf16[128,128]{1,0:T(8,128)(2,1)S(1)}, bf16[128,128]{1,0:T(8,128)(2,1)}, u32[]{:S(2)}) copy-start(bf16[128,128]{1,0:T(8,128)(2,1)} %constant.59.clone.refs_4_.refs_3_) | copy-start | bytes 98308
  27.2 2.5 %copy-start = (bf16[1024,256]{1,0:T(8,128)(2,1)S(1)}, bf16[1024,256]{1,0:T(8,128)(2,1)}, u32[]{:S(2)}) copy-start(bf16[1024,256]{1,0:T(8,128)(2,1)} %constant.62.clone.refs_5_.refs_4_) | copy-start | bytes 1572868
  27.2 2.5 %copy-start.1 = (bf16[1024,256]{1,0:T(8,128)(2,1)S(1)}, bf16[1024,256]{1,0:T(8,128)(2,1)}, u32[]{:S(2)}) copy-start(bf16[1024,256]{1,0:T(8,128)(2,1)} %constant.61.clone.refs_4_.refs_3_) | copy-start | bytes 1572868
  27.2 2.5 %copy-start.6 = (bf16[128,128]{1,0:T(8,128)(2,1)S(1)}, bf16[128,128]{1,0:T(8,128)(2,1)}, u32[]{:S(2)}) copy-start(bf16[128,128]{1,0:T(8,128)(2,1)} %constant.64.clone.refs_7_.refs_6_) | copy-start | bytes 98308
  27.2 2.5 %copy-start.7 = (bf16[128,128]{1,0:T(8,128)(2,1)S(1)}, bf16[128,128]{1,0:T(8,128)(2,1)}, u32[]{:S(2)}) copy-start(bf16[128,128]{1,0:T(8,128)(2,1)} %constant.63.clone.refs_6_.refs_5_) | copy-start | bytes 98308
  27.2 2.5 %copy-start.11 = (s32[4]{0:T(128)S(1)}, s32[4]{0:T(128)}, u32[]{:S(2)}) copy-start(s32[4]{0:T(128)} %mask_ref.3) | copy-start | bytes 52
  27.3 1.5 %collective-permute-start.6 = (f32[2,32,640]{2,1,0:T(8,128)S(1)}, f32[2,32,640]{2,1,0:T(8,128)S(1)}, u32[]{:S(2)}, u32[]{:S(2)}) collective-permute-start(f32[2,32,640]{2,1,0:T(8,128)S(1)} %get-tuple-element.86), channel_id=1, source_target_pairs={{0,1},{1,0},{2,3},{3,2},{4,5},{5,4},{6,7},{7,6},{8,9},{9,8},{10,11... | collective-permute-start | bytes 491528 | tf_op jit(solution)/shard_map/ppermute | solution.py:494
  27.3 1.6 %collective-permute-start.5 = (f32[2,32,640]{2,1,0:T(8,128)S(1)}, f32[2,32,640]{2,1,0:T(8,128)S(1)}, u32[]{:S(2)}, u32[]{:S(2)}) collective-permute-start(f32[2,32,640]{2,1,0:T(8,128)S(1)} %get-tuple-element.87), channel_id=1, source_target_pairs={{0,1},{1,0},{2,3},{3,2},{4,5},{5,4},{6,7},{7,6},{8,9},{9,8},{10,11... | collective-permute-start | bytes 491528 | tf_op jit(solution)/shard_map/ppermute | solution.py:494
  32.4 2.8 %collective-permute-start.8 = (f32[4,32,640]{2,1,0:T(8,128)S(1)}, f32[4,32,640]{2,1,0:T(8,128)S(1)}, u32[]{:S(2)}, u32[]{:S(2)}) collective-permute-start(f32[4,32,640]{2,1,0:T(8,128)S(1)} %get-tuple-element.70), channel_id=1, source_target_pairs={{0,1},{1,0},{2,3},{3,2},{4,5},{5,4},{6,7},{7,6},{8,9},{9,8},{10,11... | collective-permute-start | bytes 983048 | tf_op jit(solution)/shard_map/ppermute | solution.py:508
  32.7 4.0 %collective-permute-start.7 = (f32[1,128]{1,0:T(1,128)S(1)}, f32[1,128]{1,0:T(1,128)S(1)}, u32[]{:S(2)}, u32[]{:S(2)}) collective-permute-start(f32[1,128]{1,0:T(1,128)S(1)} %get-tuple-element.68), channel_id=1, source_target_pairs={{0,2},{2,0},{4,6},{6,4},{8,10},{10,8},{12,14},{14,12},{1,3},{3,1},... | collective-permute-start | bytes 1544 | tf_op jit(solution)/shard_map/ppermute | solution.py:505
  36.7 3.9 %collective-permute-start.9 = (f32[1,128]{1,0:T(1,128)S(1)}, f32[1,128]{1,0:T(1,128)S(1)}, u32[]{:S(2)}, u32[]{:S(2)}) collective-permute-start(f32[1,128]{1,0:T(1,128)S(1)} %add.44), channel_id=1, source_target_pairs={{0,4},{2,6},{4,0},{6,2},{8,12},{10,14},{12,8},{14,10},{1,5},{3,7},... | collective-permute-start | bytes 1544 | tf_op jit(solution)/shard_map/ppermute | solution.py:505
  39.1 4.6 %collective-permute-start.11 = (f32[4,32,640]{2,1,0:T(8,128)}, f32[4,32,640]{2,1,0:T(8,128)S(1)}, u32[]{:S(2)}, u32[]{:S(2)}) collective-permute-start(f32[4,32,640]{2,1,0:T(8,128)} %get-tuple-element.66), channel_id=1, source_target_pairs={{0,1},{1,0},{2,3},{3,2},{4,5},{5,4},{6,7},{7,6},{8,9},{9,8},{10,11... | collective-permute-start | bytes 983048 | tf_op jit(solution)/shard_map/ppermute | solution.py:498
  40.6 3.0 %collective-permute-start.12 = (f32[4,32,640]{2,1,0:T(8,128)S(1)}, f32[4,32,640]{2,1,0:T(8,128)S(1)}, u32[]{:S(2)}, u32[]{:S(2)}) collective-permute-start(f32[4,32,640]{2,1,0:T(8,128)S(1)} %get-tuple-element.83), channel_id=1, source_target_pairs={{0,1},{1,0},{2,3},{3,2},{4,5},{5,4},{6,7},{7,6},{8,9},{9,8},{10,11... | collective-permute-start | bytes 983048 | tf_op jit(solution)/shard_map/ppermute | solution.py:522
  40.9 4.4 %collective-permute-start.10 = (f32[1,128]{1,0:T(1,128)S(1)}, f32[1,128]{1,0:T(1,128)S(1)}, u32[]{:S(2)}, u32[]{:S(2)}) collective-permute-start(f32[1,128]{1,0:T(1,128)S(1)} %add.45), channel_id=1, source_target_pairs={{0,8},{2,10},{4,12},{6,14},{8,0},{10,2},{12,4},{14,6},{1,9},{3,11}... | collective-permute-start | bytes 1544 | tf_op jit(solution)/shard_map/ppermute | solution.py:505

commit v12 on v11

--- a/solution.py
+++ b/solution.py
@@ -404,7 +404,6 @@
         name="rest",
     )(*fields)
     from_across = [lax.ppermute(part, "lat", across) for part in outer[:-1]]
-    top = lax.ppermute(courant_row, "lat", downward)
 
     sides = lax.ppermute(sides, "lon", swap)
     base, north, lat_courant = pl.pallas_call(
@@ -438,7 +437,8 @@
 
     base, scale, owner_of, surface, decay = lax.optimization_barrier((base, scale, owner_of, surface, decay))
 
-    base, outer = lax.optimization_barrier((base, outer))
+    base, outer, courant_row = lax.optimization_barrier((base, outer, courant_row))
+    top = lax.ppermute(courant_row, "lat", downward)
     from_across.append(lax.ppermute(outer[-1], "lat", across))
 
     circles = jax.ShapeDtypeStruct((half, rows, levels, width), f32)

time: 46.2 us -> 47.7 us (1.032)
  starting transfers between devices: 15.3 us -> 16.8 us
  waiting for transfers between devices: 10.8 us -> 9.98 us
  local copies, waits for them, and re-layouts: 2.11 us -> 2.81 us
    ppermute x1, waiting for transfers between devices: 5.58 us -> 0.01 us  [on_device(): from_inside = lax.ppermute(inner, 'lat', inside)]
    ppermute x1, waiting for transfers between devices: 1.29 us -> 5.99 us  [on_device(): top = lax.ppermute(courant_row, 'lat', downward)]
    ppermute x3, starting transfers between devices: 7.6 us -> 9.11 us  [send_energy(): lax.ppermute(energy, 'lat', [(i, i ^ distance) for i in range(lat_count)])]
    unnamed x38, local copies, waits for them, and re-layouts: 1.81 us -> 2.5 us
  transfers between devices with their start and end apart: 13 -> 13, of which waited for: 8 -> 7; matrix products, arithmetic and copies ran while one was open for 1% -> 1% of each run, Pallas kernels for 30% -> 30%
where the time goes in v12:
time: 47.7 us; the launch traced here: 47.4 us
  starting transfers between devices  16.8 us (35%)
  Pallas kernels  16.1 us (34%)
  waiting for transfers between devices  9.98 us (21%)
  local copies, waits for them, and re-layouts  2.81 us (6%)
  between operations  0.98 us (2%)
  other arithmetic  0.72 us (2%)
    ppermute x3, starting transfers between devices, send_energy(): lax.ppermute(energy, 'lat', [(i, i ^ distance) for i in range(lat_count)])  9.11 us
    ppermute x1, waiting for transfers between devices, on_device(): top = lax.ppermute(courant_row, 'lat', downward)  5.99 us
    pallas_call x1, Pallas kernels, on_device(): pl.pallas_call(functools.partial(base_kernel, width), in_specs=[in_hbm, i...  3.99 us
    pallas_call x2, Pallas kernels, run_inverse(): pl.pallas_call(functools.partial(inverse_kernel, radix, len(other)), in_s...  3.24 us
    ppermute x1, starting transfers between devices, on_device(): from_inside = lax.ppermute(inner, 'lat', inside)  3 us
    pallas_call x1, Pallas kernels, on_device(): pl.pallas_call(rest_kernel, in_specs=[in_hbm] * 3, out_specs=[whole] * (h...  2.67 us
    unnamed x38, local copies, waits for them, and re-layouts  2.5 us
    pallas_call x2, Pallas kernels, run_physics(): pl.pallas_call(functools.partial(physics_kernel, levels, sector, lat_coun...  2.27 us
  transfers between devices with their start and end apart: 13, of which 7 were waited for; matrix products, arithmetic and copies ran while one was open for 1% of the time, Pallas kernels for 30%

profile of v12, /device:TPU:0, one launch (start us, length us, event | category | flops | bytes accessed | tf_op | source)
XLA Modules:
  0.0 47.4 jit_solution(14971416894116544331)
XLA Ops:
  0.6 1.4 %pack.1 = f32[128,1152]{1,0:T(8,128)S(1)} custom-call(f32[4,32,4,576]{3,2,1,0:T(4,128)} %tracer_hbm.3), custom_call_target="tpu_custom_call" | custom-call | bytes 600000 | tf_op jit(solution)/shard_map/pack/pallas_call | solution.py:379
  2.0 0.0 copy-start.14
  2.0 0.0 copy-start.15
  2.0 0.0 copy-start.17
  2.0 0.0 copy-start.18
  2.0 0.0 copy-start.13
  2.1 3.0 %collective-permute-start.1 = (f32[128,1152]{1,0:T(8,128)S(1)}, f32[128,1152]{1,0:T(8,128)S(1)}, u32[]{:S(2)}, u32[]{:S(2)}) collective-permute-start(f32[128,1152]{1,0:T(8,128)S(1)} %pack.1), channel_id=1, source_target_pairs={{0,2},{2,0},{4,6},{6,4},{8,10},{10,8},{12,14},{14,12},{1,3},{3,1},... | collective-permute-start | bytes 1769480 | tf_op jit(solution)/shard_map/ppermute | solution.py:389
  5.1 2.7 %rest.1 = (f32[64,1152]{1,0:T(8,128)}, f32[64,1152]{1,0:T(8,128)S(1)}, f32[16,1152]{1,0:T(8,128)S(1)}, f32[5,4,32,128]{3,2,1,0:T(8,128)S(1)}) custom-call(f32[4,32,4,576]{3,2,1,0:T(4,128)} %tracer_hbm.3, f32[32,4,576]{2,1,0:T(4,128)} %lat_hbm.1, f32[32,4,576]{2,1,0:T(4,128)} %lon_hbm.1), custom_call_target="tpu_custom_call" | custom-call | tf_op jit(solution)/shard_map/rest/pallas_call | solution.py:392
  7.7 0.0 copy-start.12
  7.7 0.7 %copy-done.12 = f32[64,1152]{1,0:T(8,128)} copy-done((f32[64,1152]{1,0:T(8,128)}, f32[64,1152]{1,0:T(8,128)S(1)}, u32[]{:S(2)}) %copy-start.12) | copy-done | bytes 294936
  8.5 1.5 %collective-permute-start.4 = (f32[64,1152]{1,0:T(8,128)}, f32[64,1152]{1,0:T(8,128)}, u32[]{:S(2)}, u32[]{:S(2)}) collective-permute-start(f32[64,1152]{1,0:T(8,128)} %get-tuple-element.51), channel_id=1, source_target_pairs={{2,4},{4,2},{6,8},{8,6},{10,12},{12,10},{3,5},{5,3},{7,9},{9,7},{1... | collective-permute-start | bytes 884744 | tf_op jit(solution)/shard_map/ppermute | solution.py:406
  10.0 0.0 collective-permute-start
  10.0 0.0 copy-done.14
  10.0 0.0 copy-done.15
  10.0 0.0 copy-done.17
  10.0 0.0 copy-start.10
  10.1 0.1 select_multiply_fusion.refs_6_.refs_5_
  10.1 0.1 broadcast_in_dim.27
  10.2 0.1 reshape_reshape.3
  10.3 1.3 %collective-permute-done.side_ref = f32[5,4,32,128]{3,2,1,0:T(8,128)S(1)} collective-permute-done((f32[5,4,32,128]{3,2,1,0:T(8,128)S(1)}, f32[5,4,32,128]{3,2,1,0:T(8,128)S(1)}, u32[]{:S(2)}, u32[]{:S(2)}) %collective-permute-start) | collective-permute-done | bytes 327712 | tf_op jit(solution)/shard_map/ppermute | solution.py:408
  11.6 0.7 %copy-done.4 = f32[5,4,32,128]{3,2,1,0:T(8,128)} copy-done((f32[5,4,32,128]{3,2,1,0:T(8,128)}, f32[5,4,32,128]{3,2,1,0:T(8,128)S(1)}, u32[]{:S(2)}) %copy-start.4) | copy-done | bytes 327704
  12.3 1.0 %copy-done.5 = f32[5,4,32,128]{3,2,1,0:T(8,128)S(1)} copy-done((f32[5,4,32,128]{3,2,1,0:T(8,128)S(1)}, f32[5,4,32,128]{3,2,1,0:T(8,128)}, u32[]{:S(2)}) %copy-start.5) | copy-done | bytes 327704
  13.3 4.0 %base.1 = (f32[4,4,32,640]{3,2,1,0:T(8,128)S(1)}, f32[4,32,640]{2,1,0:T(8,128)S(1)}, f32[4,32,640]{2,1,0:T(8,128)S(1)}) custom-call(f32[4,32,4,576]{3,2,1,0:T(4,128)} %tracer_hbm.3, f32[32,4,576]{2,1,0:T(4,128)} %lat_hbm.1, f32[32,4,576]{2,1,0:T(4,128)} %lon_hbm.1, f32[5,4,32,128]{3,2,1,0:T(8,128)S(1)} %copy-done.5), custom_call_target="tpu_custom_call" | custom-call | tf_op jit(solution)/shard_map/base/pallas_call | solution.py:409
  17.3 1.3 %collective-permute-start.3 = (f32[16,1152]{1,0:T(8,128)S(1)}, f32[16,1152]{1,0:T(8,128)S(1)}, u32[]{:S(2)}, u32[]{:S(2)}) collective-permute-start(f32[16,1152]{1,0:T(8,128)S(1)} %get-tuple-element.57), channel_id=1, source_target_pairs={{2,0},{4,2},{6,4},{8,6},{10,8},{12,10},{14,12},{3,1},{5,3},{7,5},{... | collective-permute-start | bytes 221192 | tf_op jit(solution)/shard_map/ppermute | solution.py:441
  18.6 0.1 copy.22.refs_8_
  18.7 0.7 %collective-permute-start.2 = (f32[64,1152]{1,0:T(8,128)}, f32[64,1152]{1,0:T(8,128)S(1)}, u32[]{:S(2)}, u32[]{:S(2)}) collective-permute-start(f32[64,1152]{1,0:T(8,128)} %copy-done.12), channel_id=1, source_target_pairs={{2,4},{4,2},{6,8},{8,6},{10,12},{12,10},{3,5},{5,3},{7,9},{9,7},{1... | collective-permute-start | bytes 884744 | tf_op jit(solution)/shard_map/ppermute | solution.py:442
  19.4 0.0 collective-permute-done.4.refs_3_
  19.4 6.0 %collective-permute-done.3.refs_4_ = f32[16,1152]{1,0:T(8,128)S(1)} collective-permute-done((f32[16,1152]{1,0:T(8,128)S(1)}, f32[16,1152]{1,0:T(8,128)S(1)}, u32[]{:S(2)}, u32[]{:S(2)}) %collective-permute-start.3) | collective-permute-done | bytes 73760 | tf_op jit(solution)/shard_map/ppermute | solution.py:441
  25.4 0.0 collective-permute-done.1.refs_2_
  25.4 0.0 copy-start.2
  25.4 0.0 copy-start.3
  25.4 0.0 copy-start.8
  25.5 0.0 copy-start.9
  25.5 1.6 %physics.2 = (f32[4,32,640]{2,1,0:T(8,128)S(1)}, f32[4,32,640]{2,1,0:T(8,128)S(1)}, f32[4,8,640]{2,1,0:T(8,128)S(1)}) custom-call(f32[4,4,32,640]{3,2,1,0:T(8,128)S(1)} %get-tuple-element.54.refs_0_, f32[4,32,640]{2,1,0:T(8,128)S(1)} %get-tuple-element.55.refs_1_, f32[128,1152]{1,0:T(8,128)S(1)} %collective-permute-done.1.refs_2_, ...), custom_call_target="tpu_custom_call" | custom-call | tf_op jit(solution)/shard_map/physics/pallas_call | solution.py:451
  27.1 0.0 copy-start
  27.1 0.0 copy-start.1
  27.1 0.0 copy-start.6
  27.1 0.0 copy-start.7
  27.1 0.0 copy-start.11
  27.1 0.1 collective-permute-start.6
  27.2 0.5 %collective-permute-start.5 = (f32[2,32,640]{2,1,0:T(8,128)S(1)}, f32[2,32,640]{2,1,0:T(8,128)S(1)}, u32[]{:S(2)}, u32[]{:S(2)}) collective-permute-start(f32[2,32,640]{2,1,0:T(8,128)S(1)} %get-tuple-element.89), channel_id=1, source_target_pairs={{0,1},{1,0},{2,3},{3,2},{4,5},{5,4},{6,7},{7,6},{8,9},{9,8},{10,11... | collective-permute-start | bytes 491528 | tf_op jit(solution)/shard_map/ppermute | solution.py:494
  27.7 0.9 %collective-permute-done.6.refs_1_ = f32[2,32,640]{2,1,0:T(8,128)S(1)} collective-permute-done((f32[2,32,640]{2,1,0:T(8,128)S(1)}, f32[2,32,640]{2,1,0:T(8,128)S(1)}, u32[]{:S(2)}, u32[]{:S(2)}) %collective-permute-start.6) | collective-permute-done | bytes 163872 | tf_op jit(solution)/shard_map/ppermute | solution.py:494
  28.6 0.2 collective-permute-done.5.refs_0_
  28.9 0.0 copy-done.9
  28.9 0.7 %forward.2 = (bf16[128,1152]{1,0:T(8,128)(2,1)S(1)}, bf16[128,1152]{1,0:T(8,128)(2,1)S(1)}) custom-call(f32[4,32,640]{2,1,0:T(8,128)S(1)} %get-tuple-element.63.own_ref, f32[2,32,640]{2,1,0:T(8,128)S(1)} %collective-permute-done.5.refs_0_, f32[2,32,640]{2,1,0:T(8,128)S(1)} %collective-permute-done.6.refs_1_, bf16[1024,256]{1,0:T(8,128)(2,1)S(1)} %copy-done.3, ...), custom_call_target="tpu_custom_call" | custom-call | tf_op jit(solution)/shard_map/forward/pallas_call | solution.py:467
  29.6 2.0 %inverse.2 = (f32[32,4,576]{2,1,0:T(4,128)S(1)}, f32[4,32,640]{2,1,0:T(8,128)}) custom-call(s32[4]{0:T(128)S(1)} %copy-done.11, f32[4,32,640]{2,1,0:T(8,128)S(1)} %get-tuple-element.63.own_ref, f32[2,32,640]{2,1,0:T(8,128)S(1)} %collective-permute-done.5.refs_0_, f32[2,32,640]{2,1,0:T(8,128)S(1)} %collective-permute-done.6.refs_1_, ...), custom_call_target="tpu_custom_call" | custom-call | tf_op jit(solution)/shard_map/inverse/pallas_call | solution.py:479
  31.6 0.0 collective-permute-done.2.refs_3_
  31.6 0.7 %physics.3 = (f32[4,32,640]{2,1,0:T(8,128)S(1)}, f32[4,32,640]{2,1,0:T(8,128)S(1)}, f32[1,128]{1,0:T(1,128)S(1)}) custom-call(f32[4,4,32,640]{3,2,1,0:T(8,128)S(1)} %get-tuple-element.54.refs_0_, f32[4,32,640]{2,1,0:T(8,128)S(1)} %get-tuple-element.55.refs_1_, f32[128,1152]{1,0:T(8,128)S(1)} %collective-permute-done.1.refs_2_, ...), custom_call_target="tpu_custom_call" | custom-call | tf_op jit(solution)/shard_map/physics/pallas_call | solution.py:451
  32.3 0.3 collective-permute-start.8
  32.6 3.2 %collective-permute-start.7 = (f32[1,128]{1,0:T(1,128)S(1)}, f32[1,128]{1,0:T(1,128)S(1)}, u32[]{:S(2)}, u32[]{:S(2)}) collective-permute-start(f32[1,128]{1,0:T(1,128)S(1)} %get-tuple-element.70), channel_id=1, source_target_pairs={{0,2},{2,0},{4,6},{6,4},{8,10},{10,8},{12,14},{14,12},{1,3},{3,1},... | collective-permute-start | bytes 1544 | tf_op jit(solution)/shard_map/ppermute | solution.py:505
  35.8 0.0 collective-permute-done.8.refs_0_
  35.8 0.7 %forward.3 = (bf16[128,1152]{1,0:T(8,128)(2,1)S(1)}, bf16[128,1152]{1,0:T(8,128)(2,1)S(1)}) custom-call(f32[4,32,640]{2,1,0:T(8,128)S(1)} %get-tuple-element.71.own_ref, f32[4,32,640]{2,1,0:T(8,128)S(1)} %collective-permute-done.8.refs_0_, bf16[1024,256]{1,0:T(8,128)(2,1)S(1)} %copy-done.3, bf16[1024,256]{1,0:T(8,128)(2,1)S(1)} %copy-done.2, ...), custom_call_target="tpu_custom_call" | custom-call | tf_op jit(solution)/shard_map/forward/pallas_call | solution.py:467
  36.5 0.8 %collective-permute-done.7 = f32[1,128]{1,0:T(1,128)S(1)} collective-permute-done((f32[1,128]{1,0:T(1,128)S(1)}, f32[1,128]{1,0:T(1,128)S(1)}, u32[]{:S(2)}, u32[]{:S(2)}) %collective-permute-start.7) | collective-permute-done | bytes 544 | tf_op jit(solution)/shard_map/ppermute | solution.py:505
  37.3 3.2 %collective-permute-start.9 = (f32[1,128]{1,0:T(1,128)S(1)}, f32[1,128]{1,0:T(1,128)S(1)}, u32[]{:S(2)}, u32[]{:S(2)}) collective-permute-start(f32[1,128]{1,0:T(1,128)S(1)} %add.44), channel_id=1, source_target_pairs={{0,4},{2,6},{4,0},{6,2},{8,12},{10,14},{12,8},{14,10},{1,5},{3,7},... | collective-permute-start | bytes 1544 | tf_op jit(solution)/shard_map/ppermute | solution.py:505
  40.5 0.0 collective-permute-start.11
  40.5 1.3 %inverse.3 = (f32[32,4,576]{2,1,0:T(4,128)S(1)}, f32[4,32,640]{2,1,0:T(8,128)S(1)}) custom-call(s32[4]{0:T(128)S(1)} %copy-done.11, f32[4,32,640]{2,1,0:T(8,128)S(1)} %get-tuple-element.71.own_ref, f32[4,32,640]{2,1,0:T(8,128)S(1)} %collective-permute-done.8.refs_0_, bf16[128,1152]{1,0:T(8,128)(2,1)S(1)} %get-tuple-element.77.refs_1_, ...), custom_call_target="tpu_custom_call" | custom-call | tf_op jit(solution)/shard_map/inverse/pallas_call | solution.py:479
  41.8 0.3 collective-permute-done.9
  42.0 0.3 collective-permute-start.12
  42.4 2.7 %collective-permute-start.10 = (f32[1,128]{1,0:T(1,128)S(1)}, f32[1,128]{1,0:T(1,128)S(1)}, u32[]{:S(2)}, u32[]{:S(2)}) collective-permute-start(f32[1,128]{1,0:T(1,128)S(1)} %add.45), channel_id=1, source_target_pairs={{0,8},{2,10},{4,12},{6,14},{8,0},{10,2},{12,4},{14,6},{1,9},{3,11}... | collective-permute-start | bytes 1544 | tf_op jit(solution)/shard_map/ppermute | solution.py:505
  45.1 0.0 collective-permute-done.11.refs_2_
  45.1 0.0 collective-permute-done.12.refs_3_
  45.1 1.2 %finish.1 = f32[4,32,4,576]{3,2,1,0:T(4,128)} custom-call(f32[32,4,576]{2,1,0:T(4,128)S(1)} %get-tuple-element.83.refs_0_, f32[32,4,576]{2,1,0:T(4,128)S(1)} %get-tuple-element.84.refs_1_, f32[4,32,640]{2,1,0:T(8,128)S(1)} %collective-permute-done.11.refs_2_, f32[4,32,640]{2,1,0:T(8,128)S(1)} %collective-permute-done.12.refs_3_), custom_call_target="tpu_custom_call" | custom-call | bytes 3000000 | tf_op jit(solution)/shard_map/finish/pallas_call | solution.py:525
  46.3 0.5 %collective-permute-done.10 = f32[1,128]{1,0:T(1,128)S(1)} collective-permute-done((f32[1,128]{1,0:T(1,128)S(1)}, f32[1,128]{1,0:T(1,128)S(1)}, u32[]{:S(2)}, u32[]{:S(2)}) %collective-permute-start.10) | collective-permute-done | bytes 544 | tf_op jit(solution)/shard_map/ppermute | solution.py:505
  46.8 0.6 %fusion.1 = f32[1,1]{1,0:T(1,128)} fusion(f32[1,128]{1,0:T(1,128)S(1)} %add.46, s32[]{:T(128)S(6)} %select_n.8), kind=kLoop, calls=%fused_computation.4 | loop fusion | flops 1 | bytes 12 | tf_op jit(solution)/shard_map/div | solution.py:543
  (23 shorter events, 0.1 us)
Async XLA Ops:
  2.0 8.0 %copy-start.14 = (f32[1152]{0:T(1024)S(1)}, f32[1152]{0:T(1024)}, u32[]{:S(2)}) copy-start(f32[1152]{0:T(1024)} %constant.56.clone) | copy-start | bytes 13828
  2.0 8.0 %copy-start.15 = (f32[1152]{0:T(1024)S(1)}, f32[1152]{0:T(1024)}, u32[]{:S(2)}) copy-start(f32[1152]{0:T(1024)} %constant.54.clone) | copy-start | bytes 13828
  2.0 8.0 %copy-start.17 = (pred[1152]{0:T(1024)(128)(4,1)S(1)}, pred[1152]{0:T(1024)(128)(4,1)}, u32[]{:S(2)}) copy-start(pred[1152]{0:T(1024)(128)(4,1)} %constant.55.clone) | copy-start | bytes 3460
  2.0 8.1 %copy-start.18 = (s32[1,1,18,1]{2,3,1,0:T(1,128)S(1)}, s32[1,1,18,1]{2,3,1,0:T(1,128)}, u32[]{:S(2)}) copy-start(s32[1,1,18,1]{2,3,1,0:T(1,128)} %param.25) | copy-start | bytes 220
  2.0 8.3 %copy-start.13 = (f32[4,4,576]{2,1,0:T(4,128)S(1)}, f32[4,4,576]{2,1,0:T(4,128)}, u32[]{:S(2)}) copy-start(f32[4,4,576]{2,1,0:T(4,128)} %param.22) | copy-start | bytes 110596
  2.1 23.3 %collective-permute-start.1 = (f32[128,1152]{1,0:T(8,128)S(1)}, f32[128,1152]{1,0:T(8,128)S(1)}, u32[]{:S(2)}, u32[]{:S(2)}) collective-permute-start(f32[128,1152]{1,0:T(8,128)S(1)} %pack.1), channel_id=1, source_target_pairs={{0,2},{2,0},{4,6},{6,4},{8,10},{10,8},{12,14},{14,12},{1,3},{3,1},... | collective-permute-start | bytes 1769480 | tf_op jit(solution)/shard_map/ppermute | solution.py:389
  7.7 0.7 %copy-start.12 = (f32[64,1152]{1,0:T(8,128)}, f32[64,1152]{1,0:T(8,128)S(1)}, u32[]{:S(2)}) copy-start(f32[64,1152]{1,0:T(8,128)S(1)} %get-tuple-element.56) | copy-start | bytes 884740
  8.4 10.2 %copy-start.16 = (f32[4,32]{1,0:T(4,128)S(1)}, f32[4,32]{1,0:T(4,128)}, u32[]{:S(2)}) copy-start(f32[4,32]{1,0:T(4,128)} %param.24) | copy-start | bytes 1540
  8.5 10.9 %collective-permute-start.4 = (f32[64,1152]{1,0:T(8,128)}, f32[64,1152]{1,0:T(8,128)}, u32[]{:S(2)}, u32[]{:S(2)}) collective-permute-start(f32[64,1152]{1,0:T(8,128)} %get-tuple-element.51), channel_id=1, source_target_pairs={{2,4},{4,2},{6,8},{8,6},{10,12},{12,10},{3,5},{5,3},{7,9},{9,7},{1... | collective-permute-start | bytes 884744 | tf_op jit(solution)/shard_map/ppermute | solution.py:406
  10.0 1.6 %collective-permute-start = (f32[5,4,32,128]{3,2,1,0:T(8,128)S(1)}, f32[5,4,32,128]{3,2,1,0:T(8,128)S(1)}, u32[]{:S(2)}, u32[]{:S(2)}) collective-permute-start(f32[5,4,32,128]{3,2,1,0:T(8,128)S(1)} %get-tuple-element.48), channel_id=1, source_target_pairs={{0,1},{1,0},{2,3},{3,2},{4,5},{5,4},{6,7},{7,6},{8,9},{9,8},{10,11... | collective-permute-start | bytes 983048 | tf_op jit(solution)/shard_map/ppermute | solution.py:408
  10.0 15.4 %copy-start.10 = (f32[32,32]{1,0:T(8,128)S(1)}, f32[32,32]{1,0:T(8,128)}, u32[]{:S(2)}) copy-start(f32[32,32]{1,0:T(8,128)} %refs_7_.4) | copy-start | bytes 12292
  11.6 0.7 %copy-start.4 = (f32[5,4,32,128]{3,2,1,0:T(8,128)}, f32[5,4,32,128]{3,2,1,0:T(8,128)S(1)}, u32[]{:S(2)}) copy-start(f32[5,4,32,128]{3,2,1,0:T(8,128)S(1)} %collective-permute-done.side_ref) | copy-start | bytes 983044
  12.3 1.0 %copy-start.5 = (f32[5,4,32,128]{3,2,1,0:T(8,128)S(1)}, f32[5,4,32,128]{3,2,1,0:T(8,128)}, u32[]{:S(2)}) copy-start(f32[5,4,32,128]{3,2,1,0:T(8,128)} %copy-done.4) | copy-start | bytes 983044
  17.3 8.1 %collective-permute-start.3 = (f32[16,1152]{1,0:T(8,128)S(1)}, f32[16,1152]{1,0:T(8,128)S(1)}, u32[]{:S(2)}, u32[]{:S(2)}) collective-permute-start(f32[16,1152]{1,0:T(8,128)S(1)} %get-tuple-element.57), channel_id=1, source_target_pairs={{2,0},{4,2},{6,4},{8,6},{10,8},{12,10},{14,12},{3,1},{5,3},{7,5},{... | collective-permute-start | bytes 221192 | tf_op jit(solution)/shard_map/ppermute | solution.py:441
  18.7 12.9 %collective-permute-start.2 = (f32[64,1152]{1,0:T(8,128)}, f32[64,1152]{1,0:T(8,128)S(1)}, u32[]{:S(2)}, u32[]{:S(2)}) collective-permute-start(f32[64,1152]{1,0:T(8,128)} %copy-done.12), channel_id=1, source_target_pairs={{2,4},{4,2},{6,8},{8,6},{10,12},{12,10},{3,5},{5,3},{7,9},{9,7},{1... | collective-permute-start | bytes 884744 | tf_op jit(solution)/shard_map/ppermute | solution.py:442
  25.4 3.4 %copy-start.2 = (bf16[1024,256]{1,0:T(8,128)(2,1)S(1)}, bf16[1024,256]{1,0:T(8,128)(2,1)}, u32[]{:S(2)}) copy-start(bf16[1024,256]{1,0:T(8,128)(2,1)} %constant.58.clone.refs_3_.refs_2_) | copy-start | bytes 1572868
  25.4 3.4 %copy-start.3 = (bf16[1024,256]{1,0:T(8,128)(2,1)S(1)}, bf16[1024,256]{1,0:T(8,128)(2,1)}, u32[]{:S(2)}) copy-start(bf16[1024,256]{1,0:T(8,128)(2,1)} %constant.57.clone.refs_2_.refs_1_) | copy-start | bytes 1572868
  25.4 3.4 %copy-start.8 = (bf16[128,128]{1,0:T(8,128)(2,1)S(1)}, bf16[128,128]{1,0:T(8,128)(2,1)}, u32[]{:S(2)}) copy-start(bf16[128,128]{1,0:T(8,128)(2,1)} %constant.60.clone.refs_5_.refs_4_) | copy-start | bytes 98308
  25.5 3.4 %copy-start.9 = (bf16[128,128]{1,0:T(8,128)(2,1)S(1)}, bf16[128,128]{1,0:T(8,128)(2,1)}, u32[]{:S(2)}) copy-start(bf16[128,128]{1,0:T(8,128)(2,1)} %constant.59.clone.refs_4_.refs_3_) | copy-start | bytes 98308
  27.1 2.5 %copy-start = (bf16[1024,256]{1,0:T(8,128)(2,1)S(1)}, bf16[1024,256]{1,0:T(8,128)(2,1)}, u32[]{:S(2)}) copy-start(bf16[1024,256]{1,0:T(8,128)(2,1)} %constant.62.clone.refs_5_.refs_4_) | copy-start | bytes 1572868
  27.1 2.5 %copy-start.1 = (bf16[1024,256]{1,0:T(8,128)(2,1)S(1)}, bf16[1024,256]{1,0:T(8,128)(2,1)}, u32[]{:S(2)}) copy-start(bf16[1024,256]{1,0:T(8,128)(2,1)} %constant.61.clone.refs_4_.refs_3_) | copy-start | bytes 1572868
  27.1 2.5 %copy-start.6 = (bf16[128,128]{1,0:T(8,128)(2,1)S(1)}, bf16[128,128]{1,0:T(8,128)(2,1)}, u32[]{:S(2)}) copy-start(bf16[128,128]{1,0:T(8,128)(2,1)} %constant.64.clone.refs_7_.refs_6_) | copy-start | bytes 98308
  27.1 2.5 %copy-start.7 = (bf16[128,128]{1,0:T(8,128)(2,1)S(1)}, bf16[128,128]{1,0:T(8,128)(2,1)}, u32[]{:S(2)}) copy-start(bf16[128,128]{1,0:T(8,128)(2,1)} %constant.63.clone.refs_6_.refs_5_) | copy-start | bytes 98308
  27.1 2.5 %copy-start.11 = (s32[4]{0:T(128)S(1)}, s32[4]{0:T(128)}, u32[]{:S(2)}) copy-start(s32[4]{0:T(128)} %mask_ref.3) | copy-start | bytes 52
  27.1 1.5 %collective-permute-start.6 = (f32[2,32,640]{2,1,0:T(8,128)S(1)}, f32[2,32,640]{2,1,0:T(8,128)S(1)}, u32[]{:S(2)}, u32[]{:S(2)}) collective-permute-start(f32[2,32,640]{2,1,0:T(8,128)S(1)} %get-tuple-element.88), channel_id=1, source_target_pairs={{0,1},{1,0},{2,3},{3,2},{4,5},{5,4},{6,7},{7,6},{8,9},{9,8},{10,11... | collective-permute-start | bytes 491528 | tf_op jit(solution)/shard_map/ppermute | solution.py:494
  27.2 1.6 %collective-permute-start.5 = (f32[2,32,640]{2,1,0:T(8,128)S(1)}, f32[2,32,640]{2,1,0:T(8,128)S(1)}, u32[]{:S(2)}, u32[]{:S(2)}) collective-permute-start(f32[2,32,640]{2,1,0:T(8,128)S(1)} %get-tuple-element.89), channel_id=1, source_target_pairs={{0,1},{1,0},{2,3},{3,2},{4,5},{5,4},{6,7},{7,6},{8,9},{9,8},{10,11... | collective-permute-start | bytes 491528 | tf_op jit(solution)/shard_map/ppermute | solution.py:494
  32.3 3.5 %collective-permute-start.8 = (f32[4,32,640]{2,1,0:T(8,128)S(1)}, f32[4,32,640]{2,1,0:T(8,128)S(1)}, u32[]{:S(2)}, u32[]{:S(2)}) collective-permute-start(f32[4,32,640]{2,1,0:T(8,128)S(1)} %get-tuple-element.72), channel_id=1, source_target_pairs={{0,1},{1,0},{2,3},{3,2},{4,5},{5,4},{6,7},{7,6},{8,9},{9,8},{10,11... | collective-permute-start | bytes 983048 | tf_op jit(solution)/shard_map/ppermute | solution.py:508
  32.6 4.7 %collective-permute-start.7 = (f32[1,128]{1,0:T(1,128)S(1)}, f32[1,128]{1,0:T(1,128)S(1)}, u32[]{:S(2)}, u32[]{:S(2)}) collective-permute-start(f32[1,128]{1,0:T(1,128)S(1)} %get-tuple-element.70), channel_id=1, source_target_pairs={{0,2},{2,0},{4,6},{6,4},{8,10},{10,8},{12,14},{14,12},{1,3},{3,1},... | collective-permute-start | bytes 1544 | tf_op jit(solution)/shard_map/ppermute | solution.py:505
  37.3 4.7 %collective-permute-start.9 = (f32[1,128]{1,0:T(1,128)S(1)}, f32[1,128]{1,0:T(1,128)S(1)}, u32[]{:S(2)}, u32[]{:S(2)}) collective-permute-start(f32[1,128]{1,0:T(1,128)S(1)} %add.44), channel_id=1, source_target_pairs={{0,4},{2,6},{4,0},{6,2},{8,12},{10,14},{12,8},{14,10},{1,5},{3,7},... | collective-permute-start | bytes 1544 | tf_op jit(solution)/shard_map/ppermute | solution.py:505
  40.5 4.6 %collective-permute-start.11 = (f32[4,32,640]{2,1,0:T(8,128)}, f32[4,32,640]{2,1,0:T(8,128)S(1)}, u32[]{:S(2)}, u32[]{:S(2)}) collective-permute-start(f32[4,32,640]{2,1,0:T(8,128)} %get-tuple-element.68), channel_id=1, source_target_pairs={{0,1},{1,0},{2,3},{3,2},{4,5},{5,4},{6,7},{7,6},{8,9},{9,8},{10,11... | collective-permute-start | bytes 983048 | tf_op jit(solution)/shard_map/ppermute | solution.py:498
  42.0 3.0 %collective-permute-start.12 = (f32[4,32,640]{2,1,0:T(8,128)S(1)}, f32[4,32,640]{2,1,0:T(8,128)S(1)}, u32[]{:S(2)}, u32[]{:S(2)}) collective-permute-start(f32[4,32,640]{2,1,0:T(8,128)S(1)} %get-tuple-element.85), channel_id=1, source_target_pairs={{0,1},{1,0},{2,3},{3,2},{4,5},{5,4},{6,7},{7,6},{8,9},{9,8},{10,11... | collective-permute-start | bytes 983048 | tf_op jit(solution)/shard_map/ppermute | solution.py:522
  42.4 4.4 %collective-permute-start.10 = (f32[1,128]{1,0:T(1,128)S(1)}, f32[1,128]{1,0:T(1,128)S(1)}, u32[]{:S(2)}, u32[]{:S(2)}) collective-permute-start(f32[1,128]{1,0:T(1,128)S(1)} %add.45), channel_id=1, source_target_pairs={{0,8},{2,10},{4,12},{6,14},{8,0},{10,2},{12,4},{14,6},{1,9},{3,11}... | collective-permute-start | bytes 1544 | tf_op jit(solution)/shard_map/ppermute | solution.py:505

commit v13 on v11

--- a/solution.py
+++ b/solution.py
@@ -105,8 +105,12 @@
     courant_ref, side_ref, tracer_ref, lat_ref, lon_ref, sems = refs[-6:]
     outer_refs = refs[:-6]
     count, levels, rows, sector = tracer_ref.shape
-    pairs = [(tracer_hbm.at[t], tracer_ref.at[t]) for t in range(count)] + [(lat_hbm, lat_ref), (lon_hbm, lon_ref)]
-    copies = start_copies(pairs, sems)
+    for pairs in (
+        [(lat_hbm, lat_ref), (lon_hbm, lon_ref)],
+        [(tracer_hbm.at[t], tracer_ref.at[t]) for t in range(count)],
+    ):
+        for copy in start_copies(pairs, sems):
+            copy.wait()
     shift, whole = sector % LANES, sector // LANES * LANES
     lane = lax.broadcasted_iota(jnp.int32, (levels, LANES), 1)
     even = is_even()
@@ -116,8 +120,6 @@
         last = jnp.concatenate([values[:, whole:], values[:, whole:]], axis=1)
         side_ref[i, r] = jnp.where(lane < LANES - 2, first, last)
 
-    for copy in copies:
-        copy.wait()
     for t in range(count):
         row = [tracer_ref[t, :, r, :] for r in range(rows)]
         slot = t // len(outer_refs)

time: 46.2 us -> 47.1 us (1.019)
  Pallas kernels: 16 us -> 16.9 us
  starting transfers between devices: 15.3 us -> 16.1 us
  waiting for transfers between devices: 10.8 us -> 10 us
    ppermute x1, waiting for transfers between devices: 1.29 us -> 0.43 us  [on_device(): top = lax.ppermute(courant_row, 'lat', downward)]
    pallas_call x1, Pallas kernels: 2.67 us -> 3.53 us  [on_device(): pl.pallas_call(rest_kernel, in_specs=[in_hbm] * 3, out_specs=[whole] * (h...]
    ppermute x3, starting transfers between devices: 7.6 us -> 8.43 us  [send_energy(): lax.ppermute(energy, 'lat', [(i, i ^ distance) for i in range(lat_count)])]
  transfers between devices with their start and end apart: 13 -> 13, of which waited for: 8 -> 8; matrix products, arithmetic and copies ran while one was open for 1% -> 1% of each run, Pallas kernels for 30% -> 32%
where the time goes in v13:
time: 47.1 us; the launch traced here: 46.8 us
  Pallas kernels  16.9 us (36%)
  starting transfers between devices  16.1 us (34%)
  waiting for transfers between devices  10 us (21%)
  local copies, waits for them, and re-layouts  2.11 us (4%)
  between operations  0.97 us (2%)
  other arithmetic  0.72 us (2%)
    ppermute x3, starting transfers between devices, send_energy(): lax.ppermute(energy, 'lat', [(i, i ^ distance) for i in range(lat_count)])  8.43 us
    ppermute x1, waiting for transfers between devices, on_device(): from_inside = lax.ppermute(inner, 'lat', inside)  5.58 us
    pallas_call x1, Pallas kernels, on_device(): pl.pallas_call(functools.partial(base_kernel, width), in_specs=[in_hbm, i...  3.95 us
    pallas_call x1, Pallas kernels, on_device(): pl.pallas_call(rest_kernel, in_specs=[in_hbm] * 3, out_specs=[whole] * (h...  3.53 us
    pallas_call x2, Pallas kernels, run_inverse(): pl.pallas_call(functools.partial(inverse_kernel, radix, len(other)), in_s...  3.23 us
    ppermute x1, starting transfers between devices, on_device(): from_inside = lax.ppermute(inner, 'lat', inside)  3 us
    pallas_call x2, Pallas kernels, run_physics(): pl.pallas_call(functools.partial(physics_kernel, levels, sector, lat_coun...  2.22 us
    unnamed x38, local copies, waits for them, and re-layouts  1.81 us
  transfers between devices with their start and end apart: 13, of which 8 were waited for; matrix products, arithmetic and copies ran while one was open for 1% of the time, Pallas kernels for 32%

profile of v13, /device:TPU:0, one launch (start us, length us, event | category | flops | bytes accessed | tf_op | source)
XLA Modules:
  0.0 46.8 jit_solution(11467803487029107806)
XLA Ops:
  0.6 1.4 %pack.1 = f32[128,1152]{1,0:T(8,128)S(1)} custom-call(f32[4,32,4,576]{3,2,1,0:T(4,128)} %tracer_hbm.3), custom_call_target="tpu_custom_call" | custom-call | bytes 600000 | tf_op jit(solution)/shard_map/pack/pallas_call | solution.py:381
  2.0 0.0 copy-start.14
  2.0 0.0 copy-start.15
  2.0 0.0 copy-start.17
  2.0 0.0 copy-start.18
  2.0 0.0 copy-start.13
  2.1 3.0 %collective-permute-start.1 = (f32[128,1152]{1,0:T(8,128)S(1)}, f32[128,1152]{1,0:T(8,128)S(1)}, u32[]{:S(2)}, u32[]{:S(2)}) collective-permute-start(f32[128,1152]{1,0:T(8,128)S(1)} %pack.1), channel_id=1, source_target_pairs={{0,2},{2,0},{4,6},{6,4},{8,10},{10,8},{12,14},{14,12},{1,3},{3,1},... | collective-permute-start | bytes 1769480 | tf_op jit(solution)/shard_map/ppermute | solution.py:391
  5.1 3.5 %rest.1 = (f32[64,1152]{1,0:T(8,128)}, f32[64,1152]{1,0:T(8,128)S(1)}, f32[16,1152]{1,0:T(8,128)S(1)}, f32[5,4,32,128]{3,2,1,0:T(8,128)S(1)}) custom-call(f32[4,32,4,576]{3,2,1,0:T(4,128)} %tracer_hbm.3, f32[32,4,576]{2,1,0:T(4,128)} %lat_hbm.1, f32[32,4,576]{2,1,0:T(4,128)} %lon_hbm.1), custom_call_target="tpu_custom_call" | custom-call | tf_op jit(solution)/shard_map/rest/pallas_call | solution.py:394
  8.6 0.0 copy-start.12
  8.6 0.0 copy-start.16
  8.6 1.4 %collective-permute-start.3 = (f32[16,1152]{1,0:T(8,128)S(1)}, f32[16,1152]{1,0:T(8,128)S(1)}, u32[]{:S(2)}, u32[]{:S(2)}) collective-permute-start(f32[16,1152]{1,0:T(8,128)S(1)} %get-tuple-element.55), channel_id=1, source_target_pairs={{2,0},{4,2},{6,4},{8,6},{10,8},{12,10},{14,12},{3,1},{5,3},{7,5},{... | collective-permute-start | bytes 221192 | tf_op jit(solution)/shard_map/ppermute | solution.py:409
  10.1 1.4 %collective-permute-start.4 = (f32[64,1152]{1,0:T(8,128)}, f32[64,1152]{1,0:T(8,128)}, u32[]{:S(2)}, u32[]{:S(2)}) collective-permute-start(f32[64,1152]{1,0:T(8,128)} %get-tuple-element.50), channel_id=1, source_target_pairs={{2,4},{4,2},{6,8},{8,6},{10,12},{12,10},{3,5},{5,3},{7,9},{9,7},{1... | collective-permute-start | bytes 884744 | tf_op jit(solution)/shard_map/ppermute | solution.py:408
  11.4 0.0 collective-permute-start
  11.5 0.0 copy-start.10
  11.5 0.1 select_multiply_fusion.refs_6_.refs_5_
  11.6 0.1 broadcast_in_dim.27
  11.7 0.1 reshape_reshape.3
  11.8 0.0 copy-done.13
  11.8 1.3 %collective-permute-done.side_ref = f32[5,4,32,128]{3,2,1,0:T(8,128)S(1)} collective-permute-done((f32[5,4,32,128]{3,2,1,0:T(8,128)S(1)}, f32[5,4,32,128]{3,2,1,0:T(8,128)S(1)}, u32[]{:S(2)}, u32[]{:S(2)}) %collective-permute-start) | collective-permute-done | bytes 327712 | tf_op jit(solution)/shard_map/ppermute | solution.py:411
  13.1 0.7 %copy-done.4 = f32[5,4,32,128]{3,2,1,0:T(8,128)} copy-done((f32[5,4,32,128]{3,2,1,0:T(8,128)}, f32[5,4,32,128]{3,2,1,0:T(8,128)S(1)}, u32[]{:S(2)}) %copy-start.4) | copy-done | bytes 327704
  13.8 1.0 %copy-done.5 = f32[5,4,32,128]{3,2,1,0:T(8,128)S(1)} copy-done((f32[5,4,32,128]{3,2,1,0:T(8,128)S(1)}, f32[5,4,32,128]{3,2,1,0:T(8,128)}, u32[]{:S(2)}) %copy-start.5) | copy-done | bytes 327704
  14.8 4.0 %base.1 = (f32[4,4,32,640]{3,2,1,0:T(8,128)S(1)}, f32[4,32,640]{2,1,0:T(8,128)S(1)}, f32[4,32,640]{2,1,0:T(8,128)S(1)}) custom-call(f32[4,32,4,576]{3,2,1,0:T(4,128)} %tracer_hbm.3, f32[32,4,576]{2,1,0:T(4,128)} %lat_hbm.1, f32[32,4,576]{2,1,0:T(4,128)} %lon_hbm.1, f32[5,4,32,128]{3,2,1,0:T(8,128)S(1)} %copy-done.5), custom_call_target="tpu_custom_call" | custom-call | tf_op jit(solution)/shard_map/base/pallas_call | solution.py:412
  18.7 0.0 copy-done.16
  18.7 0.1 copy.22.refs_8_
  18.9 0.7 %collective-permute-start.2 = (f32[64,1152]{1,0:T(8,128)}, f32[64,1152]{1,0:T(8,128)S(1)}, u32[]{:S(2)}, u32[]{:S(2)}) collective-permute-start(f32[64,1152]{1,0:T(8,128)} %copy-done.12), channel_id=1, source_target_pairs={{2,4},{4,2},{6,8},{8,6},{10,12},{12,10},{3,5},{5,3},{7,9},{9,7},{1... | collective-permute-start | bytes 884744 | tf_op jit(solution)/shard_map/ppermute | solution.py:444
  19.5 0.4 collective-permute-done.3.refs_4_
  20.0 0.0 collective-permute-done.4.refs_3_
  20.0 5.6 %collective-permute-done.1.refs_2_ = f32[128,1152]{1,0:T(8,128)S(1)} collective-permute-done((f32[128,1152]{1,0:T(8,128)S(1)}, f32[128,1152]{1,0:T(8,128)S(1)}, u32[]{:S(2)}, u32[]{:S(2)}) %collective-permute-start.1) | collective-permute-done | bytes 589856 | tf_op jit(solution)/shard_map/ppermute | solution.py:391
  25.6 0.0 copy-done.10
  25.6 0.0 copy-start.2
  25.6 0.0 copy-start.3
  25.6 0.0 copy-start.8
  25.6 0.0 copy-start.9
  25.6 1.5 %physics.2 = (f32[4,32,640]{2,1,0:T(8,128)S(1)}, f32[4,32,640]{2,1,0:T(8,128)S(1)}, f32[4,8,640]{2,1,0:T(8,128)S(1)}) custom-call(f32[4,4,32,640]{3,2,1,0:T(8,128)S(1)} %get-tuple-element.52.refs_0_, f32[4,32,640]{2,1,0:T(8,128)S(1)} %get-tuple-element.53.refs_1_, f32[128,1152]{1,0:T(8,128)S(1)} %collective-permute-done.1.refs_2_, ...), custom_call_target="tpu_custom_call" | custom-call | tf_op jit(solution)/shard_map/physics/pallas_call | solution.py:453
  27.2 0.0 copy-start
  27.2 0.0 copy-start.1
  27.2 0.0 copy-start.6
  27.2 0.0 copy-start.7
  27.2 0.0 copy-start.11
  27.3 0.1 collective-permute-start.6
  27.3 0.5 %collective-permute-start.5 = (f32[2,32,640]{2,1,0:T(8,128)S(1)}, f32[2,32,640]{2,1,0:T(8,128)S(1)}, u32[]{:S(2)}, u32[]{:S(2)}) collective-permute-start(f32[2,32,640]{2,1,0:T(8,128)S(1)} %get-tuple-element.87), channel_id=1, source_target_pairs={{0,1},{1,0},{2,3},{3,2},{4,5},{5,4},{6,7},{7,6},{8,9},{9,8},{10,11... | collective-permute-start | bytes 491528 | tf_op jit(solution)/shard_map/ppermute | solution.py:496
  27.8 0.9 %collective-permute-done.6.refs_1_ = f32[2,32,640]{2,1,0:T(8,128)S(1)} collective-permute-done((f32[2,32,640]{2,1,0:T(8,128)S(1)}, f32[2,32,640]{2,1,0:T(8,128)S(1)}, u32[]{:S(2)}, u32[]{:S(2)}) %collective-permute-start.6) | collective-permute-done | bytes 163872 | tf_op jit(solution)/shard_map/ppermute | solution.py:496
  28.7 0.2 collective-permute-done.5.refs_0_
  29.0 0.0 copy-done.3
  29.0 0.7 %forward.2 = (bf16[128,1152]{1,0:T(8,128)(2,1)S(1)}, bf16[128,1152]{1,0:T(8,128)(2,1)S(1)}) custom-call(f32[4,32,640]{2,1,0:T(8,128)S(1)} %get-tuple-element.61.own_ref, f32[2,32,640]{2,1,0:T(8,128)S(1)} %collective-permute-done.5.refs_0_, f32[2,32,640]{2,1,0:T(8,128)S(1)} %collective-permute-done.6.refs_1_, bf16[1024,256]{1,0:T(8,128)(2,1)S(1)} %copy-done.3, ...), custom_call_target="tpu_custom_call" | custom-call | tf_op jit(solution)/shard_map/forward/pallas_call | solution.py:469
  29.7 2.0 %inverse.2 = (f32[32,4,576]{2,1,0:T(4,128)S(1)}, f32[4,32,640]{2,1,0:T(8,128)}) custom-call(s32[4]{0:T(128)S(1)} %copy-done.11, f32[4,32,640]{2,1,0:T(8,128)S(1)} %get-tuple-element.61.own_ref, f32[2,32,640]{2,1,0:T(8,128)S(1)} %collective-permute-done.5.refs_0_, f32[2,32,640]{2,1,0:T(8,128)S(1)} %collective-permute-done.6.refs_1_, ...), custom_call_target="tpu_custom_call" | custom-call | tf_op jit(solution)/shard_map/inverse/pallas_call | solution.py:481
  31.7 0.0 collective-permute-done.2.refs_3_
  31.7 0.7 %physics.3 = (f32[4,32,640]{2,1,0:T(8,128)S(1)}, f32[4,32,640]{2,1,0:T(8,128)S(1)}, f32[1,128]{1,0:T(1,128)S(1)}) custom-call(f32[4,4,32,640]{3,2,1,0:T(8,128)S(1)} %get-tuple-element.52.refs_0_, f32[4,32,640]{2,1,0:T(8,128)S(1)} %get-tuple-element.53.refs_1_, f32[128,1152]{1,0:T(8,128)S(1)} %collective-permute-done.1.refs_2_, ...), custom_call_target="tpu_custom_call" | custom-call | tf_op jit(solution)/shard_map/physics/pallas_call | solution.py:453
  32.4 0.3 collective-permute-start.8
  32.7 3.3 %collective-permute-start.7 = (f32[1,128]{1,0:T(1,128)S(1)}, f32[1,128]{1,0:T(1,128)S(1)}, u32[]{:S(2)}, u32[]{:S(2)}) collective-permute-start(f32[1,128]{1,0:T(1,128)S(1)} %get-tuple-element.68), channel_id=1, source_target_pairs={{0,2},{2,0},{4,6},{6,4},{8,10},{10,8},{12,14},{14,12},{1,3},{3,1},... | collective-permute-start | bytes 1544 | tf_op jit(solution)/shard_map/ppermute | solution.py:507
  35.9 0.0 collective-permute-done.8.refs_0_
  35.9 0.7 %forward.3 = (bf16[128,1152]{1,0:T(8,128)(2,1)S(1)}, bf16[128,1152]{1,0:T(8,128)(2,1)S(1)}) custom-call(f32[4,32,640]{2,1,0:T(8,128)S(1)} %get-tuple-element.69.own_ref, f32[4,32,640]{2,1,0:T(8,128)S(1)} %collective-permute-done.8.refs_0_, bf16[1024,256]{1,0:T(8,128)(2,1)S(1)} %copy-done.3, bf16[1024,256]{1,0:T(8,128)(2,1)S(1)} %copy-done.2, ...), custom_call_target="tpu_custom_call" | custom-call | tf_op jit(solution)/shard_map/forward/pallas_call | solution.py:469
  36.6 0.8 %collective-permute-done.7 = f32[1,128]{1,0:T(1,128)S(1)} collective-permute-done((f32[1,128]{1,0:T(1,128)S(1)}, f32[1,128]{1,0:T(1,128)S(1)}, u32[]{:S(2)}, u32[]{:S(2)}) %collective-permute-start.7) | collective-permute-done | bytes 544 | tf_op jit(solution)/shard_map/ppermute | solution.py:507
  37.4 2.5 %collective-permute-start.9 = (f32[1,128]{1,0:T(1,128)S(1)}, f32[1,128]{1,0:T(1,128)S(1)}, u32[]{:S(2)}, u32[]{:S(2)}) collective-permute-start(f32[1,128]{1,0:T(1,128)S(1)} %add.44), channel_id=1, source_target_pairs={{0,4},{2,6},{4,0},{6,2},{8,12},{10,14},{12,8},{14,10},{1,5},{3,7},... | collective-permute-start | bytes 1544 | tf_op jit(solution)/shard_map/ppermute | solution.py:507
  39.9 0.0 collective-permute-start.11
  39.9 1.3 %inverse.3 = (f32[32,4,576]{2,1,0:T(4,128)S(1)}, f32[4,32,640]{2,1,0:T(8,128)S(1)}) custom-call(s32[4]{0:T(128)S(1)} %copy-done.11, f32[4,32,640]{2,1,0:T(8,128)S(1)} %get-tuple-element.69.own_ref, f32[4,32,640]{2,1,0:T(8,128)S(1)} %collective-permute-done.8.refs_0_, bf16[128,1152]{1,0:T(8,128)(2,1)S(1)} %get-tuple-element.75.refs_1_, ...), custom_call_target="tpu_custom_call" | custom-call | tf_op jit(solution)/shard_map/inverse/pallas_call | solution.py:481
  41.2 0.3 collective-permute-done.9
  41.4 0.3 collective-permute-start.12
  41.8 2.7 %collective-permute-start.10 = (f32[1,128]{1,0:T(1,128)S(1)}, f32[1,128]{1,0:T(1,128)S(1)}, u32[]{:S(2)}, u32[]{:S(2)}) collective-permute-start(f32[1,128]{1,0:T(1,128)S(1)} %add.45), channel_id=1, source_target_pairs={{0,8},{2,10},{4,12},{6,14},{8,0},{10,2},{12,4},{14,6},{1,9},{3,11}... | collective-permute-start | bytes 1544 | tf_op jit(solution)/shard_map/ppermute | solution.py:507
  44.5 0.0 collective-permute-done.11.refs_2_
  44.5 0.0 collective-permute-done.12.refs_3_
  44.5 1.2 %finish.1 = f32[4,32,4,576]{3,2,1,0:T(4,128)} custom-call(f32[32,4,576]{2,1,0:T(4,128)S(1)} %get-tuple-element.81.refs_0_, f32[32,4,576]{2,1,0:T(4,128)S(1)} %get-tuple-element.82.refs_1_, f32[4,32,640]{2,1,0:T(8,128)S(1)} %collective-permute-done.11.refs_2_, f32[4,32,640]{2,1,0:T(8,128)S(1)} %collective-permute-done.12.refs_3_), custom_call_target="tpu_custom_call" | custom-call | bytes 3000000 | tf_op jit(solution)/shard_map/finish/pallas_call | solution.py:527
  45.7 0.5 %collective-permute-done.10 = f32[1,128]{1,0:T(1,128)S(1)} collective-permute-done((f32[1,128]{1,0:T(1,128)S(1)}, f32[1,128]{1,0:T(1,128)S(1)}, u32[]{:S(2)}, u32[]{:S(2)}) %collective-permute-start.10) | collective-permute-done | bytes 544 | tf_op jit(solution)/shard_map/ppermute | solution.py:507
  46.2 0.6 %fusion.1 = f32[1,1]{1,0:T(1,128)} fusion(f32[1,128]{1,0:T(1,128)S(1)} %add.46, s32[]{:T(128)S(6)} %select_n.8), kind=kLoop, calls=%fused_computation.4 | loop fusion | flops 1 | bytes 12 | tf_op jit(solution)/shard_map/div | solution.py:545
  (23 shorter events, 0.1 us)
Async XLA Ops:
  2.0 9.5 %copy-start.14 = (f32[1152]{0:T(1024)S(1)}, f32[1152]{0:T(1024)}, u32[]{:S(2)}) copy-start(f32[1152]{0:T(1024)} %constant.56.clone) | copy-start | bytes 13828
  2.0 9.5 %copy-start.15 = (f32[1152]{0:T(1024)S(1)}, f32[1152]{0:T(1024)}, u32[]{:S(2)}) copy-start(f32[1152]{0:T(1024)} %constant.54.clone) | copy-start | bytes 13828
  2.0 9.5 %copy-start.17 = (pred[1152]{0:T(1024)(128)(4,1)S(1)}, pred[1152]{0:T(1024)(128)(4,1)}, u32[]{:S(2)}) copy-start(pred[1152]{0:T(1024)(128)(4,1)} %constant.55.clone) | copy-start | bytes 3460
  2.0 9.6 %copy-start.18 = (s32[1,1,18,1]{2,3,1,0:T(1,128)S(1)}, s32[1,1,18,1]{2,3,1,0:T(1,128)}, u32[]{:S(2)}) copy-start(s32[1,1,18,1]{2,3,1,0:T(1,128)} %param.25) | copy-start | bytes 220
  2.0 9.8 %copy-start.13 = (f32[4,4,576]{2,1,0:T(4,128)S(1)}, f32[4,4,576]{2,1,0:T(4,128)}, u32[]{:S(2)}) copy-start(f32[4,4,576]{2,1,0:T(4,128)} %param.22) | copy-start | bytes 110596
  2.1 23.5 %collective-permute-start.1 = (f32[128,1152]{1,0:T(8,128)S(1)}, f32[128,1152]{1,0:T(8,128)S(1)}, u32[]{:S(2)}, u32[]{:S(2)}) collective-permute-start(f32[128,1152]{1,0:T(8,128)S(1)} %pack.1), channel_id=1, source_target_pairs={{0,2},{2,0},{4,6},{6,4},{8,10},{10,8},{12,14},{14,12},{1,3},{3,1},... | collective-permute-start | bytes 1769480 | tf_op jit(solution)/shard_map/ppermute | solution.py:391
  8.6 2.9 %copy-start.12 = (f32[64,1152]{1,0:T(8,128)}, f32[64,1152]{1,0:T(8,128)S(1)}, u32[]{:S(2)}) copy-start(f32[64,1152]{1,0:T(8,128)S(1)} %get-tuple-element.54) | copy-start | bytes 884740
  8.6 10.1 %copy-start.16 = (f32[4,32]{1,0:T(4,128)S(1)}, f32[4,32]{1,0:T(4,128)}, u32[]{:S(2)}) copy-start(f32[4,32]{1,0:T(4,128)} %param.24) | copy-start | bytes 1540
  8.6 11.3 %collective-permute-start.3 = (f32[16,1152]{1,0:T(8,128)S(1)}, f32[16,1152]{1,0:T(8,128)S(1)}, u32[]{:S(2)}, u32[]{:S(2)}) collective-permute-start(f32[16,1152]{1,0:T(8,128)S(1)} %get-tuple-element.55), channel_id=1, source_target_pairs={{2,0},{4,2},{6,4},{8,6},{10,8},{12,10},{14,12},{3,1},{5,3},{7,5},{... | collective-permute-start | bytes 221192 | tf_op jit(solution)/shard_map/ppermute | solution.py:409
  10.1 9.9 %collective-permute-start.4 = (f32[64,1152]{1,0:T(8,128)}, f32[64,1152]{1,0:T(8,128)}, u32[]{:S(2)}, u32[]{:S(2)}) collective-permute-start(f32[64,1152]{1,0:T(8,128)} %get-tuple-element.50), channel_id=1, source_target_pairs={{2,4},{4,2},{6,8},{8,6},{10,12},{12,10},{3,5},{5,3},{7,9},{9,7},{1... | collective-permute-start | bytes 884744 | tf_op jit(solution)/shard_map/ppermute | solution.py:408
  11.4 1.6 %collective-permute-start = (f32[5,4,32,128]{3,2,1,0:T(8,128)S(1)}, f32[5,4,32,128]{3,2,1,0:T(8,128)S(1)}, u32[]{:S(2)}, u32[]{:S(2)}) collective-permute-start(f32[5,4,32,128]{3,2,1,0:T(8,128)S(1)} %get-tuple-element.47), channel_id=1, source_target_pairs={{0,1},{1,0},{2,3},{3,2},{4,5},{5,4},{6,7},{7,6},{8,9},{9,8},{10,11... | collective-permute-start | bytes 983048 | tf_op jit(solution)/shard_map/ppermute | solution.py:411
  11.5 14.0 %copy-start.10 = (f32[32,32]{1,0:T(8,128)S(1)}, f32[32,32]{1,0:T(8,128)}, u32[]{:S(2)}) copy-start(f32[32,32]{1,0:T(8,128)} %refs_7_.4) | copy-start | bytes 12292
  13.1 0.7 %copy-start.4 = (f32[5,4,32,128]{3,2,1,0:T(8,128)}, f32[5,4,32,128]{3,2,1,0:T(8,128)S(1)}, u32[]{:S(2)}) copy-start(f32[5,4,32,128]{3,2,1,0:T(8,128)S(1)} %collective-permute-done.side_ref) | copy-start | bytes 983044
  13.8 1.0 %copy-start.5 = (f32[5,4,32,128]{3,2,1,0:T(8,128)S(1)}, f32[5,4,32,128]{3,2,1,0:T(8,128)}, u32[]{:S(2)}) copy-start(f32[5,4,32,128]{3,2,1,0:T(8,128)} %copy-done.4) | copy-start | bytes 983044
  18.9 12.8 %collective-permute-start.2 = (f32[64,1152]{1,0:T(8,128)}, f32[64,1152]{1,0:T(8,128)S(1)}, u32[]{:S(2)}, u32[]{:S(2)}) collective-permute-start(f32[64,1152]{1,0:T(8,128)} %copy-done.12), channel_id=1, source_target_pairs={{2,4},{4,2},{6,8},{8,6},{10,12},{12,10},{3,5},{5,3},{7,9},{9,7},{1... | collective-permute-start | bytes 884744 | tf_op jit(solution)/shard_map/ppermute | solution.py:444
  25.6 3.4 %copy-start.2 = (bf16[1024,256]{1,0:T(8,128)(2,1)S(1)}, bf16[1024,256]{1,0:T(8,128)(2,1)}, u32[]{:S(2)}) copy-start(bf16[1024,256]{1,0:T(8,128)(2,1)} %constant.58.clone.refs_3_.refs_2_) | copy-start | bytes 1572868
  25.6 3.4 %copy-start.3 = (bf16[1024,256]{1,0:T(8,128)(2,1)S(1)}, bf16[1024,256]{1,0:T(8,128)(2,1)}, u32[]{:S(2)}) copy-start(bf16[1024,256]{1,0:T(8,128)(2,1)} %constant.57.clone.refs_2_.refs_1_) | copy-start | bytes 1572868
  25.6 3.4 %copy-start.8 = (bf16[128,128]{1,0:T(8,128)(2,1)S(1)}, bf16[128,128]{1,0:T(8,128)(2,1)}, u32[]{:S(2)}) copy-start(bf16[128,128]{1,0:T(8,128)(2,1)} %constant.60.clone.refs_5_.refs_4_) | copy-start | bytes 98308
  25.6 3.4 %copy-start.9 = (bf16[128,128]{1,0:T(8,128)(2,1)S(1)}, bf16[128,128]{1,0:T(8,128)(2,1)}, u32[]{:S(2)}) copy-start(bf16[128,128]{1,0:T(8,128)(2,1)} %constant.59.clone.refs_4_.refs_3_) | copy-start | bytes 98308
  27.2 2.5 %copy-start = (bf16[1024,256]{1,0:T(8,128)(2,1)S(1)}, bf16[1024,256]{1,0:T(8,128)(2,1)}, u32[]{:S(2)}) copy-start(bf16[1024,256]{1,0:T(8,128)(2,1)} %constant.62.clone.refs_5_.refs_4_) | copy-start | bytes 1572868
  27.2 2.5 %copy-start.1 = (bf16[1024,256]{1,0:T(8,128)(2,1)S(1)}, bf16[1024,256]{1,0:T(8,128)(2,1)}, u32[]{:S(2)}) copy-start(bf16[1024,256]{1,0:T(8,128)(2,1)} %constant.61.clone.refs_4_.refs_3_) | copy-start | bytes 1572868
  27.2 2.5 %copy-start.6 = (bf16[128,128]{1,0:T(8,128)(2,1)S(1)}, bf16[128,128]{1,0:T(8,128)(2,1)}, u32[]{:S(2)}) copy-start(bf16[128,128]{1,0:T(8,128)(2,1)} %constant.64.clone.refs_7_.refs_6_) | copy-start | bytes 98308
  27.2 2.5 %copy-start.7 = (bf16[128,128]{1,0:T(8,128)(2,1)S(1)}, bf16[128,128]{1,0:T(8,128)(2,1)}, u32[]{:S(2)}) copy-start(bf16[128,128]{1,0:T(8,128)(2,1)} %constant.63.clone.refs_6_.refs_5_) | copy-start | bytes 98308
  27.2 2.5 %copy-start.11 = (s32[4]{0:T(128)S(1)}, s32[4]{0:T(128)}, u32[]{:S(2)}) copy-start(s32[4]{0:T(128)} %mask_ref.3) | copy-start | bytes 52
  27.3 1.5 %collective-permute-start.6 = (f32[2,32,640]{2,1,0:T(8,128)S(1)}, f32[2,32,640]{2,1,0:T(8,128)S(1)}, u32[]{:S(2)}, u32[]{:S(2)}) collective-permute-start(f32[2,32,640]{2,1,0:T(8,128)S(1)} %get-tuple-element.86), channel_id=1, source_target_pairs={{0,1},{1,0},{2,3},{3,2},{4,5},{5,4},{6,7},{7,6},{8,9},{9,8},{10,11... | collective-permute-start | bytes 491528 | tf_op jit(solution)/shard_map/ppermute | solution.py:496
  27.3 1.6 %collective-permute-start.5 = (f32[2,32,640]{2,1,0:T(8,128)S(1)}, f32[2,32,640]{2,1,0:T(8,128)S(1)}, u32[]{:S(2)}, u32[]{:S(2)}) collective-permute-start(f32[2,32,640]{2,1,0:T(8,128)S(1)} %get-tuple-element.87), channel_id=1, source_target_pairs={{0,1},{1,0},{2,3},{3,2},{4,5},{5,4},{6,7},{7,6},{8,9},{9,8},{10,11... | collective-permute-start | bytes 491528 | tf_op jit(solution)/shard_map/ppermute | solution.py:496
  32.4 3.6 %collective-permute-start.8 = (f32[4,32,640]{2,1,0:T(8,128)S(1)}, f32[4,32,640]{2,1,0:T(8,128)S(1)}, u32[]{:S(2)}, u32[]{:S(2)}) collective-permute-start(f32[4,32,640]{2,1,0:T(8,128)S(1)} %get-tuple-element.70), channel_id=1, source_target_pairs={{0,1},{1,0},{2,3},{3,2},{4,5},{5,4},{6,7},{7,6},{8,9},{9,8},{10,11... | collective-permute-start | bytes 983048 | tf_op jit(solution)/shard_map/ppermute | solution.py:510
  32.7 4.8 %collective-permute-start.7 = (f32[1,128]{1,0:T(1,128)S(1)}, f32[1,128]{1,0:T(1,128)S(1)}, u32[]{:S(2)}, u32[]{:S(2)}) collective-permute-start(f32[1,128]{1,0:T(1,128)S(1)} %get-tuple-element.68), channel_id=1, source_target_pairs={{0,2},{2,0},{4,6},{6,4},{8,10},{10,8},{12,14},{14,12},{1,3},{3,1},... | collective-permute-start | bytes 1544 | tf_op jit(solution)/shard_map/ppermute | solution.py:507
  37.4 4.0 %collective-permute-start.9 = (f32[1,128]{1,0:T(1,128)S(1)}, f32[1,128]{1,0:T(1,128)S(1)}, u32[]{:S(2)}, u32[]{:S(2)}) collective-permute-start(f32[1,128]{1,0:T(1,128)S(1)} %add.44), channel_id=1, source_target_pairs={{0,4},{2,6},{4,0},{6,2},{8,12},{10,14},{12,8},{14,10},{1,5},{3,7},... | collective-permute-start | bytes 1544 | tf_op jit(solution)/shard_map/ppermute | solution.py:507
  39.9 4.6 %collective-permute-start.11 = (f32[4,32,640]{2,1,0:T(8,128)}, f32[4,32,640]{2,1,0:T(8,128)S(1)}, u32[]{:S(2)}, u32[]{:S(2)}) collective-permute-start(f32[4,32,640]{2,1,0:T(8,128)} %get-tuple-element.66), channel_id=1, source_target_pairs={{0,1},{1,0},{2,3},{3,2},{4,5},{5,4},{6,7},{7,6},{8,9},{9,8},{10,11... | collective-permute-start | bytes 983048 | tf_op jit(solution)/shard_map/ppermute | solution.py:500
  41.4 3.0 %collective-permute-start.12 = (f32[4,32,640]{2,1,0:T(8,128)S(1)}, f32[4,32,640]{2,1,0:T(8,128)S(1)}, u32[]{:S(2)}, u32[]{:S(2)}) collective-permute-start(f32[4,32,640]{2,1,0:T(8,128)S(1)} %get-tuple-element.83), channel_id=1, source_target_pairs={{0,1},{1,0},{2,3},{3,2},{4,5},{5,4},{6,7},{7,6},{8,9},{9,8},{10,11... | collective-permute-start | bytes 983048 | tf_op jit(solution)/shard_map/ppermute | solution.py:524
  41.8 4.4 %collective-permute-start.10 = (f32[1,128]{1,0:T(1,128)S(1)}, f32[1,128]{1,0:T(1,128)S(1)}, u32[]{:S(2)}, u32[]{:S(2)}) collective-permute-start(f32[1,128]{1,0:T(1,128)S(1)} %add.45), channel_id=1, source_target_pairs={{0,8},{2,10},{4,12},{6,14},{8,0},{10,2},{12,4},{14,6},{1,9},{3,11}... | collective-permute-start | bytes 1544 | tf_op jit(solution)/shard_map/ppermute | solution.py:507

commit v14 on v10

--- a/solution.py
+++ b/solution.py
@@ -123,18 +123,19 @@
         store_side(count, r, lon_ref[:, r, :])
 
 
-def base_kernel(width, not_pole_ref, tracer_hbm, lat_hbm, lon_hbm, side_ref, base_ref, north_ref, courant_ref, *scratch):
-    tracer_ref, lat_ref, lon_ref, sems = scratch
+def base_kernel(width, not_pole_ref, tracer_hbm, lat_hbm, lon_hbm, side_hbm, base_ref, north_ref, courant_ref, *scratch):
+    tracer_ref, lat_ref, lon_ref, side_ref, sems = scratch
     tracer_count, levels, rows, sector = tracer_ref.shape
     whole = sector // LANES * LANES
     pairs = [(lat_hbm, lat_ref), (lon_hbm, lon_ref)] + [(tracer_hbm.at[t], tracer_ref.at[t]) for t in range(tracer_count)]
-    copies = start_copies(pairs, sems)
+    copies = start_copies(pairs + [(side_hbm, side_ref)], sems)
 
     def beside(values, side):
         return jnp.concatenate([values[:, :whole], values[:, whole:], side[:, sector - whole :]], axis=1)
 
     copies[0].wait()
     copies[1].wait()
+    copies[tracer_count + 2].wait()
     nothing = jnp.zeros((levels, LANES), jnp.float32)
     for r in range(rows):
         courant = lat_ref[:, r, :] if r else lat_ref[:, r, :] * not_pole_ref[0]
@@ -402,18 +403,18 @@
     not_pole = (lat > 0).astype(f32).reshape(1)
     base, north, lat_courant = pl.pallas_call(
         functools.partial(base_kernel, width),
-        in_specs=[scalars, in_hbm, in_hbm, in_hbm, whole],
+        in_specs=[scalars] + [in_hbm] * 4,
         out_specs=[whole] * 3,
         out_shape=[
             jax.ShapeDtypeStruct((tracer_count, rows, levels, width), f32),
             jax.ShapeDtypeStruct((tracer_count, levels, width), f32),
             jax.ShapeDtypeStruct((rows, levels, width), f32),
         ],
-        scratch_shapes=field_buffers + [pltpu.SemaphoreType.DMA((tracer_count + 2,))],
+        scratch_shapes=field_buffers + [pltpu.VMEM(sides.shape, f32), pltpu.SemaphoreType.DMA((tracer_count + 3,))],
         compiler_params=params(),
         cost_estimate=cost(0, 0),
         name="base",
-    )(not_pole, *fields, sides)
+    )(not_pole, *fields, pltpu.with_memory_space_constraint(sides, pltpu.HBM))
 
     surface = jnp.pad(surface_flux, ((0, 0), (0, 0), (0, width - sector)))
     decay = decay_rate[:, :, None]

time: 46.3 us -> 52.3 us (1.13)
  waiting for transfers between devices: 10.8 us -> 17.7 us
  local copies, waits for them, and re-layouts: 2.11 us -> 1.14 us
    ppermute x1, waiting for transfers between devices: 5.58 us -> 11.9 us  [on_device(): from_inside = lax.ppermute(inner, 'lat', inside)]
    unnamed x38 -> x36, local copies, waits for them, and re-layouts: 1.8 us -> 0.83 us
  transfers between devices with their start and end apart: 13 -> 13, of which waited for: 8 -> 8; matrix products, arithmetic and copies ran while one was open for 1% -> 1% of each run, Pallas kernels for 30% -> 28%
where the time goes in v14:
time: 52.3 us; the launch traced here: 52 us
  waiting for transfers between devices  17.7 us (34%)
  Pallas kernels  16.4 us (31%)
  starting transfers between devices  15 us (29%)
  local copies, waits for them, and re-layouts  1.14 us (2%)
  between operations  1 us (2%)
  other arithmetic  0.72 us (1%)
    ppermute x1, waiting for transfers between devices, on_device(): from_inside = lax.ppermute(inner, 'lat', inside)  11.9 us
    ppermute x3, starting transfers between devices, send_energy(): lax.ppermute(energy, 'lat', [(i, i ^ distance) for i in range(lat_count)])  7.28 us
    pallas_call x1, Pallas kernels, on_device(): pl.pallas_call(functools.partial(base_kernel, width), in_specs=[scalars]...  4.45 us
    pallas_call x2, Pallas kernels, run_inverse(): pl.pallas_call(functools.partial(inverse_kernel, radix, len(other)), in_s...  3.23 us
    ppermute x1, starting transfers between devices, on_device(): from_inside = lax.ppermute(inner, 'lat', inside)  3 us
    pallas_call x1, Pallas kernels, on_device(): pl.pallas_call(rest_kernel, in_specs=[scalars] + [in_hbm] * 3, out_specs=...  2.66 us
    pallas_call x2, Pallas kernels, run_physics(): pl.pallas_call(functools.partial(physics_kernel, levels, sector, lat_coun...  2.2 us
    ppermute x1, waiting for transfers between devices, on_device(): top = lax.ppermute(courant_row, 'lat', downward)  1.78 us
  transfers between devices with their start and end apart: 13, of which 8 were waited for; matrix products, arithmetic and copies ran while one was open for 1% of the time, Pallas kernels for 28%

profile of v14, /device:TPU:0, one launch (start us, length us, event | category | flops | bytes accessed | tf_op | source)
XLA Modules:
  0.0 52.0 jit_solution(15172735724976660216)
XLA Ops:
  0.6 1.3 %pack.1 = f32[128,1152]{1,0:T(8,128)S(1)} custom-call(s32[1]{0:T(128)} %bitcast.even_ref, f32[4,32,4,576]{3,2,1,0:T(4,128)} %tracer_hbm.5), custom_call_target="tpu_custom_call" | custom-call | bytes 600000 | tf_op jit(solution)/shard_map/pack/pallas_call | solution.py:373
  2.0 0.0 copy-start.13
  2.0 0.0 copy-start.14
  2.0 0.0 copy-start.16
  2.0 0.0 copy-start.17
  2.0 0.0 copy-start.12
  2.1 3.0 %collective-permute-start.1 = (f32[128,1152]{1,0:T(8,128)S(1)}, f32[128,1152]{1,0:T(8,128)S(1)}, u32[]{:S(2)}, u32[]{:S(2)}) collective-permute-start(f32[128,1152]{1,0:T(8,128)S(1)} %pack.1), channel_id=1, source_target_pairs={{0,2},{2,0},{4,6},{6,4},{8,10},{10,8},{12,14},{14,12},{1,3},{3,1},... | collective-permute-start | bytes 1769480 | tf_op jit(solution)/shard_map/ppermute | solution.py:383
  5.1 2.7 %rest.1 = (f32[64,1152]{1,0:T(8,128)}, f32[64,1152]{1,0:T(8,128)S(1)}, f32[16,1152]{1,0:T(8,128)S(1)}, f32[5,4,32,128]{3,2,1,0:T(8,128)S(1)}) custom-call(s32[1]{0:T(128)} %bitcast.even_ref, f32[4,32,4,576]{3,2,1,0:T(4,128)} %tracer_hbm.5, f32[32,4,576]{2,1,0:T(4,128)} %lat_hbm.3, f32[32,4,576]{2,1,0:T(4,128)} %lon_hbm.3), custom_call_target="tpu_custom_call" | custom-call | tf_op jit(solution)/shard_map/rest/pallas_call | solution.py:385
  7.7 0.0 copy-start.10
  7.7 0.0 copy-start.15
  7.7 1.4 %collective-permute-start.3 = (f32[16,1152]{1,0:T(8,128)S(1)}, f32[16,1152]{1,0:T(8,128)S(1)}, u32[]{:S(2)}, u32[]{:S(2)}) collective-permute-start(f32[16,1152]{1,0:T(8,128)S(1)} %get-tuple-element.51), channel_id=1, source_target_pairs={{2,0},{4,2},{6,4},{8,6},{10,8},{12,10},{14,12},{3,1},{5,3},{7,5},{... | collective-permute-start | bytes 221192 | tf_op jit(solution)/shard_map/ppermute | solution.py:400
  9.2 1.4 %collective-permute-start.4 = (f32[64,1152]{1,0:T(8,128)}, f32[64,1152]{1,0:T(8,128)}, u32[]{:S(2)}, u32[]{:S(2)}) collective-permute-start(f32[64,1152]{1,0:T(8,128)} %get-tuple-element.46), channel_id=1, source_target_pairs={{2,4},{4,2},{6,8},{8,6},{10,12},{12,10},{3,5},{5,3},{7,9},{9,7},{1... | collective-permute-start | bytes 884744 | tf_op jit(solution)/shard_map/ppermute | solution.py:399
  10.6 0.0 copy-done.10
  10.6 0.0 collective-permute-start
  10.6 0.0 copy-done.13
  10.6 0.0 copy-done.14
  10.6 0.0 copy-done.16
  10.7 0.1 select_multiply_fusion.refs_6_.refs_5_
  10.8 0.1 broadcast_in_dim.27
  10.8 0.1 reshape_reshape.3
  10.9 0.0 copy-done.12
  11.0 1.2 %collective-permute-done.side_hbm = f32[5,4,32,128]{3,2,1,0:T(8,128)S(1)} collective-permute-done((f32[5,4,32,128]{3,2,1,0:T(8,128)S(1)}, f32[5,4,32,128]{3,2,1,0:T(8,128)S(1)}, u32[]{:S(2)}, u32[]{:S(2)}) %collective-permute-start) | collective-permute-done | bytes 327712 | tf_op jit(solution)/shard_map/ppermute | solution.py:402
  12.2 0.7 %copy-done.11 = f32[5,4,32,128]{3,2,1,0:T(8,128)} copy-done((f32[5,4,32,128]{3,2,1,0:T(8,128)}, f32[5,4,32,128]{3,2,1,0:T(8,128)S(1)}, u32[]{:S(2)}) %copy-start.11) | copy-done | bytes 327704
  12.9 4.5 %base.1 = (f32[4,4,32,640]{3,2,1,0:T(8,128)S(1)}, f32[4,32,640]{2,1,0:T(8,128)S(1)}, f32[4,32,640]{2,1,0:T(8,128)S(1)}) custom-call(f32[1]{0:T(128)} %bitcast.2.not_pole_ref, f32[4,32,4,576]{3,2,1,0:T(4,128)} %tracer_hbm.5, f32[32,4,576]{2,1,0:T(4,128)} %lat_hbm.3, f32[32,4,576]{2,1,0:T(4,128)} %lon_hbm.3, f32[5,4,32,128]{3,2,1,0:T(8,128)} %copy-done.11), custom_call_target="tpu_custom_call" | custom-call | tf_op jit(solution)/shard_map/base/pallas_call | solution.py:404
  17.4 0.1 copy.22.refs_10_
  17.5 0.7 %collective-permute-start.2 = (f32[64,1152]{1,0:T(8,128)}, f32[64,1152]{1,0:T(8,128)S(1)}, u32[]{:S(2)}, u32[]{:S(2)}) collective-permute-start(f32[64,1152]{1,0:T(8,128)} %copy-done.10), channel_id=1, source_target_pairs={{2,4},{4,2},{6,8},{8,6},{10,12},{12,10},{3,5},{5,3},{7,9},{9,7},{1... | collective-permute-start | bytes 884744 | tf_op jit(solution)/shard_map/ppermute | solution.py:436
  18.2 1.8 %collective-permute-done.3.refs_6_ = f32[16,1152]{1,0:T(8,128)S(1)} collective-permute-done((f32[16,1152]{1,0:T(8,128)S(1)}, f32[16,1152]{1,0:T(8,128)S(1)}, u32[]{:S(2)}, u32[]{:S(2)}) %collective-permute-start.3) | collective-permute-done | bytes 73760 | tf_op jit(solution)/shard_map/ppermute | solution.py:400
  20.0 0.0 collective-permute-done.4.refs_5_
  20.0 11.9 %collective-permute-done.1.refs_4_ = f32[128,1152]{1,0:T(8,128)S(1)} collective-permute-done((f32[128,1152]{1,0:T(8,128)S(1)}, f32[128,1152]{1,0:T(8,128)S(1)}, u32[]{:S(2)}, u32[]{:S(2)}) %collective-permute-start.1) | collective-permute-done | bytes 589856 | tf_op jit(solution)/shard_map/ppermute | solution.py:383
  31.9 0.0 copy-start.2
  31.9 0.0 copy-start.3
  31.9 0.0 copy-start.6
  31.9 0.0 copy-start.7
  32.0 1.5 %physics.2 = (f32[4,32,640]{2,1,0:T(8,128)S(1)}, f32[4,32,640]{2,1,0:T(8,128)S(1)}, f32[4,8,640]{2,1,0:T(8,128)S(1)}) custom-call(s32[1]{0:T(128)} %bitcast.even_ref, s32[1]{0:T(128)S(6)} %sub.7.refs_0_.give_ref, s32[1]{0:T(128)} %bitcast.1.refs_1_.keep_ref, f32[4,4,32,640]{3,2,1,0:T(8,128)S(1)} %get-tuple-element.48.refs_2_, ...), custom_call_target="tpu_custom_call" | custom-call | tf_op jit(solution)/shard_map/physics/pallas_call | solution.py:447
  33.5 0.0 copy-start
  33.5 0.0 copy-start.1
  33.5 0.0 copy-start.4
  33.5 0.0 copy-start.5
  33.6 0.0 copy-start.9
  33.6 0.1 collective-permute-start.6
  33.7 0.5 collective-permute-start.5
  34.2 0.9 %collective-permute-done.6.refs_1_ = f32[2,32,640]{2,1,0:T(8,128)S(1)} collective-permute-done((f32[2,32,640]{2,1,0:T(8,128)S(1)}, f32[2,32,640]{2,1,0:T(8,128)S(1)}, u32[]{:S(2)}, u32[]{:S(2)}) %collective-permute-start.6) | collective-permute-done | bytes 163872 | tf_op jit(solution)/shard_map/ppermute | solution.py:490
  35.1 0.2 collective-permute-done.5.refs_0_
  35.3 0.0 copy-done.3
  35.3 0.7 %forward.2 = (bf16[128,1152]{1,0:T(8,128)(2,1)S(1)}, bf16[128,1152]{1,0:T(8,128)(2,1)S(1)}) custom-call(f32[4,32,640]{2,1,0:T(8,128)S(1)} %get-tuple-element.57.own_ref, f32[2,32,640]{2,1,0:T(8,128)S(1)} %collective-permute-done.5.refs_0_, f32[2,32,640]{2,1,0:T(8,128)S(1)} %collective-permute-done.6.refs_1_, bf16[1024,256]{1,0:T(8,128)(2,1)S(1)} %copy-done.3, ...), custom_call_target="tpu_custom_call" | custom-call | tf_op jit(solution)/shard_map/forward/pallas_call | solution.py:463
  36.1 2.0 %inverse.2 = (f32[32,4,576]{2,1,0:T(4,128)S(1)}, f32[4,32,640]{2,1,0:T(8,128)}) custom-call(s32[4]{0:T(128)S(1)} %copy-done.9, f32[4,32,640]{2,1,0:T(8,128)S(1)} %get-tuple-element.57.own_ref, f32[2,32,640]{2,1,0:T(8,128)S(1)} %collective-permute-done.5.refs_0_, f32[2,32,640]{2,1,0:T(8,128)S(1)} %collective-permute-done.6.refs_1_, ...), custom_call_target="tpu_custom_call" | custom-call | tf_op jit(solution)/shard_map/inverse/pallas_call | solution.py:475
  38.0 0.0 collective-permute-done.2.refs_5_
  38.0 0.7 %physics.3 = (f32[4,32,640]{2,1,0:T(8,128)S(1)}, f32[4,32,640]{2,1,0:T(8,128)S(1)}, f32[1,128]{1,0:T(1,128)S(1)}) custom-call(s32[1]{0:T(128)} %bitcast.even_ref, s32[1]{0:T(128)S(6)} %sub.7.refs_0_.give_ref, s32[1]{0:T(128)} %bitcast.1.refs_1_.keep_ref, f32[4,4,32,640]{3,2,1,0:T(8,128)S(1)} %get-tuple-element.48.refs_2_, ...), custom_call_target="tpu_custom_call" | custom-call | tf_op jit(solution)/shard_map/physics/pallas_call | solution.py:447
  38.7 0.3 collective-permute-start.8
  39.0 2.4 %collective-permute-start.7 = (f32[1,128]{1,0:T(1,128)S(1)}, f32[1,128]{1,0:T(1,128)S(1)}, u32[]{:S(2)}, u32[]{:S(2)}) collective-permute-start(f32[1,128]{1,0:T(1,128)S(1)} %get-tuple-element.64), channel_id=1, source_target_pairs={{0,2},{2,0},{4,6},{6,4},{8,10},{10,8},{12,14},{14,12},{1,3},{3,1},... | collective-permute-start | bytes 1544 | tf_op jit(solution)/shard_map/ppermute | solution.py:501
  41.4 0.0 collective-permute-done.8.refs_0_
  41.5 0.7 %forward.3 = (bf16[128,1152]{1,0:T(8,128)(2,1)S(1)}, bf16[128,1152]{1,0:T(8,128)(2,1)S(1)}) custom-call(f32[4,32,640]{2,1,0:T(8,128)S(1)} %get-tuple-element.65.own_ref, f32[4,32,640]{2,1,0:T(8,128)S(1)} %collective-permute-done.8.refs_0_, bf16[1024,256]{1,0:T(8,128)(2,1)S(1)} %copy-done.3, bf16[1024,256]{1,0:T(8,128)(2,1)S(1)} %copy-done.2, ...), custom_call_target="tpu_custom_call" | custom-call | tf_op jit(solution)/shard_map/forward/pallas_call | solution.py:463
  42.1 0.8 %collective-permute-done.7 = f32[1,128]{1,0:T(1,128)S(1)} collective-permute-done((f32[1,128]{1,0:T(1,128)S(1)}, f32[1,128]{1,0:T(1,128)S(1)}, u32[]{:S(2)}, u32[]{:S(2)}) %collective-permute-start.7) | collective-permute-done | bytes 544 | tf_op jit(solution)/shard_map/ppermute | solution.py:501
  43.0 2.1 %collective-permute-start.9 = (f32[1,128]{1,0:T(1,128)S(1)}, f32[1,128]{1,0:T(1,128)S(1)}, u32[]{:S(2)}, u32[]{:S(2)}) collective-permute-start(f32[1,128]{1,0:T(1,128)S(1)} %add.49), channel_id=1, source_target_pairs={{0,4},{2,6},{4,0},{6,2},{8,12},{10,14},{12,8},{14,10},{1,5},{3,7},... | collective-permute-start | bytes 1544 | tf_op jit(solution)/shard_map/ppermute | solution.py:501
  45.1 0.0 collective-permute-start.11
  45.1 1.3 %inverse.3 = (f32[32,4,576]{2,1,0:T(4,128)S(1)}, f32[4,32,640]{2,1,0:T(8,128)S(1)}) custom-call(s32[4]{0:T(128)S(1)} %copy-done.9, f32[4,32,640]{2,1,0:T(8,128)S(1)} %get-tuple-element.65.own_ref, f32[4,32,640]{2,1,0:T(8,128)S(1)} %collective-permute-done.8.refs_0_, bf16[128,1152]{1,0:T(8,128)(2,1)S(1)} %get-tuple-element.71.refs_1_, ...), custom_call_target="tpu_custom_call" | custom-call | tf_op jit(solution)/shard_map/inverse/pallas_call | solution.py:475
  46.4 0.3 collective-permute-done.9
  46.6 0.3 collective-permute-start.12
  46.9 2.7 %collective-permute-start.10 = (f32[1,128]{1,0:T(1,128)S(1)}, f32[1,128]{1,0:T(1,128)S(1)}, u32[]{:S(2)}, u32[]{:S(2)}) collective-permute-start(f32[1,128]{1,0:T(1,128)S(1)} %add.50), channel_id=1, source_target_pairs={{0,8},{2,10},{4,12},{6,14},{8,0},{10,2},{12,4},{14,6},{1,9},{3,11}... | collective-permute-start | bytes 1544 | tf_op jit(solution)/shard_map/ppermute | solution.py:501
  49.7 0.0 collective-permute-done.11.refs_2_
  49.7 0.0 collective-permute-done.12.refs_3_
  49.7 1.2 %finish.1 = f32[4,32,4,576]{3,2,1,0:T(4,128)} custom-call(s32[1]{0:T(128)} %bitcast.1.refs_1_.keep_ref, s32[1]{0:T(128)S(6)} %sub.7.refs_0_.give_ref, f32[32,4,576]{2,1,0:T(4,128)S(1)} %get-tuple-element.77.refs_0_, f32[32,4,576]{2,1,0:T(4,128)S(1)} %get-tuple-element.78.refs_1_, f32[4,32,640]{2,1,0:T(8,128)S(1)} %collective-permute-done.11.refs_2_, ...), custom_call_target="tpu_custom_call" | custom-call | bytes 3000000 | tf_op jit(solution)/shard_map/finish/pallas_call | solution.py:521
  50.9 0.5 %collective-permute-done.10 = f32[1,128]{1,0:T(1,128)S(1)} collective-permute-done((f32[1,128]{1,0:T(1,128)S(1)}, f32[1,128]{1,0:T(1,128)S(1)}, u32[]{:S(2)}, u32[]{:S(2)}) %collective-permute-start.10) | collective-permute-done | bytes 544 | tf_op jit(solution)/shard_map/ppermute | solution.py:501
  51.4 0.6 %fusion.1 = f32[1,1]{1,0:T(1,128)} fusion(f32[1,128]{1,0:T(1,128)S(1)} %add.51, s32[]{:T(128)S(6)} %select_n.16), kind=kLoop, calls=%fused_computation.4 | loop fusion | flops 1 | bytes 12 | tf_op jit(solution)/shard_map/div | solution.py:539
  (21 shorter events, 0.1 us)
Async XLA Ops:
  2.0 8.6 %copy-start.13 = (f32[1152]{0:T(1024)S(1)}, f32[1152]{0:T(1024)}, u32[]{:S(2)}) copy-start(f32[1152]{0:T(1024)} %constant.73.clone) | copy-start | bytes 13828
  2.0 8.6 %copy-start.14 = (f32[1152]{0:T(1024)S(1)}, f32[1152]{0:T(1024)}, u32[]{:S(2)}) copy-start(f32[1152]{0:T(1024)} %constant.71.clone) | copy-start | bytes 13828
  2.0 8.6 %copy-start.16 = (pred[1152]{0:T(1024)(128)(4,1)S(1)}, pred[1152]{0:T(1024)(128)(4,1)}, u32[]{:S(2)}) copy-start(pred[1152]{0:T(1024)(128)(4,1)} %constant.72.clone) | copy-start | bytes 3460
  2.0 8.7 %copy-start.17 = (s32[1,1,18,1]{2,3,1,0:T(1,128)S(1)}, s32[1,1,18,1]{2,3,1,0:T(1,128)}, u32[]{:S(2)}) copy-start(s32[1,1,18,1]{2,3,1,0:T(1,128)} %param.25) | copy-start | bytes 220
  2.0 8.9 %copy-start.12 = (f32[4,4,576]{2,1,0:T(4,128)S(1)}, f32[4,4,576]{2,1,0:T(4,128)}, u32[]{:S(2)}) copy-start(f32[4,4,576]{2,1,0:T(4,128)} %param.22) | copy-start | bytes 110596
  2.1 29.8 %collective-permute-start.1 = (f32[128,1152]{1,0:T(8,128)S(1)}, f32[128,1152]{1,0:T(8,128)S(1)}, u32[]{:S(2)}, u32[]{:S(2)}) collective-permute-start(f32[128,1152]{1,0:T(8,128)S(1)} %pack.1), channel_id=1, source_target_pairs={{0,2},{2,0},{4,6},{6,4},{8,10},{10,8},{12,14},{14,12},{1,3},{3,1},... | collective-permute-start | bytes 1769480 | tf_op jit(solution)/shard_map/ppermute | solution.py:383
  7.7 2.8 %copy-start.10 = (f32[64,1152]{1,0:T(8,128)}, f32[64,1152]{1,0:T(8,128)S(1)}, u32[]{:S(2)}) copy-start(f32[64,1152]{1,0:T(8,128)S(1)} %get-tuple-element.50) | copy-start | bytes 884740
  7.7 9.7 %copy-start.15 = (f32[4,32]{1,0:T(4,128)S(1)}, f32[4,32]{1,0:T(4,128)}, u32[]{:S(2)}) copy-start(f32[4,32]{1,0:T(4,128)} %param.24) | copy-start | bytes 1540
  7.7 12.2 %collective-permute-start.3 = (f32[16,1152]{1,0:T(8,128)S(1)}, f32[16,1152]{1,0:T(8,128)S(1)}, u32[]{:S(2)}, u32[]{:S(2)}) collective-permute-start(f32[16,1152]{1,0:T(8,128)S(1)} %get-tuple-element.51), channel_id=1, source_target_pairs={{2,0},{4,2},{6,4},{8,6},{10,8},{12,10},{14,12},{3,1},{5,3},{7,5},{... | collective-permute-start | bytes 221192 | tf_op jit(solution)/shard_map/ppermute | solution.py:400
  9.2 10.8 %collective-permute-start.4 = (f32[64,1152]{1,0:T(8,128)}, f32[64,1152]{1,0:T(8,128)}, u32[]{:S(2)}, u32[]{:S(2)}) collective-permute-start(f32[64,1152]{1,0:T(8,128)} %get-tuple-element.46), channel_id=1, source_target_pairs={{2,4},{4,2},{6,8},{8,6},{10,12},{12,10},{3,5},{5,3},{7,9},{9,7},{1... | collective-permute-start | bytes 884744 | tf_op jit(solution)/shard_map/ppermute | solution.py:399
  10.6 1.6 %collective-permute-start = (f32[5,4,32,128]{3,2,1,0:T(8,128)S(1)}, f32[5,4,32,128]{3,2,1,0:T(8,128)S(1)}, u32[]{:S(2)}, u32[]{:S(2)}) collective-permute-start(f32[5,4,32,128]{3,2,1,0:T(8,128)S(1)} %get-tuple-element.43), channel_id=1, source_target_pairs={{0,1},{1,0},{2,3},{3,2},{4,5},{5,4},{6,7},{7,6},{8,9},{9,8},{10,11... | collective-permute-start | bytes 983048 | tf_op jit(solution)/shard_map/ppermute | solution.py:402
  10.7 21.2 %copy-start.8 = (f32[32,32]{1,0:T(8,128)S(1)}, f32[32,32]{1,0:T(8,128)}, u32[]{:S(2)}) copy-start(f32[32,32]{1,0:T(8,128)} %refs_9_.3) | copy-start | bytes 12292
  12.2 0.7 %copy-start.11 = (f32[5,4,32,128]{3,2,1,0:T(8,128)}, f32[5,4,32,128]{3,2,1,0:T(8,128)S(1)}, u32[]{:S(2)}) copy-start(f32[5,4,32,128]{3,2,1,0:T(8,128)S(1)} %collective-permute-done.side_hbm) | copy-start | bytes 983044
  17.5 20.5 %collective-permute-start.2 = (f32[64,1152]{1,0:T(8,128)}, f32[64,1152]{1,0:T(8,128)S(1)}, u32[]{:S(2)}, u32[]{:S(2)}) collective-permute-start(f32[64,1152]{1,0:T(8,128)} %copy-done.10), channel_id=1, source_target_pairs={{2,4},{4,2},{6,8},{8,6},{10,12},{12,10},{3,5},{5,3},{7,9},{9,7},{1... | collective-permute-start | bytes 884744 | tf_op jit(solution)/shard_map/ppermute | solution.py:436
  31.9 3.4 %copy-start.2 = (bf16[1024,256]{1,0:T(8,128)(2,1)S(1)}, bf16[1024,256]{1,0:T(8,128)(2,1)}, u32[]{:S(2)}) copy-start(bf16[1024,256]{1,0:T(8,128)(2,1)} %constant.75.clone.refs_3_.refs_2_) | copy-start | bytes 1572868
  31.9 3.4 %copy-start.3 = (bf16[1024,256]{1,0:T(8,128)(2,1)S(1)}, bf16[1024,256]{1,0:T(8,128)(2,1)}, u32[]{:S(2)}) copy-start(bf16[1024,256]{1,0:T(8,128)(2,1)} %constant.74.clone.refs_2_.refs_1_) | copy-start | bytes 1572868
  31.9 3.4 %copy-start.6 = (bf16[128,128]{1,0:T(8,128)(2,1)S(1)}, bf16[128,128]{1,0:T(8,128)(2,1)}, u32[]{:S(2)}) copy-start(bf16[128,128]{1,0:T(8,128)(2,1)} %constant.77.clone.refs_5_.refs_4_) | copy-start | bytes 98308
  31.9 3.4 %copy-start.7 = (bf16[128,128]{1,0:T(8,128)(2,1)S(1)}, bf16[128,128]{1,0:T(8,128)(2,1)}, u32[]{:S(2)}) copy-start(bf16[128,128]{1,0:T(8,128)(2,1)} %constant.76.clone.refs_4_.refs_3_) | copy-start | bytes 98308
  33.5 2.5 %copy-start = (bf16[1024,256]{1,0:T(8,128)(2,1)S(1)}, bf16[1024,256]{1,0:T(8,128)(2,1)}, u32[]{:S(2)}) copy-start(bf16[1024,256]{1,0:T(8,128)(2,1)} %constant.79.clone.refs_5_.refs_4_) | copy-start | bytes 1572868
  33.5 2.5 %copy-start.1 = (bf16[1024,256]{1,0:T(8,128)(2,1)S(1)}, bf16[1024,256]{1,0:T(8,128)(2,1)}, u32[]{:S(2)}) copy-start(bf16[1024,256]{1,0:T(8,128)(2,1)} %constant.78.clone.refs_4_.refs_3_) | copy-start | bytes 1572868
  33.5 2.5 %copy-start.4 = (bf16[128,128]{1,0:T(8,128)(2,1)S(1)}, bf16[128,128]{1,0:T(8,128)(2,1)}, u32[]{:S(2)}) copy-start(bf16[128,128]{1,0:T(8,128)(2,1)} %constant.81.clone.refs_7_.refs_6_) | copy-start | bytes 98308
  33.5 2.5 %copy-start.5 = (bf16[128,128]{1,0:T(8,128)(2,1)S(1)}, bf16[128,128]{1,0:T(8,128)(2,1)}, u32[]{:S(2)}) copy-start(bf16[128,128]{1,0:T(8,128)(2,1)} %constant.80.clone.refs_6_.refs_5_) | copy-start | bytes 98308
  33.6 2.5 %copy-start.9 = (s32[4]{0:T(128)S(1)}, s32[4]{0:T(128)}, u32[]{:S(2)}) copy-start(s32[4]{0:T(128)} %mask_ref.3) | copy-start | bytes 52
  33.6 1.5 %collective-permute-start.6 = (f32[2,32,640]{2,1,0:T(8,128)S(1)}, f32[2,32,640]{2,1,0:T(8,128)S(1)}, u32[]{:S(2)}, u32[]{:S(2)}) collective-permute-start(f32[2,32,640]{2,1,0:T(8,128)S(1)} %get-tuple-element.82), channel_id=1, source_target_pairs={{0,1},{1,0},{2,3},{3,2},{4,5},{5,4},{6,7},{7,6},{8,9},{9,8},{10,11... | collective-permute-start | bytes 491528 | tf_op jit(solution)/shard_map/ppermute | solution.py:490
  33.7 1.6 %collective-permute-start.5 = (f32[2,32,640]{2,1,0:T(8,128)S(1)}, f32[2,32,640]{2,1,0:T(8,128)S(1)}, u32[]{:S(2)}, u32[]{:S(2)}) collective-permute-start(f32[2,32,640]{2,1,0:T(8,128)S(1)} %get-tuple-element.83), channel_id=1, source_target_pairs={{0,1},{1,0},{2,3},{3,2},{4,5},{5,4},{6,7},{7,6},{8,9},{9,8},{10,11... | collective-permute-start | bytes 491528 | tf_op jit(solution)/shard_map/ppermute | solution.py:490
  38.7 2.8 %collective-permute-start.8 = (f32[4,32,640]{2,1,0:T(8,128)S(1)}, f32[4,32,640]{2,1,0:T(8,128)S(1)}, u32[]{:S(2)}, u32[]{:S(2)}) collective-permute-start(f32[4,32,640]{2,1,0:T(8,128)S(1)} %get-tuple-element.66), channel_id=1, source_target_pairs={{0,1},{1,0},{2,3},{3,2},{4,5},{5,4},{6,7},{7,6},{8,9},{9,8},{10,11... | collective-permute-start | bytes 983048 | tf_op jit(solution)/shard_map/ppermute | solution.py:504
  39.0 4.0 %collective-permute-start.7 = (f32[1,128]{1,0:T(1,128)S(1)}, f32[1,128]{1,0:T(1,128)S(1)}, u32[]{:S(2)}, u32[]{:S(2)}) collective-permute-start(f32[1,128]{1,0:T(1,128)S(1)} %get-tuple-element.64), channel_id=1, source_target_pairs={{0,2},{2,0},{4,6},{6,4},{8,10},{10,8},{12,14},{14,12},{1,3},{3,1},... | collective-permute-start | bytes 1544 | tf_op jit(solution)/shard_map/ppermute | solution.py:501
  43.0 3.6 %collective-permute-start.9 = (f32[1,128]{1,0:T(1,128)S(1)}, f32[1,128]{1,0:T(1,128)S(1)}, u32[]{:S(2)}, u32[]{:S(2)}) collective-permute-start(f32[1,128]{1,0:T(1,128)S(1)} %add.49), channel_id=1, source_target_pairs={{0,4},{2,6},{4,0},{6,2},{8,12},{10,14},{12,8},{14,10},{1,5},{3,7},... | collective-permute-start | bytes 1544 | tf_op jit(solution)/shard_map/ppermute | solution.py:501
  45.1 4.6 %collective-permute-start.11 = (f32[4,32,640]{2,1,0:T(8,128)}, f32[4,32,640]{2,1,0:T(8,128)S(1)}, u32[]{:S(2)}, u32[]{:S(2)}) collective-permute-start(f32[4,32,640]{2,1,0:T(8,128)} %get-tuple-element.62), channel_id=1, source_target_pairs={{0,1},{1,0},{2,3},{3,2},{4,5},{5,4},{6,7},{7,6},{8,9},{9,8},{10,11... | collective-permute-start | bytes 983048 | tf_op jit(solution)/shard_map/ppermute | solution.py:494
  46.6 3.0 %collective-permute-start.12 = (f32[4,32,640]{2,1,0:T(8,128)S(1)}, f32[4,32,640]{2,1,0:T(8,128)S(1)}, u32[]{:S(2)}, u32[]{:S(2)}) collective-permute-start(f32[4,32,640]{2,1,0:T(8,128)S(1)} %get-tuple-element.79), channel_id=1, source_target_pairs={{0,1},{1,0},{2,3},{3,2},{4,5},{5,4},{6,7},{7,6},{8,9},{9,8},{10,11... | collective-permute-start | bytes 983048 | tf_op jit(solution)/shard_map/ppermute | solution.py:518
  46.9 4.4 %collective-permute-start.10 = (f32[1,128]{1,0:T(1,128)S(1)}, f32[1,128]{1,0:T(1,128)S(1)}, u32[]{:S(2)}, u32[]{:S(2)}) collective-permute-start(f32[1,128]{1,0:T(1,128)S(1)} %add.50), channel_id=1, source_target_pairs={{0,8},{2,10},{4,12},{6,14},{8,0},{10,2},{12,4},{14,6},{1,9},{3,11}... | collective-permute-start | bytes 1544 | tf_op jit(solution)/shard_map/ppermute | solution.py:501

commit v15 on v11

--- a/solution.py
+++ b/solution.py
@@ -91,45 +91,48 @@
     return copies
 
 
-def pack_kernel(tracer_hbm, out_ref, row_ref, sems):
-    count, levels = row_ref.shape[:2]
+def pack_kernel(tracers, tracer_hbm, out_ref, row_ref, sems):
+    levels = row_ref.shape[1]
     first_row = pl.multiple_of(jnp.where(is_even(), tracer_hbm.shape[2] - 2, 0), 2)
-    sources = [tracer_hbm.at[t, :, pl.ds(first_row, 2), :] for t in range(count)]
-    copies = start_copies([(sources[t], row_ref.at[t]) for t in range(count)], sems)
-    for t in range(count):
-        copies[t].wait()
-        out_ref[levels * t : levels * (t + 1), :] = pack_rows(row_ref[t, :, 0, :], row_ref[t, :, 1, :])
+    sources = [tracer_hbm.at[t, :, pl.ds(first_row, 2), :] for t in tracers]
+    copies = start_copies([(source, row_ref.at[i]) for i, source in enumerate(sources)], sems)
+    for i, copy in enumerate(copies):
+        copy.wait()
+        out_ref[levels * i : levels * (i + 1), :] = pack_rows(row_ref[i, :, 0, :], row_ref[i, :, 1, :])
 
 
 def rest_kernel(tracer_hbm, lat_hbm, lon_hbm, *refs):
     courant_ref, side_ref, tracer_ref, lat_ref, lon_ref, sems = refs[-6:]
-    outer_refs = refs[:-6]
     count, levels, rows, sector = tracer_ref.shape
+    half = count // 2
+    outer_refs, inner_refs = refs[:half], refs[half:-6]
     pairs = [(tracer_hbm.at[t], tracer_ref.at[t]) for t in range(count)] + [(lat_hbm, lat_ref), (lon_hbm, lon_ref)]
-    copies = start_copies(pairs, sems)
+    for copy in start_copies(pairs, sems):
+        copy.wait()
     shift, whole = sector % LANES, sector // LANES * LANES
     lane = lax.broadcasted_iota(jnp.int32, (levels, LANES), 1)
     even = is_even()
 
-    def store_side(i, r, values):
+    def side_of(values):
         first = pltpu.roll(values[:, :LANES], shift, 1)
         last = jnp.concatenate([values[:, whole:], values[:, whole:]], axis=1)
-        side_ref[i, r] = jnp.where(lane < LANES - 2, first, last)
-
-    for copy in copies:
-        copy.wait()
+        return jnp.where(lane < LANES - 2, first, last)
+
+    def store_sides(i, values):
+        for r in range(0, rows, 2):
+            side_ref[i, r // 2] = jnp.where(lane < shift, pltpu.roll(side_of(values[r]), shift, 1), side_of(values[r + 1]))
+
     for t in range(count):
         row = [tracer_ref[t, :, r, :] for r in range(rows)]
-        slot = t // len(outer_refs)
-        outer_refs[t % len(outer_refs)][levels * slot : levels * (slot + 1), :] = pack_rows(
-            jnp.where(even, row[0], row[rows - 2]), jnp.where(even, row[1], row[rows - 1])
-        )
-        for r in range(rows):
-            store_side(t, r, row[r])
+        place = slice(levels * (t // half), levels * (t // half + 1))
+        top, bottom = pack_rows(row[rows - 2], row[rows - 1]), pack_rows(row[0], row[1])
+        outer_refs[t % half][place, :] = jnp.where(even, bottom, top)
+        if t % half:
+            inner_refs[t % half - 1][place, :] = jnp.where(even, top, bottom)
+        store_sides(t, row)
     courant = lat_ref[:, 0, :]
     courant_ref[...] = pack_rows(courant[: levels // 2], courant[levels // 2 :])
-    for r in range(rows):
-        store_side(count, r, lon_ref[:, r, :])
+    store_sides(count, [lon_ref[:, r, :] for r in range(rows)])
 
 
 def base_kernel(width, tracer_hbm, lat_hbm, lon_hbm, side_ref, base_ref, north_ref, courant_ref, *scratch):
@@ -139,8 +142,9 @@
     pairs = [(lat_hbm, lat_ref), (lon_hbm, lon_ref)] + [(tracer_hbm.at[t], tracer_ref.at[t]) for t in range(tracer_count)]
     copies = start_copies(pairs, sems)
 
-    def beside(values, side):
-        return jnp.concatenate([values[:, :whole], values[:, whole:], side[:, sector - whole :]], axis=1)
+    def beside(values, side, part=0):
+        begin = (sector - whole) * part
+        return jnp.concatenate([values[:, :whole], values[:, whole:], side[:, begin : begin + width - sector]], axis=1)
 
     copies[0].wait()
     copies[1].wait()
@@ -150,7 +154,7 @@
         courant_ref[r] = beside(courant, nothing)
     for t in range(tracer_count):
         copies[t + 2].wait()
-        q = [beside(tracer_ref[t, :, r, :], side_ref[t, r]) for r in range(rows)]
+        q = [beside(tracer_ref[t, :, r, :], side_ref[t, r // 2], r % 2) for r in range(rows)]
         north_ref[t] = NEAR * q[3] - FAR * q[2]
         own_flux = [
             courant_ref[0] * (NEAR * q[0] - FAR * q[1]),
@@ -160,7 +164,7 @@
         ]
         for r in range(rows):
             west, west2, east = pltpu.roll(q[r], 1, 1), pltpu.roll(q[r], 2, 1), pltpu.roll(q[r], width - 1, 1)
-            flux = beside(lon_ref[:, r, :], side_ref[tracer_count, r]) * (NEAR * (q[r] + west) - FAR * (east + west2))
+            flux = beside(lon_ref[:, r, :], side_ref[tracer_count, r // 2], r % 2) * (NEAR * (q[r] + west) - FAR * (east + west2))
             value = q[r] - (pltpu.roll(flux, width - 1, 1) - flux) + own_flux[r]
             if r + 1 < rows:
                 value = value - own_flux[r + 1]
@@ -184,7 +188,7 @@
     for half, physics_ref in zip(halves, physics_refs):
         first = first_of(half, base_ref.shape[0])
         t = first + chunk
-        inner = inner_ref[pl.ds(pl.multiple_of(levels * t, levels), levels), :]
+        inner = jnp.where(first == 0, inner_ref[:levels, :], inner_ref[levels:, :])
         outer = jnp.where(first == 0, outer_ref[:levels, :], outer_ref[levels:, :])
         low, high = jnp.where(even, outer, inner), jnp.where(even, inner, outer)
         low_a, low_b = low[:, :width], second_half(low, sector)
@@ -376,34 +380,37 @@
     fields = [pltpu.with_memory_space_constraint(array, pltpu.HBM) for array in (tracers, courant_lat, courant_lon)]
     field_buffers = [pltpu.VMEM(array.shape, f32) for array in (tracers, courant_lat, courant_lon)]
     half = tracer_count // 2
+    chunk_rows = pltpu.VMEM((levels * 2, length), f32)
     inner = pl.pallas_call(
-        pack_kernel,
+        functools.partial(pack_kernel, (0, half)),
         in_specs=[in_hbm],
         out_specs=whole,
-        out_shape=pltpu.VMEM((levels * tracer_count, length), f32),
-        scratch_shapes=[pltpu.VMEM((tracer_count, levels, 2, sector), f32), pltpu.SemaphoreType.DMA((tracer_count,))],
+        out_shape=chunk_rows,
+        scratch_shapes=[pltpu.VMEM((2, levels, 2, sector), f32), pltpu.SemaphoreType.DMA((2,))],
         compiler_params=params(),
         cost_estimate=cost(0, 600_000),
         name="pack",
     )(fields[0])
-    from_inside = lax.ppermute(inner, "lat", inside)
+    from_inside = [lax.ppermute(inner, "lat", inside)]
     fields, inner = lax.optimization_barrier((fields, inner))
     fields = [pltpu.with_memory_space_constraint(array, pltpu.HBM) for array in fields]
-    *outer, courant_row, sides = pl.pallas_call(
+    *packed, courant_row, sides = pl.pallas_call(
         rest_kernel,
         in_specs=[in_hbm] * 3,
-        out_specs=[whole] * (half + 2),
-        out_shape=[pltpu.VMEM((levels * 2, length), f32)] * half
+        out_specs=[whole] * (2 * half + 1),
+        out_shape=[chunk_rows] * (2 * half - 1)
         + [
             jax.ShapeDtypeStruct((levels // 2, length), f32),
-            jax.ShapeDtypeStruct((tracer_count + 1, rows, levels, LANES), f32),
+            jax.ShapeDtypeStruct((tracer_count + 1, rows // 2, levels, LANES), f32),
         ],
         scratch_shapes=field_buffers + [pltpu.SemaphoreType.DMA((tracer_count + 2,))],
         compiler_params=params(),
         cost_estimate=cost(0, 0),
         name="rest",
     )(*fields)
-    from_across = [lax.ppermute(part, "lat", across) for part in outer[:-1]]
+    outer, inner = packed[:half], packed[half:]
+    from_across = [lax.ppermute(part, "lat", across) for part in outer]
+    from_inside += [lax.ppermute(part, "lat", inside) for part in inner]
     top = lax.ppermute(courant_row, "lat", downward)
 
     sides = lax.ppermute(sides, "lon", swap)
@@ -438,9 +445,6 @@
 
     base, scale, owner_of, surface, decay = lax.optimization_barrier((base, scale, owner_of, surface, decay))
 
-    base, outer = lax.optimization_barrier((base, outer))
-    from_across.append(lax.ppermute(outer[-1], "lat", across))
-
     circles = jax.ShapeDtypeStruct((half, rows, levels, width), f32)
     result_shape = jax.ShapeDtypeStruct((levels, rows, sector), f32)
     out_shape = jax.ShapeDtypeStruct(tracers.shape, f32)
@@ -456,7 +460,7 @@
             compiler_params=params(),
             cost_estimate=cost(0, 0),
             name="physics",
-        )(base, north, from_inside, from_across[chunk], top, lat_courant, surface, mixing, decay, owner_of, energy)
+        )(base, north, from_inside[chunk], from_across[chunk], top, lat_courant, surface, mixing, decay, owner_of, energy)
         return results, energy
 
     forward, inverse = ([jnp.asarray(part) for table in tables for part in split_table(table)] for tables in (forward, inverse))

time: 46.2 us -> 47 us (1.017)
  starting transfers between devices: 15.3 us -> 17.1 us
  local copies, waits for them, and re-layouts: 2.11 us -> 0.42 us
  waiting for transfers between devices: 10.8 us -> 11.6 us
    ppermute x3 -> x4, waiting for transfers between devices: 5.58 us -> 9 us  [the longest x1 8.99 us: on_device(): from_inside += [lax.ppermute(part, 'lat', inside) for part in inner]]
    ppermute x3 -> x4, starting transfers between devices: 5.07 us -> 7.06 us  [the longest x1 3 us: on_device(): from_inside = [lax.ppermute(inner, 'lat', inside)]]
    unnamed x38 -> x34, local copies, waits for them, and re-layouts: 1.81 us -> 0.11 us
    ppermute x1, waiting for transfers between devices: 1.29 us -> 0.01 us  [on_device(): top = lax.ppermute(courant_row, 'lat', downward)]
    ppermute x1, waiting for transfers between devices: 1.26 us -> 0.01 us  [on_device(): sides = lax.ppermute(sides, 'lon', swap)]
    pallas_call x2, Pallas kernels: 2.22 us -> 1.2 us  [run_physics(): pl.pallas_call(functools.partial(physics_kernel, levels, sector, lat_coun...]
    pallas_call x2, Pallas kernels: 4.03 us -> 4.87 us  [the longest x1 3.02 us: on_device(): pl.pallas_call(rest_kernel, in_specs=[in_hbm] * 3, out_specs=[whole] * (2...]
  transfers between devices with their start and end apart: 13 -> 14, of which waited for: 8 -> 6; matrix products, arithmetic and copies ran while one was open for 1% -> 1% of each run, Pallas kernels for 30% -> 28%
where the time goes in v15:
time: 47 us; the launch traced here: 46.7 us
  starting transfers between devices  17.1 us (36%)
  Pallas kernels  15.8 us (34%)
  waiting for transfers between devices  11.6 us (25%)
  between operations  1.02 us (2%)
  other arithmetic  0.72 us (2%)
    ppermute x1, waiting for transfers between devices, on_device(): from_inside += [lax.ppermute(part, 'lat', inside) for part in inner]  8.99 us
    ppermute x3, starting transfers between devices, send_energy(): lax.ppermute(energy, 'lat', [(i, i ^ distance) for i in range(lat_count)])  7.72 us
    pallas_call x1, Pallas kernels, on_device(): pl.pallas_call(functools.partial(base_kernel, width), in_specs=[in_hbm, i...  3.95 us
    pallas_call x2, Pallas kernels, run_inverse(): pl.pallas_call(functools.partial(inverse_kernel, radix, len(other)), in_s...  3.23 us
    pallas_call x1, Pallas kernels, on_device(): pl.pallas_call(rest_kernel, in_specs=[in_hbm] * 3, out_specs=[whole] * (2...  3.02 us
    ppermute x1, starting transfers between devices, on_device(): from_inside = [lax.ppermute(inner, 'lat', inside)]  3 us
    ppermute x1, starting transfers between devices, on_device(): from_inside += [lax.ppermute(part, 'lat', inside) for part in inner]  2.71 us
    pallas_call x1, Pallas kernels, on_device(): pl.pallas_call(functools.partial(pack_kernel, (0, half)), in_specs=[in_hb...  1.85 us
  transfers between devices with their start and end apart: 14, of which 6 were waited for; matrix products, arithmetic and copies ran while one was open for 1% of the time, Pallas kernels for 28%

profile of v15, /device:TPU:0, one launch (start us, length us, event | category | flops | bytes accessed | tf_op | source)
XLA Modules:
  0.0 46.7 jit_solution(6857989051515432472)
XLA Ops:
  0.6 1.9 %pack.1 = f32[64,1152]{1,0:T(8,128)} custom-call(f32[4,32,4,576]{3,2,1,0:T(4,128)} %tracer_hbm.3), custom_call_target="tpu_custom_call" | custom-call | bytes 600000 | tf_op jit(solution)/shard_map/pack/pallas_call | solution.py:384
  2.5 0.0 copy-start.12
  2.5 0.0 copy-start.13
  2.5 0.0 copy-start.15
  2.5 0.0 copy-start.16
  2.5 0.0 copy-start.11
  2.6 3.0 %collective-permute-start.4 = (f32[64,1152]{1,0:T(8,128)}, f32[64,1152]{1,0:T(8,128)S(1)}, u32[]{:S(2)}, u32[]{:S(2)}) collective-permute-start(f32[64,1152]{1,0:T(8,128)} %pack.1), channel_id=1, source_target_pairs={{0,2},{2,0},{4,6},{6,4},{8,10},{10,8},{12,14},{14,12},{1,3},{3,1},... | collective-permute-start | bytes 884744 | tf_op jit(solution)/shard_map/ppermute | solution.py:394
  5.6 3.0 %rest.1 = (f32[64,1152]{1,0:T(8,128)}, f32[64,1152]{1,0:T(8,128)}, f32[64,1152]{1,0:T(8,128)}, f32[16,1152]{1,0:T(8,128)}, f32[5,2,32,128]{3,2,1,0:T(8,128)S(1)}) custom-call(f32[4,32,4,576]{3,2,1,0:T(4,128)} %tracer_hbm.3, f32[32,4,576]{2,1,0:T(4,128)} %lat_hbm.1, f32[32,4,576]{2,1,0:T(4,128)} %lon_hbm.1), custom_call_target="tpu_custom_call" | custom-call | tf_op jit(solution)/shard_map/rest/pallas_call | solution.py:397
  8.6 0.0 copy-start.14
  8.6 0.0 copy-start.8
  8.6 1.3 %collective-permute-start.3 = (f32[16,1152]{1,0:T(8,128)}, f32[16,1152]{1,0:T(8,128)S(1)}, u32[]{:S(2)}, u32[]{:S(2)}) collective-permute-start(f32[16,1152]{1,0:T(8,128)} %get-tuple-element.52), channel_id=1, source_target_pairs={{2,0},{4,2},{6,4},{8,6},{10,8},{12,10},{14,12},{3,1},{5,3},{7,5},{... | collective-permute-start | bytes 221192 | tf_op jit(solution)/shard_map/ppermute | solution.py:414
  9.9 0.1 collective-permute-start
  10.0 2.7 %collective-permute-start.1 = (f32[64,1152]{1,0:T(8,128)}, f32[64,1152]{1,0:T(8,128)S(1)}, u32[]{:S(2)}, u32[]{:S(2)}) collective-permute-start(f32[64,1152]{1,0:T(8,128)} %get-tuple-element.50), channel_id=1, source_target_pairs={{0,2},{2,0},{4,6},{6,4},{8,10},{10,8},{12,14},{14,12},{1,3},{3,1},... | collective-permute-start | bytes 884744 | tf_op jit(solution)/shard_map/ppermute | solution.py:413
  12.7 0.7 %collective-permute-start.5 = (f32[64,1152]{1,0:T(8,128)}, f32[64,1152]{1,0:T(8,128)S(1)}, u32[]{:S(2)}, u32[]{:S(2)}) collective-permute-start(f32[64,1152]{1,0:T(8,128)} %get-tuple-element.57), channel_id=1, source_target_pairs={{2,4},{4,2},{6,8},{8,6},{10,12},{12,10},{3,5},{5,3},{7,9},{9,7},{1... | collective-permute-start | bytes 884744 | tf_op jit(solution)/shard_map/ppermute | solution.py:412
  13.5 0.1 select_multiply_fusion.refs_6_.refs_5_
  13.5 0.1 broadcast_in_dim.27
  13.6 0.1 reshape_reshape.3
  13.7 0.0 collective-permute-done.side_ref
  13.7 0.7 %collective-permute-start.2 = (f32[64,1152]{1,0:T(8,128)}, f32[64,1152]{1,0:T(8,128)S(1)}, u32[]{:S(2)}, u32[]{:S(2)}) collective-permute-start(f32[64,1152]{1,0:T(8,128)} %get-tuple-element.51), channel_id=1, source_target_pairs={{2,4},{4,2},{6,8},{8,6},{10,12},{12,10},{3,5},{5,3},{7,9},{9,7},{1... | collective-permute-start | bytes 884744 | tf_op jit(solution)/shard_map/ppermute | solution.py:412
  14.4 4.0 %base.1 = (f32[4,4,32,640]{3,2,1,0:T(8,128)S(1)}, f32[4,32,640]{2,1,0:T(8,128)S(1)}, f32[4,32,640]{2,1,0:T(8,128)S(1)}) custom-call(f32[4,32,4,576]{3,2,1,0:T(4,128)} %tracer_hbm.3, f32[32,4,576]{2,1,0:T(4,128)} %lat_hbm.1, f32[32,4,576]{2,1,0:T(4,128)} %lon_hbm.1, f32[5,2,32,128]{3,2,1,0:T(8,128)S(1)} %collective-permute-done.side_ref), custom_call_target="tpu_custom_call" | custom-call | tf_op jit(solution)/shard_map/base/pallas_call | solution.py:417
  18.4 0.1 copy.22.refs_8_
  18.5 0.0 collective-permute-done.3.refs_4_
  18.5 0.0 collective-permute-done.4.refs_2_
  18.5 0.0 collective-permute-done.5.refs_3_
  18.5 0.0 copy-done.8
  18.5 0.0 copy-start.2
  18.6 0.0 copy-start.3
  18.6 0.0 copy-start.6
  18.6 0.0 copy-start.7
  18.6 0.5 %physics.2 = (f32[4,32,640]{2,1,0:T(8,128)S(1)}, f32[4,32,640]{2,1,0:T(8,128)S(1)}, f32[4,8,640]{2,1,0:T(8,128)S(1)}) custom-call(f32[4,4,32,640]{3,2,1,0:T(8,128)S(1)} %get-tuple-element.48.refs_0_, f32[4,32,640]{2,1,0:T(8,128)S(1)} %get-tuple-element.49.refs_1_, f32[64,1152]{1,0:T(8,128)S(1)} %collective-permute-done.4.refs_2_, ...), custom_call_target="tpu_custom_call" | custom-call | tf_op jit(solution)/shard_map/physics/pallas_call | solution.py:455
  19.1 0.0 copy-start
  19.1 0.0 copy-start.1
  19.2 0.0 copy-start.4
  19.2 0.0 copy-start.5
  19.2 0.0 copy-start.10
  19.2 0.2 collective-permute-start.7
  19.5 0.3 collective-permute-start.6
  19.8 0.9 %collective-permute-done.7.refs_1_ = f32[2,32,640]{2,1,0:T(8,128)S(1)} collective-permute-done((f32[2,32,640]{2,1,0:T(8,128)S(1)}, f32[2,32,640]{2,1,0:T(8,128)S(1)}, u32[]{:S(2)}, u32[]{:S(2)}) %collective-permute-start.7) | collective-permute-done | bytes 163872 | tf_op jit(solution)/shard_map/ppermute | solution.py:498
  20.7 0.2 collective-permute-done.6.refs_0_
  20.9 0.7 %forward.2 = (bf16[128,1152]{1,0:T(8,128)(2,1)S(1)}, bf16[128,1152]{1,0:T(8,128)(2,1)S(1)}) custom-call(f32[4,32,640]{2,1,0:T(8,128)S(1)} %get-tuple-element.59.own_ref, f32[2,32,640]{2,1,0:T(8,128)S(1)} %collective-permute-done.6.refs_0_, f32[2,32,640]{2,1,0:T(8,128)S(1)} %collective-permute-done.7.refs_1_, bf16[1024,256]{1,0:T(8,128)(2,1)S(1)} %copy-done.3, ...), custom_call_target="tpu_custom_call" | custom-call | tf_op jit(solution)/shard_map/forward/pallas_call | solution.py:471
  21.6 0.0 copy-start.9
  21.7 0.0 copy-done
  21.7 0.0 copy-done.1
  21.7 0.0 copy-done.4
  21.7 2.0 %inverse.2 = (f32[32,4,576]{2,1,0:T(4,128)S(1)}, f32[4,32,640]{2,1,0:T(8,128)}) custom-call(s32[4]{0:T(128)S(1)} %copy-done.10, f32[4,32,640]{2,1,0:T(8,128)S(1)} %get-tuple-element.59.own_ref, f32[2,32,640]{2,1,0:T(8,128)S(1)} %collective-permute-done.6.refs_0_, f32[2,32,640]{2,1,0:T(8,128)S(1)} %collective-permute-done.7.refs_1_, ...), custom_call_target="tpu_custom_call" | custom-call | tf_op jit(solution)/shard_map/inverse/pallas_call | solution.py:483
  23.7 9.0 %collective-permute-done.1.refs_2_ = f32[64,1152]{1,0:T(8,128)S(1)} collective-permute-done((f32[64,1152]{1,0:T(8,128)}, f32[64,1152]{1,0:T(8,128)S(1)}, u32[]{:S(2)}, u32[]{:S(2)}) %collective-permute-start.1) | collective-permute-done | bytes 294944 | tf_op jit(solution)/shard_map/ppermute | solution.py:413
  32.7 0.0 collective-permute-done.2.refs_3_
  32.7 0.7 %physics.3 = (f32[4,32,640]{2,1,0:T(8,128)S(1)}, f32[4,32,640]{2,1,0:T(8,128)S(1)}, f32[1,128]{1,0:T(1,128)S(1)}) custom-call(f32[4,4,32,640]{3,2,1,0:T(8,128)S(1)} %get-tuple-element.48.refs_0_, f32[4,32,640]{2,1,0:T(8,128)S(1)} %get-tuple-element.49.refs_1_, f32[64,1152]{1,0:T(8,128)S(1)} %collective-permute-done.1.refs_2_, ...), custom_call_target="tpu_custom_call" | custom-call | tf_op jit(solution)/shard_map/physics/pallas_call | solution.py:455
  33.4 0.0 collective-permute-start.9
  33.4 2.4 %collective-permute-start.8 = (f32[1,128]{1,0:T(1,128)S(1)}, f32[1,128]{1,0:T(1,128)S(1)}, u32[]{:S(2)}, u32[]{:S(2)}) collective-permute-start(f32[1,128]{1,0:T(1,128)S(1)} %get-tuple-element.66), channel_id=1, source_target_pairs={{0,2},{2,0},{4,6},{6,4},{8,10},{10,8},{12,14},{14,12},{1,3},{3,1},... | collective-permute-start | bytes 1544 | tf_op jit(solution)/shard_map/ppermute | solution.py:509
  35.8 0.0 collective-permute-done.9.refs_0_
  35.8 0.7 %forward.3 = (bf16[128,1152]{1,0:T(8,128)(2,1)S(1)}, bf16[128,1152]{1,0:T(8,128)(2,1)S(1)}) custom-call(f32[4,32,640]{2,1,0:T(8,128)S(1)} %get-tuple-element.67.own_ref, f32[4,32,640]{2,1,0:T(8,128)S(1)} %collective-permute-done.9.refs_0_, bf16[1024,256]{1,0:T(8,128)(2,1)S(1)} %copy-done.3, bf16[1024,256]{1,0:T(8,128)(2,1)S(1)} %copy-done.2, ...), custom_call_target="tpu_custom_call" | custom-call | tf_op jit(solution)/shard_map/forward/pallas_call | solution.py:471
  36.5 0.8 %collective-permute-done.8 = f32[1,128]{1,0:T(1,128)S(1)} collective-permute-done((f32[1,128]{1,0:T(1,128)S(1)}, f32[1,128]{1,0:T(1,128)S(1)}, u32[]{:S(2)}, u32[]{:S(2)}) %collective-permute-start.8) | collective-permute-done | bytes 544 | tf_op jit(solution)/shard_map/ppermute | solution.py:509
  37.4 2.5 %collective-permute-start.10 = (f32[1,128]{1,0:T(1,128)S(1)}, f32[1,128]{1,0:T(1,128)S(1)}, u32[]{:S(2)}, u32[]{:S(2)}) collective-permute-start(f32[1,128]{1,0:T(1,128)S(1)} %add.44), channel_id=1, source_target_pairs={{0,4},{2,6},{4,0},{6,2},{8,12},{10,14},{12,8},{14,10},{1,5},{3,7},... | collective-permute-start | bytes 1544 | tf_op jit(solution)/shard_map/ppermute | solution.py:509
  39.8 0.0 collective-permute-start.12
  39.8 1.2 %inverse.3 = (f32[32,4,576]{2,1,0:T(4,128)S(1)}, f32[4,32,640]{2,1,0:T(8,128)S(1)}) custom-call(s32[4]{0:T(128)S(1)} %copy-done.10, f32[4,32,640]{2,1,0:T(8,128)S(1)} %get-tuple-element.67.own_ref, f32[4,32,640]{2,1,0:T(8,128)S(1)} %collective-permute-done.9.refs_0_, bf16[128,1152]{1,0:T(8,128)(2,1)S(1)} %get-tuple-element.73.refs_1_, ...), custom_call_target="tpu_custom_call" | custom-call | tf_op jit(solution)/shard_map/inverse/pallas_call | solution.py:483
  41.1 0.3 collective-permute-done.10
  41.4 0.3 collective-permute-start.13
  41.7 2.8 %collective-permute-start.11 = (f32[1,128]{1,0:T(1,128)S(1)}, f32[1,128]{1,0:T(1,128)S(1)}, u32[]{:S(2)}, u32[]{:S(2)}) collective-permute-start(f32[1,128]{1,0:T(1,128)S(1)} %add.45), channel_id=1, source_target_pairs={{0,8},{2,10},{4,12},{6,14},{8,0},{10,2},{12,4},{14,6},{1,9},{3,11}... | collective-permute-start | bytes 1544 | tf_op jit(solution)/shard_map/ppermute | solution.py:509
  44.5 0.0 collective-permute-done.12.refs_2_
  44.5 0.0 collective-permute-done.13.refs_3_
  44.5 1.2 %finish.1 = f32[4,32,4,576]{3,2,1,0:T(4,128)} custom-call(f32[32,4,576]{2,1,0:T(4,128)S(1)} %get-tuple-element.79.refs_0_, f32[32,4,576]{2,1,0:T(4,128)S(1)} %get-tuple-element.80.refs_1_, f32[4,32,640]{2,1,0:T(8,128)S(1)} %collective-permute-done.12.refs_2_, f32[4,32,640]{2,1,0:T(8,128)S(1)} %collective-permute-done.13.refs_3_), custom_call_target="tpu_custom_call" | custom-call | bytes 3000000 | tf_op jit(solution)/shard_map/finish/pallas_call | solution.py:529
  45.7 0.4 collective-permute-done.11
  46.1 0.6 %fusion.1 = f32[1,1]{1,0:T(1,128)} fusion(f32[1,128]{1,0:T(1,128)S(1)} %add.46, s32[]{:T(128)S(6)} %select_n.8), kind=kLoop, calls=%fused_computation.4 | loop fusion | flops 1 | bytes 12 | tf_op jit(solution)/shard_map/div | solution.py:547
  (21 shorter events, 0.1 us)
Async XLA Ops:
  2.5 10.9 %copy-start.12 = (f32[1152]{0:T(1024)S(1)}, f32[1152]{0:T(1024)}, u32[]{:S(2)}) copy-start(f32[1152]{0:T(1024)} %constant.56.clone) | copy-start | bytes 13828
  2.5 10.9 %copy-start.13 = (f32[1152]{0:T(1024)S(1)}, f32[1152]{0:T(1024)}, u32[]{:S(2)}) copy-start(f32[1152]{0:T(1024)} %constant.54.clone) | copy-start | bytes 13828
  2.5 10.9 %copy-start.15 = (pred[1152]{0:T(1024)(128)(4,1)S(1)}, pred[1152]{0:T(1024)(128)(4,1)}, u32[]{:S(2)}) copy-start(pred[1152]{0:T(1024)(128)(4,1)} %constant.55.clone) | copy-start | bytes 3460
  2.5 11.0 %copy-start.16 = (s32[1,1,18,1]{2,3,1,0:T(1,128)S(1)}, s32[1,1,18,1]{2,3,1,0:T(1,128)}, u32[]{:S(2)}) copy-start(s32[1,1,18,1]{2,3,1,0:T(1,128)} %param.25) | copy-start | bytes 220
  2.5 11.2 %copy-start.11 = (f32[4,4,576]{2,1,0:T(4,128)S(1)}, f32[4,4,576]{2,1,0:T(4,128)}, u32[]{:S(2)}) copy-start(f32[4,4,576]{2,1,0:T(4,128)} %param.22) | copy-start | bytes 110596
  2.6 16.0 %collective-permute-start.4 = (f32[64,1152]{1,0:T(8,128)}, f32[64,1152]{1,0:T(8,128)S(1)}, u32[]{:S(2)}, u32[]{:S(2)}) collective-permute-start(f32[64,1152]{1,0:T(8,128)} %pack.1), channel_id=1, source_target_pairs={{0,2},{2,0},{4,6},{6,4},{8,10},{10,8},{12,14},{14,12},{1,3},{3,1},... | collective-permute-start | bytes 884744 | tf_op jit(solution)/shard_map/ppermute | solution.py:394
  8.6 9.8 %copy-start.14 = (f32[4,32]{1,0:T(4,128)S(1)}, f32[4,32]{1,0:T(4,128)}, u32[]{:S(2)}) copy-start(f32[4,32]{1,0:T(4,128)} %param.24) | copy-start | bytes 1540
  8.6 9.9 %copy-start.8 = (f32[32,32]{1,0:T(8,128)S(1)}, f32[32,32]{1,0:T(8,128)}, u32[]{:S(2)}) copy-start(f32[32,32]{1,0:T(8,128)} %refs_7_.4) | copy-start | bytes 12292
  8.6 9.9 %collective-permute-start.3 = (f32[16,1152]{1,0:T(8,128)}, f32[16,1152]{1,0:T(8,128)S(1)}, u32[]{:S(2)}, u32[]{:S(2)}) collective-permute-start(f32[16,1152]{1,0:T(8,128)} %get-tuple-element.52), channel_id=1, source_target_pairs={{2,0},{4,2},{6,4},{8,6},{10,8},{12,10},{14,12},{3,1},{5,3},{7,5},{... | collective-permute-start | bytes 221192 | tf_op jit(solution)/shard_map/ppermute | solution.py:414
  9.9 3.8 %collective-permute-start = (f32[5,2,32,128]{3,2,1,0:T(8,128)S(1)}, f32[5,2,32,128]{3,2,1,0:T(8,128)S(1)}, u32[]{:S(2)}, u32[]{:S(2)}) collective-permute-start(f32[5,2,32,128]{3,2,1,0:T(8,128)S(1)} %get-tuple-element.46), channel_id=1, source_target_pairs={{0,1},{1,0},{2,3},{3,2},{4,5},{5,4},{6,7},{7,6},{8,9},{9,8},{10,11... | collective-permute-start | bytes 491528 | tf_op jit(solution)/shard_map/ppermute | solution.py:416
  10.0 22.7 %collective-permute-start.1 = (f32[64,1152]{1,0:T(8,128)}, f32[64,1152]{1,0:T(8,128)S(1)}, u32[]{:S(2)}, u32[]{:S(2)}) collective-permute-start(f32[64,1152]{1,0:T(8,128)} %get-tuple-element.50), channel_id=1, source_target_pairs={{0,2},{2,0},{4,6},{6,4},{8,10},{10,8},{12,14},{14,12},{1,3},{3,1},... | collective-permute-start | bytes 884744 | tf_op jit(solution)/shard_map/ppermute | solution.py:413
  12.7 5.8 %collective-permute-start.5 = (f32[64,1152]{1,0:T(8,128)}, f32[64,1152]{1,0:T(8,128)S(1)}, u32[]{:S(2)}, u32[]{:S(2)}) collective-permute-start(f32[64,1152]{1,0:T(8,128)} %get-tuple-element.57), channel_id=1, source_target_pairs={{2,4},{4,2},{6,8},{8,6},{10,12},{12,10},{3,5},{5,3},{7,9},{9,7},{1... | collective-permute-start | bytes 884744 | tf_op jit(solution)/shard_map/ppermute | solution.py:412
  13.7 18.9 %collective-permute-start.2 = (f32[64,1152]{1,0:T(8,128)}, f32[64,1152]{1,0:T(8,128)S(1)}, u32[]{:S(2)}, u32[]{:S(2)}) collective-permute-start(f32[64,1152]{1,0:T(8,128)} %get-tuple-element.51), channel_id=1, source_target_pairs={{2,4},{4,2},{6,8},{8,6},{10,12},{12,10},{3,5},{5,3},{7,9},{9,7},{1... | collective-permute-start | bytes 884744 | tf_op jit(solution)/shard_map/ppermute | solution.py:412
  18.5 2.4 %copy-start.2 = (bf16[1024,256]{1,0:T(8,128)(2,1)S(1)}, bf16[1024,256]{1,0:T(8,128)(2,1)}, u32[]{:S(2)}) copy-start(bf16[1024,256]{1,0:T(8,128)(2,1)} %constant.58.clone.refs_3_.refs_2_) | copy-start | bytes 1572868
  18.6 2.4 %copy-start.3 = (bf16[1024,256]{1,0:T(8,128)(2,1)S(1)}, bf16[1024,256]{1,0:T(8,128)(2,1)}, u32[]{:S(2)}) copy-start(bf16[1024,256]{1,0:T(8,128)(2,1)} %constant.57.clone.refs_2_.refs_1_) | copy-start | bytes 1572868
  18.6 2.4 %copy-start.6 = (bf16[128,128]{1,0:T(8,128)(2,1)S(1)}, bf16[128,128]{1,0:T(8,128)(2,1)}, u32[]{:S(2)}) copy-start(bf16[128,128]{1,0:T(8,128)(2,1)} %constant.60.clone.refs_5_.refs_4_) | copy-start | bytes 98308
  18.6 2.4 %copy-start.7 = (bf16[128,128]{1,0:T(8,128)(2,1)S(1)}, bf16[128,128]{1,0:T(8,128)(2,1)}, u32[]{:S(2)}) copy-start(bf16[128,128]{1,0:T(8,128)(2,1)} %constant.59.clone.refs_4_.refs_3_) | copy-start | bytes 98308
  19.1 2.5 %copy-start = (bf16[1024,256]{1,0:T(8,128)(2,1)S(1)}, bf16[1024,256]{1,0:T(8,128)(2,1)}, u32[]{:S(2)}) copy-start(bf16[1024,256]{1,0:T(8,128)(2,1)} %constant.62.clone.refs_5_.refs_4_) | copy-start | bytes 1572868
  19.1 2.5 %copy-start.1 = (bf16[1024,256]{1,0:T(8,128)(2,1)S(1)}, bf16[1024,256]{1,0:T(8,128)(2,1)}, u32[]{:S(2)}) copy-start(bf16[1024,256]{1,0:T(8,128)(2,1)} %constant.61.clone.refs_4_.refs_3_) | copy-start | bytes 1572868
  19.2 2.5 %copy-start.4 = (bf16[128,128]{1,0:T(8,128)(2,1)S(1)}, bf16[128,128]{1,0:T(8,128)(2,1)}, u32[]{:S(2)}) copy-start(bf16[128,128]{1,0:T(8,128)(2,1)} %constant.64.clone.refs_7_.refs_6_) | copy-start | bytes 98308
  19.2 2.5 %copy-start.5 = (bf16[128,128]{1,0:T(8,128)(2,1)S(1)}, bf16[128,128]{1,0:T(8,128)(2,1)}, u32[]{:S(2)}) copy-start(bf16[128,128]{1,0:T(8,128)(2,1)} %constant.63.clone.refs_6_.refs_5_) | copy-start | bytes 98308
  19.2 2.5 %copy-start.10 = (s32[4]{0:T(128)S(1)}, s32[4]{0:T(128)}, u32[]{:S(2)}) copy-start(s32[4]{0:T(128)} %mask_ref.3) | copy-start | bytes 52
  19.2 1.5 %collective-permute-start.7 = (f32[2,32,640]{2,1,0:T(8,128)S(1)}, f32[2,32,640]{2,1,0:T(8,128)S(1)}, u32[]{:S(2)}, u32[]{:S(2)}) collective-permute-start(f32[2,32,640]{2,1,0:T(8,128)S(1)} %get-tuple-element.84), channel_id=1, source_target_pairs={{0,1},{1,0},{2,3},{3,2},{4,5},{5,4},{6,7},{7,6},{8,9},{9,8},{10,11... | collective-permute-start | bytes 491528 | tf_op jit(solution)/shard_map/ppermute | solution.py:498
  19.5 1.5 %collective-permute-start.6 = (f32[2,32,640]{2,1,0:T(8,128)S(1)}, f32[2,32,640]{2,1,0:T(8,128)S(1)}, u32[]{:S(2)}, u32[]{:S(2)}) collective-permute-start(f32[2,32,640]{2,1,0:T(8,128)S(1)} %get-tuple-element.85), channel_id=1, source_target_pairs={{0,1},{1,0},{2,3},{3,2},{4,5},{5,4},{6,7},{7,6},{8,9},{9,8},{10,11... | collective-permute-start | bytes 491528 | tf_op jit(solution)/shard_map/ppermute | solution.py:498
  21.6 11.0 %copy-start.9 = (f32[32,32]{1,0:T(8,128)S(1)}, f32[32,32]{1,0:T(8,128)}, u32[]{:S(2)}) copy-start(f32[32,32]{1,0:T(8,128)} %refs_7_.4) | copy-start | bytes 12292
  33.4 2.5 %collective-permute-start.9 = (f32[4,32,640]{2,1,0:T(8,128)S(1)}, f32[4,32,640]{2,1,0:T(8,128)S(1)}, u32[]{:S(2)}, u32[]{:S(2)}) collective-permute-start(f32[4,32,640]{2,1,0:T(8,128)S(1)} %get-tuple-element.68), channel_id=1, source_target_pairs={{0,1},{1,0},{2,3},{3,2},{4,5},{5,4},{6,7},{7,6},{8,9},{9,8},{10,11... | collective-permute-start | bytes 983048 | tf_op jit(solution)/shard_map/ppermute | solution.py:512
  33.4 4.0 %collective-permute-start.8 = (f32[1,128]{1,0:T(1,128)S(1)}, f32[1,128]{1,0:T(1,128)S(1)}, u32[]{:S(2)}, u32[]{:S(2)}) collective-permute-start(f32[1,128]{1,0:T(1,128)S(1)} %get-tuple-element.66), channel_id=1, source_target_pairs={{0,2},{2,0},{4,6},{6,4},{8,10},{10,8},{12,14},{14,12},{1,3},{3,1},... | collective-permute-start | bytes 1544 | tf_op jit(solution)/shard_map/ppermute | solution.py:509
  37.4 4.0 %collective-permute-start.10 = (f32[1,128]{1,0:T(1,128)S(1)}, f32[1,128]{1,0:T(1,128)S(1)}, u32[]{:S(2)}, u32[]{:S(2)}) collective-permute-start(f32[1,128]{1,0:T(1,128)S(1)} %add.44), channel_id=1, source_target_pairs={{0,4},{2,6},{4,0},{6,2},{8,12},{10,14},{12,8},{14,10},{1,5},{3,7},... | collective-permute-start | bytes 1544 | tf_op jit(solution)/shard_map/ppermute | solution.py:509
  39.8 4.7 %collective-permute-start.12 = (f32[4,32,640]{2,1,0:T(8,128)}, f32[4,32,640]{2,1,0:T(8,128)S(1)}, u32[]{:S(2)}, u32[]{:S(2)}) collective-permute-start(f32[4,32,640]{2,1,0:T(8,128)} %get-tuple-element.64), channel_id=1, source_target_pairs={{0,1},{1,0},{2,3},{3,2},{4,5},{5,4},{6,7},{7,6},{8,9},{9,8},{10,11... | collective-permute-start | bytes 983048 | tf_op jit(solution)/shard_map/ppermute | solution.py:502
  41.4 3.1 %collective-permute-start.13 = (f32[4,32,640]{2,1,0:T(8,128)S(1)}, f32[4,32,640]{2,1,0:T(8,128)S(1)}, u32[]{:S(2)}, u32[]{:S(2)}) collective-permute-start(f32[4,32,640]{2,1,0:T(8,128)S(1)} %get-tuple-element.81), channel_id=1, source_target_pairs={{0,1},{1,0},{2,3},{3,2},{4,5},{5,4},{6,7},{7,6},{8,9},{9,8},{10,11... | collective-permute-start | bytes 983048 | tf_op jit(solution)/shard_map/ppermute | solution.py:526
  41.7 4.4 %collective-permute-start.11 = (f32[1,128]{1,0:T(1,128)S(1)}, f32[1,128]{1,0:T(1,128)S(1)}, u32[]{:S(2)}, u32[]{:S(2)}) collective-permute-start(f32[1,128]{1,0:T(1,128)S(1)} %add.45), channel_id=1, source_target_pairs={{0,8},{2,10},{4,12},{6,14},{8,0},{10,2},{12,4},{14,6},{1,9},{3,11}... | collective-permute-start | bytes 1544 | tf_op jit(solution)/shard_map/ppermute | solution.py:509

commit v16 on v15

--- a/solution.py
+++ b/solution.py
@@ -174,7 +174,11 @@
 def physics_kernel(levels, sector, owner_count, chunk, halves, *refs):
     base_ref, north_ref, inner_ref, outer_ref = refs[:4]
     top_ref, courant_ref, surface_ref, mixing_ref, decay_ref, owner_ref, energy_in_ref = refs[4:11]
-    physics_refs, energy_ref = refs[11:-1], refs[-1]
+    physics_refs, energy_ref, scratch = refs[11 : 11 + len(halves)], refs[11 + len(halves)], refs[12 + len(halves) :]
+    if scratch:
+        for copy in start_copies([(inner_ref, scratch[0]), (outer_ref, scratch[1])], scratch[2]):
+            copy.wait()
+        inner_ref, outer_ref = scratch[:2]
     rows, width = base_ref.shape[1], base_ref.shape[-1]
     courant = [courant_ref[r] for r in range(rows)]
     even = is_even()
@@ -449,18 +453,23 @@
     result_shape = jax.ShapeDtypeStruct((levels, rows, sector), f32)
     out_shape = jax.ShapeDtypeStruct(tracers.shape, f32)
 
+    def rows_of(chunk):
+        parts = (from_inside[chunk], from_across[chunk])
+        return parts if chunk == half - 1 else [pltpu.with_memory_space_constraint(part, pltpu.HBM) for part in parts]
+
     def run_physics(chunk, energy, last=False):
         shapes = [jax.ShapeDtypeStruct(circles.shape[1:], f32)] * 2
         shapes.append(jax.ShapeDtypeStruct((1, LANES) if last else energy.shape, f32))
         *results, energy = pl.pallas_call(
             functools.partial(physics_kernel, levels, sector, lat_count if last else 0, chunk, ("give", "keep")),
-            in_specs=[whole] * 11,
+            in_specs=[whole] * 2 + ([whole] if last else [in_hbm]) * 2 + [whole] * 7,
             out_specs=[whole] * len(shapes),
+            scratch_shapes=[] if last else [chunk_rows] * 2 + [pltpu.SemaphoreType.DMA((2,))],
             out_shape=shapes,
             compiler_params=params(),
             cost_estimate=cost(0, 0),
             name="physics",
-        )(base, north, from_inside[chunk], from_across[chunk], top, lat_courant, surface, mixing, decay, owner_of, energy)
+        )(base, north, *rows_of(chunk), top, lat_courant, surface, mixing, decay, owner_of, energy)
         return results, energy
 
     forward, inverse = ([jnp.asarray(part) for table in tables for part in split_table(table)] for tables in (forward, inverse))

time: 47 us -> 46.2 us (0.983)
  waiting for transfers between devices: 11.6 us -> 9.75 us
  starting transfers between devices: 17.1 us -> 17.7 us
  Pallas kernels: 15.8 us -> 16.3 us
    ppermute x1, waiting for transfers between devices: 8.99 us -> 7 us  [on_device(): from_inside += [lax.ppermute(part, 'lat', inside) for part in inner]]
    pallas_call x2, Pallas kernels: 1.2 us -> 2.34 us  [run_physics(): pl.pallas_call(functools.partial(physics_kernel, levels, sector, lat_coun...]
    pallas_call x1, Pallas kernels: 1.85 us -> 1.14 us  [on_device(): pl.pallas_call(functools.partial(pack_kernel, (0, half)), in_specs=[in_hb...]
    ppermute x2, starting transfers between devices: 1.35 us -> 2.05 us  [on_device(): from_across = [lax.ppermute(part, 'lat', across) for part in outer]]
  transfers between devices with their start and end apart: 14 -> 14, of which waited for: 6 -> 6; matrix products, arithmetic and copies ran while one was open for 1% -> 1% of each run, Pallas kernels for 28% -> 31%
where the time goes in v16:
time: 46.2 us; the launch traced here: 45.9 us
  starting transfers between devices  17.7 us (38%)
  Pallas kernels  16.3 us (35%)
  waiting for transfers between devices  9.75 us (21%)
  between operations  1 us (2%)
  other arithmetic  0.72 us (2%)
    ppermute x3, starting transfers between devices, send_energy(): lax.ppermute(energy, 'lat', [(i, i ^ distance) for i in range(lat_count)])  7.66 us
    ppermute x1, waiting for transfers between devices, on_device(): from_inside += [lax.ppermute(part, 'lat', inside) for part in inner]  7 us
    pallas_call x1, Pallas kernels, on_device(): pl.pallas_call(functools.partial(base_kernel, width), in_specs=[in_hbm, i...  3.97 us
    pallas_call x2, Pallas kernels, run_inverse(): pl.pallas_call(functools.partial(inverse_kernel, radix, len(other)), in_s...  3.23 us
    ppermute x1, starting transfers between devices, on_device(): from_inside = [lax.ppermute(inner, 'lat', inside)]  3 us
    pallas_call x1, Pallas kernels, on_device(): pl.pallas_call(rest_kernel, in_specs=[in_hbm] * 3, out_specs=[whole] * (2...  3 us
    ppermute x1, starting transfers between devices, on_device(): from_inside += [lax.ppermute(part, 'lat', inside) for part in inner]  2.71 us
    pallas_call x2, Pallas kernels, run_physics(): pl.pallas_call(functools.partial(physics_kernel, levels, sector, lat_coun...  2.34 us
  transfers between devices with their start and end apart: 14, of which 6 were waited for; matrix products, arithmetic and copies ran while one was open for 1% of the time, Pallas kernels for 31%

profile of v16, /device:TPU:0, one launch (start us, length us, event | category | flops | bytes accessed | tf_op | source)
XLA Modules:
  0.0 45.9 jit_solution(5222169026403455937)
XLA Ops:
  0.6 1.1 %pack.1 = f32[64,1152]{1,0:T(8,128)S(1)} custom-call(f32[4,32,4,576]{3,2,1,0:T(4,128)} %tracer_hbm.3), custom_call_target="tpu_custom_call" | custom-call | bytes 600000 | tf_op jit(solution)/shard_map/pack/pallas_call | solution.py:388
  1.8 0.0 copy-start.11
  1.8 0.0 copy-start.12
  1.8 0.0 copy-start.14
  1.8 0.0 copy-start.15
  1.8 0.0 copy-start.10
  1.8 3.0 %collective-permute-start.4 = (f32[64,1152]{1,0:T(8,128)S(1)}, f32[64,1152]{1,0:T(8,128)}, u32[]{:S(2)}, u32[]{:S(2)}) collective-permute-start(f32[64,1152]{1,0:T(8,128)S(1)} %pack.1), channel_id=1, source_target_pairs={{0,2},{2,0},{4,6},{6,4},{8,10},{10,8},{12,14},{14,12},{1,3},{3,1},... | collective-permute-start | bytes 884744 | tf_op jit(solution)/shard_map/ppermute | solution.py:398
  4.8 3.0 %rest.1 = (f32[64,1152]{1,0:T(8,128)}, f32[64,1152]{1,0:T(8,128)}, f32[64,1152]{1,0:T(8,128)}, f32[16,1152]{1,0:T(8,128)S(1)}, f32[5,2,32,128]{3,2,1,0:T(8,128)S(1)}) custom-call(f32[4,32,4,576]{3,2,1,0:T(4,128)} %tracer_hbm.3, f32[32,4,576]{2,1,0:T(4,128)} %lat_hbm.1, f32[32,4,576]{2,1,0:T(4,128)} %lon_hbm.1), custom_call_target="tpu_custom_call" | custom-call | tf_op jit(solution)/shard_map/rest/pallas_call | solution.py:401
  7.8 0.0 copy-start.13
  7.9 0.0 copy-start.8
  7.9 1.3 %collective-permute-start.3 = (f32[16,1152]{1,0:T(8,128)S(1)}, f32[16,1152]{1,0:T(8,128)S(1)}, u32[]{:S(2)}, u32[]{:S(2)}) collective-permute-start(f32[16,1152]{1,0:T(8,128)S(1)} %get-tuple-element.52), channel_id=1, source_target_pairs={{2,0},{4,2},{6,4},{8,6},{10,8},{12,10},{14,12},{3,1},{5,3},{7,5},{... | collective-permute-start | bytes 221192 | tf_op jit(solution)/shard_map/ppermute | solution.py:418
  9.2 0.1 collective-permute-start
  9.3 2.7 %collective-permute-start.1 = (f32[64,1152]{1,0:T(8,128)}, f32[64,1152]{1,0:T(8,128)S(1)}, u32[]{:S(2)}, u32[]{:S(2)}) collective-permute-start(f32[64,1152]{1,0:T(8,128)} %get-tuple-element.50), channel_id=1, source_target_pairs={{0,2},{2,0},{4,6},{6,4},{8,10},{10,8},{12,14},{14,12},{1,3},{3,1},... | collective-permute-start | bytes 884744 | tf_op jit(solution)/shard_map/ppermute | solution.py:417
  12.0 1.4 %collective-permute-start.5 = (f32[64,1152]{1,0:T(8,128)}, f32[64,1152]{1,0:T(8,128)}, u32[]{:S(2)}, u32[]{:S(2)}) collective-permute-start(f32[64,1152]{1,0:T(8,128)} %get-tuple-element.57), channel_id=1, source_target_pairs={{2,4},{4,2},{6,8},{8,6},{10,12},{12,10},{3,5},{5,3},{7,9},{9,7},{1... | collective-permute-start | bytes 884744 | tf_op jit(solution)/shard_map/ppermute | solution.py:416
  13.4 0.0 copy-done.11
  13.4 0.0 copy-done.12
  13.4 0.1 select_multiply_fusion.refs_6_.refs_5_
  13.5 0.1 broadcast_in_dim.27
  13.6 0.1 reshape_reshape.3
  13.7 0.0 copy-done.10
  13.7 0.0 collective-permute-done.side_ref
  13.7 0.7 %collective-permute-start.2 = (f32[64,1152]{1,0:T(8,128)}, f32[64,1152]{1,0:T(8,128)S(1)}, u32[]{:S(2)}, u32[]{:S(2)}) collective-permute-start(f32[64,1152]{1,0:T(8,128)} %get-tuple-element.51), channel_id=1, source_target_pairs={{2,4},{4,2},{6,8},{8,6},{10,12},{12,10},{3,5},{5,3},{7,9},{9,7},{1... | collective-permute-start | bytes 884744 | tf_op jit(solution)/shard_map/ppermute | solution.py:416
  14.4 4.0 %base.1 = (f32[4,4,32,640]{3,2,1,0:T(8,128)S(1)}, f32[4,32,640]{2,1,0:T(8,128)S(1)}, f32[4,32,640]{2,1,0:T(8,128)S(1)}) custom-call(f32[4,32,4,576]{3,2,1,0:T(4,128)} %tracer_hbm.3, f32[32,4,576]{2,1,0:T(4,128)} %lat_hbm.1, f32[32,4,576]{2,1,0:T(4,128)} %lon_hbm.1, f32[5,2,32,128]{3,2,1,0:T(8,128)S(1)} %collective-permute-done.side_ref), custom_call_target="tpu_custom_call" | custom-call | tf_op jit(solution)/shard_map/base/pallas_call | solution.py:421
  18.4 0.1 copy.22.refs_8_
  18.5 0.0 collective-permute-done.3.refs_4_
  18.5 0.0 collective-permute-done.4.refs_2_
  18.5 0.0 collective-permute-done.5.refs_3_
  18.5 0.0 copy-start.2
  18.5 0.0 copy-start.3
  18.6 0.0 copy-start.6
  18.6 0.0 copy-start.7
  18.6 1.7 %physics.2 = (f32[4,32,640]{2,1,0:T(8,128)S(1)}, f32[4,32,640]{2,1,0:T(8,128)S(1)}, f32[4,8,640]{2,1,0:T(8,128)S(1)}) custom-call(f32[4,4,32,640]{3,2,1,0:T(8,128)S(1)} %get-tuple-element.48.refs_0_, f32[4,32,640]{2,1,0:T(8,128)S(1)} %get-tuple-element.49.refs_1_, f32[64,1152]{1,0:T(8,128)} %collective-permute-done.4.refs_2_, ...), custom_call_target="tpu_custom_call" | custom-call | tf_op jit(solution)/shard_map/physics/pallas_call | solution.py:463
  20.3 0.0 copy-start
  20.3 0.0 copy-start.1
  20.3 0.0 copy-start.4
  20.3 0.0 copy-start.5
  20.3 0.0 copy-start.9
  20.3 0.2 collective-permute-start.7
  20.6 0.3 collective-permute-start.6
  20.9 0.9 %collective-permute-done.7.refs_1_ = f32[2,32,640]{2,1,0:T(8,128)S(1)} collective-permute-done((f32[2,32,640]{2,1,0:T(8,128)S(1)}, f32[2,32,640]{2,1,0:T(8,128)S(1)}, u32[]{:S(2)}, u32[]{:S(2)}) %collective-permute-start.7) | collective-permute-done | bytes 163872 | tf_op jit(solution)/shard_map/ppermute | solution.py:507
  21.8 0.2 collective-permute-done.6.refs_0_
  22.1 0.0 copy-done.6
  22.1 0.0 copy-done.7
  22.1 0.7 %forward.2 = (bf16[128,1152]{1,0:T(8,128)(2,1)S(1)}, bf16[128,1152]{1,0:T(8,128)(2,1)S(1)}) custom-call(f32[4,32,640]{2,1,0:T(8,128)S(1)} %get-tuple-element.59.own_ref, f32[2,32,640]{2,1,0:T(8,128)S(1)} %collective-permute-done.6.refs_0_, f32[2,32,640]{2,1,0:T(8,128)S(1)} %collective-permute-done.7.refs_1_, bf16[1024,256]{1,0:T(8,128)(2,1)S(1)} %copy-done.3, ...), custom_call_target="tpu_custom_call" | custom-call | tf_op jit(solution)/shard_map/forward/pallas_call | solution.py:480
  22.8 2.0 %inverse.2 = (f32[32,4,576]{2,1,0:T(4,128)S(1)}, f32[4,32,640]{2,1,0:T(8,128)}) custom-call(s32[4]{0:T(128)S(1)} %copy-done.9, f32[4,32,640]{2,1,0:T(8,128)S(1)} %get-tuple-element.59.own_ref, f32[2,32,640]{2,1,0:T(8,128)S(1)} %collective-permute-done.6.refs_0_, f32[2,32,640]{2,1,0:T(8,128)S(1)} %collective-permute-done.7.refs_1_, ...), custom_call_target="tpu_custom_call" | custom-call | tf_op jit(solution)/shard_map/inverse/pallas_call | solution.py:492
  24.8 7.0 %collective-permute-done.1.refs_2_ = f32[64,1152]{1,0:T(8,128)S(1)} collective-permute-done((f32[64,1152]{1,0:T(8,128)}, f32[64,1152]{1,0:T(8,128)S(1)}, u32[]{:S(2)}, u32[]{:S(2)}) %collective-permute-start.1) | collective-permute-done | bytes 294944 | tf_op jit(solution)/shard_map/ppermute | solution.py:417
  31.8 0.0 collective-permute-done.2.refs_3_
  31.8 0.7 %physics.3 = (f32[4,32,640]{2,1,0:T(8,128)S(1)}, f32[4,32,640]{2,1,0:T(8,128)S(1)}, f32[1,128]{1,0:T(1,128)S(1)}) custom-call(f32[4,4,32,640]{3,2,1,0:T(8,128)S(1)} %get-tuple-element.48.refs_0_, f32[4,32,640]{2,1,0:T(8,128)S(1)} %get-tuple-element.49.refs_1_, f32[64,1152]{1,0:T(8,128)S(1)} %collective-permute-done.1.refs_2_, ...), custom_call_target="tpu_custom_call" | custom-call | tf_op jit(solution)/shard_map/physics/pallas_call | solution.py:463
  32.5 0.0 collective-permute-start.9
  32.5 2.4 %collective-permute-start.8 = (f32[1,128]{1,0:T(1,128)S(1)}, f32[1,128]{1,0:T(1,128)S(1)}, u32[]{:S(2)}, u32[]{:S(2)}) collective-permute-start(f32[1,128]{1,0:T(1,128)S(1)} %get-tuple-element.66), channel_id=1, source_target_pairs={{0,2},{2,0},{4,6},{6,4},{8,10},{10,8},{12,14},{14,12},{1,3},{3,1},... | collective-permute-start | bytes 1544 | tf_op jit(solution)/shard_map/ppermute | solution.py:518
  35.0 0.0 collective-permute-done.9.refs_0_
  35.0 0.7 %forward.3 = (bf16[128,1152]{1,0:T(8,128)(2,1)S(1)}, bf16[128,1152]{1,0:T(8,128)(2,1)S(1)}) custom-call(f32[4,32,640]{2,1,0:T(8,128)S(1)} %get-tuple-element.67.own_ref, f32[4,32,640]{2,1,0:T(8,128)S(1)} %collective-permute-done.9.refs_0_, bf16[1024,256]{1,0:T(8,128)(2,1)S(1)} %copy-done.3, bf16[1024,256]{1,0:T(8,128)(2,1)S(1)} %copy-done.2, ...), custom_call_target="tpu_custom_call" | custom-call | tf_op jit(solution)/shard_map/forward/pallas_call | solution.py:480
  35.7 0.8 %collective-permute-done.8 = f32[1,128]{1,0:T(1,128)S(1)} collective-permute-done((f32[1,128]{1,0:T(1,128)S(1)}, f32[1,128]{1,0:T(1,128)S(1)}, u32[]{:S(2)}, u32[]{:S(2)}) %collective-permute-start.8) | collective-permute-done | bytes 544 | tf_op jit(solution)/shard_map/ppermute | solution.py:518
  36.5 2.5 %collective-permute-start.10 = (f32[1,128]{1,0:T(1,128)S(1)}, f32[1,128]{1,0:T(1,128)S(1)}, u32[]{:S(2)}, u32[]{:S(2)}) collective-permute-start(f32[1,128]{1,0:T(1,128)S(1)} %add.44), channel_id=1, source_target_pairs={{0,4},{2,6},{4,0},{6,2},{8,12},{10,14},{12,8},{14,10},{1,5},{3,7},... | collective-permute-start | bytes 1544 | tf_op jit(solution)/shard_map/ppermute | solution.py:518
  39.0 0.0 collective-permute-start.12
  39.0 1.3 %inverse.3 = (f32[32,4,576]{2,1,0:T(4,128)S(1)}, f32[4,32,640]{2,1,0:T(8,128)S(1)}) custom-call(s32[4]{0:T(128)S(1)} %copy-done.9, f32[4,32,640]{2,1,0:T(8,128)S(1)} %get-tuple-element.67.own_ref, f32[4,32,640]{2,1,0:T(8,128)S(1)} %collective-permute-done.9.refs_0_, bf16[128,1152]{1,0:T(8,128)(2,1)S(1)} %get-tuple-element.73.refs_1_, ...), custom_call_target="tpu_custom_call" | custom-call | tf_op jit(solution)/shard_map/inverse/pallas_call | solution.py:492
  40.2 0.3 collective-permute-done.10
  40.5 0.3 collective-permute-start.13
  40.8 2.7 %collective-permute-start.11 = (f32[1,128]{1,0:T(1,128)S(1)}, f32[1,128]{1,0:T(1,128)S(1)}, u32[]{:S(2)}, u32[]{:S(2)}) collective-permute-start(f32[1,128]{1,0:T(1,128)S(1)} %add.45), channel_id=1, source_target_pairs={{0,8},{2,10},{4,12},{6,14},{8,0},{10,2},{12,4},{14,6},{1,9},{3,11}... | collective-permute-start | bytes 1544 | tf_op jit(solution)/shard_map/ppermute | solution.py:518
  43.5 0.0 collective-permute-done.12.refs_2_
  43.6 0.0 collective-permute-done.13.refs_3_
  43.6 1.2 %finish.1 = f32[4,32,4,576]{3,2,1,0:T(4,128)} custom-call(f32[32,4,576]{2,1,0:T(4,128)S(1)} %get-tuple-element.79.refs_0_, f32[32,4,576]{2,1,0:T(4,128)S(1)} %get-tuple-element.80.refs_1_, f32[4,32,640]{2,1,0:T(8,128)S(1)} %collective-permute-done.12.refs_2_, f32[4,32,640]{2,1,0:T(8,128)S(1)} %collective-permute-done.13.refs_3_), custom_call_target="tpu_custom_call" | custom-call | bytes 3000000 | tf_op jit(solution)/shard_map/finish/pallas_call | solution.py:538
  44.8 0.5 %collective-permute-done.11 = f32[1,128]{1,0:T(1,128)S(1)} collective-permute-done((f32[1,128]{1,0:T(1,128)S(1)}, f32[1,128]{1,0:T(1,128)S(1)}, u32[]{:S(2)}, u32[]{:S(2)}) %collective-permute-start.11) | collective-permute-done | bytes 544 | tf_op jit(solution)/shard_map/ppermute | solution.py:518
  45.3 0.6 %fusion.1 = f32[1,1]{1,0:T(1,128)} fusion(f32[1,128]{1,0:T(1,128)S(1)} %add.46, s32[]{:T(128)S(6)} %select_n.8), kind=kLoop, calls=%fused_computation.4 | loop fusion | flops 1 | bytes 12 | tf_op jit(solution)/shard_map/div | solution.py:556
  (19 shorter events, 0.1 us)
Async XLA Ops:
  1.8 11.6 %copy-start.11 = (f32[1152]{0:T(1024)S(1)}, f32[1152]{0:T(1024)}, u32[]{:S(2)}) copy-start(f32[1152]{0:T(1024)} %constant.56.clone) | copy-start | bytes 13828
  1.8 11.6 %copy-start.12 = (f32[1152]{0:T(1024)S(1)}, f32[1152]{0:T(1024)}, u32[]{:S(2)}) copy-start(f32[1152]{0:T(1024)} %constant.54.clone) | copy-start | bytes 13828
  1.8 11.6 %copy-start.14 = (pred[1152]{0:T(1024)(128)(4,1)S(1)}, pred[1152]{0:T(1024)(128)(4,1)}, u32[]{:S(2)}) copy-start(pred[1152]{0:T(1024)(128)(4,1)} %constant.55.clone) | copy-start | bytes 3460
  1.8 11.7 %copy-start.15 = (s32[1,1,18,1]{2,3,1,0:T(1,128)S(1)}, s32[1,1,18,1]{2,3,1,0:T(1,128)}, u32[]{:S(2)}) copy-start(s32[1,1,18,1]{2,3,1,0:T(1,128)} %param.25) | copy-start | bytes 220
  1.8 11.8 %copy-start.10 = (f32[4,4,576]{2,1,0:T(4,128)S(1)}, f32[4,4,576]{2,1,0:T(4,128)}, u32[]{:S(2)}) copy-start(f32[4,4,576]{2,1,0:T(4,128)} %param.22) | copy-start | bytes 110596
  1.8 16.6 %collective-permute-start.4 = (f32[64,1152]{1,0:T(8,128)S(1)}, f32[64,1152]{1,0:T(8,128)}, u32[]{:S(2)}, u32[]{:S(2)}) collective-permute-start(f32[64,1152]{1,0:T(8,128)S(1)} %pack.1), channel_id=1, source_target_pairs={{0,2},{2,0},{4,6},{6,4},{8,10},{10,8},{12,14},{14,12},{1,3},{3,1},... | collective-permute-start | bytes 884744 | tf_op jit(solution)/shard_map/ppermute | solution.py:398
  7.8 10.5 %copy-start.13 = (f32[4,32]{1,0:T(4,128)S(1)}, f32[4,32]{1,0:T(4,128)}, u32[]{:S(2)}) copy-start(f32[4,32]{1,0:T(4,128)} %param.24) | copy-start | bytes 1540
  7.9 10.7 %copy-start.8 = (f32[32,32]{1,0:T(8,128)S(1)}, f32[32,32]{1,0:T(8,128)}, u32[]{:S(2)}) copy-start(f32[32,32]{1,0:T(8,128)} %refs_7_.4) | copy-start | bytes 12292
  7.9 10.6 %collective-permute-start.3 = (f32[16,1152]{1,0:T(8,128)S(1)}, f32[16,1152]{1,0:T(8,128)S(1)}, u32[]{:S(2)}, u32[]{:S(2)}) collective-permute-start(f32[16,1152]{1,0:T(8,128)S(1)} %get-tuple-element.52), channel_id=1, source_target_pairs={{2,0},{4,2},{6,4},{8,6},{10,8},{12,10},{14,12},{3,1},{5,3},{7,5},{... | collective-permute-start | bytes 221192 | tf_op jit(solution)/shard_map/ppermute | solution.py:418
  9.2 4.5 %collective-permute-start = (f32[5,2,32,128]{3,2,1,0:T(8,128)S(1)}, f32[5,2,32,128]{3,2,1,0:T(8,128)S(1)}, u32[]{:S(2)}, u32[]{:S(2)}) collective-permute-start(f32[5,2,32,128]{3,2,1,0:T(8,128)S(1)} %get-tuple-element.46), channel_id=1, source_target_pairs={{0,1},{1,0},{2,3},{3,2},{4,5},{5,4},{6,7},{7,6},{8,9},{9,8},{10,11... | collective-permute-start | bytes 491528 | tf_op jit(solution)/shard_map/ppermute | solution.py:420
  9.3 22.5 %collective-permute-start.1 = (f32[64,1152]{1,0:T(8,128)}, f32[64,1152]{1,0:T(8,128)S(1)}, u32[]{:S(2)}, u32[]{:S(2)}) collective-permute-start(f32[64,1152]{1,0:T(8,128)} %get-tuple-element.50), channel_id=1, source_target_pairs={{0,2},{2,0},{4,6},{6,4},{8,10},{10,8},{12,14},{14,12},{1,3},{3,1},... | collective-permute-start | bytes 884744 | tf_op jit(solution)/shard_map/ppermute | solution.py:417
  12.0 6.5 %collective-permute-start.5 = (f32[64,1152]{1,0:T(8,128)}, f32[64,1152]{1,0:T(8,128)}, u32[]{:S(2)}, u32[]{:S(2)}) collective-permute-start(f32[64,1152]{1,0:T(8,128)} %get-tuple-element.57), channel_id=1, source_target_pairs={{2,4},{4,2},{6,8},{8,6},{10,12},{12,10},{3,5},{5,3},{7,9},{9,7},{1... | collective-permute-start | bytes 884744 | tf_op jit(solution)/shard_map/ppermute | solution.py:416
  13.7 18.1 %collective-permute-start.2 = (f32[64,1152]{1,0:T(8,128)}, f32[64,1152]{1,0:T(8,128)S(1)}, u32[]{:S(2)}, u32[]{:S(2)}) collective-permute-start(f32[64,1152]{1,0:T(8,128)} %get-tuple-element.51), channel_id=1, source_target_pairs={{2,4},{4,2},{6,8},{8,6},{10,12},{12,10},{3,5},{5,3},{7,9},{9,7},{1... | collective-permute-start | bytes 884744 | tf_op jit(solution)/shard_map/ppermute | solution.py:416
  18.5 3.5 %copy-start.2 = (bf16[1024,256]{1,0:T(8,128)(2,1)S(1)}, bf16[1024,256]{1,0:T(8,128)(2,1)}, u32[]{:S(2)}) copy-start(bf16[1024,256]{1,0:T(8,128)(2,1)} %constant.58.clone.refs_3_.refs_2_) | copy-start | bytes 1572868
  18.5 3.5 %copy-start.3 = (bf16[1024,256]{1,0:T(8,128)(2,1)S(1)}, bf16[1024,256]{1,0:T(8,128)(2,1)}, u32[]{:S(2)}) copy-start(bf16[1024,256]{1,0:T(8,128)(2,1)} %constant.57.clone.refs_2_.refs_1_) | copy-start | bytes 1572868
  18.6 3.5 %copy-start.6 = (bf16[128,128]{1,0:T(8,128)(2,1)S(1)}, bf16[128,128]{1,0:T(8,128)(2,1)}, u32[]{:S(2)}) copy-start(bf16[128,128]{1,0:T(8,128)(2,1)} %constant.60.clone.refs_5_.refs_4_) | copy-start | bytes 98308
  18.6 3.5 %copy-start.7 = (bf16[128,128]{1,0:T(8,128)(2,1)S(1)}, bf16[128,128]{1,0:T(8,128)(2,1)}, u32[]{:S(2)}) copy-start(bf16[128,128]{1,0:T(8,128)(2,1)} %constant.59.clone.refs_4_.refs_3_) | copy-start | bytes 98308
  20.3 2.5 %copy-start = (bf16[1024,256]{1,0:T(8,128)(2,1)S(1)}, bf16[1024,256]{1,0:T(8,128)(2,1)}, u32[]{:S(2)}) copy-start(bf16[1024,256]{1,0:T(8,128)(2,1)} %constant.62.clone.refs_5_.refs_4_) | copy-start | bytes 1572868
  20.3 2.5 %copy-start.1 = (bf16[1024,256]{1,0:T(8,128)(2,1)S(1)}, bf16[1024,256]{1,0:T(8,128)(2,1)}, u32[]{:S(2)}) copy-start(bf16[1024,256]{1,0:T(8,128)(2,1)} %constant.61.clone.refs_4_.refs_3_) | copy-start | bytes 1572868
  20.3 2.5 %copy-start.4 = (bf16[128,128]{1,0:T(8,128)(2,1)S(1)}, bf16[128,128]{1,0:T(8,128)(2,1)}, u32[]{:S(2)}) copy-start(bf16[128,128]{1,0:T(8,128)(2,1)} %constant.64.clone.refs_7_.refs_6_) | copy-start | bytes 98308
  20.3 2.5 %copy-start.5 = (bf16[128,128]{1,0:T(8,128)(2,1)S(1)}, bf16[128,128]{1,0:T(8,128)(2,1)}, u32[]{:S(2)}) copy-start(bf16[128,128]{1,0:T(8,128)(2,1)} %constant.63.clone.refs_6_.refs_5_) | copy-start | bytes 98308
  20.3 2.5 %copy-start.9 = (s32[4]{0:T(128)S(1)}, s32[4]{0:T(128)}, u32[]{:S(2)}) copy-start(s32[4]{0:T(128)} %mask_ref.3) | copy-start | bytes 52
  20.3 1.5 %collective-permute-start.7 = (f32[2,32,640]{2,1,0:T(8,128)S(1)}, f32[2,32,640]{2,1,0:T(8,128)S(1)}, u32[]{:S(2)}, u32[]{:S(2)}) collective-permute-start(f32[2,32,640]{2,1,0:T(8,128)S(1)} %get-tuple-element.84), channel_id=1, source_target_pairs={{0,1},{1,0},{2,3},{3,2},{4,5},{5,4},{6,7},{7,6},{8,9},{9,8},{10,11... | collective-permute-start | bytes 491528 | tf_op jit(solution)/shard_map/ppermute | solution.py:507
  20.6 1.5 %collective-permute-start.6 = (f32[2,32,640]{2,1,0:T(8,128)S(1)}, f32[2,32,640]{2,1,0:T(8,128)S(1)}, u32[]{:S(2)}, u32[]{:S(2)}) collective-permute-start(f32[2,32,640]{2,1,0:T(8,128)S(1)} %get-tuple-element.85), channel_id=1, source_target_pairs={{0,1},{1,0},{2,3},{3,2},{4,5},{5,4},{6,7},{7,6},{8,9},{9,8},{10,11... | collective-permute-start | bytes 491528 | tf_op jit(solution)/shard_map/ppermute | solution.py:507
  32.5 2.5 %collective-permute-start.9 = (f32[4,32,640]{2,1,0:T(8,128)S(1)}, f32[4,32,640]{2,1,0:T(8,128)S(1)}, u32[]{:S(2)}, u32[]{:S(2)}) collective-permute-start(f32[4,32,640]{2,1,0:T(8,128)S(1)} %get-tuple-element.68), channel_id=1, source_target_pairs={{0,1},{1,0},{2,3},{3,2},{4,5},{5,4},{6,7},{7,6},{8,9},{9,8},{10,11... | collective-permute-start | bytes 983048 | tf_op jit(solution)/shard_map/ppermute | solution.py:521
  32.5 4.0 %collective-permute-start.8 = (f32[1,128]{1,0:T(1,128)S(1)}, f32[1,128]{1,0:T(1,128)S(1)}, u32[]{:S(2)}, u32[]{:S(2)}) collective-permute-start(f32[1,128]{1,0:T(1,128)S(1)} %get-tuple-element.66), channel_id=1, source_target_pairs={{0,2},{2,0},{4,6},{6,4},{8,10},{10,8},{12,14},{14,12},{1,3},{3,1},... | collective-permute-start | bytes 1544 | tf_op jit(solution)/shard_map/ppermute | solution.py:518
  36.5 4.0 %collective-permute-start.10 = (f32[1,128]{1,0:T(1,128)S(1)}, f32[1,128]{1,0:T(1,128)S(1)}, u32[]{:S(2)}, u32[]{:S(2)}) collective-permute-start(f32[1,128]{1,0:T(1,128)S(1)} %add.44), channel_id=1, source_target_pairs={{0,4},{2,6},{4,0},{6,2},{8,12},{10,14},{12,8},{14,10},{1,5},{3,7},... | collective-permute-start | bytes 1544 | tf_op jit(solution)/shard_map/ppermute | solution.py:518
  39.0 4.6 %collective-permute-start.12 = (f32[4,32,640]{2,1,0:T(8,128)}, f32[4,32,640]{2,1,0:T(8,128)S(1)}, u32[]{:S(2)}, u32[]{:S(2)}) collective-permute-start(f32[4,32,640]{2,1,0:T(8,128)} %get-tuple-element.64), channel_id=1, source_target_pairs={{0,1},{1,0},{2,3},{3,2},{4,5},{5,4},{6,7},{7,6},{8,9},{9,8},{10,11... | collective-permute-start | bytes 983048 | tf_op jit(solution)/shard_map/ppermute | solution.py:511
  40.5 3.0 %collective-permute-start.13 = (f32[4,32,640]{2,1,0:T(8,128)S(1)}, f32[4,32,640]{2,1,0:T(8,128)S(1)}, u32[]{:S(2)}, u32[]{:S(2)}) collective-permute-start(f32[4,32,640]{2,1,0:T(8,128)S(1)} %get-tuple-element.81), channel_id=1, source_target_pairs={{0,1},{1,0},{2,3},{3,2},{4,5},{5,4},{6,7},{7,6},{8,9},{9,8},{10,11... | collective-permute-start | bytes 983048 | tf_op jit(solution)/shard_map/ppermute | solution.py:535
  40.8 4.4 %collective-permute-start.11 = (f32[1,128]{1,0:T(1,128)S(1)}, f32[1,128]{1,0:T(1,128)S(1)}, u32[]{:S(2)}, u32[]{:S(2)}) collective-permute-start(f32[1,128]{1,0:T(1,128)S(1)} %add.45), channel_id=1, source_target_pairs={{0,8},{2,10},{4,12},{6,14},{8,0},{10,2},{12,4},{14,6},{1,9},{3,11}... | collective-permute-start | bytes 1544 | tf_op jit(solution)/shard_map/ppermute | solution.py:518

commit v17 on v16

--- a/solution.py
+++ b/solution.py
@@ -186,6 +186,8 @@
     top = jnp.concatenate([top[:, :width], second_half(top, sector)], axis=0)
     mix_high, mix_low = split_high_low(mixing_ref[...])
     mix = jnp.concatenate([mix_high, mix_high, mix_low, mix_low], axis=1)
+    nothing = jnp.zeros_like(mix)
+    mix = jnp.concatenate([jnp.concatenate([mix, nothing], axis=1), jnp.concatenate([nothing, mix], axis=1)], axis=0)
     level = lax.broadcasted_iota(jnp.int32, (8, width), 0)
     lane = lax.broadcasted_iota(jnp.int32, (8, width), 1)
     energies = [energy_in_ref[r] for r in range(rows)]
@@ -203,10 +205,12 @@
         north = top * (NEAR * high_a - FAR * high_b + north_ref[t])
         extra = [south + south_in, -south_in, north_in, -north_in - north]
         for r in range(rows):
-            advected = base_ref[t, r] + extra[r]
-            part_high, part_low = split_high_low(advected)
-            stacked = jnp.concatenate([part_high, part_low, part_high, part_low], axis=0)
-            mixed = jnp.dot(mix, stacked, preferred_element_type=jnp.float32)
+            if r % 2 == 0:
+                pair = [base_ref[t, r + i] + extra[r + i] for i in range(2)]
+                parts = [split_high_low(row) for row in pair]
+                stacked = jnp.concatenate([part for high_low in parts for part in high_low * 2], axis=0)
+                both = jnp.dot(mix, stacked, preferred_element_type=jnp.float32)
+            advected, mixed = pair[r % 2], both[levels * (r % 2) : levels * (r % 2 + 1)]
             surface = jnp.where(level == 7, surface_ref[t, r : r + 1, :], 0.0)
             mixed = jnp.concatenate([mixed[: levels - 8], mixed[levels - 8 :] + surface], axis=0)
             physics = mixed / (1.0 + decay_ref[t] * mixed * mixed)

time: 46.2 us -> 46.2 us (level)
  no operation moved by 1% of the time
where the time goes in v17:
time: 46.2 us; the launch traced here: 45.9 us
  starting transfers between devices  17.7 us (38%)
  Pallas kernels  16.3 us (35%)
  waiting for transfers between devices  9.73 us (21%)
  between operations  1 us (2%)
  other arithmetic  0.72 us (2%)
    ppermute x3, starting transfers between devices, send_energy(): lax.ppermute(energy, 'lat', [(i, i ^ distance) for i in range(lat_count)])  7.66 us
    ppermute x1, waiting for transfers between devices, on_device(): from_inside += [lax.ppermute(part, 'lat', inside) for part in inner]  6.99 us
    pallas_call x1, Pallas kernels, on_device(): pl.pallas_call(functools.partial(base_kernel, width), in_specs=[in_hbm, i...  3.97 us
    pallas_call x2, Pallas kernels, run_inverse(): pl.pallas_call(functools.partial(inverse_kernel, radix, len(other)), in_s...  3.23 us
    ppermute x1, starting transfers between devices, on_device(): from_inside = [lax.ppermute(inner, 'lat', inside)]  3 us
    pallas_call x1, Pallas kernels, on_device(): pl.pallas_call(rest_kernel, in_specs=[in_hbm] * 3, out_specs=[whole] * (2...  3 us
    ppermute x1, starting transfers between devices, on_device(): from_inside += [lax.ppermute(part, 'lat', inside) for part in inner]  2.71 us
    pallas_call x2, Pallas kernels, run_physics(): pl.pallas_call(functools.partial(physics_kernel, levels, sector, lat_coun...  2.4 us
  transfers between devices with their start and end apart: 14, of which 6 were waited for; matrix products, arithmetic and copies ran while one was open for 1% of the time, Pallas kernels for 31%

profile of v17, /device:TPU:0, one launch (start us, length us, event | category | flops | bytes accessed | tf_op | source)
XLA Modules:
  0.0 45.9 jit_solution(5631854972364142187)
XLA Ops:
  0.6 1.1 %pack.1 = f32[64,1152]{1,0:T(8,128)S(1)} custom-call(f32[4,32,4,576]{3,2,1,0:T(4,128)} %tracer_hbm.3), custom_call_target="tpu_custom_call" | custom-call | bytes 600000 | tf_op jit(solution)/shard_map/pack/pallas_call | solution.py:392
  1.8 0.0 copy-start.11
  1.8 0.0 copy-start.12
  1.8 0.0 copy-start.14
  1.8 0.0 copy-start.15
  1.8 0.0 copy-start.10
  1.8 3.0 %collective-permute-start.4 = (f32[64,1152]{1,0:T(8,128)S(1)}, f32[64,1152]{1,0:T(8,128)}, u32[]{:S(2)}, u32[]{:S(2)}) collective-permute-start(f32[64,1152]{1,0:T(8,128)S(1)} %pack.1), channel_id=1, source_target_pairs={{0,2},{2,0},{4,6},{6,4},{8,10},{10,8},{12,14},{14,12},{1,3},{3,1},... | collective-permute-start | bytes 884744 | tf_op jit(solution)/shard_map/ppermute | solution.py:402
  4.8 3.0 %rest.1 = (f32[64,1152]{1,0:T(8,128)}, f32[64,1152]{1,0:T(8,128)}, f32[64,1152]{1,0:T(8,128)}, f32[16,1152]{1,0:T(8,128)S(1)}, f32[5,2,32,128]{3,2,1,0:T(8,128)S(1)}) custom-call(f32[4,32,4,576]{3,2,1,0:T(4,128)} %tracer_hbm.3, f32[32,4,576]{2,1,0:T(4,128)} %lat_hbm.1, f32[32,4,576]{2,1,0:T(4,128)} %lon_hbm.1), custom_call_target="tpu_custom_call" | custom-call | tf_op jit(solution)/shard_map/rest/pallas_call | solution.py:405
  7.8 0.0 copy-start.13
  7.9 0.0 copy-start.8
  7.9 1.3 %collective-permute-start.3 = (f32[16,1152]{1,0:T(8,128)S(1)}, f32[16,1152]{1,0:T(8,128)S(1)}, u32[]{:S(2)}, u32[]{:S(2)}) collective-permute-start(f32[16,1152]{1,0:T(8,128)S(1)} %get-tuple-element.52), channel_id=1, source_target_pairs={{2,0},{4,2},{6,4},{8,6},{10,8},{12,10},{14,12},{3,1},{5,3},{7,5},{... | collective-permute-start | bytes 221192 | tf_op jit(solution)/shard_map/ppermute | solution.py:422
  9.2 0.1 collective-permute-start
  9.3 2.7 %collective-permute-start.1 = (f32[64,1152]{1,0:T(8,128)}, f32[64,1152]{1,0:T(8,128)S(1)}, u32[]{:S(2)}, u32[]{:S(2)}) collective-permute-start(f32[64,1152]{1,0:T(8,128)} %get-tuple-element.50), channel_id=1, source_target_pairs={{0,2},{2,0},{4,6},{6,4},{8,10},{10,8},{12,14},{14,12},{1,3},{3,1},... | collective-permute-start | bytes 884744 | tf_op jit(solution)/shard_map/ppermute | solution.py:421
  12.0 1.4 %collective-permute-start.5 = (f32[64,1152]{1,0:T(8,128)}, f32[64,1152]{1,0:T(8,128)}, u32[]{:S(2)}, u32[]{:S(2)}) collective-permute-start(f32[64,1152]{1,0:T(8,128)} %get-tuple-element.57), channel_id=1, source_target_pairs={{2,4},{4,2},{6,8},{8,6},{10,12},{12,10},{3,5},{5,3},{7,9},{9,7},{1... | collective-permute-start | bytes 884744 | tf_op jit(solution)/shard_map/ppermute | solution.py:420
  13.4 0.1 select_multiply_fusion.refs_6_.refs_5_
  13.5 0.1 broadcast_in_dim.27
  13.6 0.1 reshape_reshape.3
  13.7 0.0 copy-done.10
  13.7 0.0 collective-permute-done.side_ref
  13.7 0.7 %collective-permute-start.2 = (f32[64,1152]{1,0:T(8,128)}, f32[64,1152]{1,0:T(8,128)S(1)}, u32[]{:S(2)}, u32[]{:S(2)}) collective-permute-start(f32[64,1152]{1,0:T(8,128)} %get-tuple-element.51), channel_id=1, source_target_pairs={{2,4},{4,2},{6,8},{8,6},{10,12},{12,10},{3,5},{5,3},{7,9},{9,7},{1... | collective-permute-start | bytes 884744 | tf_op jit(solution)/shard_map/ppermute | solution.py:420
  14.4 4.0 %base.1 = (f32[4,4,32,640]{3,2,1,0:T(8,128)S(1)}, f32[4,32,640]{2,1,0:T(8,128)S(1)}, f32[4,32,640]{2,1,0:T(8,128)S(1)}) custom-call(f32[4,32,4,576]{3,2,1,0:T(4,128)} %tracer_hbm.3, f32[32,4,576]{2,1,0:T(4,128)} %lat_hbm.1, f32[32,4,576]{2,1,0:T(4,128)} %lon_hbm.1, f32[5,2,32,128]{3,2,1,0:T(8,128)S(1)} %collective-permute-done.side_ref), custom_call_target="tpu_custom_call" | custom-call | tf_op jit(solution)/shard_map/base/pallas_call | solution.py:425
  18.4 0.1 copy.22.refs_8_
  18.5 0.0 collective-permute-done.3.refs_4_
  18.5 0.0 collective-permute-done.4.refs_2_
  18.5 0.0 collective-permute-done.5.refs_3_
  18.5 0.0 copy-start.2
  18.5 0.0 copy-start.3
  18.6 0.0 copy-start.6
  18.6 0.0 copy-start.7
  18.6 1.7 %physics.2 = (f32[4,32,640]{2,1,0:T(8,128)S(1)}, f32[4,32,640]{2,1,0:T(8,128)S(1)}, f32[4,8,640]{2,1,0:T(8,128)S(1)}) custom-call(f32[4,4,32,640]{3,2,1,0:T(8,128)S(1)} %get-tuple-element.48.refs_0_, f32[4,32,640]{2,1,0:T(8,128)S(1)} %get-tuple-element.49.refs_1_, f32[64,1152]{1,0:T(8,128)} %collective-permute-done.4.refs_2_, ...), custom_call_target="tpu_custom_call" | custom-call | tf_op jit(solution)/shard_map/physics/pallas_call | solution.py:467
  20.3 0.0 copy-start
  20.3 0.0 copy-start.1
  20.3 0.0 copy-start.4
  20.3 0.0 copy-start.5
  20.3 0.0 copy-start.9
  20.4 0.2 collective-permute-start.7
  20.6 0.3 collective-permute-start.6
  20.9 0.9 %collective-permute-done.7.refs_1_ = f32[2,32,640]{2,1,0:T(8,128)S(1)} collective-permute-done((f32[2,32,640]{2,1,0:T(8,128)S(1)}, f32[2,32,640]{2,1,0:T(8,128)S(1)}, u32[]{:S(2)}, u32[]{:S(2)}) %collective-permute-start.7) | collective-permute-done | bytes 163872 | tf_op jit(solution)/shard_map/ppermute | solution.py:511
  21.8 0.2 collective-permute-done.6.refs_0_
  22.1 0.0 copy-done.2
  22.1 0.7 %forward.2 = (bf16[128,1152]{1,0:T(8,128)(2,1)S(1)}, bf16[128,1152]{1,0:T(8,128)(2,1)S(1)}) custom-call(f32[4,32,640]{2,1,0:T(8,128)S(1)} %get-tuple-element.59.own_ref, f32[2,32,640]{2,1,0:T(8,128)S(1)} %collective-permute-done.6.refs_0_, f32[2,32,640]{2,1,0:T(8,128)S(1)} %collective-permute-done.7.refs_1_, bf16[1024,256]{1,0:T(8,128)(2,1)S(1)} %copy-done.3, ...), custom_call_target="tpu_custom_call" | custom-call | tf_op jit(solution)/shard_map/forward/pallas_call | solution.py:484
  22.8 0.0 copy-done
  22.8 0.0 copy-done.1
  22.8 0.0 copy-done.4
  22.8 2.0 %inverse.2 = (f32[32,4,576]{2,1,0:T(4,128)S(1)}, f32[4,32,640]{2,1,0:T(8,128)}) custom-call(s32[4]{0:T(128)S(1)} %copy-done.9, f32[4,32,640]{2,1,0:T(8,128)S(1)} %get-tuple-element.59.own_ref, f32[2,32,640]{2,1,0:T(8,128)S(1)} %collective-permute-done.6.refs_0_, f32[2,32,640]{2,1,0:T(8,128)S(1)} %collective-permute-done.7.refs_1_, ...), custom_call_target="tpu_custom_call" | custom-call | tf_op jit(solution)/shard_map/inverse/pallas_call | solution.py:496
  24.8 7.0 %collective-permute-done.1.refs_2_ = f32[64,1152]{1,0:T(8,128)S(1)} collective-permute-done((f32[64,1152]{1,0:T(8,128)}, f32[64,1152]{1,0:T(8,128)S(1)}, u32[]{:S(2)}, u32[]{:S(2)}) %collective-permute-start.1) | collective-permute-done | bytes 294944 | tf_op jit(solution)/shard_map/ppermute | solution.py:421
  31.8 0.0 collective-permute-done.2.refs_3_
  31.8 0.7 %physics.3 = (f32[4,32,640]{2,1,0:T(8,128)S(1)}, f32[4,32,640]{2,1,0:T(8,128)S(1)}, f32[1,128]{1,0:T(1,128)S(1)}) custom-call(f32[4,4,32,640]{3,2,1,0:T(8,128)S(1)} %get-tuple-element.48.refs_0_, f32[4,32,640]{2,1,0:T(8,128)S(1)} %get-tuple-element.49.refs_1_, f32[64,1152]{1,0:T(8,128)S(1)} %collective-permute-done.1.refs_2_, ...), custom_call_target="tpu_custom_call" | custom-call | tf_op jit(solution)/shard_map/physics/pallas_call | solution.py:467
  32.5 0.0 collective-permute-start.9
  32.6 2.4 %collective-permute-start.8 = (f32[1,128]{1,0:T(1,128)S(1)}, f32[1,128]{1,0:T(1,128)S(1)}, u32[]{:S(2)}, u32[]{:S(2)}) collective-permute-start(f32[1,128]{1,0:T(1,128)S(1)} %get-tuple-element.66), channel_id=1, source_target_pairs={{0,2},{2,0},{4,6},{6,4},{8,10},{10,8},{12,14},{14,12},{1,3},{3,1},... | collective-permute-start | bytes 1544 | tf_op jit(solution)/shard_map/ppermute | solution.py:522
  35.0 0.0 collective-permute-done.9.refs_0_
  35.0 0.7 %forward.3 = (bf16[128,1152]{1,0:T(8,128)(2,1)S(1)}, bf16[128,1152]{1,0:T(8,128)(2,1)S(1)}) custom-call(f32[4,32,640]{2,1,0:T(8,128)S(1)} %get-tuple-element.67.own_ref, f32[4,32,640]{2,1,0:T(8,128)S(1)} %collective-permute-done.9.refs_0_, bf16[1024,256]{1,0:T(8,128)(2,1)S(1)} %copy-done.3, bf16[1024,256]{1,0:T(8,128)(2,1)S(1)} %copy-done.2, ...), custom_call_target="tpu_custom_call" | custom-call | tf_op jit(solution)/shard_map/forward/pallas_call | solution.py:484
  35.7 0.8 %collective-permute-done.8 = f32[1,128]{1,0:T(1,128)S(1)} collective-permute-done((f32[1,128]{1,0:T(1,128)S(1)}, f32[1,128]{1,0:T(1,128)S(1)}, u32[]{:S(2)}, u32[]{:S(2)}) %collective-permute-start.8) | collective-permute-done | bytes 544 | tf_op jit(solution)/shard_map/ppermute | solution.py:522
  36.5 2.5 %collective-permute-start.10 = (f32[1,128]{1,0:T(1,128)S(1)}, f32[1,128]{1,0:T(1,128)S(1)}, u32[]{:S(2)}, u32[]{:S(2)}) collective-permute-start(f32[1,128]{1,0:T(1,128)S(1)} %add.44), channel_id=1, source_target_pairs={{0,4},{2,6},{4,0},{6,2},{8,12},{10,14},{12,8},{14,10},{1,5},{3,7},... | collective-permute-start | bytes 1544 | tf_op jit(solution)/shard_map/ppermute | solution.py:522
  39.0 0.0 collective-permute-start.12
  39.0 1.3 %inverse.3 = (f32[32,4,576]{2,1,0:T(4,128)S(1)}, f32[4,32,640]{2,1,0:T(8,128)S(1)}) custom-call(s32[4]{0:T(128)S(1)} %copy-done.9, f32[4,32,640]{2,1,0:T(8,128)S(1)} %get-tuple-element.67.own_ref, f32[4,32,640]{2,1,0:T(8,128)S(1)} %collective-permute-done.9.refs_0_, bf16[128,1152]{1,0:T(8,128)(2,1)S(1)} %get-tuple-element.73.refs_1_, ...), custom_call_target="tpu_custom_call" | custom-call | tf_op jit(solution)/shard_map/inverse/pallas_call | solution.py:496
  40.3 0.3 collective-permute-done.10
  40.6 0.3 collective-permute-start.13
  40.9 2.7 %collective-permute-start.11 = (f32[1,128]{1,0:T(1,128)S(1)}, f32[1,128]{1,0:T(1,128)S(1)}, u32[]{:S(2)}, u32[]{:S(2)}) collective-permute-start(f32[1,128]{1,0:T(1,128)S(1)} %add.45), channel_id=1, source_target_pairs={{0,8},{2,10},{4,12},{6,14},{8,0},{10,2},{12,4},{14,6},{1,9},{3,11}... | collective-permute-start | bytes 1544 | tf_op jit(solution)/shard_map/ppermute | solution.py:522
  43.6 0.0 collective-permute-done.12.refs_2_
  43.6 0.0 collective-permute-done.13.refs_3_
  43.6 1.2 %finish.1 = f32[4,32,4,576]{3,2,1,0:T(4,128)} custom-call(f32[32,4,576]{2,1,0:T(4,128)S(1)} %get-tuple-element.79.refs_0_, f32[32,4,576]{2,1,0:T(4,128)S(1)} %get-tuple-element.80.refs_1_, f32[4,32,640]{2,1,0:T(8,128)S(1)} %collective-permute-done.12.refs_2_, f32[4,32,640]{2,1,0:T(8,128)S(1)} %collective-permute-done.13.refs_3_), custom_call_target="tpu_custom_call" | custom-call | bytes 3000000 | tf_op jit(solution)/shard_map/finish/pallas_call | solution.py:542
  44.8 0.5 %collective-permute-done.11 = f32[1,128]{1,0:T(1,128)S(1)} collective-permute-done((f32[1,128]{1,0:T(1,128)S(1)}, f32[1,128]{1,0:T(1,128)S(1)}, u32[]{:S(2)}, u32[]{:S(2)}) %collective-permute-start.11) | collective-permute-done | bytes 544 | tf_op jit(solution)/shard_map/ppermute | solution.py:522
  45.3 0.6 %fusion.1 = f32[1,1]{1,0:T(1,128)} fusion(f32[1,128]{1,0:T(1,128)S(1)} %add.46, s32[]{:T(128)S(6)} %select_n.8), kind=kLoop, calls=%fused_computation.4 | loop fusion | flops 1 | bytes 12 | tf_op jit(solution)/shard_map/div | solution.py:560
  (19 shorter events, 0.1 us)
Async XLA Ops:
  1.8 11.6 %copy-start.11 = (f32[1152]{0:T(1024)S(1)}, f32[1152]{0:T(1024)}, u32[]{:S(2)}) copy-start(f32[1152]{0:T(1024)} %constant.56.clone) | copy-start | bytes 13828
  1.8 11.6 %copy-start.12 = (f32[1152]{0:T(1024)S(1)}, f32[1152]{0:T(1024)}, u32[]{:S(2)}) copy-start(f32[1152]{0:T(1024)} %constant.54.clone) | copy-start | bytes 13828
  1.8 11.6 %copy-start.14 = (pred[1152]{0:T(1024)(128)(4,1)S(1)}, pred[1152]{0:T(1024)(128)(4,1)}, u32[]{:S(2)}) copy-start(pred[1152]{0:T(1024)(128)(4,1)} %constant.55.clone) | copy-start | bytes 3460
  1.8 11.7 %copy-start.15 = (s32[1,1,18,1]{2,3,1,0:T(1,128)S(1)}, s32[1,1,18,1]{2,3,1,0:T(1,128)}, u32[]{:S(2)}) copy-start(s32[1,1,18,1]{2,3,1,0:T(1,128)} %param.25) | copy-start | bytes 220
  1.8 11.8 %copy-start.10 = (f32[4,4,576]{2,1,0:T(4,128)S(1)}, f32[4,4,576]{2,1,0:T(4,128)}, u32[]{:S(2)}) copy-start(f32[4,4,576]{2,1,0:T(4,128)} %param.22) | copy-start | bytes 110596
  1.8 16.6 %collective-permute-start.4 = (f32[64,1152]{1,0:T(8,128)S(1)}, f32[64,1152]{1,0:T(8,128)}, u32[]{:S(2)}, u32[]{:S(2)}) collective-permute-start(f32[64,1152]{1,0:T(8,128)S(1)} %pack.1), channel_id=1, source_target_pairs={{0,2},{2,0},{4,6},{6,4},{8,10},{10,8},{12,14},{14,12},{1,3},{3,1},... | collective-permute-start | bytes 884744 | tf_op jit(solution)/shard_map/ppermute | solution.py:402
  7.8 10.5 %copy-start.13 = (f32[4,32]{1,0:T(4,128)S(1)}, f32[4,32]{1,0:T(4,128)}, u32[]{:S(2)}) copy-start(f32[4,32]{1,0:T(4,128)} %param.24) | copy-start | bytes 1540
  7.9 10.7 %copy-start.8 = (f32[32,32]{1,0:T(8,128)S(1)}, f32[32,32]{1,0:T(8,128)}, u32[]{:S(2)}) copy-start(f32[32,32]{1,0:T(8,128)} %refs_7_.4) | copy-start | bytes 12292
  7.9 10.6 %collective-permute-start.3 = (f32[16,1152]{1,0:T(8,128)S(1)}, f32[16,1152]{1,0:T(8,128)S(1)}, u32[]{:S(2)}, u32[]{:S(2)}) collective-permute-start(f32[16,1152]{1,0:T(8,128)S(1)} %get-tuple-element.52), channel_id=1, source_target_pairs={{2,0},{4,2},{6,4},{8,6},{10,8},{12,10},{14,12},{3,1},{5,3},{7,5},{... | collective-permute-start | bytes 221192 | tf_op jit(solution)/shard_map/ppermute | solution.py:422
  9.2 4.5 %collective-permute-start = (f32[5,2,32,128]{3,2,1,0:T(8,128)S(1)}, f32[5,2,32,128]{3,2,1,0:T(8,128)S(1)}, u32[]{:S(2)}, u32[]{:S(2)}) collective-permute-start(f32[5,2,32,128]{3,2,1,0:T(8,128)S(1)} %get-tuple-element.46), channel_id=1, source_target_pairs={{0,1},{1,0},{2,3},{3,2},{4,5},{5,4},{6,7},{7,6},{8,9},{9,8},{10,11... | collective-permute-start | bytes 491528 | tf_op jit(solution)/shard_map/ppermute | solution.py:424
  9.3 22.5 %collective-permute-start.1 = (f32[64,1152]{1,0:T(8,128)}, f32[64,1152]{1,0:T(8,128)S(1)}, u32[]{:S(2)}, u32[]{:S(2)}) collective-permute-start(f32[64,1152]{1,0:T(8,128)} %get-tuple-element.50), channel_id=1, source_target_pairs={{0,2},{2,0},{4,6},{6,4},{8,10},{10,8},{12,14},{14,12},{1,3},{3,1},... | collective-permute-start | bytes 884744 | tf_op jit(solution)/shard_map/ppermute | solution.py:421
  12.0 6.5 %collective-permute-start.5 = (f32[64,1152]{1,0:T(8,128)}, f32[64,1152]{1,0:T(8,128)}, u32[]{:S(2)}, u32[]{:S(2)}) collective-permute-start(f32[64,1152]{1,0:T(8,128)} %get-tuple-element.57), channel_id=1, source_target_pairs={{2,4},{4,2},{6,8},{8,6},{10,12},{12,10},{3,5},{5,3},{7,9},{9,7},{1... | collective-permute-start | bytes 884744 | tf_op jit(solution)/shard_map/ppermute | solution.py:420
  13.7 18.1 %collective-permute-start.2 = (f32[64,1152]{1,0:T(8,128)}, f32[64,1152]{1,0:T(8,128)S(1)}, u32[]{:S(2)}, u32[]{:S(2)}) collective-permute-start(f32[64,1152]{1,0:T(8,128)} %get-tuple-element.51), channel_id=1, source_target_pairs={{2,4},{4,2},{6,8},{8,6},{10,12},{12,10},{3,5},{5,3},{7,9},{9,7},{1... | collective-permute-start | bytes 884744 | tf_op jit(solution)/shard_map/ppermute | solution.py:420
  18.5 3.5 %copy-start.2 = (bf16[1024,256]{1,0:T(8,128)(2,1)S(1)}, bf16[1024,256]{1,0:T(8,128)(2,1)}, u32[]{:S(2)}) copy-start(bf16[1024,256]{1,0:T(8,128)(2,1)} %constant.58.clone.refs_3_.refs_2_) | copy-start | bytes 1572868
  18.5 3.5 %copy-start.3 = (bf16[1024,256]{1,0:T(8,128)(2,1)S(1)}, bf16[1024,256]{1,0:T(8,128)(2,1)}, u32[]{:S(2)}) copy-start(bf16[1024,256]{1,0:T(8,128)(2,1)} %constant.57.clone.refs_2_.refs_1_) | copy-start | bytes 1572868
  18.6 3.5 %copy-start.6 = (bf16[128,128]{1,0:T(8,128)(2,1)S(1)}, bf16[128,128]{1,0:T(8,128)(2,1)}, u32[]{:S(2)}) copy-start(bf16[128,128]{1,0:T(8,128)(2,1)} %constant.60.clone.refs_5_.refs_4_) | copy-start | bytes 98308
  18.6 3.5 %copy-start.7 = (bf16[128,128]{1,0:T(8,128)(2,1)S(1)}, bf16[128,128]{1,0:T(8,128)(2,1)}, u32[]{:S(2)}) copy-start(bf16[128,128]{1,0:T(8,128)(2,1)} %constant.59.clone.refs_4_.refs_3_) | copy-start | bytes 98308
  20.3 2.5 %copy-start = (bf16[1024,256]{1,0:T(8,128)(2,1)S(1)}, bf16[1024,256]{1,0:T(8,128)(2,1)}, u32[]{:S(2)}) copy-start(bf16[1024,256]{1,0:T(8,128)(2,1)} %constant.62.clone.refs_5_.refs_4_) | copy-start | bytes 1572868
  20.3 2.5 %copy-start.1 = (bf16[1024,256]{1,0:T(8,128)(2,1)S(1)}, bf16[1024,256]{1,0:T(8,128)(2,1)}, u32[]{:S(2)}) copy-start(bf16[1024,256]{1,0:T(8,128)(2,1)} %constant.61.clone.refs_4_.refs_3_) | copy-start | bytes 1572868
  20.3 2.5 %copy-start.4 = (bf16[128,128]{1,0:T(8,128)(2,1)S(1)}, bf16[128,128]{1,0:T(8,128)(2,1)}, u32[]{:S(2)}) copy-start(bf16[128,128]{1,0:T(8,128)(2,1)} %constant.64.clone.refs_7_.refs_6_) | copy-start | bytes 98308
  20.3 2.5 %copy-start.5 = (bf16[128,128]{1,0:T(8,128)(2,1)S(1)}, bf16[128,128]{1,0:T(8,128)(2,1)}, u32[]{:S(2)}) copy-start(bf16[128,128]{1,0:T(8,128)(2,1)} %constant.63.clone.refs_6_.refs_5_) | copy-start | bytes 98308
  20.3 2.5 %copy-start.9 = (s32[4]{0:T(128)S(1)}, s32[4]{0:T(128)}, u32[]{:S(2)}) copy-start(s32[4]{0:T(128)} %mask_ref.3) | copy-start | bytes 52
  20.4 1.5 %collective-permute-start.7 = (f32[2,32,640]{2,1,0:T(8,128)S(1)}, f32[2,32,640]{2,1,0:T(8,128)S(1)}, u32[]{:S(2)}, u32[]{:S(2)}) collective-permute-start(f32[2,32,640]{2,1,0:T(8,128)S(1)} %get-tuple-element.84), channel_id=1, source_target_pairs={{0,1},{1,0},{2,3},{3,2},{4,5},{5,4},{6,7},{7,6},{8,9},{9,8},{10,11... | collective-permute-start | bytes 491528 | tf_op jit(solution)/shard_map/ppermute | solution.py:511
  20.6 1.5 %collective-permute-start.6 = (f32[2,32,640]{2,1,0:T(8,128)S(1)}, f32[2,32,640]{2,1,0:T(8,128)S(1)}, u32[]{:S(2)}, u32[]{:S(2)}) collective-permute-start(f32[2,32,640]{2,1,0:T(8,128)S(1)} %get-tuple-element.85), channel_id=1, source_target_pairs={{0,1},{1,0},{2,3},{3,2},{4,5},{5,4},{6,7},{7,6},{8,9},{9,8},{10,11... | collective-permute-start | bytes 491528 | tf_op jit(solution)/shard_map/ppermute | solution.py:511
  32.5 2.5 %collective-permute-start.9 = (f32[4,32,640]{2,1,0:T(8,128)S(1)}, f32[4,32,640]{2,1,0:T(8,128)S(1)}, u32[]{:S(2)}, u32[]{:S(2)}) collective-permute-start(f32[4,32,640]{2,1,0:T(8,128)S(1)} %get-tuple-element.68), channel_id=1, source_target_pairs={{0,1},{1,0},{2,3},{3,2},{4,5},{5,4},{6,7},{7,6},{8,9},{9,8},{10,11... | collective-permute-start | bytes 983048 | tf_op jit(solution)/shard_map/ppermute | solution.py:525
  32.6 4.0 %collective-permute-start.8 = (f32[1,128]{1,0:T(1,128)S(1)}, f32[1,128]{1,0:T(1,128)S(1)}, u32[]{:S(2)}, u32[]{:S(2)}) collective-permute-start(f32[1,128]{1,0:T(1,128)S(1)} %get-tuple-element.66), channel_id=1, source_target_pairs={{0,2},{2,0},{4,6},{6,4},{8,10},{10,8},{12,14},{14,12},{1,3},{3,1},... | collective-permute-start | bytes 1544 | tf_op jit(solution)/shard_map/ppermute | solution.py:522
  36.5 4.0 %collective-permute-start.10 = (f32[1,128]{1,0:T(1,128)S(1)}, f32[1,128]{1,0:T(1,128)S(1)}, u32[]{:S(2)}, u32[]{:S(2)}) collective-permute-start(f32[1,128]{1,0:T(1,128)S(1)} %add.44), channel_id=1, source_target_pairs={{0,4},{2,6},{4,0},{6,2},{8,12},{10,14},{12,8},{14,10},{1,5},{3,7},... | collective-permute-start | bytes 1544 | tf_op jit(solution)/shard_map/ppermute | solution.py:522
  39.0 4.6 %collective-permute-start.12 = (f32[4,32,640]{2,1,0:T(8,128)}, f32[4,32,640]{2,1,0:T(8,128)S(1)}, u32[]{:S(2)}, u32[]{:S(2)}) collective-permute-start(f32[4,32,640]{2,1,0:T(8,128)} %get-tuple-element.64), channel_id=1, source_target_pairs={{0,1},{1,0},{2,3},{3,2},{4,5},{5,4},{6,7},{7,6},{8,9},{9,8},{10,11... | collective-permute-start | bytes 983048 | tf_op jit(solution)/shard_map/ppermute | solution.py:515
  40.6 3.0 %collective-permute-start.13 = (f32[4,32,640]{2,1,0:T(8,128)S(1)}, f32[4,32,640]{2,1,0:T(8,128)S(1)}, u32[]{:S(2)}, u32[]{:S(2)}) collective-permute-start(f32[4,32,640]{2,1,0:T(8,128)S(1)} %get-tuple-element.81), channel_id=1, source_target_pairs={{0,1},{1,0},{2,3},{3,2},{4,5},{5,4},{6,7},{7,6},{8,9},{9,8},{10,11... | collective-permute-start | bytes 983048 | tf_op jit(solution)/shard_map/ppermute | solution.py:539
  40.9 4.4 %collective-permute-start.11 = (f32[1,128]{1,0:T(1,128)S(1)}, f32[1,128]{1,0:T(1,128)S(1)}, u32[]{:S(2)}, u32[]{:S(2)}) collective-permute-start(f32[1,128]{1,0:T(1,128)S(1)} %add.45), channel_id=1, source_target_pairs={{0,8},{2,10},{4,12},{6,14},{8,0},{10,2},{12,4},{14,6},{1,9},{3,11}... | collective-permute-start | bytes 1544 | tf_op jit(solution)/shard_map/ppermute | solution.py:522

commit v18 on v16

--- a/solution.py
+++ b/solution.py
@@ -220,17 +220,18 @@
             energy_ref[r] = energies[r]
         return
     energies = [jnp.where(lane < sector, energy, 0.0) for energy in energies]
-    spot = lax.broadcasted_iota(jnp.int32, (1, LANES), 1)
-    result = jnp.zeros((1, LANES), jnp.float32)
+    sums = []
     for owner in range(owner_count):
         chosen = jnp.zeros((8, LANES), jnp.float32)
         for r in range(rows):
             picked = jnp.where(owner_ref[r : r + 1, :] == owner, energies[r], 0.0)
             for k in range(width // LANES):
                 chosen = chosen + picked[:, LANES * k : LANES * (k + 1)]
-        total = jnp.sum(jnp.sum(chosen, axis=0, keepdims=True), axis=1, keepdims=True)
-        result = jnp.where(spot == owner, total, result)
-    energy_ref[...] = result
+        sums.append(jnp.sum(chosen, axis=0, keepdims=True))
+    totals = jnp.sum(jnp.concatenate(sums, axis=0), axis=1, keepdims=True)
+    shape = (owner_count, LANES)
+    diagonal = lax.broadcasted_iota(jnp.int32, shape, 0) == lax.broadcasted_iota(jnp.int32, shape, 1)
+    energy_ref[...] = jnp.sum(jnp.where(diagonal, totals, 0.0), axis=0, keepdims=True)
 
 
 def waves_of(radix):

time: 46.2 us -> 46.1 us (level)
  no operation moved by 1% of the time
where the time goes in v18:
time: 46.1 us; the launch traced here: 45.9 us
  starting transfers between devices  17.7 us (38%)
  Pallas kernels  16.3 us (35%)
  waiting for transfers between devices  9.75 us (21%)
  between operations  1 us (2%)
  other arithmetic  0.72 us (2%)
    ppermute x3, starting transfers between devices, send_energy(): lax.ppermute(energy, 'lat', [(i, i ^ distance) for i in range(lat_count)])  7.66 us
    ppermute x1, waiting for transfers between devices, on_device(): from_inside += [lax.ppermute(part, 'lat', inside) for part in inner]  7 us
    pallas_call x1, Pallas kernels, on_device(): pl.pallas_call(functools.partial(base_kernel, width), in_specs=[in_hbm, i...  3.97 us
    pallas_call x2, Pallas kernels, run_inverse(): pl.pallas_call(functools.partial(inverse_kernel, radix, len(other)), in_s...  3.23 us
    ppermute x1, starting transfers between devices, on_device(): from_inside = [lax.ppermute(inner, 'lat', inside)]  3 us
    pallas_call x1, Pallas kernels, on_device(): pl.pallas_call(rest_kernel, in_specs=[in_hbm] * 3, out_specs=[whole] * (2...  3 us
    ppermute x1, starting transfers between devices, on_device(): from_inside += [lax.ppermute(part, 'lat', inside) for part in inner]  2.71 us
    pallas_call x2, Pallas kernels, run_physics(): pl.pallas_call(functools.partial(physics_kernel, levels, sector, lat_coun...  2.36 us
  transfers between devices with their start and end apart: 14, of which 6 were waited for; matrix products, arithmetic and copies ran while one was open for 1% of the time, Pallas kernels for 31%

profile of v18, /device:TPU:0, one launch (start us, length us, event | category | flops | bytes accessed | tf_op | source)
XLA Modules:
  0.0 45.9 jit_solution(11124750817682295573)
XLA Ops:
  0.6 1.1 %pack.1 = f32[64,1152]{1,0:T(8,128)S(1)} custom-call(f32[4,32,4,576]{3,2,1,0:T(4,128)} %tracer_hbm.3), custom_call_target="tpu_custom_call" | custom-call | bytes 600000 | tf_op jit(solution)/shard_map/pack/pallas_call | solution.py:389
  1.8 0.0 copy-start.11
  1.8 0.0 copy-start.12
  1.8 0.0 copy-start.14
  1.8 0.0 copy-start.15
  1.8 0.0 copy-start.10
  1.8 3.0 %collective-permute-start.4 = (f32[64,1152]{1,0:T(8,128)S(1)}, f32[64,1152]{1,0:T(8,128)}, u32[]{:S(2)}, u32[]{:S(2)}) collective-permute-start(f32[64,1152]{1,0:T(8,128)S(1)} %pack.1), channel_id=1, source_target_pairs={{0,2},{2,0},{4,6},{6,4},{8,10},{10,8},{12,14},{14,12},{1,3},{3,1},... | collective-permute-start | bytes 884744 | tf_op jit(solution)/shard_map/ppermute | solution.py:399
  4.8 3.0 %rest.1 = (f32[64,1152]{1,0:T(8,128)}, f32[64,1152]{1,0:T(8,128)}, f32[64,1152]{1,0:T(8,128)}, f32[16,1152]{1,0:T(8,128)S(1)}, f32[5,2,32,128]{3,2,1,0:T(8,128)S(1)}) custom-call(f32[4,32,4,576]{3,2,1,0:T(4,128)} %tracer_hbm.3, f32[32,4,576]{2,1,0:T(4,128)} %lat_hbm.1, f32[32,4,576]{2,1,0:T(4,128)} %lon_hbm.1), custom_call_target="tpu_custom_call" | custom-call | tf_op jit(solution)/shard_map/rest/pallas_call | solution.py:402
  7.8 0.0 copy-start.13
  7.9 0.0 copy-start.8
  7.9 1.3 %collective-permute-start.3 = (f32[16,1152]{1,0:T(8,128)S(1)}, f32[16,1152]{1,0:T(8,128)S(1)}, u32[]{:S(2)}, u32[]{:S(2)}) collective-permute-start(f32[16,1152]{1,0:T(8,128)S(1)} %get-tuple-element.52), channel_id=1, source_target_pairs={{2,0},{4,2},{6,4},{8,6},{10,8},{12,10},{14,12},{3,1},{5,3},{7,5},{... | collective-permute-start | bytes 221192 | tf_op jit(solution)/shard_map/ppermute | solution.py:419
  9.2 0.1 collective-permute-start
  9.3 2.7 %collective-permute-start.1 = (f32[64,1152]{1,0:T(8,128)}, f32[64,1152]{1,0:T(8,128)S(1)}, u32[]{:S(2)}, u32[]{:S(2)}) collective-permute-start(f32[64,1152]{1,0:T(8,128)} %get-tuple-element.50), channel_id=1, source_target_pairs={{0,2},{2,0},{4,6},{6,4},{8,10},{10,8},{12,14},{14,12},{1,3},{3,1},... | collective-permute-start | bytes 884744 | tf_op jit(solution)/shard_map/ppermute | solution.py:418
  12.0 1.4 %collective-permute-start.5 = (f32[64,1152]{1,0:T(8,128)}, f32[64,1152]{1,0:T(8,128)}, u32[]{:S(2)}, u32[]{:S(2)}) collective-permute-start(f32[64,1152]{1,0:T(8,128)} %get-tuple-element.57), channel_id=1, source_target_pairs={{2,4},{4,2},{6,8},{8,6},{10,12},{12,10},{3,5},{5,3},{7,9},{9,7},{1... | collective-permute-start | bytes 884744 | tf_op jit(solution)/shard_map/ppermute | solution.py:417
  13.4 0.0 copy-done.11
  13.4 0.0 copy-done.12
  13.4 0.1 select_multiply_fusion.refs_6_.refs_5_
  13.5 0.1 broadcast_in_dim.27
  13.6 0.1 reshape_reshape.3
  13.7 0.0 copy-done.10
  13.7 0.0 collective-permute-done.side_ref
  13.7 0.7 %collective-permute-start.2 = (f32[64,1152]{1,0:T(8,128)}, f32[64,1152]{1,0:T(8,128)S(1)}, u32[]{:S(2)}, u32[]{:S(2)}) collective-permute-start(f32[64,1152]{1,0:T(8,128)} %get-tuple-element.51), channel_id=1, source_target_pairs={{2,4},{4,2},{6,8},{8,6},{10,12},{12,10},{3,5},{5,3},{7,9},{9,7},{1... | collective-permute-start | bytes 884744 | tf_op jit(solution)/shard_map/ppermute | solution.py:417
  14.4 4.0 %base.1 = (f32[4,4,32,640]{3,2,1,0:T(8,128)S(1)}, f32[4,32,640]{2,1,0:T(8,128)S(1)}, f32[4,32,640]{2,1,0:T(8,128)S(1)}) custom-call(f32[4,32,4,576]{3,2,1,0:T(4,128)} %tracer_hbm.3, f32[32,4,576]{2,1,0:T(4,128)} %lat_hbm.1, f32[32,4,576]{2,1,0:T(4,128)} %lon_hbm.1, f32[5,2,32,128]{3,2,1,0:T(8,128)S(1)} %collective-permute-done.side_ref), custom_call_target="tpu_custom_call" | custom-call | tf_op jit(solution)/shard_map/base/pallas_call | solution.py:422
  18.4 0.1 copy.22.refs_8_
  18.5 0.0 collective-permute-done.3.refs_4_
  18.5 0.0 collective-permute-done.4.refs_2_
  18.5 0.0 collective-permute-done.5.refs_3_
  18.5 0.0 copy-start.2
  18.5 0.0 copy-start.3
  18.6 0.0 copy-start.6
  18.6 0.0 copy-start.7
  18.6 1.7 %physics.2 = (f32[4,32,640]{2,1,0:T(8,128)S(1)}, f32[4,32,640]{2,1,0:T(8,128)S(1)}, f32[4,8,640]{2,1,0:T(8,128)S(1)}) custom-call(f32[4,4,32,640]{3,2,1,0:T(8,128)S(1)} %get-tuple-element.48.refs_0_, f32[4,32,640]{2,1,0:T(8,128)S(1)} %get-tuple-element.49.refs_1_, f32[64,1152]{1,0:T(8,128)} %collective-permute-done.4.refs_2_, ...), custom_call_target="tpu_custom_call" | custom-call | tf_op jit(solution)/shard_map/physics/pallas_call | solution.py:464
  20.3 0.0 copy-start
  20.3 0.0 copy-start.1
  20.3 0.0 copy-start.4
  20.3 0.0 copy-start.5
  20.3 0.0 copy-start.9
  20.3 0.2 collective-permute-start.7
  20.6 0.3 collective-permute-start.6
  20.9 0.9 %collective-permute-done.7.refs_1_ = f32[2,32,640]{2,1,0:T(8,128)S(1)} collective-permute-done((f32[2,32,640]{2,1,0:T(8,128)S(1)}, f32[2,32,640]{2,1,0:T(8,128)S(1)}, u32[]{:S(2)}, u32[]{:S(2)}) %collective-permute-start.7) | collective-permute-done | bytes 163872 | tf_op jit(solution)/shard_map/ppermute | solution.py:508
  21.8 0.2 collective-permute-done.6.refs_0_
  22.1 0.0 copy-done.6
  22.1 0.0 copy-done.7
  22.1 0.7 %forward.2 = (bf16[128,1152]{1,0:T(8,128)(2,1)S(1)}, bf16[128,1152]{1,0:T(8,128)(2,1)S(1)}) custom-call(f32[4,32,640]{2,1,0:T(8,128)S(1)} %get-tuple-element.59.own_ref, f32[2,32,640]{2,1,0:T(8,128)S(1)} %collective-permute-done.6.refs_0_, f32[2,32,640]{2,1,0:T(8,128)S(1)} %collective-permute-done.7.refs_1_, bf16[1024,256]{1,0:T(8,128)(2,1)S(1)} %copy-done.3, ...), custom_call_target="tpu_custom_call" | custom-call | tf_op jit(solution)/shard_map/forward/pallas_call | solution.py:481
  22.8 2.0 %inverse.2 = (f32[32,4,576]{2,1,0:T(4,128)S(1)}, f32[4,32,640]{2,1,0:T(8,128)}) custom-call(s32[4]{0:T(128)S(1)} %copy-done.9, f32[4,32,640]{2,1,0:T(8,128)S(1)} %get-tuple-element.59.own_ref, f32[2,32,640]{2,1,0:T(8,128)S(1)} %collective-permute-done.6.refs_0_, f32[2,32,640]{2,1,0:T(8,128)S(1)} %collective-permute-done.7.refs_1_, ...), custom_call_target="tpu_custom_call" | custom-call | tf_op jit(solution)/shard_map/inverse/pallas_call | solution.py:493
  24.8 7.0 %collective-permute-done.1.refs_2_ = f32[64,1152]{1,0:T(8,128)S(1)} collective-permute-done((f32[64,1152]{1,0:T(8,128)}, f32[64,1152]{1,0:T(8,128)S(1)}, u32[]{:S(2)}, u32[]{:S(2)}) %collective-permute-start.1) | collective-permute-done | bytes 294944 | tf_op jit(solution)/shard_map/ppermute | solution.py:418
  31.8 0.0 collective-permute-done.2.refs_3_
  31.8 0.7 %physics.3 = (f32[4,32,640]{2,1,0:T(8,128)S(1)}, f32[4,32,640]{2,1,0:T(8,128)S(1)}, f32[1,128]{1,0:T(1,128)S(1)}) custom-call(f32[4,4,32,640]{3,2,1,0:T(8,128)S(1)} %get-tuple-element.48.refs_0_, f32[4,32,640]{2,1,0:T(8,128)S(1)} %get-tuple-element.49.refs_1_, f32[64,1152]{1,0:T(8,128)S(1)} %collective-permute-done.1.refs_2_, ...), custom_call_target="tpu_custom_call" | custom-call | tf_op jit(solution)/shard_map/physics/pallas_call | solution.py:464
  32.5 0.0 collective-permute-start.9
  32.5 2.4 %collective-permute-start.8 = (f32[1,128]{1,0:T(1,128)S(1)}, f32[1,128]{1,0:T(1,128)S(1)}, u32[]{:S(2)}, u32[]{:S(2)}) collective-permute-start(f32[1,128]{1,0:T(1,128)S(1)} %get-tuple-element.66), channel_id=1, source_target_pairs={{0,2},{2,0},{4,6},{6,4},{8,10},{10,8},{12,14},{14,12},{1,3},{3,1},... | collective-permute-start | bytes 1544 | tf_op jit(solution)/shard_map/ppermute | solution.py:519
  34.9 0.0 collective-permute-done.9.refs_0_
  34.9 0.7 %forward.3 = (bf16[128,1152]{1,0:T(8,128)(2,1)S(1)}, bf16[128,1152]{1,0:T(8,128)(2,1)S(1)}) custom-call(f32[4,32,640]{2,1,0:T(8,128)S(1)} %get-tuple-element.67.own_ref, f32[4,32,640]{2,1,0:T(8,128)S(1)} %collective-permute-done.9.refs_0_, bf16[1024,256]{1,0:T(8,128)(2,1)S(1)} %copy-done.3, bf16[1024,256]{1,0:T(8,128)(2,1)S(1)} %copy-done.2, ...), custom_call_target="tpu_custom_call" | custom-call | tf_op jit(solution)/shard_map/forward/pallas_call | solution.py:481
  35.6 0.8 %collective-permute-done.8 = f32[1,128]{1,0:T(1,128)S(1)} collective-permute-done((f32[1,128]{1,0:T(1,128)S(1)}, f32[1,128]{1,0:T(1,128)S(1)}, u32[]{:S(2)}, u32[]{:S(2)}) %collective-permute-start.8) | collective-permute-done | bytes 544 | tf_op jit(solution)/shard_map/ppermute | solution.py:519
  36.5 2.5 %collective-permute-start.10 = (f32[1,128]{1,0:T(1,128)S(1)}, f32[1,128]{1,0:T(1,128)S(1)}, u32[]{:S(2)}, u32[]{:S(2)}) collective-permute-start(f32[1,128]{1,0:T(1,128)S(1)} %add.44), channel_id=1, source_target_pairs={{0,4},{2,6},{4,0},{6,2},{8,12},{10,14},{12,8},{14,10},{1,5},{3,7},... | collective-permute-start | bytes 1544 | tf_op jit(solution)/shard_map/ppermute | solution.py:519
  39.0 0.0 collective-permute-start.12
  39.0 1.3 %inverse.3 = (f32[32,4,576]{2,1,0:T(4,128)S(1)}, f32[4,32,640]{2,1,0:T(8,128)S(1)}) custom-call(s32[4]{0:T(128)S(1)} %copy-done.9, f32[4,32,640]{2,1,0:T(8,128)S(1)} %get-tuple-element.67.own_ref, f32[4,32,640]{2,1,0:T(8,128)S(1)} %collective-permute-done.9.refs_0_, bf16[128,1152]{1,0:T(8,128)(2,1)S(1)} %get-tuple-element.73.refs_1_, ...), custom_call_target="tpu_custom_call" | custom-call | tf_op jit(solution)/shard_map/inverse/pallas_call | solution.py:493
  40.2 0.3 collective-permute-done.10
  40.5 0.3 collective-permute-start.13
  40.8 2.7 %collective-permute-start.11 = (f32[1,128]{1,0:T(1,128)S(1)}, f32[1,128]{1,0:T(1,128)S(1)}, u32[]{:S(2)}, u32[]{:S(2)}) collective-permute-start(f32[1,128]{1,0:T(1,128)S(1)} %add.45), channel_id=1, source_target_pairs={{0,8},{2,10},{4,12},{6,14},{8,0},{10,2},{12,4},{14,6},{1,9},{3,11}... | collective-permute-start | bytes 1544 | tf_op jit(solution)/shard_map/ppermute | solution.py:519
  43.5 0.0 collective-permute-done.12.refs_2_
  43.5 0.0 collective-permute-done.13.refs_3_
  43.5 1.2 %finish.1 = f32[4,32,4,576]{3,2,1,0:T(4,128)} custom-call(f32[32,4,576]{2,1,0:T(4,128)S(1)} %get-tuple-element.79.refs_0_, f32[32,4,576]{2,1,0:T(4,128)S(1)} %get-tuple-element.80.refs_1_, f32[4,32,640]{2,1,0:T(8,128)S(1)} %collective-permute-done.12.refs_2_, f32[4,32,640]{2,1,0:T(8,128)S(1)} %collective-permute-done.13.refs_3_), custom_call_target="tpu_custom_call" | custom-call | bytes 3000000 | tf_op jit(solution)/shard_map/finish/pallas_call | solution.py:539
  44.7 0.5 %collective-permute-done.11 = f32[1,128]{1,0:T(1,128)S(1)} collective-permute-done((f32[1,128]{1,0:T(1,128)S(1)}, f32[1,128]{1,0:T(1,128)S(1)}, u32[]{:S(2)}, u32[]{:S(2)}) %collective-permute-start.11) | collective-permute-done | bytes 544 | tf_op jit(solution)/shard_map/ppermute | solution.py:519
  45.3 0.6 %fusion.1 = f32[1,1]{1,0:T(1,128)} fusion(f32[1,128]{1,0:T(1,128)S(1)} %add.46, s32[]{:T(128)S(6)} %select_n.8), kind=kLoop, calls=%fused_computation.4 | loop fusion | flops 1 | bytes 12 | tf_op jit(solution)/shard_map/div | solution.py:557
  (19 shorter events, 0.1 us)
Async XLA Ops:
  1.8 11.6 %copy-start.11 = (f32[1152]{0:T(1024)S(1)}, f32[1152]{0:T(1024)}, u32[]{:S(2)}) copy-start(f32[1152]{0:T(1024)} %constant.56.clone) | copy-start | bytes 13828
  1.8 11.6 %copy-start.12 = (f32[1152]{0:T(1024)S(1)}, f32[1152]{0:T(1024)}, u32[]{:S(2)}) copy-start(f32[1152]{0:T(1024)} %constant.54.clone) | copy-start | bytes 13828
  1.8 11.6 %copy-start.14 = (pred[1152]{0:T(1024)(128)(4,1)S(1)}, pred[1152]{0:T(1024)(128)(4,1)}, u32[]{:S(2)}) copy-start(pred[1152]{0:T(1024)(128)(4,1)} %constant.55.clone) | copy-start | bytes 3460
  1.8 11.7 %copy-start.15 = (s32[1,1,18,1]{2,3,1,0:T(1,128)S(1)}, s32[1,1,18,1]{2,3,1,0:T(1,128)}, u32[]{:S(2)}) copy-start(s32[1,1,18,1]{2,3,1,0:T(1,128)} %param.25) | copy-start | bytes 220
  1.8 11.8 %copy-start.10 = (f32[4,4,576]{2,1,0:T(4,128)S(1)}, f32[4,4,576]{2,1,0:T(4,128)}, u32[]{:S(2)}) copy-start(f32[4,4,576]{2,1,0:T(4,128)} %param.22) | copy-start | bytes 110596
  1.8 16.6 %collective-permute-start.4 = (f32[64,1152]{1,0:T(8,128)S(1)}, f32[64,1152]{1,0:T(8,128)}, u32[]{:S(2)}, u32[]{:S(2)}) collective-permute-start(f32[64,1152]{1,0:T(8,128)S(1)} %pack.1), channel_id=1, source_target_pairs={{0,2},{2,0},{4,6},{6,4},{8,10},{10,8},{12,14},{14,12},{1,3},{3,1},... | collective-permute-start | bytes 884744 | tf_op jit(solution)/shard_map/ppermute | solution.py:399
  7.8 10.5 %copy-start.13 = (f32[4,32]{1,0:T(4,128)S(1)}, f32[4,32]{1,0:T(4,128)}, u32[]{:S(2)}) copy-start(f32[4,32]{1,0:T(4,128)} %param.24) | copy-start | bytes 1540
  7.9 10.7 %copy-start.8 = (f32[32,32]{1,0:T(8,128)S(1)}, f32[32,32]{1,0:T(8,128)}, u32[]{:S(2)}) copy-start(f32[32,32]{1,0:T(8,128)} %refs_7_.4) | copy-start | bytes 12292
  7.9 10.6 %collective-permute-start.3 = (f32[16,1152]{1,0:T(8,128)S(1)}, f32[16,1152]{1,0:T(8,128)S(1)}, u32[]{:S(2)}, u32[]{:S(2)}) collective-permute-start(f32[16,1152]{1,0:T(8,128)S(1)} %get-tuple-element.52), channel_id=1, source_target_pairs={{2,0},{4,2},{6,4},{8,6},{10,8},{12,10},{14,12},{3,1},{5,3},{7,5},{... | collective-permute-start | bytes 221192 | tf_op jit(solution)/shard_map/ppermute | solution.py:419
  9.2 4.5 %collective-permute-start = (f32[5,2,32,128]{3,2,1,0:T(8,128)S(1)}, f32[5,2,32,128]{3,2,1,0:T(8,128)S(1)}, u32[]{:S(2)}, u32[]{:S(2)}) collective-permute-start(f32[5,2,32,128]{3,2,1,0:T(8,128)S(1)} %get-tuple-element.46), channel_id=1, source_target_pairs={{0,1},{1,0},{2,3},{3,2},{4,5},{5,4},{6,7},{7,6},{8,9},{9,8},{10,11... | collective-permute-start | bytes 491528 | tf_op jit(solution)/shard_map/ppermute | solution.py:421
  9.3 22.5 %collective-permute-start.1 = (f32[64,1152]{1,0:T(8,128)}, f32[64,1152]{1,0:T(8,128)S(1)}, u32[]{:S(2)}, u32[]{:S(2)}) collective-permute-start(f32[64,1152]{1,0:T(8,128)} %get-tuple-element.50), channel_id=1, source_target_pairs={{0,2},{2,0},{4,6},{6,4},{8,10},{10,8},{12,14},{14,12},{1,3},{3,1},... | collective-permute-start | bytes 884744 | tf_op jit(solution)/shard_map/ppermute | solution.py:418
  12.0 6.5 %collective-permute-start.5 = (f32[64,1152]{1,0:T(8,128)}, f32[64,1152]{1,0:T(8,128)}, u32[]{:S(2)}, u32[]{:S(2)}) collective-permute-start(f32[64,1152]{1,0:T(8,128)} %get-tuple-element.57), channel_id=1, source_target_pairs={{2,4},{4,2},{6,8},{8,6},{10,12},{12,10},{3,5},{5,3},{7,9},{9,7},{1... | collective-permute-start | bytes 884744 | tf_op jit(solution)/shard_map/ppermute | solution.py:417
  13.7 18.1 %collective-permute-start.2 = (f32[64,1152]{1,0:T(8,128)}, f32[64,1152]{1,0:T(8,128)S(1)}, u32[]{:S(2)}, u32[]{:S(2)}) collective-permute-start(f32[64,1152]{1,0:T(8,128)} %get-tuple-element.51), channel_id=1, source_target_pairs={{2,4},{4,2},{6,8},{8,6},{10,12},{12,10},{3,5},{5,3},{7,9},{9,7},{1... | collective-permute-start | bytes 884744 | tf_op jit(solution)/shard_map/ppermute | solution.py:417
  18.5 3.5 %copy-start.2 = (bf16[1024,256]{1,0:T(8,128)(2,1)S(1)}, bf16[1024,256]{1,0:T(8,128)(2,1)}, u32[]{:S(2)}) copy-start(bf16[1024,256]{1,0:T(8,128)(2,1)} %constant.58.clone.refs_3_.refs_2_) | copy-start | bytes 1572868
  18.5 3.5 %copy-start.3 = (bf16[1024,256]{1,0:T(8,128)(2,1)S(1)}, bf16[1024,256]{1,0:T(8,128)(2,1)}, u32[]{:S(2)}) copy-start(bf16[1024,256]{1,0:T(8,128)(2,1)} %constant.57.clone.refs_2_.refs_1_) | copy-start | bytes 1572868
  18.6 3.5 %copy-start.6 = (bf16[128,128]{1,0:T(8,128)(2,1)S(1)}, bf16[128,128]{1,0:T(8,128)(2,1)}, u32[]{:S(2)}) copy-start(bf16[128,128]{1,0:T(8,128)(2,1)} %constant.60.clone.refs_5_.refs_4_) | copy-start | bytes 98308
  18.6 3.5 %copy-start.7 = (bf16[128,128]{1,0:T(8,128)(2,1)S(1)}, bf16[128,128]{1,0:T(8,128)(2,1)}, u32[]{:S(2)}) copy-start(bf16[128,128]{1,0:T(8,128)(2,1)} %constant.59.clone.refs_4_.refs_3_) | copy-start | bytes 98308
  20.3 2.5 %copy-start = (bf16[1024,256]{1,0:T(8,128)(2,1)S(1)}, bf16[1024,256]{1,0:T(8,128)(2,1)}, u32[]{:S(2)}) copy-start(bf16[1024,256]{1,0:T(8,128)(2,1)} %constant.62.clone.refs_5_.refs_4_) | copy-start | bytes 1572868
  20.3 2.5 %copy-start.1 = (bf16[1024,256]{1,0:T(8,128)(2,1)S(1)}, bf16[1024,256]{1,0:T(8,128)(2,1)}, u32[]{:S(2)}) copy-start(bf16[1024,256]{1,0:T(8,128)(2,1)} %constant.61.clone.refs_4_.refs_3_) | copy-start | bytes 1572868
  20.3 2.5 %copy-start.4 = (bf16[128,128]{1,0:T(8,128)(2,1)S(1)}, bf16[128,128]{1,0:T(8,128)(2,1)}, u32[]{:S(2)}) copy-start(bf16[128,128]{1,0:T(8,128)(2,1)} %constant.64.clone.refs_7_.refs_6_) | copy-start | bytes 98308
  20.3 2.5 %copy-start.5 = (bf16[128,128]{1,0:T(8,128)(2,1)S(1)}, bf16[128,128]{1,0:T(8,128)(2,1)}, u32[]{:S(2)}) copy-start(bf16[128,128]{1,0:T(8,128)(2,1)} %constant.63.clone.refs_6_.refs_5_) | copy-start | bytes 98308
  20.3 2.5 %copy-start.9 = (s32[4]{0:T(128)S(1)}, s32[4]{0:T(128)}, u32[]{:S(2)}) copy-start(s32[4]{0:T(128)} %mask_ref.3) | copy-start | bytes 52
  20.3 1.5 %collective-permute-start.7 = (f32[2,32,640]{2,1,0:T(8,128)S(1)}, f32[2,32,640]{2,1,0:T(8,128)S(1)}, u32[]{:S(2)}, u32[]{:S(2)}) collective-permute-start(f32[2,32,640]{2,1,0:T(8,128)S(1)} %get-tuple-element.84), channel_id=1, source_target_pairs={{0,1},{1,0},{2,3},{3,2},{4,5},{5,4},{6,7},{7,6},{8,9},{9,8},{10,11... | collective-permute-start | bytes 491528 | tf_op jit(solution)/shard_map/ppermute | solution.py:508
  20.6 1.5 %collective-permute-start.6 = (f32[2,32,640]{2,1,0:T(8,128)S(1)}, f32[2,32,640]{2,1,0:T(8,128)S(1)}, u32[]{:S(2)}, u32[]{:S(2)}) collective-permute-start(f32[2,32,640]{2,1,0:T(8,128)S(1)} %get-tuple-element.85), channel_id=1, source_target_pairs={{0,1},{1,0},{2,3},{3,2},{4,5},{5,4},{6,7},{7,6},{8,9},{9,8},{10,11... | collective-permute-start | bytes 491528 | tf_op jit(solution)/shard_map/ppermute | solution.py:508
  32.5 2.5 %collective-permute-start.9 = (f32[4,32,640]{2,1,0:T(8,128)S(1)}, f32[4,32,640]{2,1,0:T(8,128)S(1)}, u32[]{:S(2)}, u32[]{:S(2)}) collective-permute-start(f32[4,32,640]{2,1,0:T(8,128)S(1)} %get-tuple-element.68), channel_id=1, source_target_pairs={{0,1},{1,0},{2,3},{3,2},{4,5},{5,4},{6,7},{7,6},{8,9},{9,8},{10,11... | collective-permute-start | bytes 983048 | tf_op jit(solution)/shard_map/ppermute | solution.py:522
  32.5 4.0 %collective-permute-start.8 = (f32[1,128]{1,0:T(1,128)S(1)}, f32[1,128]{1,0:T(1,128)S(1)}, u32[]{:S(2)}, u32[]{:S(2)}) collective-permute-start(f32[1,128]{1,0:T(1,128)S(1)} %get-tuple-element.66), channel_id=1, source_target_pairs={{0,2},{2,0},{4,6},{6,4},{8,10},{10,8},{12,14},{14,12},{1,3},{3,1},... | collective-permute-start | bytes 1544 | tf_op jit(solution)/shard_map/ppermute | solution.py:519
  36.5 4.0 %collective-permute-start.10 = (f32[1,128]{1,0:T(1,128)S(1)}, f32[1,128]{1,0:T(1,128)S(1)}, u32[]{:S(2)}, u32[]{:S(2)}) collective-permute-start(f32[1,128]{1,0:T(1,128)S(1)} %add.44), channel_id=1, source_target_pairs={{0,4},{2,6},{4,0},{6,2},{8,12},{10,14},{12,8},{14,10},{1,5},{3,7},... | collective-permute-start | bytes 1544 | tf_op jit(solution)/shard_map/ppermute | solution.py:519
  39.0 4.6 %collective-permute-start.12 = (f32[4,32,640]{2,1,0:T(8,128)}, f32[4,32,640]{2,1,0:T(8,128)S(1)}, u32[]{:S(2)}, u32[]{:S(2)}) collective-permute-start(f32[4,32,640]{2,1,0:T(8,128)} %get-tuple-element.64), channel_id=1, source_target_pairs={{0,1},{1,0},{2,3},{3,2},{4,5},{5,4},{6,7},{7,6},{8,9},{9,8},{10,11... | collective-permute-start | bytes 983048 | tf_op jit(solution)/shard_map/ppermute | solution.py:512
  40.5 3.0 %collective-permute-start.13 = (f32[4,32,640]{2,1,0:T(8,128)S(1)}, f32[4,32,640]{2,1,0:T(8,128)S(1)}, u32[]{:S(2)}, u32[]{:S(2)}) collective-permute-start(f32[4,32,640]{2,1,0:T(8,128)S(1)} %get-tuple-element.81), channel_id=1, source_target_pairs={{0,1},{1,0},{2,3},{3,2},{4,5},{5,4},{6,7},{7,6},{8,9},{9,8},{10,11... | collective-permute-start | bytes 983048 | tf_op jit(solution)/shard_map/ppermute | solution.py:536
  40.8 4.4 %collective-permute-start.11 = (f32[1,128]{1,0:T(1,128)S(1)}, f32[1,128]{1,0:T(1,128)S(1)}, u32[]{:S(2)}, u32[]{:S(2)}) collective-permute-start(f32[1,128]{1,0:T(1,128)S(1)} %add.45), channel_id=1, source_target_pairs={{0,8},{2,10},{4,12},{6,14},{8,0},{10,2},{12,4},{14,6},{1,9},{3,11}... | collective-permute-start | bytes 1544 | tf_op jit(solution)/shard_map/ppermute | solution.py:519
